TPU v7x, 256 devices: a whole 4x4x8 slice. The times are simulated.
256 devices in a mesh: seq: 64 (over x, z, y_hi), ch: 4 (over y_lo, core).
Axes of the slice: x: 4, y: 4 (y_hi: 2, y_lo: 2; y = y_hi * 2 + y_lo), z: 8, core: 2. Of those that a mesh axis runs over, the one named last changes fastest.
Arguments:
- bins_in: bfloat16 [65536, 1536], P('seq', 'ch'), may hold values from -6 to 6
- pre_scale: float32 [3, 1536], P(None, 'ch'), may hold values from 0.5 to 2
- pre_shift: float32 [3, 1536], P(None, 'ch'), may hold values from -1 to 1
- conv_weight: bfloat16 [3, 3, 1536, 1536], P(None, None, None, 'ch'), may hold values from -0.09375 to 0.09375
- conv_bias: float32 [3, 1536], P(None, 'ch'), may hold values from -0.5 to 0.5
Outputs:
- bins_out: bfloat16 [65536, 1536], P('seq', 'ch')
All inputs are finite; a program needn't handle non-finite values.
Results may differ from a plain program's by a relative error of at most 0.015.
Values may be sent and summed in bfloat16 or wider, within the bound.
No kernel may reach another device: no remote copies, remote signals or barrier semaphores. Data moves between devices by JAX's collectives and lax.ppermute only.
A program may use at most 64 MiB of HBM per device.

v0:
```python
import jax
import jax.numpy as jnp
from jax import lax
from jax.sharding import PartitionSpec as P

LAYERS = 3
FIRST_SPACING1 = 64
SECOND_SPACING2 = 512
THIRD_SPACING3 = 4096


def shifted(array, axis, by):
    size = lax.axis_size(axis)
    pairs = [(i, i + by) for i in range(size) if 0 <= i + by < size]
    return lax.ppermute(array, axis, pairs)


def neighbours(source, dilation, bin_rows):
    if dilation < bin_rows:
        to_next = source[bin_rows - dilation :]
        to_prev = source[:dilation]
        hop_count = 1
    else:
        to_next = source
        to_prev = source
        hop_count = dilation // bin_rows
    lower_rim = shifted(to_next, "seq", hop_count)
    upper_rim = shifted(to_prev, "seq", -hop_count)
    return (lower_rim, upper_rim)


def arrange(lower_rim, centre, upper_rim, dilation, bin_rows):
    if dilation < bin_rows:
        extended = jnp.concatenate([lower_rim, centre, upper_rim], axis=0)
        return (extended[:bin_rows], centre, extended[2 * dilation : 2 * dilation + bin_rows])
    return (lower_rim, centre, upper_rim)


def per_device(bins_in, pre_scale, pre_shift, conv_weight, conv_bias):
    layer_spacings = (FIRST_SPACING1, SECOND_SPACING2, THIRD_SPACING3)
    bin_rows = bins_in.shape[0]
    stream = bins_in
    for layer_index in range(LAYERS):
        dilation = layer_spacings[layer_index]
        activated = jax.nn.gelu(
            stream.astype(jnp.float32) * pre_scale[layer_index] + pre_shift[layer_index],
            approximate=False,
        ).astype(jnp.bfloat16)
        weights = conv_weight[layer_index]
        gathered = lax.all_gather(activated, "ch", axis=1, tiled=True)
        lower_rim, upper_rim = neighbours(gathered, dilation, bin_rows)
        tap_inputs = arrange(lower_rim, gathered, upper_rim, dilation, bin_rows)
        summed = jnp.dot(tap_inputs[0], weights[0], preferred_element_type=jnp.float32)
        summed = summed + jnp.dot(tap_inputs[1], weights[1], preferred_element_type=jnp.float32)
        summed = summed + jnp.dot(tap_inputs[2], weights[2], preferred_element_type=jnp.float32)
        stream = (stream.astype(jnp.float32) + summed + conv_bias[layer_index]).astype(jnp.bfloat16)
    return stream


def solution(mesh):
    return jax.shard_map(
        per_device,
        mesh=mesh,
        in_specs=(
            P("seq", "ch"),
            P(None, "ch"),
            P(None, "ch"),
            P(None, None, None, "ch"),
            P(None, "ch"),
        ),
        out_specs=P("seq", "ch"),
        check_vma=False,
    )
```

profile of v0, /device:TPU:6, one launch (start us, length us, event | category | flops | bytes accessed | tf_op | source)
XLA Modules:
  0.0 410.4 jit_solution(4895235360986012002)
XLA Ops:
  7.4 5.3 %fusion.12 = bf16[1024,384]{1,0:T(8,128)(2,1)} fusion(bf16[1024,384]{1,0:T(8,128)(2,1)} %param.5, f32[384]{0:T(512)S(1)} %get-tuple-element.12, f32[384]{0:T(512)S(1)} %get-tuple-element.23), kind=kLoop, calls=%fused_computation.25 | loop fusion | flops 26738688 | bytes 1575936 | tf_op jit(solution)/shard_map/convert_element_type | solution.py:48
  12.9 43.0 %all-gather.4.cloned.1.call-done = bf16[1024,1536]{1,0:T(8,128)(2,1)} async-done(((bf16[1024,384]{1,0:T(8,128)(2,1)}), bf16[1024,1536]{1,0:T(8,128)(2,1)}) %all-gather.4.cloned.1.call-update) | async-done | bytes 3145744 | tf_op jit(solution)/shard_map/all_gather | solution.py:50
  55.8 1.0 fusion.117
  56.9 4.6 %collective-permute-start = (bf16[64,1536]{1,0:T(8,128)(2,1)S(1)}, bf16[64,1536]{1,0:T(8,128)(2,1)S(1)}, u32[]{:S(2)}, u32[]{:S(2)}) collective-permute-start(bf16[64,1536]{1,0:T(8,128)(2,1)S(1)} %get-tuple-element.17), channel_id=1, source_target_pairs={{0,4},{4,8},{8,12},{12,16},{16,20},{20,24},{24,28},{28,32},{32,36}... | collective-permute-start | bytes 589832 | tf_op jit(solution)/shard_map/ppermute | solution.py:15
  61.5 6.0 %collective-permute-start.1 = (bf16[64,1536]{1,0:T(8,128)(2,1)S(1)}, bf16[64,1536]{1,0:T(8,128)(2,1)S(1)}, u32[]{:S(2)}, u32[]{:S(2)}) collective-permute-start(bf16[64,1536]{1,0:T(8,128)(2,1)S(1)} %get-tuple-element.16), channel_id=1, source_target_pairs={{4,0},{8,4},{12,8},{16,12},{20,16},{24,20},{28,24},{32,28},{36,32}... | collective-permute-start | bytes 589832 | tf_op jit(solution)/shard_map/ppermute | solution.py:15
  67.5 4.0 fusion.94
  71.6 3.1 fusion.6
  74.9 7.9 %fusion.26 = (bf16[1024,384]{1,0:T(8,128)(2,1)}, bf16[1024,384]{1,0:T(8,128)(2,1)S(1)}) fusion(f32[384]{0:T(512)S(1)} %get-tuple-element.13, f32[384]{0:T(512)S(1)} %get-tuple-element.22, f32[384]{0:T(512)S(1)} %get-tuple-element.6, bf16[3,3,1536,384]{3,2,1,0:T(8,128)(2,1)} %param.8, bf16[64,1536]{1,0:T(8,128)(2,1)S(1)} %collective-permute-done.1, ...), kind=kOutput, calls=%fused_computation.39 | convolution fusion | flops 1243348992 | bytes 10031616 | tf_op jit(solution)/shard_map/dot_general | solution.py:55
  82.9 41.2 %all-gather.6.cloned.1.call-done = bf16[1024,1536]{1,0:T(8,128)(2,1)} async-done(((bf16[1024,384]{1,0:T(8,128)(2,1)}), bf16[1024,1536]{1,0:T(8,128)(2,1)}) %all-gather.6.cloned.1.call-update) | async-done | bytes 3145744 | tf_op jit(solution)/shard_map/all_gather | solution.py:50
  124.1 2.2 fusion.116
  126.3 4.6 %collective-permute-start.2 = (bf16[512,1536]{1,0:T(8,128)(2,1)S(1)}, bf16[512,1536]{1,0:T(8,128)(2,1)S(1)}, u32[]{:S(2)}, u32[]{:S(2)}) collective-permute-start(bf16[512,1536]{1,0:T(8,128)(2,1)S(1)} %get-tuple-element.15), channel_id=1, source_target_pairs={{0,4},{4,8},{8,12},{12,16},{16,20},{20,24},{24,28},{28,32},{32,36}... | collective-permute-start | bytes 4718600 | tf_op jit(solution)/shard_map/ppermute | solution.py:15
  131.0 5.9 %collective-permute-start.3 = (bf16[512,1536]{1,0:T(8,128)(2,1)S(1)}, bf16[512,1536]{1,0:T(8,128)(2,1)S(1)}, u32[]{:S(2)}, u32[]{:S(2)}) collective-permute-start(bf16[512,1536]{1,0:T(8,128)(2,1)S(1)} %get-tuple-element.14), channel_id=1, source_target_pairs={{4,0},{8,4},{12,8},{16,12},{20,16},{24,20},{28,24},{32,28},{36,32}... | collective-permute-start | bytes 4718600 | tf_op jit(solution)/shard_map/ppermute | solution.py:15
  136.9 3.1 fusion.90
  140.0 59.1 %collective-permute-done.2 = bf16[512,1536]{1,0:T(8,128)(2,1)S(1)} collective-permute-done((bf16[512,1536]{1,0:T(8,128)(2,1)S(1)}, bf16[512,1536]{1,0:T(8,128)(2,1)S(1)}, u32[]{:S(2)}, u32[]{:S(2)}) %collective-permute-start.2) | collective-permute-done | bytes 1572896 | tf_op jit(solution)/shard_map/ppermute | solution.py:15
  199.1 3.0 fusion.2
  202.2 1.2 collective-permute-done.3
  203.4 7.5 %fusion.40 = (bf16[1024,384]{1,0:T(8,128)(2,1)}, bf16[1024,384]{1,0:T(8,128)(2,1)S(1)}) fusion(f32[384]{0:T(512)S(1)} %get-tuple-element.11, f32[384]{0:T(512)S(1)} %get-tuple-element.24, f32[384]{0:T(512)S(1)} %get-tuple-element.7, bf16[3,3,1536,384]{3,2,1,0:T(8,128)(2,1)} %param.8, bf16[512,1536]{1,0:T(8,128)(2,1)S(1)} %collective-permute-done.3, ...), kind=kOutput, calls=%fused_computation.53 | convolution fusion | flops 1243348992 | bytes 11407872 | tf_op jit(solution)/shard_map/dot_general | solution.py:55
  210.9 41.2 %all-gather.8.cloned.1.call-done = bf16[1024,1536]{1,0:T(8,128)(2,1)} async-done(((bf16[1024,384]{1,0:T(8,128)(2,1)}), bf16[1024,1536]{1,0:T(8,128)(2,1)}) %all-gather.8.cloned.1.call-update) | async-done | bytes 3145744 | tf_op jit(solution)/shard_map/all_gather | solution.py:50
  252.1 4.4 %collective-permute-start.4 = (bf16[1024,1536]{1,0:T(8,128)(2,1)}, bf16[1024,1536]{1,0:T(8,128)(2,1)S(1)}, u32[]{:S(2)}, u32[]{:S(2)}) collective-permute-start(bf16[1024,1536]{1,0:T(8,128)(2,1)} %all-gather.8.cloned.1.call-done), channel_id=1, source_target_pairs={{0,16},{4,20},{8,24},{12,28},{16,32},{20,36},{24,40},{28,44},{32,4... | collective-permute-start | bytes 9437192 | tf_op jit(solution)/shard_map/ppermute | solution.py:15
  256.5 4.4 %collective-permute-start.5 = (bf16[1024,1536]{1,0:T(8,128)(2,1)}, bf16[1024,1536]{1,0:T(8,128)(2,1)S(1)}, u32[]{:S(2)}, u32[]{:S(2)}) collective-permute-start(bf16[1024,1536]{1,0:T(8,128)(2,1)} %all-gather.8.cloned.1.call-done), channel_id=1, source_target_pairs={{16,0},{20,4},{24,8},{28,12},{32,16},{36,20},{40,24},{44,28},{48,3... | collective-permute-start | bytes 9437192 | tf_op jit(solution)/shard_map/ppermute | solution.py:15
  260.9 4.0 fusion.85
  264.9 131.7 %collective-permute-done.4 = bf16[1024,1536]{1,0:T(8,128)(2,1)S(1)} collective-permute-done((bf16[1024,1536]{1,0:T(8,128)(2,1)}, bf16[1024,1536]{1,0:T(8,128)(2,1)S(1)}, u32[]{:S(2)}, u32[]{:S(2)}) %collective-permute-start.4) | collective-permute-done | bytes 3145760 | tf_op jit(solution)/shard_map/ppermute | solution.py:15
  396.7 3.1 fusion.87
  399.7 4.1 %fusion.49 = bf16[1024,384]{1,0:T(8,128)(2,1)} fusion(bf16[1024,384]{1,0:T(8,128)(2,1)S(1)} %get-tuple-element.21, f32[1024,384]{1,0:T(8,128)S(1)} %fusion.87, f32[1024,384]{1,0:T(8,128)S(1)} %fusion.85, bf16[1024,1536]{1,0:T(8,128)(2,1)S(1)} %collective-permute-done.5, bf16[3,3,1536,384]{3,2,1,0:T(8,128)(2,1)} %param.8, f32[384]{0:T(512)S(1)} %get-tuple-element.5), kind=kOutput, calls=%fused_computation.62 | convolution fusion | flops 1210318848 | bytes 9045504 | tf_op jit(solution)/shard_map/dot_general | solution.py:55
  (19 shorter events, 1.3 us)
Async XLA Ops:
  6.5 6.3 %copy-start.3 = (f32[3,384]{1,0:T(4,128)S(1)}, f32[3,384]{1,0:T(4,128)}, u32[]{:S(2)}) copy-start(f32[3,384]{1,0:T(4,128)} %param.9) | copy-start | bytes 13828
  6.5 49.3 %all-gather.4.cloned.1.call-start = ((), (), s32[]{:S(2)}) async-start(), calls=%async_computation | async-start | bytes 3932160 | tf_op jit(solution)/shard_map/all_gather | solution.py:50
  12.8 111.3 %all-gather.6.cloned.1.call-start = ((), (), s32[]{:S(2)}) async-start(), calls=%async_computation.1 | async-start | bytes 3932160 | tf_op jit(solution)/shard_map/all_gather | solution.py:50
  56.9 14.7 %collective-permute-start = (bf16[64,1536]{1,0:T(8,128)(2,1)S(1)}, bf16[64,1536]{1,0:T(8,128)(2,1)S(1)}, u32[]{:S(2)}, u32[]{:S(2)}) collective-permute-start(bf16[64,1536]{1,0:T(8,128)(2,1)S(1)} %get-tuple-element.17), channel_id=1, source_target_pairs={{0,4},{4,8},{8,12},{12,16},{16,20},{20,24},{24,28},{28,32},{32,36}... | collective-permute-start | bytes 589832 | tf_op jit(solution)/shard_map/ppermute | solution.py:15
  61.5 10.0 %copy-start.2 = (bf16[1024,1536]{1,0:T(8,128)(2,1)S(1)}, bf16[1024,1536]{1,0:T(8,128)(2,1)}, u32[]{:S(2)}) copy-start(bf16[1024,1536]{1,0:T(8,128)(2,1)} %all-gather.4.cloned.1.call-done) | copy-start | bytes 9437188
  61.5 13.4 %collective-permute-start.1 = (bf16[64,1536]{1,0:T(8,128)(2,1)S(1)}, bf16[64,1536]{1,0:T(8,128)(2,1)S(1)}, u32[]{:S(2)}, u32[]{:S(2)}) collective-permute-start(bf16[64,1536]{1,0:T(8,128)(2,1)S(1)} %get-tuple-element.16), channel_id=1, source_target_pairs={{4,0},{8,4},{12,8},{16,12},{20,16},{24,20},{28,24},{32,28},{36,32}... | collective-permute-start | bytes 589832 | tf_op jit(solution)/shard_map/ppermute | solution.py:15
  71.5 3.4 copy-start.1
  82.8 169.2 %all-gather.8.cloned.1.call-start = ((), (), s32[]{:S(2)}) async-start(), calls=%async_computation.2 | async-start | bytes 3932160 | tf_op jit(solution)/shard_map/all_gather | solution.py:50
  124.1 12.8 %copy-start = (bf16[1024,1536]{1,0:T(8,128)(2,1)S(1)}, bf16[1024,1536]{1,0:T(8,128)(2,1)}, u32[]{:S(2)}) copy-start(bf16[1024,1536]{1,0:T(8,128)(2,1)} %all-gather.6.cloned.1.call-done) | copy-start | bytes 9437188
  126.3 72.8 %collective-permute-start.2 = (bf16[512,1536]{1,0:T(8,128)(2,1)S(1)}, bf16[512,1536]{1,0:T(8,128)(2,1)S(1)}, u32[]{:S(2)}, u32[]{:S(2)}) collective-permute-start(bf16[512,1536]{1,0:T(8,128)(2,1)S(1)} %get-tuple-element.15), channel_id=1, source_target_pairs={{0,4},{4,8},{8,12},{12,16},{16,20},{20,24},{24,28},{28,32},{32,36}... | collective-permute-start | bytes 4718600 | tf_op jit(solution)/shard_map/ppermute | solution.py:15
  131.0 72.4 %collective-permute-start.3 = (bf16[512,1536]{1,0:T(8,128)(2,1)S(1)}, bf16[512,1536]{1,0:T(8,128)(2,1)S(1)}, u32[]{:S(2)}, u32[]{:S(2)}) collective-permute-start(bf16[512,1536]{1,0:T(8,128)(2,1)S(1)} %get-tuple-element.14), channel_id=1, source_target_pairs={{4,0},{8,4},{12,8},{16,12},{20,16},{24,20},{28,24},{32,28},{36,32}... | collective-permute-start | bytes 4718600 | tf_op jit(solution)/shard_map/ppermute | solution.py:15
  252.1 144.6 %collective-permute-start.4 = (bf16[1024,1536]{1,0:T(8,128)(2,1)}, bf16[1024,1536]{1,0:T(8,128)(2,1)S(1)}, u32[]{:S(2)}, u32[]{:S(2)}) collective-permute-start(bf16[1024,1536]{1,0:T(8,128)(2,1)} %all-gather.8.cloned.1.call-done), channel_id=1, source_target_pairs={{0,16},{4,20},{8,24},{12,28},{16,32},{20,36},{24,40},{28,44},{32,4... | collective-permute-start | bytes 9437192 | tf_op jit(solution)/shard_map/ppermute | solution.py:15
  256.5 143.2 %collective-permute-start.5 = (bf16[1024,1536]{1,0:T(8,128)(2,1)}, bf16[1024,1536]{1,0:T(8,128)(2,1)S(1)}, u32[]{:S(2)}, u32[]{:S(2)}) collective-permute-start(bf16[1024,1536]{1,0:T(8,128)(2,1)} %all-gather.8.cloned.1.call-done), channel_id=1, source_target_pairs={{16,0},{20,4},{24,8},{28,12},{32,16},{36,20},{40,24},{44,28},{48,3... | collective-permute-start | bytes 9437192 | tf_op jit(solution)/shard_map/ppermute | solution.py:15
Sparse Core Ops, SparseCore 0:
  12.9 42.9 all-gather.3
  83.0 41.0 all-gather.5
  211.0 41.0 all-gather.7
where the time goes:
time: 411 us; the launch traced here: 410 us
  waiting for transfers between devices  318 us (77%)
  matrix products  39.7 us (10%)
  starting transfers between devices  30.1 us (7%)
  between operations  13.2 us (3%)
  other arithmetic  5.32 us (1%)
  local copies, waits for them, and re-layouts  4.22 us (1%)
    ppermute x6, waiting for transfers between devices, shifted(): return lax.ppermute(array, axis, pairs)  192 us
    all_gather x3, waiting for transfers between devices, per_device(): gathered = lax.all_gather(activated, 'ch', axis=1, tiled=True)  125 us
    ppermute x6, starting transfers between devices, shifted(): return lax.ppermute(array, axis, pairs)  30 us
    dot_general x3, matrix products, per_device(): jnp.dot(tap_inputs[2], weights[2], preferred_element_type=jnp.float32)  19.5 us
    dot_general x3, matrix products, per_device(): jnp.dot(tap_inputs[1], weights[1], preferred_element_type=jnp.float32)  11 us
    dot_general x3, matrix products, per_device(): jnp.dot(tap_inputs[0], weights[0], preferred_element_type=jnp.float32)  9.22 us
  transfers between devices with their start and end apart: 9, of which 7 were waited for; matrix products, arithmetic and copies ran while one was open for 5% of the time, Pallas kernels for 0%

commit v1 on v0

v1 whole, which is shorter than its diff:
```python
import jax
import jax.numpy as jnp
from jax import lax
from jax.experimental import pallas as pl
from jax.experimental.pallas import tpu as pltpu
from jax.sharding import PartitionSpec as P

F32 = jnp.float32
BF16 = jnp.bfloat16
ERFC = (
    -1.26551223, 1.00002368, 0.37409196, 0.09678418, -0.18628806,
    0.27886807, -1.13520398, 1.48851587, -0.82215223, 0.17087277,
)
RIM = 64
FIRST = 576
VMEM = pl.BlockSpec(memory_space=pltpu.VMEM)
SMEM = pl.BlockSpec(memory_space=pltpu.SMEM)


def gelu(x):
    z = jnp.abs(x) * 0.7071067811865476
    t = 1.0 / (1.0 + 0.5 * z)
    poly = jnp.full_like(t, ERFC[-1])
    for c in ERFC[-2::-1]:
        poly = poly * t + c
    e = t * jnp.exp(poly - z * z)
    return 0.5 * x * jnp.where(x >= 0.0, 2.0 - e, e)


def shifted(array, by):
    size = lax.axis_size("seq")
    pairs = [(i, i + by) for i in range(size) if 0 <= i + by < size]
    return lax.ppermute(array, "seq", pairs)


def chip_swap(array):
    return lax.ppermute(array, "ch", [(i, i ^ 2) for i in range(4)])


def core_swap(array):
    return lax.ppermute(array, "ch", [(i, i ^ 1) for i in range(4)])


def gathered(own):
    far = chip_swap(own)
    return (own, core_swap(own), far, core_swap(far))


def place(ch_ref, pieces, rows, buf, at, count):
    width = pieces[0].shape[1]
    for p, piece in enumerate(pieces):
        j = ch_ref[0] ^ p
        col = pl.multiple_of(j * width, 128)
        buf[at : at + count, pl.ds(col, width)] = piece[rows : rows + count, :]


def taps(buf, w_ref, at, count):
    acc = jnp.dot(buf[at - RIM : at - RIM + count, :], w_ref[0, 0], preferred_element_type=F32)
    acc += jnp.dot(buf[at : at + count, :], w_ref[0, 1], preferred_element_type=F32)
    acc += jnp.dot(buf[at + RIM : at + RIM + count, :], w_ref[0, 2], preferred_element_type=F32)
    return acc


def finish(acc, bins, vec_ref, s_ref, a_ref, at, count):
    s = (bins.astype(F32) + acc + vec_ref[0:1, :]).astype(BF16)
    s_ref[at : at + count, :] = s
    a_ref[at : at + count, :] = gelu(s.astype(F32) * vec_ref[1:2, :] + vec_ref[2:3, :]).astype(BF16)


def first_kernel(ch_ref, p0, p1, p2, p3, w_ref, bins_ref, vec_ref, s_ref, a_ref, buf):
    place(ch_ref, (p0, p1, p2, p3), 0, buf, 0, FIRST)
    count = FIRST - 2 * RIM
    half = count // 2
    for at in (RIM, RIM + half):
        acc = taps(buf, w_ref, at, half)
        finish(acc, bins_ref[at : at + half, :], vec_ref, s_ref, a_ref, at - RIM, half)


def second_kernel(ch_ref, p0, p1, p2, p3, r0, r1, r2, r3, w_ref, bins_ref, vec_ref, s_ref, a_ref, buf):
    rows = bins_ref.shape[0]
    rest = rows - FIRST
    early, late = (p0, p1, p2, p3), (r0, r1, r2, r3)
    place(ch_ref, late, rest, buf, 0, RIM)
    place(ch_ref, early, 0, buf, RIM, FIRST)
    place(ch_ref, late, 0, buf, RIM + FIRST, rest)
    place(ch_ref, late, rest + RIM, buf, RIM + rows, RIM)
    acc = taps(buf, w_ref, RIM, RIM)
    finish(acc, bins_ref[:RIM, :], vec_ref, s_ref, a_ref, 0, RIM)
    start = FIRST - RIM
    half = (rows - start) // 2
    for i in range(2):
        at = start + i * half
        acc = taps(buf, w_ref, RIM + at, half)
        finish(acc, bins_ref[at : at + half, :], vec_ref, s_ref, a_ref, RIM + i * half, half)


def product_kernel(ch_ref, p0, p1, p2, p3, w_ref, o0, o1, o2, buf):
    rows = p0.shape[0]
    place(ch_ref, (p0, p1, p2, p3), 0, buf, 0, rows)
    for k, o in ((0, o0), (2, o2), (1, o1)):
        o[...] = jnp.dot(buf[...], w_ref[0, k], preferred_element_type=F32).astype(BF16)


def call(kernel, args, outs, scratch_rows, flops):
    width = outs[0][1]
    return pl.pallas_call(
        kernel,
        out_shape=[jax.ShapeDtypeStruct(o, BF16) for o in outs],
        in_specs=[SMEM] + [VMEM] * (len(args) - 1),
        out_specs=[VMEM] * len(outs),
        scratch_shapes=[pltpu.VMEM((scratch_rows, 4 * width), BF16)],
        compiler_params=pltpu.CompilerParams(vmem_limit_bytes=40 * 1024 * 1024),
        cost_estimate=pl.CostEstimate(flops=flops, bytes_accessed=8 * 1024 * 1024, transcendentals=0),
    )(*args)


def per_device(bins_in, pre_scale, pre_shift, conv_weight, conv_bias):
    rows, width = bins_in.shape
    ch = lax.axis_index("ch").astype(jnp.int32).reshape(1)
    hop1 = 1
    hop2 = 4096 // rows
    mac = 2 * 4 * width * width * 3

    act = gelu(bins_in.astype(F32) * pre_scale[0] + pre_shift[0]).astype(BF16)
    early = gathered(act[:FIRST])
    low = shifted(act[rows - RIM :], 1)
    high = shifted(act[:RIM], -1)
    late = gathered(jnp.concatenate([act[FIRST:], low, high], axis=0))

    vec0 = jnp.stack([conv_bias[0], pre_scale[1], pre_shift[1]])
    n0 = FIRST - 2 * RIM
    n1 = rows - n0
    s_x0, a_x0 = call(first_kernel, (ch, *early, conv_weight[0:1], bins_in, vec0), [(n0, width)] * 2, FIRST, mac * n0)
    g_x0 = gathered(a_x0)
    s_x1, a_x1 = call(
        second_kernel, (ch, *early, *late, conv_weight[0:1], bins_in, vec0), [(n1, width)] * 2, rows + 2 * RIM, mac * n1
    )
    g_x1 = gathered(a_x1)

    p0a, p1a, p2a = call(product_kernel, (ch, *g_x0, conv_weight[1:2]), [(n0, width)] * 3, n0, mac * n0)
    from_next_a = shifted(p2a, -hop1)
    p0b, p1b, p2b = call(product_kernel, (ch, *g_x1, conv_weight[1:2]), [(n1, width)] * 3, n1, mac * n1)
    from_next_b = shifted(p2b[:RIM], -hop1)
    from_prev = shifted(p0b[RIM:], hop1)

    f = lambda v: v.astype(F32)
    cat = lambda *v: jnp.concatenate([f(x) for x in v], axis=0)
    s2_hi = f(s_x1[RIM:]) + f(p1b[RIM:]) + cat(p0b[:RIM], p0a) + cat(from_next_b, from_next_a) + conv_bias[1]
    s2_hi = s2_hi.astype(BF16)
    a2_hi = gelu(f(s2_hi) * pre_scale[2] + pre_shift[2]).astype(BF16)
    g_hi = gathered(a2_hi)
    s2_lo = cat(s_x1[:RIM], s_x0) + cat(p1b[:RIM], p1a) + f(p2b[RIM:]) + f(from_prev) + conv_bias[1]
    s2_lo = s2_lo.astype(BF16)
    a2_lo = gelu(f(s2_lo) * pre_scale[2] + pre_shift[2]).astype(BF16)
    g_lo = gathered(a2_lo)

    out = []
    for g, s2 in ((g_hi, s2_hi), (g_lo, s2_lo)):
        q0, q1, q2 = call(product_kernel, (ch, *g, conv_weight[2:3]), [s2.shape] * 3, s2.shape[0], mac * s2.shape[0])
        up = shifted(q0, hop2)
        down = shifted(q2, -hop2)
        out.append((f(s2) + f(q1) + f(up) + f(down) + conv_bias[2]).astype(BF16))
    return jnp.concatenate([out[1], out[0]], axis=0)


def solution(mesh):
    return jax.shard_map(
        per_device,
        mesh=mesh,
        in_specs=(
            P("seq", "ch"),
            P(None, "ch"),
            P(None, "ch"),
            P(None, None, None, "ch"),
            P(None, "ch"),
        ),
        out_specs=P("seq", "ch"),
        check_vma=False,
    )
```

time: 411 us -> 172 us (0.42)
  waiting for transfers between devices: 318 us -> 78.7 us
  matrix products: 39.7 us -> 0 us
  Pallas kernels: 0 us -> 22 us
  starting transfers between devices: 30.1 us -> 51 us
  between operations: 13.2 us -> 0.32 us
  local copies, waits for them, and re-layouts: 4.22 us -> 10.3 us
    all_gather x3 -> x0, waiting for transfers between devices: 125 us -> none  [per_device(): gathered = lax.all_gather(activated, 'ch', axis=1, tiled=True)]
    ppermute x6 -> x27, waiting for transfers between devices: 192 us -> 78.7 us  [the longest x6 47.6 us: chip_swap(): return lax.ppermute(array, 'ch', [(i, i ^ 2) for i in range(4)])]
    dot_general x9 -> x0, matrix products: 39.7 us -> none  [the longest x3 19.5 us: per_device(): jnp.dot(tap_inputs[2], weights[2], preferred_element_type=jnp.float32)]
    pallas_call x0 -> x6, Pallas kernels: none -> 22 us  [call(): pl.pallas_call(kernel, out_shape=[jax.ShapeDtypeStruct(o, BF16) for o in...]
    ppermute x6 -> x27, starting transfers between devices: 30 us -> 51 us  [the longest x9 43.2 us: shifted(): return lax.ppermute(array, 'seq', pairs)]
    slice x4 -> x11, local copies, waits for them, and re-layouts: 4.2 us -> 9.13 us  [the longest x1 6.5 us: per_device(): conv_weight[2:3]]
  transfers between devices with their start and end apart: 9 -> 27, of which waited for: 7 -> 11; matrix products, arithmetic and copies ran while one was open for 5% -> 5% of each run, Pallas kernels for 0% -> 9%
where the time goes in v1:
time: 172 us; the launch traced here: 170 us
  waiting for transfers between devices  78.7 us (46%)
  starting transfers between devices  51 us (30%)
  Pallas kernels  22 us (13%)
  local copies, waits for them, and re-layouts  10.3 us (6%)
  other arithmetic  7.85 us (5%)
    ppermute x6, waiting for transfers between devices, chip_swap(): return lax.ppermute(array, 'ch', [(i, i ^ 2) for i in range(4)])  47.6 us
    ppermute x9, starting transfers between devices, shifted(): return lax.ppermute(array, 'seq', pairs)  43.2 us
    ppermute x9, waiting for transfers between devices, shifted(): return lax.ppermute(array, 'seq', pairs)  31.1 us
    pallas_call x6, Pallas kernels, call(): pl.pallas_call(kernel, out_shape=[jax.ShapeDtypeStruct(o, BF16) for o in...  22 us
    slice x1, local copies, waits for them, and re-layouts, per_device(): conv_weight[2:3]  6.5 us
    ppermute x6, starting transfers between devices, chip_swap(): return lax.ppermute(array, 'ch', [(i, i ^ 2) for i in range(4)])  6.23 us
  transfers between devices with their start and end apart: 27, of which 11 were waited for; matrix products, arithmetic and copies ran while one was open for 5% of the time, Pallas kernels for 9%

profile of v1, /device:TPU:6, one launch (start us, length us, event | category | flops | bytes accessed | tf_op | source)
XLA Modules:
  0.0 170.1 jit_solution(501720051489431108)
XLA Ops:
  0.9 3.0 %fusion.1 = bf16[1024,384]{1,0:T(8,128)(2,1)S(1)} fusion(bf16[1024,384]{1,0:T(8,128)(2,1)} %bins_ref.3, f32[384]{0:T(512)S(1)} %get-tuple-element.42, f32[384]{0:T(512)S(1)} %get-tuple-element.60), kind=kLoop, calls=%fused_computation.2 | loop fusion | flops 13762560 | bytes 1575936 | tf_op jit(solution)/shard_map/convert_element_type | solution.py:124
  3.9 5.1 %collective-permute-start.3 = (bf16[64,384]{1,0:T(8,128)(2,1)S(1)}, bf16[64,384]{1,0:T(8,128)(2,1)S(1)}, u32[]{:S(2)}, u32[]{:S(2)}) collective-permute-start(bf16[64,384]{1,0:T(8,128)(2,1)S(1)} %get-tuple-element.50), channel_id=1, source_target_pairs={{0,4},{4,8},{8,12},{12,16},{16,20},{20,24},{24,28},{28,32},{32,36}... | collective-permute-start | bytes 147464 | tf_op jit(solution)/shard_map/ppermute | solution.py:33
  9.0 7.5 %collective-permute-start.4 = (bf16[64,384]{1,0:T(8,128)(2,1)S(1)}, bf16[64,384]{1,0:T(8,128)(2,1)S(1)}, u32[]{:S(2)}, u32[]{:S(2)}) collective-permute-start(bf16[64,384]{1,0:T(8,128)(2,1)S(1)} %get-tuple-element.51), channel_id=1, source_target_pairs={{4,0},{8,4},{12,8},{16,12},{20,16},{24,20},{28,24},{32,28},{36,32}... | collective-permute-start | bytes 147464 | tf_op jit(solution)/shard_map/ppermute | solution.py:33
  20.8 9.9 %collective-permute-done.1.p2 = bf16[576,384]{1,0:T(8,128)(2,1)} collective-permute-done((bf16[576,384]{1,0:T(8,128)(2,1)}, bf16[576,384]{1,0:T(8,128)(2,1)}, u32[]{:S(2)}, u32[]{:S(2)}) %collective-permute-start.1) | collective-permute-done | bytes 442400 | tf_op jit(solution)/shard_map/ppermute | solution.py:37
  30.8 8.0 %collective-permute-done.6.r2 = bf16[576,384]{1,0:T(8,128)(2,1)} collective-permute-done((bf16[576,384]{1,0:T(8,128)(2,1)}, bf16[576,384]{1,0:T(8,128)(2,1)}, u32[]{:S(2)}, u32[]{:S(2)}) %collective-permute-start.6) | collective-permute-done | bytes 442400 | tf_op jit(solution)/shard_map/ppermute | solution.py:37
  38.8 6.5 %fusion.39 = (bf16[1,3,1536,384]{3,2,1,0:T(8,128)(2,1)}, bf16[1,3,1536,384]{3,2,1,0:T(8,128)(2,1)S(1)}, bf16[1,3,1536,384]{3,2,1,0:T(8,128)(2,1)}) fusion(bf16[3,3,1536,384]{3,2,1,0:T(8,128)(2,1)} %param.8), kind=kLoop, calls=%fused_computation.58 | loop fusion | bytes 21233664 | tf_op jit(solution)/shard_map/slice | solution.py:159
  47.3 6.3 %shard_map.55 = (bf16[576,384]{1,0:T(8,128)(2,1)S(1)}, bf16[576,384]{1,0:T(8,128)(2,1)S(1)}) custom-call(s32[1]{0:T(128)} %bitcast.ch_ref, bf16[576,384]{1,0:T(8,128)(2,1)} %slice.103.p0, bf16[576,384]{1,0:T(8,128)(2,1)} %collective-permute-done.p1, bf16[576,384]{1,0:T(8,128)(2,1)} %collective-permute-done.1.p2, bf16[576,384]{1,0:T(8,128)(2,1)} %collective-permute-done.2.p3, ...), custom_call_target="tpu_custom_call" | custom-call | flops 2038431744 | bytes 8388608 | tf_op jit(solution)/shard_map/pallas_call | solution.py:106
  54.6 4.7 %shard_map.56 = (bf16[448,384]{1,0:T(8,128)(2,1)S(1)}, bf16[448,384]{1,0:T(8,128)(2,1)S(1)}) custom-call(s32[1]{0:T(128)} %bitcast.ch_ref, bf16[576,384]{1,0:T(8,128)(2,1)} %slice.103.p0, bf16[576,384]{1,0:T(8,128)(2,1)} %collective-permute-done.p1, bf16[576,384]{1,0:T(8,128)(2,1)} %collective-permute-done.1.p2, bf16[576,384]{1,0:T(8,128)(2,1)} %collective-permute-done.2.p3, ...), custom_call_target="tpu_custom_call" | custom-call | flops 1585446912 | bytes 8388608 | tf_op jit(solution)/shard_map/pallas_call | solution.py:106
  60.6 6.2 %collective-permute-done.9.p2 = bf16[576,384]{1,0:T(8,128)(2,1)S(1)} collective-permute-done((bf16[576,384]{1,0:T(8,128)(2,1)S(1)}, bf16[576,384]{1,0:T(8,128)(2,1)S(1)}, u32[]{:S(2)}, u32[]{:S(2)}) %collective-permute-start.9) | collective-permute-done | bytes 442400 | tf_op jit(solution)/shard_map/ppermute | solution.py:37
  67.4 6.5 %collective-permute-done.12.p2 = bf16[448,384]{1,0:T(8,128)(2,1)S(1)} collective-permute-done((bf16[448,384]{1,0:T(8,128)(2,1)S(1)}, bf16[448,384]{1,0:T(8,128)(2,1)S(1)}, u32[]{:S(2)}, u32[]{:S(2)}) %collective-permute-start.12) | collective-permute-done | bytes 344096 | tf_op jit(solution)/shard_map/ppermute | solution.py:37
  73.8 3.1 %shard_map.57 = (bf16[576,384]{1,0:T(8,128)(2,1)S(1)}, bf16[576,384]{1,0:T(8,128)(2,1)S(1)}, bf16[576,384]{1,0:T(8,128)(2,1)S(1)}) custom-call(s32[1]{0:T(128)} %bitcast.ch_ref, bf16[576,384]{1,0:T(8,128)(2,1)S(1)} %get-tuple-element.23.p0, bf16[576,384]{1,0:T(8,128)(2,1)S(1)} %collective-permute-done.8.p1, bf16[576,384]{1,0:T(8,128)(2,1)S(1)} %collective-permute-done.9.p2, ...), custom_call_target="tpu_custom_call" | custom-call | flops 2038431744 | bytes 8388608 | tf_op jit(solution)/shard_map/pallas_call | solution.py:106
  78.9 2.4 %shard_map.58 = (bf16[448,384]{1,0:T(8,128)(2,1)S(1)}, bf16[448,384]{1,0:T(8,128)(2,1)S(1)}, bf16[448,384]{1,0:T(8,128)(2,1)S(1)}) custom-call(s32[1]{0:T(128)} %bitcast.ch_ref, bf16[448,384]{1,0:T(8,128)(2,1)S(1)} %get-tuple-element.25.p0, bf16[448,384]{1,0:T(8,128)(2,1)S(1)} %collective-permute-done.11.p1, ...), custom_call_target="tpu_custom_call" | custom-call | flops 1585446912 | bytes 8388608 | tf_op jit(solution)/shard_map/pallas_call | solution.py:106
  81.3 8.4 %collective-permute-start.21 = (bf16[448,384]{1,0:T(8,128)(2,1)S(1)}, bf16[448,384]{1,0:T(8,128)(2,1)S(1)}, u32[]{:S(2)}, u32[]{:S(2)}) collective-permute-start(bf16[448,384]{1,0:T(8,128)(2,1)S(1)} %get-tuple-element.33), channel_id=1, source_target_pairs={{4,0},{8,4},{12,8},{16,12},{20,16},{24,20},{28,24},{32,28},{36,32}... | collective-permute-start | bytes 1032200 | tf_op jit(solution)/shard_map/ppermute | solution.py:33
  89.8 2.6 %collective-permute-start.20 = (bf16[64,384]{1,0:T(8,128)(2,1)S(1)}, bf16[64,384]{1,0:T(8,128)(2,1)S(1)}, u32[]{:S(2)}, u32[]{:S(2)}) collective-permute-start(bf16[64,384]{1,0:T(8,128)(2,1)S(1)} %slice.102), channel_id=1, source_target_pairs={{4,0},{8,4},{12,8},{16,12},{20,16},{24,20},{28,24},{32,28},{36,32}... | collective-permute-start | bytes 147464 | tf_op jit(solution)/shard_map/ppermute | solution.py:33
  92.4 10.9 %collective-permute-done.20 = bf16[64,384]{1,0:T(8,128)(2,1)S(1)} collective-permute-done((bf16[64,384]{1,0:T(8,128)(2,1)S(1)}, bf16[64,384]{1,0:T(8,128)(2,1)S(1)}, u32[]{:S(2)}, u32[]{:S(2)}) %collective-permute-start.20) | collective-permute-done | bytes 49184 | tf_op jit(solution)/shard_map/ppermute | solution.py:33
  103.3 2.5 %fusion.16 = (bf16[512,384]{1,0:T(8,128)(2,1)S(1)}, bf16[512,384]{1,0:T(8,128)(2,1)S(1)}, bf16[512,384]{1,0:T(8,128)(2,1)S(1)}, bf16[512,384]{1,0:T(8,128)(2,1)S(1)}) fusion(f32[384]{0:T(512)S(1)} %get-tuple-element.41, f32[384]{0:T(512)S(1)} %get-tuple-element.61, f32[384]{0:T(512)S(1)} %get-tuple-element.38, ...), kind=kLoop, calls=%fused_computation.24 | loop fusion | flops 19660800 | bytes 4723200 | tf_op jit(solution)/shard_map/convert_element_type | solution.py:154
  108.0 9.9 %collective-permute-done.16.p2 = bf16[512,384]{1,0:T(8,128)(2,1)S(1)} collective-permute-done((bf16[512,384]{1,0:T(8,128)(2,1)S(1)}, bf16[512,384]{1,0:T(8,128)(2,1)S(1)}, u32[]{:S(2)}, u32[]{:S(2)}) %collective-permute-start.16) | collective-permute-done | bytes 393248 | tf_op jit(solution)/shard_map/ppermute | solution.py:37
  118.4 7.0 %collective-permute-done.23.p2 = bf16[512,384]{1,0:T(8,128)(2,1)S(1)} collective-permute-done((bf16[512,384]{1,0:T(8,128)(2,1)S(1)}, bf16[512,384]{1,0:T(8,128)(2,1)S(1)}, u32[]{:S(2)}, u32[]{:S(2)}) %collective-permute-start.23) | collective-permute-done | bytes 393248 | tf_op jit(solution)/shard_map/ppermute | solution.py:37
  125.5 2.7 %shard_map.59 = (bf16[512,384]{1,0:T(8,128)(2,1)S(1)}, bf16[512,384]{1,0:T(8,128)(2,1)S(1)}, bf16[512,384]{1,0:T(8,128)(2,1)S(1)}) custom-call(s32[1]{0:T(128)} %bitcast.ch_ref, bf16[512,384]{1,0:T(8,128)(2,1)S(1)} %get-tuple-element.43.p0, bf16[512,384]{1,0:T(8,128)(2,1)S(1)} %collective-permute-done.15.p1, ...), custom_call_target="tpu_custom_call" | custom-call | flops 1811939328 | bytes 8388608 | tf_op jit(solution)/shard_map/pallas_call | solution.py:106
  130.2 6.9 %collective-permute-start.19 = (bf16[512,384]{1,0:T(8,128)(2,1)S(1)}, bf16[512,384]{1,0:T(8,128)(2,1)S(1)}, u32[]{:S(2)}, u32[]{:S(2)}) collective-permute-start(bf16[512,384]{1,0:T(8,128)(2,1)S(1)} %get-tuple-element.31), channel_id=1, source_target_pairs={{16,0},{20,4},{24,8},{28,12},{32,16},{36,20},{40,24},{44,28},{48,3... | collective-permute-start | bytes 1179656 | tf_op jit(solution)/shard_map/ppermute | solution.py:33
  137.1 2.7 %shard_map.60 = (bf16[512,384]{1,0:T(8,128)(2,1)S(1)}, bf16[512,384]{1,0:T(8,128)(2,1)S(1)}, bf16[512,384]{1,0:T(8,128)(2,1)S(1)}) custom-call(s32[1]{0:T(128)} %bitcast.ch_ref, bf16[512,384]{1,0:T(8,128)(2,1)S(1)} %get-tuple-element.52.p0, bf16[512,384]{1,0:T(8,128)(2,1)S(1)} %collective-permute-done.22.p1, ...), custom_call_target="tpu_custom_call" | custom-call | flops 1811939328 | bytes 8388608 | tf_op jit(solution)/shard_map/pallas_call | solution.py:106
  141.8 6.9 %collective-permute-start.26 = (bf16[512,384]{1,0:T(8,128)(2,1)S(1)}, bf16[512,384]{1,0:T(8,128)(2,1)S(1)}, u32[]{:S(2)}, u32[]{:S(2)}) collective-permute-start(bf16[512,384]{1,0:T(8,128)(2,1)S(1)} %get-tuple-element.36), channel_id=1, source_target_pairs={{16,0},{20,4},{24,8},{28,12},{32,16},{36,20},{40,24},{44,28},{48,3... | collective-permute-start | bytes 1179656 | tf_op jit(solution)/shard_map/ppermute | solution.py:33
  148.7 6.0 %collective-permute-done.18 = bf16[512,384]{1,0:T(8,128)(2,1)S(1)} collective-permute-done((bf16[512,384]{1,0:T(8,128)(2,1)S(1)}, bf16[512,384]{1,0:T(8,128)(2,1)S(1)}, u32[]{:S(2)}, u32[]{:S(2)}) %collective-permute-start.18) | collective-permute-done | bytes 393248 | tf_op jit(solution)/shard_map/ppermute | solution.py:33
  155.2 13.5 %collective-permute-done.25 = bf16[512,384]{1,0:T(8,128)(2,1)S(1)} collective-permute-done((bf16[512,384]{1,0:T(8,128)(2,1)S(1)}, bf16[512,384]{1,0:T(8,128)(2,1)S(1)}, u32[]{:S(2)}, u32[]{:S(2)}) %collective-permute-start.25) | collective-permute-done | bytes 393248 | tf_op jit(solution)/shard_map/ppermute | solution.py:33
  (59 shorter events, 20.2 us)
Async XLA Ops:
  3.9 14.1 %collective-permute-start.3 = (bf16[64,384]{1,0:T(8,128)(2,1)S(1)}, bf16[64,384]{1,0:T(8,128)(2,1)S(1)}, u32[]{:S(2)}, u32[]{:S(2)}) collective-permute-start(bf16[64,384]{1,0:T(8,128)(2,1)S(1)} %get-tuple-element.50), channel_id=1, source_target_pairs={{0,4},{4,8},{8,12},{12,16},{16,20},{20,24},{24,28},{28,32},{32,36}... | collective-permute-start | bytes 147464 | tf_op jit(solution)/shard_map/ppermute | solution.py:33
  9.0 9.2 %collective-permute-start.4 = (bf16[64,384]{1,0:T(8,128)(2,1)S(1)}, bf16[64,384]{1,0:T(8,128)(2,1)S(1)}, u32[]{:S(2)}, u32[]{:S(2)}) collective-permute-start(bf16[64,384]{1,0:T(8,128)(2,1)S(1)} %get-tuple-element.51), channel_id=1, source_target_pairs={{4,0},{8,4},{12,8},{16,12},{20,16},{24,20},{28,24},{32,28},{36,32}... | collective-permute-start | bytes 147464 | tf_op jit(solution)/shard_map/ppermute | solution.py:33
  17.3 13.4 %collective-permute-start.1 = (bf16[576,384]{1,0:T(8,128)(2,1)}, bf16[576,384]{1,0:T(8,128)(2,1)}, u32[]{:S(2)}, u32[]{:S(2)}) collective-permute-start(bf16[576,384]{1,0:T(8,128)(2,1)} %slice.103.p0), channel_id=1, source_target_pairs={{0,2},{1,3},{2,0},{3,1},{4,6},{5,7},{6,4},{7,5},{8,10},{9,11},{10,... | collective-permute-start | bytes 1327112 | tf_op jit(solution)/shard_map/ppermute | solution.py:37
  19.1 19.6 %collective-permute-start.6 = (bf16[576,384]{1,0:T(8,128)(2,1)}, bf16[576,384]{1,0:T(8,128)(2,1)}, u32[]{:S(2)}, u32[]{:S(2)}) collective-permute-start(bf16[576,384]{1,0:T(8,128)(2,1)} %pad_maximum_fusion.1.r0), channel_id=1, source_target_pairs={{0,2},{1,3},{2,0},{3,1},{4,6},{5,7},{6,4},{7,5},{8,10},{9,11},{10,... | collective-permute-start | bytes 1327112 | tf_op jit(solution)/shard_map/ppermute | solution.py:37
  20.3 25.8 %collective-permute-start = (bf16[576,384]{1,0:T(8,128)(2,1)}, bf16[576,384]{1,0:T(8,128)(2,1)}, u32[]{:S(2)}, u32[]{:S(2)}) collective-permute-start(bf16[576,384]{1,0:T(8,128)(2,1)} %slice.103.p0), channel_id=1, source_target_pairs={{0,1},{1,0},{2,3},{3,2},{4,5},{5,4},{6,7},{7,6},{8,9},{9,8},{10,11... | collective-permute-start | bytes 1327112 | tf_op jit(solution)/shard_map/ppermute | solution.py:41
  20.3 25.8 %collective-permute-start.5 = (bf16[576,384]{1,0:T(8,128)(2,1)}, bf16[576,384]{1,0:T(8,128)(2,1)}, u32[]{:S(2)}, u32[]{:S(2)}) collective-permute-start(bf16[576,384]{1,0:T(8,128)(2,1)} %pad_maximum_fusion.1.r0), channel_id=1, source_target_pairs={{0,1},{1,0},{2,3},{3,2},{4,5},{5,4},{6,7},{7,6},{8,9},{9,8},{10,11... | collective-permute-start | bytes 1327112 | tf_op jit(solution)/shard_map/ppermute | solution.py:41
  30.8 15.4 %collective-permute-start.2 = (bf16[576,384]{1,0:T(8,128)(2,1)}, bf16[576,384]{1,0:T(8,128)(2,1)}, u32[]{:S(2)}, u32[]{:S(2)}) collective-permute-start(bf16[576,384]{1,0:T(8,128)(2,1)} %collective-permute-done.1.p2), channel_id=1, source_target_pairs={{0,1},{1,0},{2,3},{3,2},{4,5},{5,4},{6,7},{7,6},{8,9},{9,8},{10,11... | collective-permute-start | bytes 1327112 | tf_op jit(solution)/shard_map/ppermute | solution.py:41
  53.6 13.2 %collective-permute-start.9 = (bf16[576,384]{1,0:T(8,128)(2,1)S(1)}, bf16[576,384]{1,0:T(8,128)(2,1)S(1)}, u32[]{:S(2)}, u32[]{:S(2)}) collective-permute-start(bf16[576,384]{1,0:T(8,128)(2,1)S(1)} %get-tuple-element.23.p0), channel_id=1, source_target_pairs={{0,2},{1,3},{2,0},{3,1},{4,6},{5,7},{6,4},{7,5},{8,10},{9,11},{10,... | collective-permute-start | bytes 1327112 | tf_op jit(solution)/shard_map/ppermute | solution.py:37
  59.3 14.5 %collective-permute-start.12 = (bf16[448,384]{1,0:T(8,128)(2,1)S(1)}, bf16[448,384]{1,0:T(8,128)(2,1)S(1)}, u32[]{:S(2)}, u32[]{:S(2)}) collective-permute-start(bf16[448,384]{1,0:T(8,128)(2,1)S(1)} %get-tuple-element.25.p0), channel_id=1, source_target_pairs={{0,2},{1,3},{2,0},{3,1},{4,6},{5,7},{6,4},{7,5},{8,10},{9,11},{10,... | collective-permute-start | bytes 1032200 | tf_op jit(solution)/shard_map/ppermute | solution.py:37
  60.6 13.2 %collective-permute-start.8 = (bf16[576,384]{1,0:T(8,128)(2,1)S(1)}, bf16[576,384]{1,0:T(8,128)(2,1)S(1)}, u32[]{:S(2)}, u32[]{:S(2)}) collective-permute-start(bf16[576,384]{1,0:T(8,128)(2,1)S(1)} %get-tuple-element.23.p0), channel_id=1, source_target_pairs={{0,1},{1,0},{2,3},{3,2},{4,5},{5,4},{6,7},{7,6},{8,9},{9,8},{10,11... | collective-permute-start | bytes 1327112 | tf_op jit(solution)/shard_map/ppermute | solution.py:41
  66.8 12.0 %collective-permute-start.11 = (bf16[448,384]{1,0:T(8,128)(2,1)S(1)}, bf16[448,384]{1,0:T(8,128)(2,1)S(1)}, u32[]{:S(2)}, u32[]{:S(2)}) collective-permute-start(bf16[448,384]{1,0:T(8,128)(2,1)S(1)} %get-tuple-element.25.p0), channel_id=1, source_target_pairs={{0,1},{1,0},{2,3},{3,2},{4,5},{5,4},{6,7},{7,6},{8,9},{9,8},{10,11... | collective-permute-start | bytes 1032200 | tf_op jit(solution)/shard_map/ppermute | solution.py:41
  77.0 26.4 %collective-permute-start.14 = (bf16[512,384]{1,0:T(8,128)(2,1)S(1)}, bf16[512,384]{1,0:T(8,128)(2,1)S(1)}, u32[]{:S(2)}, u32[]{:S(2)}) collective-permute-start(bf16[512,384]{1,0:T(8,128)(2,1)S(1)} %slice.93), channel_id=1, source_target_pairs={{0,4},{4,8},{8,12},{12,16},{16,20},{20,24},{24,28},{28,32},{32,36}... | collective-permute-start | bytes 1179656 | tf_op jit(solution)/shard_map/ppermute | solution.py:33
  81.3 22.0 %collective-permute-start.21 = (bf16[448,384]{1,0:T(8,128)(2,1)S(1)}, bf16[448,384]{1,0:T(8,128)(2,1)S(1)}, u32[]{:S(2)}, u32[]{:S(2)}) collective-permute-start(bf16[448,384]{1,0:T(8,128)(2,1)S(1)} %get-tuple-element.33), channel_id=1, source_target_pairs={{4,0},{8,4},{12,8},{16,12},{20,16},{24,20},{28,24},{32,28},{36,32}... | collective-permute-start | bytes 1032200 | tf_op jit(solution)/shard_map/ppermute | solution.py:33
  89.8 13.5 %collective-permute-start.20 = (bf16[64,384]{1,0:T(8,128)(2,1)S(1)}, bf16[64,384]{1,0:T(8,128)(2,1)S(1)}, u32[]{:S(2)}, u32[]{:S(2)}) collective-permute-start(bf16[64,384]{1,0:T(8,128)(2,1)S(1)} %slice.102), channel_id=1, source_target_pairs={{4,0},{8,4},{12,8},{16,12},{20,16},{24,20},{28,24},{32,28},{36,32}... | collective-permute-start | bytes 147464 | tf_op jit(solution)/shard_map/ppermute | solution.py:33
  105.9 12.1 %collective-permute-start.16 = (bf16[512,384]{1,0:T(8,128)(2,1)S(1)}, bf16[512,384]{1,0:T(8,128)(2,1)S(1)}, u32[]{:S(2)}, u32[]{:S(2)}) collective-permute-start(bf16[512,384]{1,0:T(8,128)(2,1)S(1)} %get-tuple-element.43.p0), channel_id=1, source_target_pairs={{0,2},{1,3},{2,0},{3,1},{4,6},{5,7},{6,4},{7,5},{8,10},{9,11},{10,... | collective-permute-start | bytes 1179656 | tf_op jit(solution)/shard_map/ppermute | solution.py:37
  106.6 18.8 %collective-permute-start.23 = (bf16[512,384]{1,0:T(8,128)(2,1)S(1)}, bf16[512,384]{1,0:T(8,128)(2,1)S(1)}, u32[]{:S(2)}, u32[]{:S(2)}) collective-permute-start(bf16[512,384]{1,0:T(8,128)(2,1)S(1)} %get-tuple-element.52.p0), channel_id=1, source_target_pairs={{0,2},{1,3},{2,0},{3,1},{4,6},{5,7},{6,4},{7,5},{8,10},{9,11},{10,... | collective-permute-start | bytes 1179656 | tf_op jit(solution)/shard_map/ppermute | solution.py:37
  108.0 17.5 %collective-permute-start.15 = (bf16[512,384]{1,0:T(8,128)(2,1)S(1)}, bf16[512,384]{1,0:T(8,128)(2,1)S(1)}, u32[]{:S(2)}, u32[]{:S(2)}) collective-permute-start(bf16[512,384]{1,0:T(8,128)(2,1)S(1)} %get-tuple-element.43.p0), channel_id=1, source_target_pairs={{0,1},{1,0},{2,3},{3,2},{4,5},{5,4},{6,7},{7,6},{8,9},{9,8},{10,11... | collective-permute-start | bytes 1179656 | tf_op jit(solution)/shard_map/ppermute | solution.py:41
  117.9 7.6 %collective-permute-start.17 = (bf16[512,384]{1,0:T(8,128)(2,1)S(1)}, bf16[512,384]{1,0:T(8,128)(2,1)S(1)}, u32[]{:S(2)}, u32[]{:S(2)}) collective-permute-start(bf16[512,384]{1,0:T(8,128)(2,1)S(1)} %collective-permute-done.16.p2), channel_id=1, source_target_pairs={{0,1},{1,0},{2,3},{3,2},{4,5},{5,4},{6,7},{7,6},{8,9},{9,8},{10,11... | collective-permute-start | bytes 1179656 | tf_op jit(solution)/shard_map/ppermute | solution.py:41
  117.9 19.2 %collective-permute-start.22 = (bf16[512,384]{1,0:T(8,128)(2,1)S(1)}, bf16[512,384]{1,0:T(8,128)(2,1)S(1)}, u32[]{:S(2)}, u32[]{:S(2)}) collective-permute-start(bf16[512,384]{1,0:T(8,128)(2,1)S(1)} %get-tuple-element.52.p0), channel_id=1, source_target_pairs={{0,1},{1,0},{2,3},{3,2},{4,5},{5,4},{6,7},{7,6},{8,9},{9,8},{10,11... | collective-permute-start | bytes 1179656 | tf_op jit(solution)/shard_map/ppermute | solution.py:41
  125.5 11.6 %collective-permute-start.24 = (bf16[512,384]{1,0:T(8,128)(2,1)S(1)}, bf16[512,384]{1,0:T(8,128)(2,1)S(1)}, u32[]{:S(2)}, u32[]{:S(2)}) collective-permute-start(bf16[512,384]{1,0:T(8,128)(2,1)S(1)} %collective-permute-done.23.p2), channel_id=1, source_target_pairs={{0,1},{1,0},{2,3},{3,2},{4,5},{5,4},{6,7},{7,6},{8,9},{9,8},{10,11... | collective-permute-start | bytes 1179656 | tf_op jit(solution)/shard_map/ppermute | solution.py:41
  128.2 26.5 %collective-permute-start.18 = (bf16[512,384]{1,0:T(8,128)(2,1)S(1)}, bf16[512,384]{1,0:T(8,128)(2,1)S(1)}, u32[]{:S(2)}, u32[]{:S(2)}) collective-permute-start(bf16[512,384]{1,0:T(8,128)(2,1)S(1)} %get-tuple-element.30), channel_id=1, source_target_pairs={{0,16},{4,20},{8,24},{12,28},{16,32},{20,36},{24,40},{28,44},{32,4... | collective-permute-start | bytes 1179656 | tf_op jit(solution)/shard_map/ppermute | solution.py:33
  130.2 25.0 %collective-permute-start.19 = (bf16[512,384]{1,0:T(8,128)(2,1)S(1)}, bf16[512,384]{1,0:T(8,128)(2,1)S(1)}, u32[]{:S(2)}, u32[]{:S(2)}) collective-permute-start(bf16[512,384]{1,0:T(8,128)(2,1)S(1)} %get-tuple-element.31), channel_id=1, source_target_pairs={{16,0},{20,4},{24,8},{28,12},{32,16},{36,20},{40,24},{44,28},{48,3... | collective-permute-start | bytes 1179656 | tf_op jit(solution)/shard_map/ppermute | solution.py:33
  139.9 28.8 %collective-permute-start.25 = (bf16[512,384]{1,0:T(8,128)(2,1)S(1)}, bf16[512,384]{1,0:T(8,128)(2,1)S(1)}, u32[]{:S(2)}, u32[]{:S(2)}) collective-permute-start(bf16[512,384]{1,0:T(8,128)(2,1)S(1)} %get-tuple-element.35), channel_id=1, source_target_pairs={{0,16},{4,20},{8,24},{12,28},{16,32},{20,36},{24,40},{28,44},{32,4... | collective-permute-start | bytes 1179656 | tf_op jit(solution)/shard_map/ppermute | solution.py:33
  141.8 26.9 %collective-permute-start.26 = (bf16[512,384]{1,0:T(8,128)(2,1)S(1)}, bf16[512,384]{1,0:T(8,128)(2,1)S(1)}, u32[]{:S(2)}, u32[]{:S(2)}) collective-permute-start(bf16[512,384]{1,0:T(8,128)(2,1)S(1)} %get-tuple-element.36), channel_id=1, source_target_pairs={{16,0},{20,4},{24,8},{28,12},{32,16},{36,20},{40,24},{44,28},{48,3... | collective-permute-start | bytes 1179656 | tf_op jit(solution)/shard_map/ppermute | solution.py:33
  (6 other events, 63.0 us)

commit v2 on v1

v2 whole, which is shorter than its diff:
```python
import functools

import jax
import jax.numpy as jnp
from jax import lax
from jax.experimental import pallas as pl
from jax.experimental.pallas import tpu as pltpu
from jax.sharding import PartitionSpec as P

F32 = jnp.float32
BF16 = jnp.bfloat16
ERFC = (
    -1.26551223, 1.00002368, 0.37409196, 0.09678418, -0.18628806,
    0.27886807, -1.13520398, 1.48851587, -0.82215223, 0.17087277,
)
RIM = 64
FIRST = 576
VMEM = pl.BlockSpec(memory_space=pltpu.VMEM)
SMEM = pl.BlockSpec(memory_space=pltpu.SMEM)


def gelu(x):
    z = jnp.abs(x) * 0.7071067811865476
    t = 1.0 / (1.0 + 0.5 * z)
    poly = jnp.full_like(t, ERFC[-1])
    for c in ERFC[-2::-1]:
        poly = poly * t + c
    e = t * jnp.exp(poly - z * z)
    return 0.5 * x * jnp.where(x >= 0.0, 2.0 - e, e)


def shifted(array, by):
    size = lax.axis_size("seq")
    pairs = [(i, i + by) for i in range(size) if 0 <= i + by < size]
    return lax.ppermute(array, "seq", pairs)


def chip_swap(array):
    return lax.ppermute(array, "ch", [(i, i ^ 2) for i in range(4)])


def core_swap(array):
    return lax.ppermute(array, "ch", [(i, i ^ 1) for i in range(4)])


def gathered(own):
    far = chip_swap(own)
    return (own, core_swap(own), far, core_swap(far))


def place(ch_ref, pieces, rows, buf, at, count):
    width = pieces[0].shape[1]
    for p, piece in enumerate(pieces):
        j = ch_ref[0] ^ p
        col = pl.multiple_of(j * width, 128)
        buf[at : at + count, pl.ds(col, width)] = piece[rows : rows + count, :]


def fetch(layer, w_hbm, w_ref, sems):
    copies = [pltpu.make_async_copy(w_hbm.at[layer, k], w_ref.at[k], sems.at[k]) for k in range(3)]
    for copy in copies:
        copy.start()
    return copies


def tap(buf, w_ref, k, at, count):
    lo = at + (k - 1) * RIM
    return jnp.dot(buf[lo : lo + count, :], w_ref[k], preferred_element_type=F32)


def finish(acc, bins, vec_ref, s_ref, a_ref, at, count):
    s = (bins.astype(F32) + acc + vec_ref[0:1, :]).astype(BF16)
    s_ref[at : at + count, :] = s
    a_ref[at : at + count, :] = gelu(s.astype(F32) * vec_ref[1:2, :] + vec_ref[2:3, :]).astype(BF16)


def first_kernel(ch_ref, p0, p1, p2, p3, bins_ref, vec_ref, w_hbm, s_ref, a_ref, buf, w_ref, sems):
    copies = fetch(0, w_hbm, w_ref, sems)
    place(ch_ref, (p0, p1, p2, p3), 0, buf, 0, FIRST)
    for copy in copies:
        copy.wait()
    count = FIRST - 2 * RIM
    half = count // 2
    for at in (RIM, RIM + half):
        acc = tap(buf, w_ref, 0, at, half) + tap(buf, w_ref, 1, at, half) + tap(buf, w_ref, 2, at, half)
        finish(acc, bins_ref[at : at + half, :], vec_ref, s_ref, a_ref, at - RIM, half)


def second_kernel(ch_ref, p0, p1, p2, p3, r0, r1, r2, r3, bins_ref, vec_ref, w_hbm, s_ref, a_ref, buf, w_ref, sems):
    copies = fetch(0, w_hbm, w_ref, sems)
    rows = bins_ref.shape[0]
    rest = rows - FIRST
    early, late = (p0, p1, p2, p3), (r0, r1, r2, r3)
    place(ch_ref, late, rest, buf, 0, RIM)
    place(ch_ref, early, 0, buf, RIM, FIRST)
    place(ch_ref, late, 0, buf, RIM + FIRST, rest)
    place(ch_ref, late, rest + RIM, buf, RIM + rows, RIM)
    for copy in copies:
        copy.wait()
    start = FIRST - RIM
    half = (rows - start) // 2
    for at, to, count in ((0, 0, RIM), (start, RIM, half), (start + half, RIM + half, half)):
        lo = RIM + at
        acc = tap(buf, w_ref, 0, lo, count) + tap(buf, w_ref, 1, lo, count) + tap(buf, w_ref, 2, lo, count)
        finish(acc, bins_ref[at : at + count, :], vec_ref, s_ref, a_ref, to, count)


def product_kernel(layer, ch_ref, p0, p1, p2, p3, w_hbm, o0, o1, o2, buf, w_ref, sems):
    copies = fetch(layer, w_hbm, w_ref, sems)
    rows = p0.shape[0]
    place(ch_ref, (p0, p1, p2, p3), 0, buf, 0, rows)
    for k, o in ((0, o0), (1, o1), (2, o2)):
        copies[k].wait()
        o[...] = jnp.dot(buf[...], w_ref[k], preferred_element_type=F32).astype(BF16)


def call(kernel, args, outs, scratch_rows, flops):
    width = outs[0][1]
    return pl.pallas_call(
        kernel,
        out_shape=[jax.ShapeDtypeStruct(o, BF16) for o in outs],
        in_specs=[SMEM] + [VMEM] * (len(args) - 2) + [pl.BlockSpec(memory_space=pltpu.HBM)],
        out_specs=[VMEM] * len(outs),
        scratch_shapes=[
            pltpu.VMEM((scratch_rows, 4 * width), BF16),
            pltpu.VMEM((3, 4 * width, width), BF16),
            pltpu.SemaphoreType.DMA((3,)),
        ],
        compiler_params=pltpu.CompilerParams(vmem_limit_bytes=28 * 1024 * 1024),
        cost_estimate=pl.CostEstimate(flops=flops, bytes_accessed=8 * 1024 * 1024, transcendentals=0),
    )(*args)


def per_device(bins_in, pre_scale, pre_shift, conv_weight, conv_bias):
    rows, width = bins_in.shape
    ch = lax.axis_index("ch").astype(jnp.int32).reshape(1)
    hop1 = 1
    hop2 = 4096 // rows
    mac = 2 * 4 * width * width * 3

    f = lambda v: v.astype(F32)
    cat = lambda *v: jnp.concatenate([f(x) for x in v], axis=0)
    products1 = functools.partial(product_kernel, 1)
    products2 = functools.partial(product_kernel, 2)

    def entry(x):
        return gelu(f(x) * pre_scale[0] + pre_shift[0]).astype(BF16)

    act_early = entry(bins_in[:FIRST])
    far_early = chip_swap(act_early)
    act_late = entry(bins_in[FIRST:])
    low = shifted(act_late[-RIM:], 1)
    high = shifted(act_early[:RIM], -1)
    near_early = core_swap(act_early)
    own_late = jnp.concatenate([act_late, low, high], axis=0)
    far_late = chip_swap(own_late)
    near_late = core_swap(own_late)
    early = (act_early, near_early, far_early, core_swap(far_early))

    vec0 = jnp.stack([conv_bias[0], pre_scale[1], pre_shift[1]])
    n0 = FIRST - 2 * RIM
    n1 = rows - n0
    s_x0, a_x0 = call(first_kernel, (ch, *early, bins_in, vec0, conv_weight), [(n0, width)] * 2, FIRST, mac * n0)
    far_x0 = chip_swap(a_x0)
    near_x0 = core_swap(a_x0)
    far_late, a_x0 = lax.optimization_barrier((far_late, a_x0))
    late = (own_late, near_late, far_late, core_swap(far_late))
    s_x1, a_x1 = call(
        second_kernel, (ch, *early, *late, bins_in, vec0, conv_weight), [(n1, width)] * 2, rows + 2 * RIM, mac * n1
    )
    far_x1 = chip_swap(a_x1)
    near_x1 = core_swap(a_x1)
    far_x0, a_x1 = lax.optimization_barrier((far_x0, a_x1))
    g_x0 = (a_x0, near_x0, far_x0, core_swap(far_x0))
    p0a, p1a, p2a = call(products1, (ch, *g_x0, conv_weight), [(n0, width)] * 3, n0, mac * n0)
    from_next_a = shifted(p2a, -hop1)
    far_x1, p0a = lax.optimization_barrier((far_x1, p0a))
    g_x1 = (a_x1, near_x1, far_x1, core_swap(far_x1))
    p0b, p1b, p2b = call(products1, (ch, *g_x1, conv_weight), [(n1, width)] * 3, n1, mac * n1)
    from_next_b = shifted(p2b[:RIM], -hop1)
    from_prev = shifted(p0b[RIM:], hop1)

    s2_hi = f(s_x1[RIM:]) + f(p1b[RIM:]) + cat(p0b[:RIM], p0a) + cat(from_next_b, from_next_a) + conv_bias[1]
    s2_hi = s2_hi.astype(BF16)
    a2_hi = gelu(f(s2_hi) * pre_scale[2] + pre_shift[2]).astype(BF16)
    far_hi = chip_swap(a2_hi)
    near_hi = core_swap(a2_hi)
    from_prev, a2_hi = lax.optimization_barrier((from_prev, a2_hi))
    s2_lo = cat(s_x1[:RIM], s_x0) + cat(p1b[:RIM], p1a) + f(p2b[RIM:]) + f(from_prev) + conv_bias[1]
    s2_lo = s2_lo.astype(BF16)
    a2_lo = gelu(f(s2_lo) * pre_scale[2] + pre_shift[2]).astype(BF16)
    far_lo = chip_swap(a2_lo)
    near_lo = core_swap(a2_lo)

    def last(own, near, far, s2):
        half = s2.shape[0]
        q0, q1, q2 = call(products2, (ch, own, near, far, core_swap(far), conv_weight), [s2.shape] * 3, half, mac * half)
        return shifted(q0, hop2), q1, shifted(q2, -hop2)

    far_hi, a2_lo = lax.optimization_barrier((far_hi, a2_lo))
    up_hi, q_hi, down_hi = last(a2_hi, near_hi, far_hi, s2_hi)
    far_lo, q_hi = lax.optimization_barrier((far_lo, q_hi))
    up_lo, q_lo, down_lo = last(a2_lo, near_lo, far_lo, s2_lo)
    out_hi = (f(s2_hi) + f(q_hi) + f(up_hi) + f(down_hi) + conv_bias[2]).astype(BF16)
    out_lo = (f(s2_lo) + f(q_lo) + f(up_lo) + f(down_lo) + conv_bias[2]).astype(BF16)
    return jnp.concatenate([out_lo, out_hi], axis=0)


def solution(mesh):
    return jax.shard_map(
        per_device,
        mesh=mesh,
        in_specs=(
            P("seq", "ch"),
            P(None, "ch"),
            P(None, "ch"),
            P(None, None, None, "ch"),
            P(None, "ch"),
        ),
        out_specs=P("seq", "ch"),
        check_vma=False,
    )
```

time: 172 us -> 149 us (0.87)
  waiting for transfers between devices: 78.7 us -> 65.1 us
  local copies, waits for them, and re-layouts: 10.3 us -> 5.01 us
  starting transfers between devices: 51 us -> 45.9 us
  Pallas kernels: 22 us -> 24.4 us
    ppermute x6, waiting for transfers between devices: 47.6 us -> 21.6 us  [chip_swap(): return lax.ppermute(array, 'ch', [(i, i ^ 2) for i in range(4)])]
    ppermute x9, waiting for transfers between devices: 31.1 us -> 41.1 us  [shifted(): return lax.ppermute(array, 'seq', pairs)]
    slice x6 -> x4, local copies, waits for them, and re-layouts: 9.06 us -> 0.92 us  [the longest x1 0.89 us: per_device(): a2_hi = gelu(f(s2_hi) * pre_scale[2] + pre_shift[2]).astype(BF16)]
    ppermute x9, starting transfers between devices: 43.2 us -> 39.7 us  [shifted(): return lax.ppermute(array, 'seq', pairs)]
    unnamed x6 -> x8, local copies, waits for them, and re-layouts: 1.14 us -> 4.02 us
    pallas_call x6, Pallas kernels: 22 us -> 24.4 us  [call(): pl.pallas_call(kernel, out_shape=[jax.ShapeDtypeStruct(o, BF16) for o in...]
    ppermute x12, waiting for transfers between devices: 0.03 us -> 2.37 us  [core_swap(): return lax.ppermute(array, 'ch', [(i, i ^ 1) for i in range(4)])]
    convert_element_type x2 -> x4, other arithmetic: 3.48 us -> 5.52 us  [the longest x2 3.91 us: entry(): return gelu(f(x) * pre_scale[0] + pre_shift[0]).astype(BF16)]
  transfers between devices with their start and end apart: 27 -> 27, of which waited for: 11 -> 14; matrix products, arithmetic and copies ran while one was open for 5% -> 3% of each run, Pallas kernels for 9% -> 16%
where the time goes in v2:
time: 149 us; the launch traced here: 148 us
  waiting for transfers between devices  65.1 us (44%)
  starting transfers between devices  45.9 us (31%)
  Pallas kernels  24.4 us (16%)
  other arithmetic  7.7 us (5%)
  local copies, waits for them, and re-layouts  5.01 us (3%)
    ppermute x9, waiting for transfers between devices, shifted(): return lax.ppermute(array, 'seq', pairs)  41.1 us
    ppermute x9, starting transfers between devices, shifted(): return lax.ppermute(array, 'seq', pairs)  39.7 us
    pallas_call x6, Pallas kernels, call(): pl.pallas_call(kernel, out_shape=[jax.ShapeDtypeStruct(o, BF16) for o in...  24.4 us
    ppermute x6, waiting for transfers between devices, chip_swap(): return lax.ppermute(array, 'ch', [(i, i ^ 2) for i in range(4)])  21.6 us
    ppermute x6, starting transfers between devices, chip_swap(): return lax.ppermute(array, 'ch', [(i, i ^ 2) for i in range(4)])  5.08 us
    unnamed x8, local copies, waits for them, and re-layouts  4.02 us
    convert_element_type x2, other arithmetic, entry(): return gelu(f(x) * pre_scale[0] + pre_shift[0]).astype(BF16)  3.91 us
  transfers between devices with their start and end apart: 27, of which 14 were waited for; matrix products, arithmetic and copies ran while one was open for 3% of the time, Pallas kernels for 16%

profile of v2, /device:TPU:6, one launch (start us, length us, event | category | flops | bytes accessed | tf_op | source)
XLA Modules:
  0.0 148.4 jit_solution(9239871397124517903)
XLA Ops:
  0.9 2.1 %fusion.1.p0 = bf16[576,384]{1,0:T(8,128)(2,1)S(1)} fusion(f32[384]{0:T(512)S(1)} %get-tuple-element.66, f32[384]{0:T(512)S(1)} %get-tuple-element.77, bf16[1024,384]{1,0:T(8,128)(2,1)} %bins_ref.3), kind=kLoop, calls=%fused_computation.9 | loop fusion | flops 7741440 | bytes 887808 | tf_op jit(solution)/shard_map/convert_element_type | solution.py:147
  4.7 10.4 %collective-permute-start.4 = (bf16[64,384]{1,0:T(8,128)(2,1)S(1)}, bf16[64,384]{1,0:T(8,128)(2,1)S(1)}, u32[]{:S(2)}, u32[]{:S(2)}) collective-permute-start(bf16[64,384]{1,0:T(8,128)(2,1)S(1)} %slice.91), channel_id=1, source_target_pairs={{4,0},{8,4},{12,8},{16,12},{20,16},{24,20},{28,24},{32,28},{36,32}... | collective-permute-start | bytes 147464 | tf_op jit(solution)/shard_map/ppermute | solution.py:35
  16.9 1.9 %collective-permute-start.3 = (bf16[64,384]{1,0:T(8,128)(2,1)S(1)}, bf16[64,384]{1,0:T(8,128)(2,1)S(1)}, u32[]{:S(2)}, u32[]{:S(2)}) collective-permute-start(bf16[64,384]{1,0:T(8,128)(2,1)S(1)} %slice.90), channel_id=1, source_target_pairs={{0,4},{4,8},{8,12},{12,16},{16,20},{20,24},{24,28},{28,32},{32,36}... | collective-permute-start | bytes 147464 | tf_op jit(solution)/shard_map/ppermute | solution.py:35
  19.4 8.1 %collective-permute-done.3 = bf16[64,384]{1,0:T(8,128)(2,1)S(1)} collective-permute-done((bf16[64,384]{1,0:T(8,128)(2,1)S(1)}, bf16[64,384]{1,0:T(8,128)(2,1)S(1)}, u32[]{:S(2)}, u32[]{:S(2)}) %collective-permute-start.3) | collective-permute-done | bytes 49184 | tf_op jit(solution)/shard_map/ppermute | solution.py:35
  27.9 4.0 %copy-done = bf16[3,3,1536,384]{3,2,1,0:T(8,128)(2,1)S(1)} copy-done((bf16[3,3,1536,384]{3,2,1,0:T(8,128)(2,1)S(1)}, bf16[3,3,1536,384]{3,2,1,0:T(8,128)(2,1)}, u32[]{:S(2)}) %copy-start) | copy-done | bytes 10616856
  31.9 4.0 %shard_map.55 = (bf16[448,384]{1,0:T(8,128)(2,1)S(1)}, bf16[448,384]{1,0:T(8,128)(2,1)S(1)}) custom-call(s32[1]{0:T(128)} %bitcast.ch_ref, bf16[576,384]{1,0:T(8,128)(2,1)S(1)} %fusion.1.p0, bf16[576,384]{1,0:T(8,128)(2,1)S(1)} %collective-permute-done.p1, bf16[576,384]{1,0:T(8,128)(2,1)S(1)} %collective-permute-done.1.p2, ...), custom_call_target="tpu_custom_call" | custom-call | flops 1585446912 | bytes 8388608 | tf_op jit(solution)/shard_map/pallas_call | solution.py:119
  39.6 5.1 %shard_map.56 = (bf16[576,384]{1,0:T(8,128)(2,1)S(1)}, bf16[576,384]{1,0:T(8,128)(2,1)S(1)}) custom-call(s32[1]{0:T(128)} %bitcast.ch_ref, bf16[576,384]{1,0:T(8,128)(2,1)S(1)} %fusion.1.p0, bf16[576,384]{1,0:T(8,128)(2,1)S(1)} %collective-permute-done.p1, bf16[576,384]{1,0:T(8,128)(2,1)S(1)} %collective-permute-done.1.p2, ...), custom_call_target="tpu_custom_call" | custom-call | flops 2038431744 | bytes 8388608 | tf_op jit(solution)/shard_map/pallas_call | solution.py:119
  44.7 3.5 %collective-permute-done.8.p2 = bf16[448,384]{1,0:T(8,128)(2,1)S(1)} collective-permute-done((bf16[448,384]{1,0:T(8,128)(2,1)S(1)}, bf16[448,384]{1,0:T(8,128)(2,1)S(1)}, u32[]{:S(2)}, u32[]{:S(2)}) %collective-permute-start.8) | collective-permute-done | bytes 344096 | tf_op jit(solution)/shard_map/ppermute | solution.py:39
  49.9 3.5 %shard_map.57 = (bf16[448,384]{1,0:T(8,128)(2,1)S(1)}, bf16[448,384]{1,0:T(8,128)(2,1)S(1)}, bf16[448,384]{1,0:T(8,128)(2,1)S(1)}) custom-call(s32[1]{0:T(128)} %bitcast.ch_ref, bf16[448,384]{1,0:T(8,128)(2,1)S(1)} %get-tuple-element.39.p0, bf16[448,384]{1,0:T(8,128)(2,1)S(1)} %collective-permute-done.11.p1, bf16[448,384]{1,0:T(8,128)(2,1)S(1)} %collective-permute-done.8.p2, ...), custom_call_target="tpu_custom_call" | custom-call | flops 1585446912 | bytes 8388608 | tf_op jit(solution)/shard_map/pallas_call | solution.py:119
  53.4 7.4 %collective-permute-done.10.p2 = bf16[576,384]{1,0:T(8,128)(2,1)S(1)} collective-permute-done((bf16[576,384]{1,0:T(8,128)(2,1)S(1)}, bf16[576,384]{1,0:T(8,128)(2,1)S(1)}, u32[]{:S(2)}, u32[]{:S(2)}) %collective-permute-start.10) | collective-permute-done | bytes 442400 | tf_op jit(solution)/shard_map/ppermute | solution.py:39
  60.9 2.3 %collective-permute-start.16 = (bf16[448,384]{1,0:T(8,128)(2,1)S(1)}, bf16[448,384]{1,0:T(8,128)(2,1)S(1)}, u32[]{:S(2)}, u32[]{:S(2)}) collective-permute-start(bf16[448,384]{1,0:T(8,128)(2,1)S(1)} %get-tuple-element.48), channel_id=1, source_target_pairs={{4,0},{8,4},{12,8},{16,12},{20,16},{24,20},{28,24},{32,28},{36,32}... | collective-permute-start | bytes 1032200 | tf_op jit(solution)/shard_map/ppermute | solution.py:35
  63.2 4.2 %shard_map.58 = (bf16[576,384]{1,0:T(8,128)(2,1)S(1)}, bf16[576,384]{1,0:T(8,128)(2,1)S(1)}, bf16[576,384]{1,0:T(8,128)(2,1)S(1)}) custom-call(s32[1]{0:T(128)} %bitcast.ch_ref, bf16[576,384]{1,0:T(8,128)(2,1)S(1)} %get-tuple-element.38.p0, bf16[576,384]{1,0:T(8,128)(2,1)S(1)} %collective-permute-done.9.p1, bf16[576,384]{1,0:T(8,128)(2,1)S(1)} %collective-permute-done.10.p2, ...), custom_call_target="tpu_custom_call" | custom-call | flops 2038431744 | bytes 8388608 | tf_op jit(solution)/shard_map/pallas_call | solution.py:119
  67.4 3.3 %collective-permute-start.15 = (bf16[64,384]{1,0:T(8,128)(2,1)S(1)}, bf16[64,384]{1,0:T(8,128)(2,1)S(1)}, u32[]{:S(2)}, u32[]{:S(2)}) collective-permute-start(bf16[64,384]{1,0:T(8,128)(2,1)S(1)} %slice.85), channel_id=1, source_target_pairs={{4,0},{8,4},{12,8},{16,12},{20,16},{24,20},{28,24},{32,28},{36,32}... | collective-permute-start | bytes 147464 | tf_op jit(solution)/shard_map/ppermute | solution.py:35
  70.8 4.0 %collective-permute-start.14 = (bf16[512,384]{1,0:T(8,128)(2,1)S(1)}, bf16[512,384]{1,0:T(8,128)(2,1)S(1)}, u32[]{:S(2)}, u32[]{:S(2)}) collective-permute-start(bf16[512,384]{1,0:T(8,128)(2,1)S(1)} %slice.81), channel_id=1, source_target_pairs={{0,4},{4,8},{8,12},{12,16},{16,20},{20,24},{24,28},{28,32},{32,36}... | collective-permute-start | bytes 1179656 | tf_op jit(solution)/shard_map/ppermute | solution.py:35
  77.5 10.8 %collective-permute-done.14 = bf16[512,384]{1,0:T(8,128)(2,1)S(1)} collective-permute-done((bf16[512,384]{1,0:T(8,128)(2,1)S(1)}, bf16[512,384]{1,0:T(8,128)(2,1)S(1)}, u32[]{:S(2)}, u32[]{:S(2)}) %collective-permute-start.14) | collective-permute-done | bytes 393248 | tf_op jit(solution)/shard_map/ppermute | solution.py:35
  89.4 3.0 %collective-permute-done.17.p2 = bf16[512,384]{1,0:T(8,128)(2,1)S(1)} collective-permute-done((bf16[512,384]{1,0:T(8,128)(2,1)S(1)}, bf16[512,384]{1,0:T(8,128)(2,1)S(1)}, u32[]{:S(2)}, u32[]{:S(2)}) %collective-permute-start.17) | collective-permute-done | bytes 393248 | tf_op jit(solution)/shard_map/ppermute | solution.py:39
  94.5 3.8 %shard_map.59 = (bf16[512,384]{1,0:T(8,128)(2,1)S(1)}, bf16[512,384]{1,0:T(8,128)(2,1)S(1)}, bf16[512,384]{1,0:T(8,128)(2,1)S(1)}) custom-call(s32[1]{0:T(128)} %bitcast.ch_ref, bf16[512,384]{1,0:T(8,128)(2,1)S(1)} %get-tuple-element.51.p0, bf16[512,384]{1,0:T(8,128)(2,1)S(1)} %collective-permute-done.20.p1, ...), custom_call_target="tpu_custom_call" | custom-call | flops 1811939328 | bytes 8388608 | tf_op jit(solution)/shard_map/pallas_call | solution.py:119
  98.3 5.7 %collective-permute-done.19.p2 = bf16[512,384]{1,0:T(8,128)(2,1)S(1)} collective-permute-done((bf16[512,384]{1,0:T(8,128)(2,1)S(1)}, bf16[512,384]{1,0:T(8,128)(2,1)S(1)}, u32[]{:S(2)}, u32[]{:S(2)}) %collective-permute-start.19) | collective-permute-done | bytes 393248 | tf_op jit(solution)/shard_map/ppermute | solution.py:39
  105.9 6.9 %collective-permute-start.26 = (bf16[512,384]{1,0:T(8,128)(2,1)S(1)}, bf16[512,384]{1,0:T(8,128)(2,1)S(1)}, u32[]{:S(2)}, u32[]{:S(2)}) collective-permute-start(bf16[512,384]{1,0:T(8,128)(2,1)S(1)} %get-tuple-element.60), channel_id=1, source_target_pairs={{16,0},{20,4},{24,8},{28,12},{32,16},{36,20},{40,24},{44,28},{48,3... | collective-permute-start | bytes 1179656 | tf_op jit(solution)/shard_map/ppermute | solution.py:35
  112.9 3.8 %shard_map.60 = (bf16[512,384]{1,0:T(8,128)(2,1)S(1)}, bf16[512,384]{1,0:T(8,128)(2,1)S(1)}, bf16[512,384]{1,0:T(8,128)(2,1)S(1)}) custom-call(s32[1]{0:T(128)} %bitcast.ch_ref, bf16[512,384]{1,0:T(8,128)(2,1)S(1)} %get-tuple-element.50.p0, bf16[512,384]{1,0:T(8,128)(2,1)S(1)} %collective-permute-done.18.p1, ...), custom_call_target="tpu_custom_call" | custom-call | flops 1811939328 | bytes 8388608 | tf_op jit(solution)/shard_map/pallas_call | solution.py:119
  116.7 1.9 %collective-permute-start.23 = (bf16[512,384]{1,0:T(8,128)(2,1)S(1)}, bf16[512,384]{1,0:T(8,128)(2,1)S(1)}, u32[]{:S(2)}, u32[]{:S(2)}) collective-permute-start(bf16[512,384]{1,0:T(8,128)(2,1)S(1)} %get-tuple-element.56), channel_id=1, source_target_pairs={{0,16},{4,20},{8,24},{12,28},{16,32},{20,36},{24,40},{28,44},{32,4... | collective-permute-start | bytes 1179656 | tf_op jit(solution)/shard_map/ppermute | solution.py:35
  118.7 6.9 %collective-permute-start.24 = (bf16[512,384]{1,0:T(8,128)(2,1)S(1)}, bf16[512,384]{1,0:T(8,128)(2,1)S(1)}, u32[]{:S(2)}, u32[]{:S(2)}) collective-permute-start(bf16[512,384]{1,0:T(8,128)(2,1)S(1)} %get-tuple-element.57), channel_id=1, source_target_pairs={{16,0},{20,4},{24,8},{28,12},{32,16},{36,20},{40,24},{44,28},{48,3... | collective-permute-start | bytes 1179656 | tf_op jit(solution)/shard_map/ppermute | solution.py:35
  125.6 11.9 %collective-permute-done.25 = bf16[512,384]{1,0:T(8,128)(2,1)S(1)} collective-permute-done((bf16[512,384]{1,0:T(8,128)(2,1)S(1)}, bf16[512,384]{1,0:T(8,128)(2,1)S(1)}, u32[]{:S(2)}, u32[]{:S(2)}) %collective-permute-start.25) | collective-permute-done | bytes 393248 | tf_op jit(solution)/shard_map/ppermute | solution.py:35
  137.5 8.0 %collective-permute-done.23 = bf16[512,384]{1,0:T(8,128)(2,1)S(1)} collective-permute-done((bf16[512,384]{1,0:T(8,128)(2,1)S(1)}, bf16[512,384]{1,0:T(8,128)(2,1)S(1)}, u32[]{:S(2)}, u32[]{:S(2)}) %collective-permute-start.23) | collective-permute-done | bytes 393248 | tf_op jit(solution)/shard_map/ppermute | solution.py:35
  (61 shorter events, 21.3 us)
Async XLA Ops:
  3.0 15.9 %collective-permute-start.1 = (bf16[576,384]{1,0:T(8,128)(2,1)S(1)}, bf16[576,384]{1,0:T(8,128)(2,1)S(1)}, u32[]{:S(2)}, u32[]{:S(2)}) collective-permute-start(bf16[576,384]{1,0:T(8,128)(2,1)S(1)} %fusion.1.p0), channel_id=1, source_target_pairs={{0,2},{1,3},{2,0},{3,1},{4,6},{5,7},{6,4},{7,5},{8,10},{9,11},{10,... | collective-permute-start | bytes 1327112 | tf_op jit(solution)/shard_map/ppermute | solution.py:39
  4.7 14.7 %collective-permute-start.4 = (bf16[64,384]{1,0:T(8,128)(2,1)S(1)}, bf16[64,384]{1,0:T(8,128)(2,1)S(1)}, u32[]{:S(2)}, u32[]{:S(2)}) collective-permute-start(bf16[64,384]{1,0:T(8,128)(2,1)S(1)} %slice.91), channel_id=1, source_target_pairs={{4,0},{8,4},{12,8},{16,12},{20,16},{24,20},{28,24},{32,28},{36,32}... | collective-permute-start | bytes 147464 | tf_op jit(solution)/shard_map/ppermute | solution.py:35
  16.9 10.6 %collective-permute-start.3 = (bf16[64,384]{1,0:T(8,128)(2,1)S(1)}, bf16[64,384]{1,0:T(8,128)(2,1)S(1)}, u32[]{:S(2)}, u32[]{:S(2)}) collective-permute-start(bf16[64,384]{1,0:T(8,128)(2,1)S(1)} %slice.90), channel_id=1, source_target_pairs={{0,4},{4,8},{8,12},{12,16},{16,20},{20,24},{24,28},{28,32},{32,36}... | collective-permute-start | bytes 147464 | tf_op jit(solution)/shard_map/ppermute | solution.py:35
  18.8 9.1 %collective-permute-start = (bf16[576,384]{1,0:T(8,128)(2,1)S(1)}, bf16[576,384]{1,0:T(8,128)(2,1)S(1)}, u32[]{:S(2)}, u32[]{:S(2)}) collective-permute-start(bf16[576,384]{1,0:T(8,128)(2,1)S(1)} %fusion.1.p0), channel_id=1, source_target_pairs={{0,1},{1,0},{2,3},{3,2},{4,5},{5,4},{6,7},{7,6},{8,9},{9,8},{10,11... | collective-permute-start | bytes 1327112 | tf_op jit(solution)/shard_map/ppermute | solution.py:43
  18.9 9.0 %collective-permute-start.2 = (bf16[576,384]{1,0:T(8,128)(2,1)S(1)}, bf16[576,384]{1,0:T(8,128)(2,1)S(1)}, u32[]{:S(2)}, u32[]{:S(2)}) collective-permute-start(bf16[576,384]{1,0:T(8,128)(2,1)S(1)} %collective-permute-done.1.p2), channel_id=1, source_target_pairs={{0,1},{1,0},{2,3},{3,2},{4,5},{5,4},{6,7},{7,6},{8,9},{9,8},{10,11... | collective-permute-start | bytes 1327112 | tf_op jit(solution)/shard_map/ppermute | solution.py:43
  27.5 10.3 %collective-permute-start.6 = (bf16[576,384]{1,0:T(8,128)(2,1)S(1)}, bf16[576,384]{1,0:T(8,128)(2,1)S(1)}, u32[]{:S(2)}, u32[]{:S(2)}) collective-permute-start(bf16[576,384]{1,0:T(8,128)(2,1)S(1)} %pad_maximum_fusion.1.r0), channel_id=1, source_target_pairs={{0,2},{1,3},{2,0},{3,1},{4,6},{5,7},{6,4},{7,5},{8,10},{9,11},{10,... | collective-permute-start | bytes 1327112 | tf_op jit(solution)/shard_map/ppermute | solution.py:39
  27.8 10.6 %collective-permute-start.5 = (bf16[576,384]{1,0:T(8,128)(2,1)S(1)}, bf16[576,384]{1,0:T(8,128)(2,1)S(1)}, u32[]{:S(2)}, u32[]{:S(2)}) collective-permute-start(bf16[576,384]{1,0:T(8,128)(2,1)S(1)} %pad_maximum_fusion.1.r0), channel_id=1, source_target_pairs={{0,1},{1,0},{2,3},{3,2},{4,5},{5,4},{6,7},{7,6},{8,9},{9,8},{10,11... | collective-permute-start | bytes 1327112 | tf_op jit(solution)/shard_map/ppermute | solution.py:43
  37.8 10.5 %collective-permute-start.8 = (bf16[448,384]{1,0:T(8,128)(2,1)S(1)}, bf16[448,384]{1,0:T(8,128)(2,1)S(1)}, u32[]{:S(2)}, u32[]{:S(2)}) collective-permute-start(bf16[448,384]{1,0:T(8,128)(2,1)S(1)} %get-tuple-element.39.p0), channel_id=1, source_target_pairs={{0,2},{1,3},{2,0},{3,1},{4,6},{5,7},{6,4},{7,5},{8,10},{9,11},{10,... | collective-permute-start | bytes 1032200 | tf_op jit(solution)/shard_map/ppermute | solution.py:39
  38.4 10.4 %collective-permute-start.11 = (bf16[448,384]{1,0:T(8,128)(2,1)S(1)}, bf16[448,384]{1,0:T(8,128)(2,1)S(1)}, u32[]{:S(2)}, u32[]{:S(2)}) collective-permute-start(bf16[448,384]{1,0:T(8,128)(2,1)S(1)} %get-tuple-element.39.p0), channel_id=1, source_target_pairs={{0,1},{1,0},{2,3},{3,2},{4,5},{5,4},{6,7},{7,6},{8,9},{9,8},{10,11... | collective-permute-start | bytes 1032200 | tf_op jit(solution)/shard_map/ppermute | solution.py:43
  48.3 12.6 %collective-permute-start.10 = (bf16[576,384]{1,0:T(8,128)(2,1)S(1)}, bf16[576,384]{1,0:T(8,128)(2,1)S(1)}, u32[]{:S(2)}, u32[]{:S(2)}) collective-permute-start(bf16[576,384]{1,0:T(8,128)(2,1)S(1)} %get-tuple-element.38.p0), channel_id=1, source_target_pairs={{0,2},{1,3},{2,0},{3,1},{4,6},{5,7},{6,4},{7,5},{8,10},{9,11},{10,... | collective-permute-start | bytes 1327112 | tf_op jit(solution)/shard_map/ppermute | solution.py:39
  48.6 14.6 %collective-permute-start.9 = (bf16[576,384]{1,0:T(8,128)(2,1)S(1)}, bf16[576,384]{1,0:T(8,128)(2,1)S(1)}, u32[]{:S(2)}, u32[]{:S(2)}) collective-permute-start(bf16[576,384]{1,0:T(8,128)(2,1)S(1)} %get-tuple-element.38.p0), channel_id=1, source_target_pairs={{0,1},{1,0},{2,3},{3,2},{4,5},{5,4},{6,7},{7,6},{8,9},{9,8},{10,11... | collective-permute-start | bytes 1327112 | tf_op jit(solution)/shard_map/ppermute | solution.py:43
  60.9 2.4 %collective-permute-start.13 = (bf16[576,384]{1,0:T(8,128)(2,1)S(1)}, bf16[576,384]{1,0:T(8,128)(2,1)S(1)}, u32[]{:S(2)}, u32[]{:S(2)}) collective-permute-start(bf16[576,384]{1,0:T(8,128)(2,1)S(1)} %collective-permute-done.10.p2), channel_id=1, source_target_pairs={{0,1},{1,0},{2,3},{3,2},{4,5},{5,4},{6,7},{7,6},{8,9},{9,8},{10,11... | collective-permute-start | bytes 1327112 | tf_op jit(solution)/shard_map/ppermute | solution.py:43
  60.9 14.2 %collective-permute-start.16 = (bf16[448,384]{1,0:T(8,128)(2,1)S(1)}, bf16[448,384]{1,0:T(8,128)(2,1)S(1)}, u32[]{:S(2)}, u32[]{:S(2)}) collective-permute-start(bf16[448,384]{1,0:T(8,128)(2,1)S(1)} %get-tuple-element.48), channel_id=1, source_target_pairs={{4,0},{8,4},{12,8},{16,12},{20,16},{24,20},{28,24},{32,28},{36,32}... | collective-permute-start | bytes 1032200 | tf_op jit(solution)/shard_map/ppermute | solution.py:35
  67.4 8.4 %collective-permute-start.15 = (bf16[64,384]{1,0:T(8,128)(2,1)S(1)}, bf16[64,384]{1,0:T(8,128)(2,1)S(1)}, u32[]{:S(2)}, u32[]{:S(2)}) collective-permute-start(bf16[64,384]{1,0:T(8,128)(2,1)S(1)} %slice.85), channel_id=1, source_target_pairs={{4,0},{8,4},{12,8},{16,12},{20,16},{24,20},{28,24},{32,28},{36,32}... | collective-permute-start | bytes 147464 | tf_op jit(solution)/shard_map/ppermute | solution.py:35
  70.8 17.5 %collective-permute-start.14 = (bf16[512,384]{1,0:T(8,128)(2,1)S(1)}, bf16[512,384]{1,0:T(8,128)(2,1)S(1)}, u32[]{:S(2)}, u32[]{:S(2)}) collective-permute-start(bf16[512,384]{1,0:T(8,128)(2,1)S(1)} %slice.81), channel_id=1, source_target_pairs={{0,4},{4,8},{8,12},{12,16},{16,20},{20,24},{24,28},{28,32},{32,36}... | collective-permute-start | bytes 1179656 | tf_op jit(solution)/shard_map/ppermute | solution.py:35
  76.9 15.6 %collective-permute-start.17 = (bf16[512,384]{1,0:T(8,128)(2,1)S(1)}, bf16[512,384]{1,0:T(8,128)(2,1)S(1)}, u32[]{:S(2)}, u32[]{:S(2)}) collective-permute-start(bf16[512,384]{1,0:T(8,128)(2,1)S(1)} %get-tuple-element.51.p0), channel_id=1, source_target_pairs={{0,2},{1,3},{2,0},{3,1},{4,6},{5,7},{6,4},{7,5},{8,10},{9,11},{10,... | collective-permute-start | bytes 1179656 | tf_op jit(solution)/shard_map/ppermute | solution.py:39
  77.5 16.9 %collective-permute-start.20 = (bf16[512,384]{1,0:T(8,128)(2,1)S(1)}, bf16[512,384]{1,0:T(8,128)(2,1)S(1)}, u32[]{:S(2)}, u32[]{:S(2)}) collective-permute-start(bf16[512,384]{1,0:T(8,128)(2,1)S(1)} %get-tuple-element.51.p0), channel_id=1, source_target_pairs={{0,1},{1,0},{2,3},{3,2},{4,5},{5,4},{6,7},{7,6},{8,9},{9,8},{10,11... | collective-permute-start | bytes 1179656 | tf_op jit(solution)/shard_map/ppermute | solution.py:43
  92.5 11.5 %collective-permute-start.19 = (bf16[512,384]{1,0:T(8,128)(2,1)S(1)}, bf16[512,384]{1,0:T(8,128)(2,1)S(1)}, u32[]{:S(2)}, u32[]{:S(2)}) collective-permute-start(bf16[512,384]{1,0:T(8,128)(2,1)S(1)} %get-tuple-element.50.p0), channel_id=1, source_target_pairs={{0,2},{1,3},{2,0},{3,1},{4,6},{5,7},{6,4},{7,5},{8,10},{9,11},{10,... | collective-permute-start | bytes 1179656 | tf_op jit(solution)/shard_map/ppermute | solution.py:39
  94.2 18.6 %collective-permute-start.18 = (bf16[512,384]{1,0:T(8,128)(2,1)S(1)}, bf16[512,384]{1,0:T(8,128)(2,1)S(1)}, u32[]{:S(2)}, u32[]{:S(2)}) collective-permute-start(bf16[512,384]{1,0:T(8,128)(2,1)S(1)} %get-tuple-element.50.p0), channel_id=1, source_target_pairs={{0,1},{1,0},{2,3},{3,2},{4,5},{5,4},{6,7},{7,6},{8,9},{9,8},{10,11... | collective-permute-start | bytes 1179656 | tf_op jit(solution)/shard_map/ppermute | solution.py:43
  104.0 8.9 %collective-permute-start.22 = (bf16[512,384]{1,0:T(8,128)(2,1)S(1)}, bf16[512,384]{1,0:T(8,128)(2,1)S(1)}, u32[]{:S(2)}, u32[]{:S(2)}) collective-permute-start(bf16[512,384]{1,0:T(8,128)(2,1)S(1)} %collective-permute-done.19.p2), channel_id=1, source_target_pairs={{0,1},{1,0},{2,3},{3,2},{4,5},{5,4},{6,7},{7,6},{8,9},{9,8},{10,11... | collective-permute-start | bytes 1179656 | tf_op jit(solution)/shard_map/ppermute | solution.py:43
  104.0 33.5 %collective-permute-start.25 = (bf16[512,384]{1,0:T(8,128)(2,1)S(1)}, bf16[512,384]{1,0:T(8,128)(2,1)S(1)}, u32[]{:S(2)}, u32[]{:S(2)}) collective-permute-start(bf16[512,384]{1,0:T(8,128)(2,1)S(1)} %get-tuple-element.59), channel_id=1, source_target_pairs={{0,16},{4,20},{8,24},{12,28},{16,32},{20,36},{24,40},{28,44},{32,4... | collective-permute-start | bytes 1179656 | tf_op jit(solution)/shard_map/ppermute | solution.py:35
  105.9 31.6 %collective-permute-start.26 = (bf16[512,384]{1,0:T(8,128)(2,1)S(1)}, bf16[512,384]{1,0:T(8,128)(2,1)S(1)}, u32[]{:S(2)}, u32[]{:S(2)}) collective-permute-start(bf16[512,384]{1,0:T(8,128)(2,1)S(1)} %get-tuple-element.60), channel_id=1, source_target_pairs={{16,0},{20,4},{24,8},{28,12},{32,16},{36,20},{40,24},{44,28},{48,3... | collective-permute-start | bytes 1179656 | tf_op jit(solution)/shard_map/ppermute | solution.py:35
  116.7 28.8 %collective-permute-start.23 = (bf16[512,384]{1,0:T(8,128)(2,1)S(1)}, bf16[512,384]{1,0:T(8,128)(2,1)S(1)}, u32[]{:S(2)}, u32[]{:S(2)}) collective-permute-start(bf16[512,384]{1,0:T(8,128)(2,1)S(1)} %get-tuple-element.56), channel_id=1, source_target_pairs={{0,16},{4,20},{8,24},{12,28},{16,32},{20,36},{24,40},{28,44},{32,4... | collective-permute-start | bytes 1179656 | tf_op jit(solution)/shard_map/ppermute | solution.py:35
  118.7 28.3 %collective-permute-start.24 = (bf16[512,384]{1,0:T(8,128)(2,1)S(1)}, bf16[512,384]{1,0:T(8,128)(2,1)S(1)}, u32[]{:S(2)}, u32[]{:S(2)}) collective-permute-start(bf16[512,384]{1,0:T(8,128)(2,1)S(1)} %get-tuple-element.57), channel_id=1, source_target_pairs={{16,0},{20,4},{24,8},{28,12},{32,16},{36,20},{40,24},{44,28},{48,3... | collective-permute-start | bytes 1179656 | tf_op jit(solution)/shard_map/ppermute | solution.py:35
  (7 other events, 72.7 us)

commit v3 on v0

v3 whole, which is shorter than its diff:
```python
import functools

import jax
import jax.numpy as jnp
from jax import lax
from jax.experimental import pallas as pl
from jax.experimental.pallas import tpu as pltpu
from jax.sharding import PartitionSpec as P

F32 = jnp.float32
BF16 = jnp.bfloat16
ERFC = (
    -1.26551223, 1.00002368, 0.37409196, 0.09678418, -0.18628806,
    0.27886807, -1.13520398, 1.48851587, -0.82215223, 0.17087277,
)
ROWS = 1024
MID = ROWS // 2
W = 384
R = 64
H = 416
N = H - 2 * R
A = MID - H + R
Q = N + R - A
M = 2 * A
X0 = 2 * N
X1 = M + 2 * R
REST = ROWS - 2 * H
SPAN = M + 2 * R
PART = 96
VMEM = pl.BlockSpec(memory_space=pltpu.VMEM)
SMEM = pl.BlockSpec(memory_space=pltpu.SMEM)
HBM = pl.BlockSpec(memory_space=pltpu.HBM)


def gelu(x):
    z = jnp.abs(x) * 0.7071067811865476
    t = 1.0 / (1.0 + 0.5 * z)
    poly = jnp.full_like(t, ERFC[-1])
    for c in ERFC[-2::-1]:
        poly = poly * t + c
    e = t * jnp.exp(poly - z * z)
    return 0.5 * x * jnp.where(x >= 0.0, 2.0 - e, e)


def shifted(array, by):
    size = lax.axis_size("seq")
    pairs = [(i, i + by) for i in range(size) if 0 <= i + by < size]
    return lax.ppermute(array, "seq", pairs)


def chip_swap(array):
    return lax.ppermute(array, "ch", [(i, i ^ 2) for i in range(4)])


def core_swap(array):
    return lax.ppermute(array, "ch", [(i, i ^ 1) for i in range(4)])


def dot(a, b):
    return jnp.dot(a, b, preferred_element_type=F32)


def wide(pieces, at, count):
    return jnp.concatenate([p[at : at + count, :] for p in pieces], axis=1)


def stage_kernel(ch_ref, w_hbm, o_ref, sems):
    copies = []
    for layer in range(3):
        for k in range(3):
            for p in range(4):
                row = pl.multiple_of((ch_ref[0] ^ p) * W, 128)
                copies.append(
                    pltpu.make_async_copy(
                        w_hbm.at[layer, k, pl.ds(row, W), :],
                        o_ref.at[layer, pl.ds(p * W, W), pl.ds(k * W, W)],
                        sems.at[len(copies)],
                    )
                )
    for copy in copies:
        copy.start()
    for copy in copies:
        copy.wait()


def finish(s, vec_ref, s_ref, a_ref, at, count):
    s = (s + vec_ref[0:1, :]).astype(BF16)
    s_ref[at : at + count, :] = s
    a_ref[at : at + count, :] = gelu(s.astype(F32) * vec_ref[1:2, :] + vec_ref[2:3, :]).astype(BF16)


def ends_kernel(p0, p1, p2, p3, bins_ref, vec_ref, w_ref, s_ref, a_ref):
    pieces = (p0, p1, p2, p3)
    for half in range(2):
        acc = dot(wide(pieces, half * H, N), w_ref[0, :, 0:W])
        acc += dot(wide(pieces, half * H + R, N), w_ref[0, :, W : 2 * W])
        acc += dot(wide(pieces, half * H + 2 * R, N), w_ref[0, :, 2 * W : 3 * W])
        at = R if half == 0 else ROWS - H + R
        finish(acc + bins_ref[at : at + N, :].astype(F32), vec_ref, s_ref, a_ref, half * N, N)


def middle_kernel(e0, e1, e2, e3, r0, r1, r2, r3, bins_ref, vec_ref, w_ref, s_ref, a_ref, buf):
    early, late = (e0, e1, e2, e3), (r0, r1, r2, r3)
    plan = (
        (late, REST, R), (early, 0, 2 * R),
        (early, H - 2 * R, 2 * R), (late, 0, REST), (early, H, 2 * R),
        (early, 2 * H - 2 * R, 2 * R), (late, REST + R, R),
    )
    to = 0
    for pieces, at, count in plan:
        for p, piece in enumerate(pieces):
            buf[to : to + count, p * W : (p + 1) * W] = piece[at : at + count, :]
        to += count
    second = 3 * R
    third = second + M + 2 * R
    acc = None
    for k in range(3):
        rows = [buf[k * R : k * R + R, :], buf[second + k * R : second + k * R + M, :], buf[third + k * R : third + k * R + R, :]]
        part = dot(jnp.concatenate(rows, axis=0), w_ref[0, :, k * W : (k + 1) * W])
        acc = part if acc is None else acc + part
    f = lambda at, count: bins_ref[at : at + count, :].astype(F32)
    acc += jnp.concatenate([f(0, R), f(H - R, M), f(ROWS - R, R)], axis=0)
    finish(acc, vec_ref, s_ref, a_ref, 0, X1)


def product_kernel(layer, p0, p1, p2, p3, w_ref, o0, o1, o2):
    full = dot(wide((p0, p1, p2, p3), 0, p0.shape[0]), w_ref[layer])
    for k, o in enumerate((o0, o1, o2)):
        o[...] = full[:, k * W : (k + 1) * W].astype(BF16)


def joined(vec_ref, s_ref, a_ref, at, count, *terms):
    total = None
    for ref, lo in terms:
        part = ref[lo : lo + count, :].astype(F32)
        total = part if total is None else total + part
    finish(total, vec_ref, s_ref, a_ref, at, count)


def join_early_kernel(s, q0, q1, q2, up, down, vec_ref, s_ref, a_ref):
    lo = N - Q
    joined(vec_ref, s_ref, a_ref, 0, Q, (s, lo), (q1, lo), (q2, N), (up, 0))
    joined(vec_ref, s_ref, a_ref, Q, Q, (s, N), (q1, N), (q0, lo), (down, lo))


def join_late_kernel(s0, t0, t1, t2, s1, u0, u1, u2, up0, down0, up1, down1, vec_ref, s_ref, a_ref):
    put = functools.partial(joined, vec_ref, s_ref, a_ref)
    b = A - R
    top = R + A
    put(0, R, (s1, 0), (u1, 0), (up1, 0), (u2, top))
    put(R, b, (s0, 0), (t1, 0), (up1, R), (u2, top + R))
    put(A, b, (s1, R), (u1, R), (up0, Q), (t2, N + Q))
    put(A + b, R, (s1, R + b), (u1, R + b), (up1, A), (u2, R + M))
    put(2 * A, R, (s1, top), (u1, top), (u0, 0), (down1, 0))
    put(2 * A + R, b, (s1, top + R), (u1, top + R), (t0, 0), (down0, 0))
    put(3 * A, b, (s0, N + Q), (t1, N + Q), (u0, R), (down1, R))
    put(3 * A + b, R, (s1, R + M), (u1, R + M), (u0, R + b), (down1, R + b))


def last_early_kernel(p0, p1, p2, p3, s_ref, vec_ref, w_ref, o_ref):
    pieces = (p0, p1, p2, p3)
    n = 2 * Q
    acc = dot(wide(pieces, 0, n), w_ref[2, :, W : 2 * W])
    acc += dot(wide(pieces, n, n), w_ref[2, :, 0:W])
    acc += dot(wide(pieces, 2 * n, n), w_ref[2, :, 2 * W : 3 * W])
    o_ref[...] = (s_ref[...].astype(F32) + acc + vec_ref[0:1, :]).astype(BF16)


def out_kernel(c, s, q, up0, up1, down0, down1, vec_ref, o_ref):
    def put(to, at, count):
        up, down, lo = (up0, down0, at) if at < M else (up1, down1, at - M)
        total = vec_ref[0:1, :]
        for ref, start in ((s, at), (q, at), (up, lo), (down, lo)):
            total = total + ref[start : start + count, :].astype(F32)
        o_ref[to : to + count, :] = total.astype(BF16)

    put(0, 0, A)
    o_ref[A : A + Q, :] = c[0:Q, :]
    put(A + Q, A, A)
    put(MID, M, A)
    o_ref[A + Q + M : A + 2 * Q + M, :] = c[Q : 2 * Q, :]
    put(ROWS - A, A + M, A)


def call(kernel, args, rows, flops=0, scratch=()):
    return pl.pallas_call(
        kernel,
        out_shape=[jax.ShapeDtypeStruct((r, W), BF16) for r in rows],
        in_specs=[VMEM] * len(args),
        out_specs=[VMEM] * len(rows),
        scratch_shapes=list(scratch),
        compiler_params=pltpu.CompilerParams(vmem_limit_bytes=20 * 1024 * 1024),
        cost_estimate=pl.CostEstimate(flops=flops, bytes_accessed=1024, transcendentals=0),
    )(*args)


def staged(ch, conv_weight):
    return pl.pallas_call(
        stage_kernel,
        out_shape=jax.ShapeDtypeStruct((3, 4 * W, 3 * W), BF16),
        in_specs=[SMEM, HBM],
        out_specs=VMEM,
        scratch_shapes=[pltpu.SemaphoreType.DMA((36,))],
        compiler_params=pltpu.CompilerParams(vmem_limit_bytes=40 * 1024 * 1024),
    )(ch, conv_weight)


def per_device(bins_in, pre_scale, pre_shift, conv_weight, conv_bias):
    after = lax.optimization_barrier
    ch = lax.axis_index("ch").astype(jnp.int32).reshape(1)
    hop1, hop2 = MID // 512, 4096 // ROWS
    mac = 2 * 4 * W * W * 3
    vec0 = jnp.stack([conv_bias[0], pre_scale[1], pre_shift[1]])
    vec1 = jnp.stack([conv_bias[1], pre_scale[2], pre_shift[2]])
    vec2 = conv_bias[2:3]

    def entry(x):
        return gelu(x.astype(F32) * pre_scale[0] + pre_shift[0]).astype(BF16)

    act_e = entry(jnp.concatenate([bins_in[:H], bins_in[ROWS - H :]], axis=0))
    far_e = chip_swap(act_e)
    low = shifted(act_e[-R:], 1)
    high = shifted(act_e[:R], -1)
    near_e = core_swap(act_e)
    weights = staged(ch, conv_weight)
    own_l = jnp.concatenate([entry(bins_in[H : ROWS - H]), low, high], axis=0)
    far_l = chip_swap(own_l)
    near_l = core_swap(own_l)
    far_e, weights = after((far_e, weights))
    g_e = (act_e, near_e, far_e, core_swap(far_e))

    s_x0, a_x0 = call(ends_kernel, (*g_e, bins_in, vec0, weights), [X0] * 2, mac * X0)
    far_x0 = chip_swap(a_x0)
    near_x0 = core_swap(a_x0)
    far_l, a_x0 = after((far_l, a_x0))
    g_l = (own_l, near_l, far_l, core_swap(far_l))
    s_x1, a_x1 = call(
        middle_kernel, (*g_e, *g_l, bins_in, vec0, weights), [X1] * 2, mac * X1,
        [pltpu.VMEM((8 * R + SPAN, 4 * W), BF16)],
    )
    far_x1 = chip_swap(a_x1)
    near_x1 = core_swap(a_x1)
    far_x0, a_x1 = after((far_x0, a_x1))
    g_x0 = (a_x0, near_x0, far_x0, core_swap(far_x0))
    t0, t1, t2 = call(functools.partial(product_kernel, 1), (*g_x0, weights), [X0] * 3, mac * X0)
    up0 = shifted(t0[N:], hop1)
    down0 = shifted(t2[:N], -hop1)
    far_x1, t1 = after((far_x1, t1))
    g_x1 = (a_x1, near_x1, far_x1, core_swap(far_x1))
    u0, u1, u2 = call(functools.partial(product_kernel, 1), (*g_x1, weights), [X1] * 3, mac * X1)
    up1 = shifted(u0[R + A :], hop1)
    down1 = shifted(u2[: R + A], -hop1)

    up0, down0, u1 = after((up0, down0, u1))
    s_c, a_c = call(join_early_kernel, (s_x0, t0, t1, t2, up0, down0, vec1), [2 * Q] * 2)
    low_c = [shifted(a_c[:PART], hop2), shifted(a_c[PART:], hop2)]
    high_c = [shifted(a_c[:PART], -hop2), shifted(a_c[PART:], -hop2)]
    up1, down1, low_c[0], high_c[0], a_c = after((up1, down1, low_c[0], high_c[0], a_c))
    s_d, a_d = call(
        join_late_kernel, (s_x0, t0, t1, t2, s_x1, u0, u1, u2, up0, down0, up1, down1, vec1), [2 * M] * 2
    )
    far_d = chip_swap(a_d)
    near_d = core_swap(a_d)
    far_d, low_c[1], high_c[1] = after((far_d, low_c[1], high_c[1]))
    own_c = jnp.concatenate([a_c, *low_c, *high_c], axis=0)
    far_c = chip_swap(own_c)
    near_c = core_swap(own_c)
    g_d = (a_d, near_d, far_d, core_swap(far_d))
    q0, q1, q2 = call(functools.partial(product_kernel, 2), (*g_d, weights), [2 * M] * 3, mac * 2 * M)
    up = [shifted(q0[:M], hop2), shifted(q0[M:], hop2)]
    down = [shifted(q2[:M], -hop2), shifted(q2[M:], -hop2)]
    far_c, up[0], down[0], q1 = after((far_c, up[0], down[0], q1))
    g_c = (own_c, near_c, far_c, core_swap(far_c))
    (out_c,) = call(last_early_kernel, (*g_c, s_c, vec2, weights), [2 * Q], mac * 2 * Q)
    up[1], down[1], out_c = after((up[1], down[1], out_c))
    (out,) = call(out_kernel, (out_c, s_d, q1, *up, *down, vec2), [ROWS])
    return out


def solution(mesh):
    return jax.shard_map(
        per_device,
        mesh=mesh,
        in_specs=(
            P("seq", "ch"),
            P(None, "ch"),
            P(None, "ch"),
            P(None, None, None, "ch"),
            P(None, "ch"),
        ),
        out_specs=P("seq", "ch"),
        check_vma=False,
    )
```

time: 411 us -> 153 us (0.37)
  the two profiles are of different devices: /device:TPU:6 before, /device:TPU:23 now
where the time goes in v3:
time: 153 us
  starting transfers between devices  81.5 us (53%)
  waiting for transfers between devices  43.1 us (28%)
  Pallas kernels  24.3 us (16%)
  other arithmetic  1.97 us (1%)
  local copies, waits for them, and re-layouts  1.58 us (1%)
    ppermute x14, starting transfers between devices, shifted(): return lax.ppermute(array, 'seq', pairs)  52.7 us
    ppermute x14, waiting for transfers between devices, shifted(): return lax.ppermute(array, 'seq', pairs)  27.2 us
    ppermute x12, starting transfers between devices, core_swap(): return lax.ppermute(array, 'ch', [(i, i ^ 1) for i in range(4)])  23 us
    pallas_call x9, Pallas kernels, call(): pl.pallas_call(kernel, out_shape=[jax.ShapeDtypeStruct((r, W), BF16) for...  19.9 us
    ppermute x6, waiting for transfers between devices, chip_swap(): return lax.ppermute(array, 'ch', [(i, i ^ 2) for i in range(4)])  13.6 us
    ppermute x6, starting transfers between devices, chip_swap(): return lax.ppermute(array, 'ch', [(i, i ^ 2) for i in range(4)])  5.91 us
    pallas_call x1, Pallas kernels, staged(): pl.pallas_call(stage_kernel, out_shape=jax.ShapeDtypeStruct((3, 4 * W, 3...  4.38 us
  transfers between devices with their start and end apart: 32, of which 15 were waited for; matrix products, arithmetic and copies ran while one was open for 1% of the time, Pallas kernels for 14%

profile of v3, /device:TPU:23, one launch (start us, length us, event | category | flops | bytes accessed | tf_op | source)
XLA Modules:
  0.0 152.8 jit_solution(14443320743678422244)
XLA Ops:
  4.8 3.6 %collective-permute-start.3 = (bf16[64,384]{1,0:T(8,128)(2,1)S(1)}, bf16[64,384]{1,0:T(8,128)(2,1)S(1)}, u32[]{:S(2)}, u32[]{:S(2)}) collective-permute-start(bf16[64,384]{1,0:T(8,128)(2,1)S(1)} %get-tuple-element.93), channel_id=1, source_target_pairs={{0,4},{4,8},{8,12},{12,16},{16,20},{20,24},{24,28},{28,32},{32,36}... | collective-permute-start | bytes 147464 | tf_op jit(solution)/shard_map/ppermute | solution.py:48
  8.4 3.2 %collective-permute-start.4 = (bf16[64,384]{1,0:T(8,128)(2,1)S(1)}, bf16[64,384]{1,0:T(8,128)(2,1)S(1)}, u32[]{:S(2)}, u32[]{:S(2)}) collective-permute-start(bf16[64,384]{1,0:T(8,128)(2,1)S(1)} %get-tuple-element.94), channel_id=1, source_target_pairs={{4,0},{8,4},{12,8},{16,12},{20,16},{24,20},{28,24},{32,28},{36,32}... | collective-permute-start | bytes 147464 | tf_op jit(solution)/shard_map/ppermute | solution.py:48
  11.7 4.4 %shard_map.55.w_ref = bf16[3,1536,1152]{2,1,0:T(8,128)(2,1)S(1)} custom-call(s32[1]{0:T(128)} %bitcast.ch_ref, bf16[3,3,1536,384]{3,2,1,0:T(8,128)(2,1)} %w_hbm.1), custom_call_target="tpu_custom_call" | custom-call | tf_op jit(solution)/shard_map/pallas_call | solution.py:198
  16.0 3.1 %collective-permute-done.1.p2.e2 = bf16[832,384]{1,0:T(8,128)(2,1)S(1)} collective-permute-done((bf16[832,384]{1,0:T(8,128)(2,1)S(1)}, bf16[832,384]{1,0:T(8,128)(2,1)S(1)}, u32[]{:S(2)}, u32[]{:S(2)}) %collective-permute-start.1) | collective-permute-done | bytes 639008 | tf_op jit(solution)/shard_map/ppermute | solution.py:52
  22.9 4.0 %shard_map.56 = (bf16[576,384]{1,0:T(8,128)(2,1)S(1)}, bf16[576,384]{1,0:T(8,128)(2,1)S(1)}) custom-call(bf16[832,384]{1,0:T(8,128)(2,1)S(1)} %fusion.1.p0.e0, bf16[832,384]{1,0:T(8,128)(2,1)S(1)} %collective-permute-done.p1.e1, bf16[832,384]{1,0:T(8,128)(2,1)S(1)} %collective-permute-done.1.p2.e2, bf16[832,384]{1,0:T(8,128)(2,1)S(1)} %collective-permute-done.2.p3.e3, ...), custom_call_target="tpu_custom_call" | custom-call | flops 2038431744 | bytes 1024 | tf_op jit(solution)/shard_map/pallas_call | solution.py:186
  31.3 3.2 %shard_map.57 = (bf16[448,384]{1,0:T(8,128)(2,1)S(1)}, bf16[448,384]{1,0:T(8,128)(2,1)S(1)}) custom-call(bf16[832,384]{1,0:T(8,128)(2,1)S(1)} %fusion.1.p0.e0, bf16[832,384]{1,0:T(8,128)(2,1)S(1)} %collective-permute-done.p1.e1, bf16[832,384]{1,0:T(8,128)(2,1)S(1)} %collective-permute-done.1.p2.e2, bf16[832,384]{1,0:T(8,128)(2,1)S(1)} %collective-permute-done.2.p3.e3, ...), custom_call_target="tpu_custom_call" | custom-call | flops 1585446912 | bytes 1024 | tf_op jit(solution)/shard_map/pallas_call | solution.py:186
  34.4 4.0 %collective-permute-done.7.p2 = bf16[576,384]{1,0:T(8,128)(2,1)S(1)} collective-permute-done((bf16[576,384]{1,0:T(8,128)(2,1)S(1)}, bf16[576,384]{1,0:T(8,128)(2,1)S(1)}, u32[]{:S(2)}, u32[]{:S(2)}) %collective-permute-start.7) | collective-permute-done | bytes 442400 | tf_op jit(solution)/shard_map/ppermute | solution.py:52
  41.0 2.5 %shard_map.58 = (bf16[576,384]{1,0:T(8,128)(2,1)S(1)}, bf16[576,384]{1,0:T(8,128)(2,1)S(1)}, bf16[576,384]{1,0:T(8,128)(2,1)S(1)}) custom-call(bf16[576,384]{1,0:T(8,128)(2,1)S(1)} %get-tuple-element.52.p0, bf16[576,384]{1,0:T(8,128)(2,1)S(1)} %collective-permute-done.6.p1, bf16[576,384]{1,0:T(8,128)(2,1)S(1)} %collective-permute-done.7.p2, ...), custom_call_target="tpu_custom_call" | custom-call | flops 2038431744 | bytes 1024 | tf_op jit(solution)/shard_map/pallas_call | solution.py:186
  43.5 5.8 %collective-permute-done.11.p2 = bf16[448,384]{1,0:T(8,128)(2,1)S(1)} collective-permute-done((bf16[448,384]{1,0:T(8,128)(2,1)S(1)}, bf16[448,384]{1,0:T(8,128)(2,1)S(1)}, u32[]{:S(2)}, u32[]{:S(2)}) %collective-permute-start.11) | collective-permute-done | bytes 344096 | tf_op jit(solution)/shard_map/ppermute | solution.py:52
  50.2 2.7 %collective-permute-start.15 = (bf16[288,384]{1,0:T(8,128)(2,1)S(1)}, bf16[288,384]{1,0:T(8,128)(2,1)S(1)}, u32[]{:S(2)}, u32[]{:S(2)}) collective-permute-start(bf16[288,384]{1,0:T(8,128)(2,1)S(1)} %slice.87), channel_id=1, source_target_pairs={{4,0},{8,4},{12,8},{16,12},{20,16},{24,20},{28,24},{32,28},{36,32}... | collective-permute-start | bytes 663560 | tf_op jit(solution)/shard_map/ppermute | solution.py:48
  52.9 5.0 %collective-permute-start.14 = (bf16[288,384]{1,0:T(8,128)(2,1)S(1)}, bf16[288,384]{1,0:T(8,128)(2,1)S(1)}, u32[]{:S(2)}, u32[]{:S(2)}) collective-permute-start(bf16[288,384]{1,0:T(8,128)(2,1)S(1)} %slice.86), channel_id=1, source_target_pairs={{0,4},{4,8},{8,12},{12,16},{16,20},{20,24},{24,28},{28,32},{32,36}... | collective-permute-start | bytes 663560 | tf_op jit(solution)/shard_map/ppermute | solution.py:48
  59.9 6.6 %collective-permute-start.17 = (bf16[224,384]{1,0:T(8,128)(2,1)S(1)}, bf16[224,384]{1,0:T(8,128)(2,1)S(1)}, u32[]{:S(2)}, u32[]{:S(2)}) collective-permute-start(bf16[224,384]{1,0:T(8,128)(2,1)S(1)} %slice.89), channel_id=1, source_target_pairs={{4,0},{8,4},{12,8},{16,12},{20,16},{24,20},{28,24},{32,28},{36,32}... | collective-permute-start | bytes 516104 | tf_op jit(solution)/shard_map/ppermute | solution.py:48
  68.5 3.3 %collective-permute-done.14.up.up0 = bf16[288,384]{1,0:T(8,128)(2,1)S(1)} collective-permute-done((bf16[288,384]{1,0:T(8,128)(2,1)S(1)}, bf16[288,384]{1,0:T(8,128)(2,1)S(1)}, u32[]{:S(2)}, u32[]{:S(2)}) %collective-permute-start.14) | collective-permute-done | bytes 221216 | tf_op jit(solution)/shard_map/ppermute | solution.py:48
  72.7 4.1 %collective-permute-start.19 = (bf16[96,384]{1,0:T(8,128)(2,1)S(1)}, bf16[96,384]{1,0:T(8,128)(2,1)S(1)}, u32[]{:S(2)}, u32[]{:S(2)}) collective-permute-start(bf16[96,384]{1,0:T(8,128)(2,1)S(1)} %slice.93), channel_id=1, source_target_pairs={{16,0},{20,4},{24,8},{28,12},{32,16},{36,20},{40,24},{44,28},{48,3... | collective-permute-start | bytes 221192 | tf_op jit(solution)/shard_map/ppermute | solution.py:48
  79.2 5.7 %collective-permute-done.18 = bf16[96,384]{1,0:T(8,128)(2,1)S(1)} collective-permute-done((bf16[96,384]{1,0:T(8,128)(2,1)S(1)}, bf16[96,384]{1,0:T(8,128)(2,1)S(1)}, u32[]{:S(2)}, u32[]{:S(2)}) %collective-permute-start.18) | collective-permute-done | bytes 73760 | tf_op jit(solution)/shard_map/ppermute | solution.py:48
  89.4 4.3 %collective-permute-start.22 = (bf16[288,384]{1,0:T(8,128)(2,1)S(1)}, bf16[288,384]{1,0:T(8,128)(2,1)S(1)}, u32[]{:S(2)}, u32[]{:S(2)}) collective-permute-start(bf16[288,384]{1,0:T(8,128)(2,1)S(1)} %slice.94), channel_id=1, source_target_pairs={{0,16},{4,20},{8,24},{12,28},{16,32},{20,36},{24,40},{28,44},{32,4... | collective-permute-start | bytes 663560 | tf_op jit(solution)/shard_map/ppermute | solution.py:48
  93.7 4.1 %collective-permute-start.20 = (bf16[640,384]{1,0:T(8,128)(2,1)S(1)}, bf16[640,384]{1,0:T(8,128)(2,1)S(1)}, u32[]{:S(2)}, u32[]{:S(2)}) collective-permute-start(bf16[640,384]{1,0:T(8,128)(2,1)S(1)} %get-tuple-element.72.p0), channel_id=1, source_target_pairs={{0,1},{1,0},{2,3},{3,2},{4,5},{5,4},{6,7},{7,6},{8,9},{9,8},{10,11... | collective-permute-start | bytes 1474568 | tf_op jit(solution)/shard_map/ppermute | solution.py:56
  99.4 8.7 %collective-permute-start.24 = (bf16[640,384]{1,0:T(8,128)(2,1)S(1)}, bf16[640,384]{1,0:T(8,128)(2,1)S(1)}, u32[]{:S(2)}, u32[]{:S(2)}) collective-permute-start(bf16[640,384]{1,0:T(8,128)(2,1)S(1)} %collective-permute-done.21.p2), channel_id=1, source_target_pairs={{0,1},{1,0},{2,3},{3,2},{4,5},{5,4},{6,7},{7,6},{8,9},{9,8},{10,11... | collective-permute-start | bytes 1474568 | tf_op jit(solution)/shard_map/ppermute | solution.py:56
  109.6 2.7 %shard_map.62 = (bf16[640,384]{1,0:T(8,128)(2,1)S(1)}, bf16[640,384]{1,0:T(8,128)(2,1)S(1)}, bf16[640,384]{1,0:T(8,128)(2,1)S(1)}) custom-call(bf16[640,384]{1,0:T(8,128)(2,1)S(1)} %get-tuple-element.72.p0, bf16[640,384]{1,0:T(8,128)(2,1)S(1)} %collective-permute-done.20.p1, bf16[640,384]{1,0:T(8,128)(2,1)S(1)} %collective-permute-done.21.p2, ...), custom_call_target="tpu_custom_call" | custom-call | flops 2264924160 | bytes 1024 | tf_op jit(solution)/shard_map/pallas_call | solution.py:186
  114.4 6.4 %collective-permute-start.30 = (bf16[320,384]{1,0:T(8,128)(2,1)S(1)}, bf16[320,384]{1,0:T(8,128)(2,1)S(1)}, u32[]{:S(2)}, u32[]{:S(2)}) collective-permute-start(bf16[320,384]{1,0:T(8,128)(2,1)S(1)} %get-tuple-element.95), channel_id=1, source_target_pairs={{16,0},{20,4},{24,8},{28,12},{32,16},{36,20},{40,24},{44,28},{48,3... | collective-permute-start | bytes 737288 | tf_op jit(solution)/shard_map/ppermute | solution.py:48
  121.8 7.9 %collective-permute-done.29.up0 = bf16[320,384]{1,0:T(8,128)(2,1)S(1)} collective-permute-done((bf16[320,384]{1,0:T(8,128)(2,1)S(1)}, bf16[320,384]{1,0:T(8,128)(2,1)S(1)}, u32[]{:S(2)}, u32[]{:S(2)}) %collective-permute-start.29) | collective-permute-done | bytes 245792 | tf_op jit(solution)/shard_map/ppermute | solution.py:48
  129.7 2.5 %collective-permute-start.31 = (bf16[1152,384]{1,0:T(8,128)(2,1)S(1)}, bf16[1152,384]{1,0:T(8,128)(2,1)S(1)}, u32[]{:S(2)}, u32[]{:S(2)}) collective-permute-start(bf16[1152,384]{1,0:T(8,128)(2,1)S(1)} %collective-permute-done.28.p2), channel_id=1, source_target_pairs={{0,1},{1,0},{2,3},{3,2},{4,5},{5,4},{6,7},{7,6},{8,9},{9,8},{10,11... | collective-permute-start | bytes 2654216 | tf_op jit(solution)/shard_map/ppermute | solution.py:56
  134.1 7.1 %collective-permute-start.26 = (bf16[320,384]{1,0:T(8,128)(2,1)S(1)}, bf16[320,384]{1,0:T(8,128)(2,1)S(1)}, u32[]{:S(2)}, u32[]{:S(2)}) collective-permute-start(bf16[320,384]{1,0:T(8,128)(2,1)S(1)} %get-tuple-element.96), channel_id=1, source_target_pairs={{16,0},{20,4},{24,8},{28,12},{32,16},{36,20},{40,24},{44,28},{48,3... | collective-permute-start | bytes 737288 | tf_op jit(solution)/shard_map/ppermute | solution.py:48
  143.2 7.6 %collective-permute-done.25.up1 = bf16[320,384]{1,0:T(8,128)(2,1)S(1)} collective-permute-done((bf16[320,384]{1,0:T(8,128)(2,1)S(1)}, bf16[320,384]{1,0:T(8,128)(2,1)S(1)}, u32[]{:S(2)}, u32[]{:S(2)}) %collective-permute-start.25) | collective-permute-done | bytes 245792 | tf_op jit(solution)/shard_map/ppermute | solution.py:48
  (80 shorter events, 40.1 us)
Async XLA Ops:
  2.8 16.4 %collective-permute-start.1 = (bf16[832,384]{1,0:T(8,128)(2,1)S(1)}, bf16[832,384]{1,0:T(8,128)(2,1)S(1)}, u32[]{:S(2)}, u32[]{:S(2)}) collective-permute-start(bf16[832,384]{1,0:T(8,128)(2,1)S(1)} %fusion.1.p0.e0), channel_id=1, source_target_pairs={{0,2},{1,3},{2,0},{3,1},{4,6},{5,7},{6,4},{7,5},{8,10},{9,11},{10,... | collective-permute-start | bytes 1916936 | tf_op jit(solution)/shard_map/ppermute | solution.py:52
  3.9 18.9 %collective-permute-start = (bf16[832,384]{1,0:T(8,128)(2,1)S(1)}, bf16[832,384]{1,0:T(8,128)(2,1)S(1)}, u32[]{:S(2)}, u32[]{:S(2)}) collective-permute-start(bf16[832,384]{1,0:T(8,128)(2,1)S(1)} %fusion.1.p0.e0), channel_id=1, source_target_pairs={{0,1},{1,0},{2,3},{3,2},{4,5},{5,4},{6,7},{7,6},{8,9},{9,8},{10,11... | collective-permute-start | bytes 1916936 | tf_op jit(solution)/shard_map/ppermute | solution.py:56
  4.8 16.8 %collective-permute-start.3 = (bf16[64,384]{1,0:T(8,128)(2,1)S(1)}, bf16[64,384]{1,0:T(8,128)(2,1)S(1)}, u32[]{:S(2)}, u32[]{:S(2)}) collective-permute-start(bf16[64,384]{1,0:T(8,128)(2,1)S(1)} %get-tuple-element.93), channel_id=1, source_target_pairs={{0,4},{4,8},{8,12},{12,16},{16,20},{20,24},{24,28},{28,32},{32,36}... | collective-permute-start | bytes 147464 | tf_op jit(solution)/shard_map/ppermute | solution.py:48
  8.4 13.2 %collective-permute-start.4 = (bf16[64,384]{1,0:T(8,128)(2,1)S(1)}, bf16[64,384]{1,0:T(8,128)(2,1)S(1)}, u32[]{:S(2)}, u32[]{:S(2)}) collective-permute-start(bf16[64,384]{1,0:T(8,128)(2,1)S(1)} %get-tuple-element.94), channel_id=1, source_target_pairs={{4,0},{8,4},{12,8},{16,12},{20,16},{24,20},{28,24},{32,28},{36,32}... | collective-permute-start | bytes 147464 | tf_op jit(solution)/shard_map/ppermute | solution.py:48
  26.9 11.6 %collective-permute-start.7 = (bf16[576,384]{1,0:T(8,128)(2,1)S(1)}, bf16[576,384]{1,0:T(8,128)(2,1)S(1)}, u32[]{:S(2)}, u32[]{:S(2)}) collective-permute-start(bf16[576,384]{1,0:T(8,128)(2,1)S(1)} %get-tuple-element.52.p0), channel_id=1, source_target_pairs={{0,2},{1,3},{2,0},{3,1},{4,6},{5,7},{6,4},{7,5},{8,10},{9,11},{10,... | collective-permute-start | bytes 1327112 | tf_op jit(solution)/shard_map/ppermute | solution.py:52
  30.1 10.8 %collective-permute-start.6 = (bf16[576,384]{1,0:T(8,128)(2,1)S(1)}, bf16[576,384]{1,0:T(8,128)(2,1)S(1)}, u32[]{:S(2)}, u32[]{:S(2)}) collective-permute-start(bf16[576,384]{1,0:T(8,128)(2,1)S(1)} %get-tuple-element.52.p0), channel_id=1, source_target_pairs={{0,1},{1,0},{2,3},{3,2},{4,5},{5,4},{6,7},{7,6},{8,9},{9,8},{10,11... | collective-permute-start | bytes 1327112 | tf_op jit(solution)/shard_map/ppermute | solution.py:56
  39.6 9.7 %collective-permute-start.11 = (bf16[448,384]{1,0:T(8,128)(2,1)S(1)}, bf16[448,384]{1,0:T(8,128)(2,1)S(1)}, u32[]{:S(2)}, u32[]{:S(2)}) collective-permute-start(bf16[448,384]{1,0:T(8,128)(2,1)S(1)} %get-tuple-element.61.p0), channel_id=1, source_target_pairs={{0,2},{1,3},{2,0},{3,1},{4,6},{5,7},{6,4},{7,5},{8,10},{9,11},{10,... | collective-permute-start | bytes 1032200 | tf_op jit(solution)/shard_map/ppermute | solution.py:52
  40.6 17.2 %collective-permute-start.12 = (bf16[448,384]{1,0:T(8,128)(2,1)S(1)}, bf16[448,384]{1,0:T(8,128)(2,1)S(1)}, u32[]{:S(2)}, u32[]{:S(2)}) collective-permute-start(bf16[448,384]{1,0:T(8,128)(2,1)S(1)} %get-tuple-element.61.p0), channel_id=1, source_target_pairs={{0,1},{1,0},{2,3},{3,2},{4,5},{5,4},{6,7},{7,6},{8,9},{9,8},{10,11... | collective-permute-start | bytes 1032200 | tf_op jit(solution)/shard_map/ppermute | solution.py:56
  50.2 18.3 %collective-permute-start.15 = (bf16[288,384]{1,0:T(8,128)(2,1)S(1)}, bf16[288,384]{1,0:T(8,128)(2,1)S(1)}, u32[]{:S(2)}, u32[]{:S(2)}) collective-permute-start(bf16[288,384]{1,0:T(8,128)(2,1)S(1)} %slice.87), channel_id=1, source_target_pairs={{4,0},{8,4},{12,8},{16,12},{20,16},{24,20},{28,24},{32,28},{36,32}... | collective-permute-start | bytes 663560 | tf_op jit(solution)/shard_map/ppermute | solution.py:48
  52.9 18.9 %collective-permute-start.14 = (bf16[288,384]{1,0:T(8,128)(2,1)S(1)}, bf16[288,384]{1,0:T(8,128)(2,1)S(1)}, u32[]{:S(2)}, u32[]{:S(2)}) collective-permute-start(bf16[288,384]{1,0:T(8,128)(2,1)S(1)} %slice.86), channel_id=1, source_target_pairs={{0,4},{4,8},{8,12},{12,16},{16,20},{20,24},{24,28},{28,32},{32,36}... | collective-permute-start | bytes 663560 | tf_op jit(solution)/shard_map/ppermute | solution.py:48
  59.9 25.0 %collective-permute-start.17 = (bf16[224,384]{1,0:T(8,128)(2,1)S(1)}, bf16[224,384]{1,0:T(8,128)(2,1)S(1)}, u32[]{:S(2)}, u32[]{:S(2)}) collective-permute-start(bf16[224,384]{1,0:T(8,128)(2,1)S(1)} %slice.89), channel_id=1, source_target_pairs={{4,0},{8,4},{12,8},{16,12},{20,16},{24,20},{28,24},{32,28},{36,32}... | collective-permute-start | bytes 516104 | tf_op jit(solution)/shard_map/ppermute | solution.py:48
  66.5 18.4 %collective-permute-start.16 = (bf16[224,384]{1,0:T(8,128)(2,1)S(1)}, bf16[224,384]{1,0:T(8,128)(2,1)S(1)}, u32[]{:S(2)}, u32[]{:S(2)}) collective-permute-start(bf16[224,384]{1,0:T(8,128)(2,1)S(1)} %slice.88), channel_id=1, source_target_pairs={{0,4},{4,8},{8,12},{12,16},{16,20},{20,24},{24,28},{28,32},{32,36}... | collective-permute-start | bytes 516104 | tf_op jit(solution)/shard_map/ppermute | solution.py:48
  86.4 13.0 %collective-permute-start.21 = (bf16[640,384]{1,0:T(8,128)(2,1)S(1)}, bf16[640,384]{1,0:T(8,128)(2,1)S(1)}, u32[]{:S(2)}, u32[]{:S(2)}) collective-permute-start(bf16[640,384]{1,0:T(8,128)(2,1)S(1)} %get-tuple-element.72.p0), channel_id=1, source_target_pairs={{0,2},{1,3},{2,0},{3,1},{4,6},{5,7},{6,4},{7,5},{8,10},{9,11},{10,... | collective-permute-start | bytes 1474568 | tf_op jit(solution)/shard_map/ppermute | solution.py:52
  87.5 10.3 %collective-permute-start.23 = (bf16[288,384]{1,0:T(8,128)(2,1)S(1)}, bf16[288,384]{1,0:T(8,128)(2,1)S(1)}, u32[]{:S(2)}, u32[]{:S(2)}) collective-permute-start(bf16[288,384]{1,0:T(8,128)(2,1)S(1)} %slice.94), channel_id=1, source_target_pairs={{16,0},{20,4},{24,8},{28,12},{32,16},{36,20},{40,24},{44,28},{48,3... | collective-permute-start | bytes 663560 | tf_op jit(solution)/shard_map/ppermute | solution.py:48
  89.4 9.9 %collective-permute-start.22 = (bf16[288,384]{1,0:T(8,128)(2,1)S(1)}, bf16[288,384]{1,0:T(8,128)(2,1)S(1)}, u32[]{:S(2)}, u32[]{:S(2)}) collective-permute-start(bf16[288,384]{1,0:T(8,128)(2,1)S(1)} %slice.94), channel_id=1, source_target_pairs={{0,16},{4,20},{8,24},{12,28},{16,32},{20,36},{24,40},{28,44},{32,4... | collective-permute-start | bytes 663560 | tf_op jit(solution)/shard_map/ppermute | solution.py:48
  93.7 15.1 %collective-permute-start.20 = (bf16[640,384]{1,0:T(8,128)(2,1)S(1)}, bf16[640,384]{1,0:T(8,128)(2,1)S(1)}, u32[]{:S(2)}, u32[]{:S(2)}) collective-permute-start(bf16[640,384]{1,0:T(8,128)(2,1)S(1)} %get-tuple-element.72.p0), channel_id=1, source_target_pairs={{0,1},{1,0},{2,3},{3,2},{4,5},{5,4},{6,7},{7,6},{8,9},{9,8},{10,11... | collective-permute-start | bytes 1474568 | tf_op jit(solution)/shard_map/ppermute | solution.py:56
  99.4 10.2 %collective-permute-start.24 = (bf16[640,384]{1,0:T(8,128)(2,1)S(1)}, bf16[640,384]{1,0:T(8,128)(2,1)S(1)}, u32[]{:S(2)}, u32[]{:S(2)}) collective-permute-start(bf16[640,384]{1,0:T(8,128)(2,1)S(1)} %collective-permute-done.21.p2), channel_id=1, source_target_pairs={{0,1},{1,0},{2,3},{3,2},{4,5},{5,4},{6,7},{7,6},{8,9},{9,8},{10,11... | collective-permute-start | bytes 1474568 | tf_op jit(solution)/shard_map/ppermute | solution.py:56
  108.2 21.4 %collective-permute-start.28 = (bf16[1152,384]{1,0:T(8,128)(2,1)S(1)}, bf16[1152,384]{1,0:T(8,128)(2,1)S(1)}, u32[]{:S(2)}, u32[]{:S(2)}) collective-permute-start(bf16[1152,384]{1,0:T(8,128)(2,1)S(1)} %constant_dynamic-update-slice_fusion.p0), channel_id=1, source_target_pairs={{0,2},{1,3},{2,0},{3,1},{4,6},{5,7},{6,4},{7,5},{8,10},{9,11},{10,... | collective-permute-start | bytes 2654216 | tf_op jit(solution)/shard_map/ppermute | solution.py:52
  112.4 17.3 %collective-permute-start.29 = (bf16[320,384]{1,0:T(8,128)(2,1)S(1)}, bf16[320,384]{1,0:T(8,128)(2,1)S(1)}, u32[]{:S(2)}, u32[]{:S(2)}) collective-permute-start(bf16[320,384]{1,0:T(8,128)(2,1)S(1)} %get-tuple-element.97), channel_id=1, source_target_pairs={{0,16},{4,20},{8,24},{12,28},{16,32},{20,36},{24,40},{28,44},{32,4... | collective-permute-start | bytes 737288 | tf_op jit(solution)/shard_map/ppermute | solution.py:48
  114.4 15.3 %collective-permute-start.30 = (bf16[320,384]{1,0:T(8,128)(2,1)S(1)}, bf16[320,384]{1,0:T(8,128)(2,1)S(1)}, u32[]{:S(2)}, u32[]{:S(2)}) collective-permute-start(bf16[320,384]{1,0:T(8,128)(2,1)S(1)} %get-tuple-element.95), channel_id=1, source_target_pairs={{16,0},{20,4},{24,8},{28,12},{32,16},{36,20},{40,24},{44,28},{48,3... | collective-permute-start | bytes 737288 | tf_op jit(solution)/shard_map/ppermute | solution.py:48
  120.7 20.5 %collective-permute-start.27 = (bf16[1152,384]{1,0:T(8,128)(2,1)S(1)}, bf16[1152,384]{1,0:T(8,128)(2,1)S(1)}, u32[]{:S(2)}, u32[]{:S(2)}) collective-permute-start(bf16[1152,384]{1,0:T(8,128)(2,1)S(1)} %constant_dynamic-update-slice_fusion.p0), channel_id=1, source_target_pairs={{0,1},{1,0},{2,3},{3,2},{4,5},{5,4},{6,7},{7,6},{8,9},{9,8},{10,11... | collective-permute-start | bytes 2654216 | tf_op jit(solution)/shard_map/ppermute | solution.py:56
  129.7 11.5 %collective-permute-start.31 = (bf16[1152,384]{1,0:T(8,128)(2,1)S(1)}, bf16[1152,384]{1,0:T(8,128)(2,1)S(1)}, u32[]{:S(2)}, u32[]{:S(2)}) collective-permute-start(bf16[1152,384]{1,0:T(8,128)(2,1)S(1)} %collective-permute-done.28.p2), channel_id=1, source_target_pairs={{0,1},{1,0},{2,3},{3,2},{4,5},{5,4},{6,7},{7,6},{8,9},{9,8},{10,11... | collective-permute-start | bytes 2654216 | tf_op jit(solution)/shard_map/ppermute | solution.py:56
  132.2 18.7 %collective-permute-start.25 = (bf16[320,384]{1,0:T(8,128)(2,1)S(1)}, bf16[320,384]{1,0:T(8,128)(2,1)S(1)}, u32[]{:S(2)}, u32[]{:S(2)}) collective-permute-start(bf16[320,384]{1,0:T(8,128)(2,1)S(1)} %get-tuple-element.98), channel_id=1, source_target_pairs={{0,16},{4,20},{8,24},{12,28},{16,32},{20,36},{24,40},{28,44},{32,4... | collective-permute-start | bytes 737288 | tf_op jit(solution)/shard_map/ppermute | solution.py:48
  134.1 17.6 %collective-permute-start.26 = (bf16[320,384]{1,0:T(8,128)(2,1)S(1)}, bf16[320,384]{1,0:T(8,128)(2,1)S(1)}, u32[]{:S(2)}, u32[]{:S(2)}) collective-permute-start(bf16[320,384]{1,0:T(8,128)(2,1)S(1)} %get-tuple-element.96), channel_id=1, source_target_pairs={{16,0},{20,4},{24,8},{28,12},{32,16},{36,20},{40,24},{44,28},{48,3... | collective-permute-start | bytes 737288 | tf_op jit(solution)/shard_map/ppermute | solution.py:48
  (12 other events, 63.2 us)

commit v4 on v0

v4 whole, which is shorter than its diff:
```python
import functools

import jax
import jax.numpy as jnp
from jax import lax
from jax.experimental import pallas as pl
from jax.experimental.pallas import tpu as pltpu
from jax.sharding import PartitionSpec as P

F32 = jnp.float32
BF16 = jnp.bfloat16
ERFC = (
    -1.26551223, 1.00002368, 0.37409196, 0.09678418, -0.18628806,
    0.27886807, -1.13520398, 1.48851587, -0.82215223, 0.17087277,
)
ROWS = 1024
MID = ROWS // 2
W = 384
R = 64
FIRST = MID - R
VMEM = pl.BlockSpec(memory_space=pltpu.VMEM)
SMEM = pl.BlockSpec(memory_space=pltpu.SMEM)
HBM = pl.BlockSpec(memory_space=pltpu.HBM)


def gelu(x):
    z = jnp.abs(x) * 0.7071067811865476
    t = 1.0 / (1.0 + 0.5 * z)
    poly = jnp.full_like(t, ERFC[-1])
    for c in ERFC[-2::-1]:
        poly = poly * t + c
    e = t * jnp.exp(poly - z * z)
    return 0.5 * x * jnp.where(x >= 0.0, 2.0 - e, e)


def shifted(array, by):
    size = lax.axis_size("seq")
    pairs = [(i, i + by) for i in range(size) if 0 <= i + by < size]
    return lax.ppermute(array, "seq", pairs)


def chip_swap(array):
    return lax.ppermute(array, "ch", [(i, i ^ 2) for i in range(4)])


def core_swap(array):
    return lax.ppermute(array, "ch", [(i, i ^ 1) for i in range(4)])


def dot(a, b):
    return jnp.dot(a, b, preferred_element_type=F32)


def stage_kernel(layer, ch_ref, w_hbm, o_ref, sems):
    copies = []
    for k in range(3):
        for p in range(4):
            row = pl.multiple_of((ch_ref[0] ^ p) * W, 128)
            copies.append(
                pltpu.make_async_copy(
                    w_hbm.at[layer, k, pl.ds(row, W), :],
                    o_ref.at[pl.ds(p * W, W), pl.ds(k * W, W)],
                    sems.at[len(copies)],
                )
            )
    for copy in copies:
        copy.start()
    for copy in copies:
        copy.wait()


def finish(total, vec_ref, s_ref, a_ref):
    s = (total + vec_ref[0:1, :]).astype(BF16)
    s_ref[...] = s
    a_ref[...] = gelu(s.astype(F32) * vec_ref[1:2, :] + vec_ref[2:3, :]).astype(BF16)


def near_kernel(plan, first_row, *refs):
    groups = max(g for g, _, _ in plan) + 1
    bins_ref, vec_ref, w_ref, s_ref, a_ref, buf = refs[4 * groups :]
    to = 0
    for g, at, count in plan:
        for p, piece in enumerate(refs[4 * g : 4 * g + 4]):
            buf[to : to + count, p * W : (p + 1) * W] = piece[at : at + count, :]
        to += count
    total = bins_ref[first_row : first_row + MID, :].astype(F32)
    for k in range(3):
        total = total + dot(buf[k * R : k * R + MID, :], w_ref[:, k * W : (k + 1) * W])
    finish(total, vec_ref, s_ref, a_ref)


def product_kernel(p0, p1, p2, p3, w_ref, o0, o1, o2):
    full = dot(jnp.concatenate([p[...] for p in (p0, p1, p2, p3)], axis=1), w_ref[...])
    for k, o in enumerate((o0, o1, o2)):
        o[...] = full[:, k * W : (k + 1) * W].astype(BF16)


def join_kernel(s0, t0, t1, t2, vec_ref, s_ref, a_ref):
    f = lambda ref: ref[...].astype(F32)
    finish(f(s0) + f(t0) + f(t1) + f(t2), vec_ref, s_ref, a_ref)


def out_kernel(s_lo, q_lo, up_lo, down_lo, s_hi, q_hi, up_hi, down_hi, vec_ref, o_ref):
    for to, refs in ((0, (s_lo, q_lo, up_lo, down_lo)), (MID, (s_hi, q_hi, up_hi, down_hi))):
        total = vec_ref[0:1, :]
        for ref in refs:
            total = total + ref[...].astype(F32)
        o_ref[to : to + MID, :] = total.astype(BF16)


def call(kernel, args, rows, scratch=()):
    return pl.pallas_call(
        kernel,
        out_shape=[jax.ShapeDtypeStruct((r, W), BF16) for r in rows],
        in_specs=[VMEM] * len(args),
        out_specs=[VMEM] * len(rows),
        scratch_shapes=list(scratch),
        compiler_params=pltpu.CompilerParams(vmem_limit_bytes=20 * 1024 * 1024),
        cost_estimate=pl.CostEstimate(flops=0, bytes_accessed=1024, transcendentals=0),
    )(*args)


def staged(layer, ch, conv_weight):
    return pl.pallas_call(
        functools.partial(stage_kernel, layer),
        out_shape=jax.ShapeDtypeStruct((4 * W, 3 * W), BF16),
        in_specs=[SMEM, HBM],
        out_specs=VMEM,
        scratch_shapes=[pltpu.SemaphoreType.DMA((12,))],
        compiler_params=pltpu.CompilerParams(vmem_limit_bytes=50 * 1024 * 1024),
    )(ch, conv_weight)


def per_device(bins_in, pre_scale, pre_shift, conv_weight, conv_bias):
    after = lax.optimization_barrier
    ch = lax.axis_index("ch").astype(jnp.int32).reshape(1)
    hop1, hop2 = 1, 4096 // ROWS
    vec0 = jnp.stack([conv_bias[0], pre_scale[1], pre_shift[1]])
    vec1 = jnp.stack([conv_bias[1], pre_scale[2], pre_shift[2]])
    vec2 = conv_bias[2:3]
    halves = [MID] * 3
    scratch = [pltpu.VMEM((MID + 2 * R, 4 * W), BF16)]

    def entry(x):
        return gelu(x.astype(F32) * pre_scale[0] + pre_shift[0]).astype(BF16)

    act_1 = entry(bins_in[FIRST:])
    far_1 = chip_swap(act_1)
    near_1 = core_swap(act_1)
    act_3 = entry(bins_in[:FIRST])
    low = shifted(act_1[-R:], 1)
    high = shifted(act_3[:R], -1)
    w0 = staged(0, ch, conv_weight)
    act_2 = jnp.concatenate([low, high], axis=0)
    far_2 = chip_swap(act_2)
    near_2 = core_swap(act_2)
    far_3 = chip_swap(act_3)
    near_3 = core_swap(act_3)
    far_1, far_2, near_2, w0 = after((far_1, far_2, near_2, w0))
    g_1 = (act_1, near_1, far_1, core_swap(far_1))
    g_2 = (act_2, near_2, far_2, core_swap(far_2))
    plan_hi = ((0, 0, ROWS - FIRST), (1, R, R))
    s_hi, a_hi = call(
        functools.partial(near_kernel, plan_hi, MID), (*g_1, *g_2, bins_in, vec0, w0), halves[:2], scratch
    )
    far_hi = chip_swap(a_hi)
    near_hi = core_swap(a_hi)
    far_3, a_hi = after((far_3, a_hi))
    g_3 = (act_3, near_3, far_3, core_swap(far_3))
    plan_lo = ((1, 0, R), (2, 0, FIRST), (0, 0, 2 * R))
    s_lo, a_lo = call(
        functools.partial(near_kernel, plan_lo, 0), (*g_1, *g_2, *g_3, bins_in, vec0, w0), halves[:2], scratch
    )
    far_lo = chip_swap(a_lo)
    near_lo = core_swap(a_lo)

    ch, a_lo = after((ch, a_lo))
    w1 = staged(1, ch, conv_weight)
    far_hi, near_lo, w1 = after((far_hi, near_lo, w1))
    t0, t1, t2 = call(product_kernel, (a_hi, near_hi, far_hi, core_swap(far_hi), w1), halves)
    up = shifted(t0, hop1)
    far_lo, t1 = after((far_lo, t1))
    u0, u1, u2 = call(product_kernel, (a_lo, near_lo, far_lo, core_swap(far_lo), w1), halves)
    down = shifted(u2, -hop1)
    s_lo, a_lo = call(join_kernel, (s_lo, u1, up, t2, vec1), halves[:2])
    far_lo = chip_swap(a_lo)
    near_lo = core_swap(a_lo)
    ch, a_lo = after((ch, a_lo))
    w2 = staged(2, ch, conv_weight)
    down, w2 = after((down, w2))
    s_hi, a_hi = call(join_kernel, (s_hi, t1, u0, down, vec1), halves[:2])
    far_hi = chip_swap(a_hi)
    near_hi = core_swap(a_hi)

    def last(own, near, far):
        q0, q1, q2 = call(product_kernel, (own, near, far, core_swap(far), w2), halves)
        return q1, shifted(q0, hop2), shifted(q2, -hop2)

    far_lo, a_hi = after((far_lo, a_hi))
    q_lo, up_lo, down_lo = last(a_lo, near_lo, far_lo)
    far_hi, q_lo = after((far_hi, q_lo))
    q_hi, up_hi, down_hi = last(a_hi, near_hi, far_hi)
    (out,) = call(out_kernel, (s_lo, q_lo, up_lo, down_lo, s_hi, q_hi, up_hi, down_hi, vec2), [ROWS])
    return out


def solution(mesh):
    return jax.shard_map(
        per_device,
        mesh=mesh,
        in_specs=(
            P("seq", "ch"),
            P(None, "ch"),
            P(None, "ch"),
            P(None, None, None, "ch"),
            P(None, "ch"),
        ),
        out_specs=P("seq", "ch"),
        check_vma=False,
    )
```

time: 411 us -> 153 us (0.37)
  the two profiles are of different devices: /device:TPU:6 before, /device:TPU:48 now
where the time goes in v4:
time: 153 us; the launch traced here: 152 us
  waiting for transfers between devices  80.7 us (53%)
  starting transfers between devices  40.3 us (26%)
  Pallas kernels  26 us (17%)
  other arithmetic  3.93 us (3%)
    ppermute x8, waiting for transfers between devices, shifted(): return lax.ppermute(array, 'seq', pairs)  47.7 us
    ppermute x8, starting transfers between devices, shifted(): return lax.ppermute(array, 'seq', pairs)  30.4 us
    ppermute x7, waiting for transfers between devices, chip_swap(): return lax.ppermute(array, 'ch', [(i, i ^ 2) for i in range(4)])  30.1 us
    pallas_call x9, Pallas kernels, call(): pl.pallas_call(kernel, out_shape=[jax.ShapeDtypeStruct((r, W), BF16) for...  19.8 us
    ppermute x7, starting transfers between devices, chip_swap(): return lax.ppermute(array, 'ch', [(i, i ^ 2) for i in range(4)])  7.96 us
    pallas_call x3, Pallas kernels, staged(): pl.pallas_call(functools.partial(stage_kernel, layer), out_shape=jax.Shap...  6.2 us
    convert_element_type x2, other arithmetic, entry(): return gelu(x.astype(F32) * pre_scale[0] + pre_shift[0]).astype(BF16)  3.91 us
  transfers between devices with their start and end apart: 29, of which 16 were waited for; matrix products, arithmetic and copies ran while one was open for 1% of the time, Pallas kernels for 16%

profile of v4, /device:TPU:48, one launch (start us, length us, event | category | flops | bytes accessed | tf_op | source)
XLA Modules:
  0.0 152.1 jit_solution(2408982210106715337)
XLA Ops:
  4.3 3.9 %collective-permute-start.2 = (bf16[64,384]{1,0:T(8,128)(2,1)S(1)}, bf16[64,384]{1,0:T(8,128)(2,1)S(1)}, u32[]{:S(2)}, u32[]{:S(2)}) collective-permute-start(bf16[64,384]{1,0:T(8,128)(2,1)S(1)} %slice.54), channel_id=1, source_target_pairs={{0,4},{4,8},{8,12},{12,16},{16,20},{20,24},{24,28},{28,32},{32,36}... | collective-permute-start | bytes 147464 | tf_op jit(solution)/shard_map/ppermute | solution.py:39
  10.1 3.5 %collective-permute-start.3 = (bf16[64,384]{1,0:T(8,128)(2,1)S(1)}, bf16[64,384]{1,0:T(8,128)(2,1)S(1)}, u32[]{:S(2)}, u32[]{:S(2)}) collective-permute-start(bf16[64,384]{1,0:T(8,128)(2,1)S(1)} %slice.55), channel_id=1, source_target_pairs={{4,0},{8,4},{12,8},{16,12},{20,16},{24,20},{28,24},{32,28},{36,32}... | collective-permute-start | bytes 147464 | tf_op jit(solution)/shard_map/ppermute | solution.py:39
  13.5 2.4 %collective-permute-done.2 = bf16[64,384]{1,0:T(8,128)(2,1)S(1)} collective-permute-done((bf16[64,384]{1,0:T(8,128)(2,1)S(1)}, bf16[64,384]{1,0:T(8,128)(2,1)S(1)}, u32[]{:S(2)}, u32[]{:S(2)}) %collective-permute-start.2) | collective-permute-done | bytes 49184 | tf_op jit(solution)/shard_map/ppermute | solution.py:39
  15.9 2.5 %collective-permute-done.3 = bf16[64,384]{1,0:T(8,128)(2,1)S(1)} collective-permute-done((bf16[64,384]{1,0:T(8,128)(2,1)S(1)}, bf16[64,384]{1,0:T(8,128)(2,1)S(1)}, u32[]{:S(2)}, u32[]{:S(2)}) %collective-permute-start.3) | collective-permute-done | bytes 49184 | tf_op jit(solution)/shard_map/ppermute | solution.py:39
  20.1 2.1 %shard_map.55.refs_10_.refs_14_ = bf16[1536,1152]{1,0:T(8,128)(2,1)S(1)} custom-call(s32[1]{0:T(128)} %bitcast.ch_ref, bf16[3,3,1536,384]{3,2,1,0:T(8,128)(2,1)} %w_hbm.5), custom_call_target="tpu_custom_call" | custom-call | tf_op jit(solution)/shard_map/pallas_call | solution.py:124
  26.1 3.6 %shard_map.56 = (bf16[512,384]{1,0:T(8,128)(2,1)S(1)}, bf16[512,384]{1,0:T(8,128)(2,1)S(1)}) custom-call(bf16[576,384]{1,0:T(8,128)(2,1)S(1)} %fusion.1.refs_0_, bf16[576,384]{1,0:T(8,128)(2,1)S(1)} %collective-permute-done.refs_1_, bf16[576,384]{1,0:T(8,128)(2,1)S(1)} %collective-permute-done.1.refs_2_, ...), custom_call_target="tpu_custom_call" | custom-call | bytes 1024 | tf_op jit(solution)/shard_map/pallas_call | solution.py:112
  29.7 3.9 %collective-permute-done.9.refs_10_ = bf16[448,384]{1,0:T(8,128)(2,1)S(1)} collective-permute-done((bf16[448,384]{1,0:T(8,128)(2,1)S(1)}, bf16[448,384]{1,0:T(8,128)(2,1)S(1)}, u32[]{:S(2)}, u32[]{:S(2)}) %collective-permute-start.9) | collective-permute-done | bytes 344096 | tf_op jit(solution)/shard_map/ppermute | solution.py:43
  35.3 3.6 %shard_map.57 = (bf16[512,384]{1,0:T(8,128)(2,1)S(1)}, bf16[512,384]{1,0:T(8,128)(2,1)S(1)}) custom-call(bf16[576,384]{1,0:T(8,128)(2,1)S(1)} %fusion.1.refs_0_, bf16[576,384]{1,0:T(8,128)(2,1)S(1)} %collective-permute-done.refs_1_, bf16[576,384]{1,0:T(8,128)(2,1)S(1)} %collective-permute-done.1.refs_2_, ...), custom_call_target="tpu_custom_call" | custom-call | bytes 1024 | tf_op jit(solution)/shard_map/pallas_call | solution.py:112
  41.6 3.6 %collective-permute-done.11.p2 = bf16[512,384]{1,0:T(8,128)(2,1)S(1)} collective-permute-done((bf16[512,384]{1,0:T(8,128)(2,1)S(1)}, bf16[512,384]{1,0:T(8,128)(2,1)S(1)}, u32[]{:S(2)}, u32[]{:S(2)}) %collective-permute-start.11) | collective-permute-done | bytes 393248 | tf_op jit(solution)/shard_map/ppermute | solution.py:43
  46.9 2.2 %shard_map.59 = (bf16[512,384]{1,0:T(8,128)(2,1)S(1)}, bf16[512,384]{1,0:T(8,128)(2,1)S(1)}, bf16[512,384]{1,0:T(8,128)(2,1)S(1)}) custom-call(bf16[512,384]{1,0:T(8,128)(2,1)S(1)} %get-tuple-element.57.p0, bf16[512,384]{1,0:T(8,128)(2,1)S(1)} %collective-permute-done.14.p1, bf16[512,384]{1,0:T(8,128)(2,1)S(1)} %collective-permute-done.11.p2, ...), custom_call_target="tpu_custom_call" | custom-call | bytes 1024 | tf_op jit(solution)/shard_map/pallas_call | solution.py:112
  49.1 7.6 %collective-permute-done.13.p2 = bf16[512,384]{1,0:T(8,128)(2,1)S(1)} collective-permute-done((bf16[512,384]{1,0:T(8,128)(2,1)S(1)}, bf16[512,384]{1,0:T(8,128)(2,1)S(1)}, u32[]{:S(2)}, u32[]{:S(2)}) %collective-permute-start.13) | collective-permute-done | bytes 393248 | tf_op jit(solution)/shard_map/ppermute | solution.py:43
  56.7 4.7 %collective-permute-start.17 = (bf16[512,384]{1,0:T(8,128)(2,1)S(1)}, bf16[512,384]{1,0:T(8,128)(2,1)S(1)}, u32[]{:S(2)}, u32[]{:S(2)}) collective-permute-start(bf16[512,384]{1,0:T(8,128)(2,1)S(1)} %get-tuple-element.63), channel_id=1, source_target_pairs={{0,4},{4,8},{8,12},{12,16},{16,20},{20,24},{24,28},{28,32},{32,36}... | collective-permute-start | bytes 1179656 | tf_op jit(solution)/shard_map/ppermute | solution.py:39
  61.4 2.2 %shard_map.60 = (bf16[512,384]{1,0:T(8,128)(2,1)S(1)}, bf16[512,384]{1,0:T(8,128)(2,1)S(1)}, bf16[512,384]{1,0:T(8,128)(2,1)S(1)}) custom-call(bf16[512,384]{1,0:T(8,128)(2,1)S(1)} %get-tuple-element.54.p0, bf16[512,384]{1,0:T(8,128)(2,1)S(1)} %collective-permute-done.12.p1, bf16[512,384]{1,0:T(8,128)(2,1)S(1)} %collective-permute-done.13.p2, ...), custom_call_target="tpu_custom_call" | custom-call | bytes 1024 | tf_op jit(solution)/shard_map/pallas_call | solution.py:112
  63.6 2.7 %collective-permute-start.18 = (bf16[512,384]{1,0:T(8,128)(2,1)S(1)}, bf16[512,384]{1,0:T(8,128)(2,1)S(1)}, u32[]{:S(2)}, u32[]{:S(2)}) collective-permute-start(bf16[512,384]{1,0:T(8,128)(2,1)S(1)} %get-tuple-element.69), channel_id=1, source_target_pairs={{4,0},{8,4},{12,8},{16,12},{20,16},{24,20},{28,24},{32,28},{36,32}... | collective-permute-start | bytes 1179656 | tf_op jit(solution)/shard_map/ppermute | solution.py:39
  66.3 13.7 %collective-permute-done.17.t1 = bf16[512,384]{1,0:T(8,128)(2,1)S(1)} collective-permute-done((bf16[512,384]{1,0:T(8,128)(2,1)S(1)}, bf16[512,384]{1,0:T(8,128)(2,1)S(1)}, u32[]{:S(2)}, u32[]{:S(2)}) %collective-permute-start.17) | collective-permute-done | bytes 393248 | tf_op jit(solution)/shard_map/ppermute | solution.py:39
  85.7 6.4 %collective-permute-done.21.p2 = bf16[512,384]{1,0:T(8,128)(2,1)S(1)} collective-permute-done((bf16[512,384]{1,0:T(8,128)(2,1)S(1)}, bf16[512,384]{1,0:T(8,128)(2,1)S(1)}, u32[]{:S(2)}, u32[]{:S(2)}) %collective-permute-start.21) | collective-permute-done | bytes 393248 | tf_op jit(solution)/shard_map/ppermute | solution.py:43
  93.8 2.2 %shard_map.64 = (bf16[512,384]{1,0:T(8,128)(2,1)S(1)}, bf16[512,384]{1,0:T(8,128)(2,1)S(1)}, bf16[512,384]{1,0:T(8,128)(2,1)S(1)}) custom-call(bf16[512,384]{1,0:T(8,128)(2,1)S(1)} %get-tuple-element.74.p0, bf16[512,384]{1,0:T(8,128)(2,1)S(1)} %collective-permute-done.20.p1, bf16[512,384]{1,0:T(8,128)(2,1)S(1)} %collective-permute-done.21.p2, ...), custom_call_target="tpu_custom_call" | custom-call | bytes 1024 | tf_op jit(solution)/shard_map/pallas_call | solution.py:112
  96.0 7.6 %collective-permute-done.19.p2 = bf16[512,384]{1,0:T(8,128)(2,1)S(1)} collective-permute-done((bf16[512,384]{1,0:T(8,128)(2,1)S(1)}, bf16[512,384]{1,0:T(8,128)(2,1)S(1)}, u32[]{:S(2)}, u32[]{:S(2)}) %collective-permute-start.19) | collective-permute-done | bytes 393248 | tf_op jit(solution)/shard_map/ppermute | solution.py:43
  103.6 7.7 %collective-permute-start.23 = (bf16[512,384]{1,0:T(8,128)(2,1)S(1)}, bf16[512,384]{1,0:T(8,128)(2,1)S(1)}, u32[]{:S(2)}, u32[]{:S(2)}) collective-permute-start(bf16[512,384]{1,0:T(8,128)(2,1)S(1)} %get-tuple-element.79), channel_id=1, source_target_pairs={{0,16},{4,20},{8,24},{12,28},{16,32},{20,36},{24,40},{28,44},{32,4... | collective-permute-start | bytes 1179656 | tf_op jit(solution)/shard_map/ppermute | solution.py:39
  112.7 2.2 %shard_map.65 = (bf16[512,384]{1,0:T(8,128)(2,1)S(1)}, bf16[512,384]{1,0:T(8,128)(2,1)S(1)}, bf16[512,384]{1,0:T(8,128)(2,1)S(1)}) custom-call(bf16[512,384]{1,0:T(8,128)(2,1)S(1)} %get-tuple-element.82.p0, bf16[512,384]{1,0:T(8,128)(2,1)S(1)} %collective-permute-done.25.p1, bf16[512,384]{1,0:T(8,128)(2,1)S(1)} %collective-permute-done.19.p2, ...), custom_call_target="tpu_custom_call" | custom-call | bytes 1024 | tf_op jit(solution)/shard_map/pallas_call | solution.py:112
  114.9 5.5 %collective-permute-start.27 = (bf16[512,384]{1,0:T(8,128)(2,1)S(1)}, bf16[512,384]{1,0:T(8,128)(2,1)S(1)}, u32[]{:S(2)}, u32[]{:S(2)}) collective-permute-start(bf16[512,384]{1,0:T(8,128)(2,1)S(1)} %get-tuple-element.85), channel_id=1, source_target_pairs={{0,16},{4,20},{8,24},{12,28},{16,32},{20,36},{24,40},{28,44},{32,4... | collective-permute-start | bytes 1179656 | tf_op jit(solution)/shard_map/ppermute | solution.py:39
  121.7 9.4 %collective-permute-done.23.up_lo = bf16[512,384]{1,0:T(8,128)(2,1)S(1)} collective-permute-done((bf16[512,384]{1,0:T(8,128)(2,1)S(1)}, bf16[512,384]{1,0:T(8,128)(2,1)S(1)}, u32[]{:S(2)}, u32[]{:S(2)}) %collective-permute-start.23) | collective-permute-done | bytes 393248 | tf_op jit(solution)/shard_map/ppermute | solution.py:39
  131.1 11.2 %collective-permute-done.27.up_hi = bf16[512,384]{1,0:T(8,128)(2,1)S(1)} collective-permute-done((bf16[512,384]{1,0:T(8,128)(2,1)S(1)}, bf16[512,384]{1,0:T(8,128)(2,1)S(1)}, u32[]{:S(2)}, u32[]{:S(2)}) %collective-permute-start.27) | collective-permute-done | bytes 393248 | tf_op jit(solution)/shard_map/ppermute | solution.py:39
  142.3 8.4 %collective-permute-done.28.down_hi = bf16[512,384]{1,0:T(8,128)(2,1)S(1)} collective-permute-done((bf16[512,384]{1,0:T(8,128)(2,1)S(1)}, bf16[512,384]{1,0:T(8,128)(2,1)S(1)}, u32[]{:S(2)}, u32[]{:S(2)}) %collective-permute-start.28) | collective-permute-done | bytes 393248 | tf_op jit(solution)/shard_map/ppermute | solution.py:39
  (60 shorter events, 28.9 us)
Async XLA Ops:
  3.0 20.2 %collective-permute-start.1 = (bf16[576,384]{1,0:T(8,128)(2,1)S(1)}, bf16[576,384]{1,0:T(8,128)(2,1)S(1)}, u32[]{:S(2)}, u32[]{:S(2)}) collective-permute-start(bf16[576,384]{1,0:T(8,128)(2,1)S(1)} %fusion.1.refs_0_), channel_id=1, source_target_pairs={{0,2},{1,3},{2,0},{3,1},{4,6},{5,7},{6,4},{7,5},{8,10},{9,11},{10,... | collective-permute-start | bytes 1327112 | tf_op jit(solution)/shard_map/ppermute | solution.py:43
  4.3 11.6 %collective-permute-start.2 = (bf16[64,384]{1,0:T(8,128)(2,1)S(1)}, bf16[64,384]{1,0:T(8,128)(2,1)S(1)}, u32[]{:S(2)}, u32[]{:S(2)}) collective-permute-start(bf16[64,384]{1,0:T(8,128)(2,1)S(1)} %slice.54), channel_id=1, source_target_pairs={{0,4},{4,8},{8,12},{12,16},{16,20},{20,24},{24,28},{28,32},{32,36}... | collective-permute-start | bytes 147464 | tf_op jit(solution)/shard_map/ppermute | solution.py:39
  10.1 8.4 %collective-permute-start.3 = (bf16[64,384]{1,0:T(8,128)(2,1)S(1)}, bf16[64,384]{1,0:T(8,128)(2,1)S(1)}, u32[]{:S(2)}, u32[]{:S(2)}) collective-permute-start(bf16[64,384]{1,0:T(8,128)(2,1)S(1)} %slice.55), channel_id=1, source_target_pairs={{4,0},{8,4},{12,8},{16,12},{20,16},{24,20},{28,24},{32,28},{36,32}... | collective-permute-start | bytes 147464 | tf_op jit(solution)/shard_map/ppermute | solution.py:39
  18.5 4.7 %collective-permute-start.4 = (bf16[128,384]{1,0:T(8,128)(2,1)S(1)}, bf16[128,384]{1,0:T(8,128)(2,1)S(1)}, u32[]{:S(2)}, u32[]{:S(2)}) collective-permute-start(bf16[128,384]{1,0:T(8,128)(2,1)S(1)} %constant_dynamic-update-slice_fusion.refs_4_), channel_id=1, source_target_pairs={{0,2},{1,3},{2,0},{3,1},{4,6},{5,7},{6,4},{7,5},{8,10},{9,11},{10,... | collective-permute-start | bytes 294920 | tf_op jit(solution)/shard_map/ppermute | solution.py:43
  19.6 3.6 %collective-permute-start.5 = (bf16[128,384]{1,0:T(8,128)(2,1)S(1)}, bf16[128,384]{1,0:T(8,128)(2,1)S(1)}, u32[]{:S(2)}, u32[]{:S(2)}) collective-permute-start(bf16[128,384]{1,0:T(8,128)(2,1)S(1)} %constant_dynamic-update-slice_fusion.refs_4_), channel_id=1, source_target_pairs={{0,1},{1,0},{2,3},{3,2},{4,5},{5,4},{6,7},{7,6},{8,9},{9,8},{10,11... | collective-permute-start | bytes 294920 | tf_op jit(solution)/shard_map/ppermute | solution.py:47
  19.6 5.3 %collective-permute-start = (bf16[576,384]{1,0:T(8,128)(2,1)S(1)}, bf16[576,384]{1,0:T(8,128)(2,1)S(1)}, u32[]{:S(2)}, u32[]{:S(2)}) collective-permute-start(bf16[576,384]{1,0:T(8,128)(2,1)S(1)} %fusion.1.refs_0_), channel_id=1, source_target_pairs={{0,1},{1,0},{2,3},{3,2},{4,5},{5,4},{6,7},{7,6},{8,9},{9,8},{10,11... | collective-permute-start | bytes 1327112 | tf_op jit(solution)/shard_map/ppermute | solution.py:47
  23.2 10.5 %collective-permute-start.9 = (bf16[448,384]{1,0:T(8,128)(2,1)S(1)}, bf16[448,384]{1,0:T(8,128)(2,1)S(1)}, u32[]{:S(2)}, u32[]{:S(2)}) collective-permute-start(bf16[448,384]{1,0:T(8,128)(2,1)S(1)} %fusion.4.refs_8_), channel_id=1, source_target_pairs={{0,2},{1,3},{2,0},{3,1},{4,6},{5,7},{6,4},{7,5},{8,10},{9,11},{10,... | collective-permute-start | bytes 1032200 | tf_op jit(solution)/shard_map/ppermute | solution.py:43
  24.3 10.4 %collective-permute-start.8 = (bf16[448,384]{1,0:T(8,128)(2,1)S(1)}, bf16[448,384]{1,0:T(8,128)(2,1)S(1)}, u32[]{:S(2)}, u32[]{:S(2)}) collective-permute-start(bf16[448,384]{1,0:T(8,128)(2,1)S(1)} %fusion.4.refs_8_), channel_id=1, source_target_pairs={{0,1},{1,0},{2,3},{3,2},{4,5},{5,4},{6,7},{7,6},{8,9},{9,8},{10,11... | collective-permute-start | bytes 1032200 | tf_op jit(solution)/shard_map/ppermute | solution.py:47
  33.7 11.5 %collective-permute-start.11 = (bf16[512,384]{1,0:T(8,128)(2,1)S(1)}, bf16[512,384]{1,0:T(8,128)(2,1)S(1)}, u32[]{:S(2)}, u32[]{:S(2)}) collective-permute-start(bf16[512,384]{1,0:T(8,128)(2,1)S(1)} %get-tuple-element.57.p0), channel_id=1, source_target_pairs={{0,2},{1,3},{2,0},{3,1},{4,6},{5,7},{6,4},{7,5},{8,10},{9,11},{10,... | collective-permute-start | bytes 1179656 | tf_op jit(solution)/shard_map/ppermute | solution.py:43
  38.9 6.3 %collective-permute-start.12 = (bf16[512,384]{1,0:T(8,128)(2,1)S(1)}, bf16[512,384]{1,0:T(8,128)(2,1)S(1)}, u32[]{:S(2)}, u32[]{:S(2)}) collective-permute-start(bf16[512,384]{1,0:T(8,128)(2,1)S(1)} %get-tuple-element.54.p0), channel_id=1, source_target_pairs={{0,1},{1,0},{2,3},{3,2},{4,5},{5,4},{6,7},{7,6},{8,9},{9,8},{10,11... | collective-permute-start | bytes 1179656 | tf_op jit(solution)/shard_map/ppermute | solution.py:47
  39.1 7.1 %collective-permute-start.14 = (bf16[512,384]{1,0:T(8,128)(2,1)S(1)}, bf16[512,384]{1,0:T(8,128)(2,1)S(1)}, u32[]{:S(2)}, u32[]{:S(2)}) collective-permute-start(bf16[512,384]{1,0:T(8,128)(2,1)S(1)} %get-tuple-element.57.p0), channel_id=1, source_target_pairs={{0,1},{1,0},{2,3},{3,2},{4,5},{5,4},{6,7},{7,6},{8,9},{9,8},{10,11... | collective-permute-start | bytes 1179656 | tf_op jit(solution)/shard_map/ppermute | solution.py:47
  45.2 11.5 %collective-permute-start.13 = (bf16[512,384]{1,0:T(8,128)(2,1)S(1)}, bf16[512,384]{1,0:T(8,128)(2,1)S(1)}, u32[]{:S(2)}, u32[]{:S(2)}) collective-permute-start(bf16[512,384]{1,0:T(8,128)(2,1)S(1)} %get-tuple-element.54.p0), channel_id=1, source_target_pairs={{0,2},{1,3},{2,0},{3,1},{4,6},{5,7},{6,4},{7,5},{8,10},{9,11},{10,... | collective-permute-start | bytes 1179656 | tf_op jit(solution)/shard_map/ppermute | solution.py:43
  56.7 4.7 %collective-permute-start.16 = (bf16[512,384]{1,0:T(8,128)(2,1)S(1)}, bf16[512,384]{1,0:T(8,128)(2,1)S(1)}, u32[]{:S(2)}, u32[]{:S(2)}) collective-permute-start(bf16[512,384]{1,0:T(8,128)(2,1)S(1)} %collective-permute-done.13.p2), channel_id=1, source_target_pairs={{0,1},{1,0},{2,3},{3,2},{4,5},{5,4},{6,7},{7,6},{8,9},{9,8},{10,11... | collective-permute-start | bytes 1179656 | tf_op jit(solution)/shard_map/ppermute | solution.py:47
  56.7 23.3 %collective-permute-start.17 = (bf16[512,384]{1,0:T(8,128)(2,1)S(1)}, bf16[512,384]{1,0:T(8,128)(2,1)S(1)}, u32[]{:S(2)}, u32[]{:S(2)}) collective-permute-start(bf16[512,384]{1,0:T(8,128)(2,1)S(1)} %get-tuple-element.63), channel_id=1, source_target_pairs={{0,4},{4,8},{8,12},{12,16},{16,20},{20,24},{24,28},{28,32},{32,36}... | collective-permute-start | bytes 1179656 | tf_op jit(solution)/shard_map/ppermute | solution.py:39
  63.6 20.8 %collective-permute-start.18 = (bf16[512,384]{1,0:T(8,128)(2,1)S(1)}, bf16[512,384]{1,0:T(8,128)(2,1)S(1)}, u32[]{:S(2)}, u32[]{:S(2)}) collective-permute-start(bf16[512,384]{1,0:T(8,128)(2,1)S(1)} %get-tuple-element.69), channel_id=1, source_target_pairs={{4,0},{8,4},{12,8},{16,12},{20,16},{24,20},{28,24},{32,28},{36,32}... | collective-permute-start | bytes 1179656 | tf_op jit(solution)/shard_map/ppermute | solution.py:39
  81.3 10.8 %collective-permute-start.21 = (bf16[512,384]{1,0:T(8,128)(2,1)S(1)}, bf16[512,384]{1,0:T(8,128)(2,1)S(1)}, u32[]{:S(2)}, u32[]{:S(2)}) collective-permute-start(bf16[512,384]{1,0:T(8,128)(2,1)S(1)} %get-tuple-element.74.p0), channel_id=1, source_target_pairs={{0,2},{1,3},{2,0},{3,1},{4,6},{5,7},{6,4},{7,5},{8,10},{9,11},{10,... | collective-permute-start | bytes 1179656 | tf_op jit(solution)/shard_map/ppermute | solution.py:43
  82.4 11.0 %collective-permute-start.20 = (bf16[512,384]{1,0:T(8,128)(2,1)S(1)}, bf16[512,384]{1,0:T(8,128)(2,1)S(1)}, u32[]{:S(2)}, u32[]{:S(2)}) collective-permute-start(bf16[512,384]{1,0:T(8,128)(2,1)S(1)} %get-tuple-element.74.p0), channel_id=1, source_target_pairs={{0,1},{1,0},{2,3},{3,2},{4,5},{5,4},{6,7},{7,6},{8,9},{9,8},{10,11... | collective-permute-start | bytes 1179656 | tf_op jit(solution)/shard_map/ppermute | solution.py:47
  92.1 11.5 %collective-permute-start.19 = (bf16[512,384]{1,0:T(8,128)(2,1)S(1)}, bf16[512,384]{1,0:T(8,128)(2,1)S(1)}, u32[]{:S(2)}, u32[]{:S(2)}) collective-permute-start(bf16[512,384]{1,0:T(8,128)(2,1)S(1)} %get-tuple-element.82.p0), channel_id=1, source_target_pairs={{0,2},{1,3},{2,0},{3,1},{4,6},{5,7},{6,4},{7,5},{8,10},{9,11},{10,... | collective-permute-start | bytes 1179656 | tf_op jit(solution)/shard_map/ppermute | solution.py:43
  93.2 19.5 %collective-permute-start.25 = (bf16[512,384]{1,0:T(8,128)(2,1)S(1)}, bf16[512,384]{1,0:T(8,128)(2,1)S(1)}, u32[]{:S(2)}, u32[]{:S(2)}) collective-permute-start(bf16[512,384]{1,0:T(8,128)(2,1)S(1)} %get-tuple-element.82.p0), channel_id=1, source_target_pairs={{0,1},{1,0},{2,3},{3,2},{4,5},{5,4},{6,7},{7,6},{8,9},{9,8},{10,11... | collective-permute-start | bytes 1179656 | tf_op jit(solution)/shard_map/ppermute | solution.py:47
  103.6 9.0 %collective-permute-start.26 = (bf16[512,384]{1,0:T(8,128)(2,1)S(1)}, bf16[512,384]{1,0:T(8,128)(2,1)S(1)}, u32[]{:S(2)}, u32[]{:S(2)}) collective-permute-start(bf16[512,384]{1,0:T(8,128)(2,1)S(1)} %collective-permute-done.19.p2), channel_id=1, source_target_pairs={{0,1},{1,0},{2,3},{3,2},{4,5},{5,4},{6,7},{7,6},{8,9},{9,8},{10,11... | collective-permute-start | bytes 1179656 | tf_op jit(solution)/shard_map/ppermute | solution.py:47
  103.6 27.5 %collective-permute-start.23 = (bf16[512,384]{1,0:T(8,128)(2,1)S(1)}, bf16[512,384]{1,0:T(8,128)(2,1)S(1)}, u32[]{:S(2)}, u32[]{:S(2)}) collective-permute-start(bf16[512,384]{1,0:T(8,128)(2,1)S(1)} %get-tuple-element.79), channel_id=1, source_target_pairs={{0,16},{4,20},{8,24},{12,28},{16,32},{20,36},{24,40},{28,44},{32,4... | collective-permute-start | bytes 1179656 | tf_op jit(solution)/shard_map/ppermute | solution.py:39
  111.4 19.8 %collective-permute-start.24 = (bf16[512,384]{1,0:T(8,128)(2,1)S(1)}, bf16[512,384]{1,0:T(8,128)(2,1)S(1)}, u32[]{:S(2)}, u32[]{:S(2)}) collective-permute-start(bf16[512,384]{1,0:T(8,128)(2,1)S(1)} %get-tuple-element.80), channel_id=1, source_target_pairs={{16,0},{20,4},{24,8},{28,12},{32,16},{36,20},{40,24},{44,28},{48,3... | collective-permute-start | bytes 1179656 | tf_op jit(solution)/shard_map/ppermute | solution.py:39
  114.9 27.4 %collective-permute-start.27 = (bf16[512,384]{1,0:T(8,128)(2,1)S(1)}, bf16[512,384]{1,0:T(8,128)(2,1)S(1)}, u32[]{:S(2)}, u32[]{:S(2)}) collective-permute-start(bf16[512,384]{1,0:T(8,128)(2,1)S(1)} %get-tuple-element.85), channel_id=1, source_target_pairs={{0,16},{4,20},{8,24},{12,28},{16,32},{20,36},{24,40},{28,44},{32,4... | collective-permute-start | bytes 1179656 | tf_op jit(solution)/shard_map/ppermute | solution.py:39
  120.4 30.3 %collective-permute-start.28 = (bf16[512,384]{1,0:T(8,128)(2,1)S(1)}, bf16[512,384]{1,0:T(8,128)(2,1)S(1)}, u32[]{:S(2)}, u32[]{:S(2)}) collective-permute-start(bf16[512,384]{1,0:T(8,128)(2,1)S(1)} %get-tuple-element.86), channel_id=1, source_target_pairs={{16,0},{20,4},{24,8},{28,12},{32,16},{36,20},{40,24},{44,28},{48,3... | collective-permute-start | bytes 1179656 | tf_op jit(solution)/shard_map/ppermute | solution.py:39
  (7 other events, 20.1 us)

commit v5 on v4

--- a/solution.py
+++ b/solution.py
@@ -45,6 +45,11 @@
 
 def core_swap(array):
     return lax.ppermute(array, "ch", [(i, i ^ 1) for i in range(4)])
+
+
+def core_swaps(array, parts):
+    n = array.shape[0] // parts
+    return [core_swap(array[i * n : i * n + n]) for i in range(parts)]
 
 
 def dot(a, b):
@@ -89,8 +94,10 @@
     finish(total, vec_ref, s_ref, a_ref)
 
 
-def product_kernel(p0, p1, p2, p3, w_ref, o0, o1, o2):
-    full = dot(jnp.concatenate([p[...] for p in (p0, p1, p2, p3)], axis=1), w_ref[...])
+def product_kernel(*refs):
+    pieces, (w_ref, o0, o1, o2) = refs[:-4], refs[-4:]
+    near_far = jnp.concatenate([p[...] for p in pieces[3:]], axis=0)
+    full = dot(jnp.concatenate([p[...] for p in pieces[:3]] + [near_far], axis=1), w_ref[...])
     for k, o in enumerate((o0, o1, o2)):
         o[...] = full[:, k * W : (k + 1) * W].astype(BF16)
 
@@ -156,7 +163,7 @@
     near_2 = core_swap(act_2)
     far_3 = chip_swap(act_3)
     near_3 = core_swap(act_3)
-    far_1, far_2, near_2, w0 = after((far_1, far_2, near_2, w0))
+    far_1, far_2, far_3, w0 = after((far_1, far_2, far_3, w0))
     g_1 = (act_1, near_1, far_1, core_swap(far_1))
     g_2 = (act_2, near_2, far_2, core_swap(far_2))
     plan_hi = ((0, 0, ROWS - FIRST), (1, R, R))
@@ -165,7 +172,7 @@
     )
     far_hi = chip_swap(a_hi)
     near_hi = core_swap(a_hi)
-    far_3, a_hi = after((far_3, a_hi))
+    near_3, a_hi = after((near_3, a_hi))
     g_3 = (act_3, near_3, far_3, core_swap(far_3))
     plan_lo = ((1, 0, R), (2, 0, FIRST), (0, 0, 2 * R))
     s_lo, a_lo = call(
@@ -176,11 +183,11 @@
 
     ch, a_lo = after((ch, a_lo))
     w1 = staged(1, ch, conv_weight)
-    far_hi, near_lo, w1 = after((far_hi, near_lo, w1))
-    t0, t1, t2 = call(product_kernel, (a_hi, near_hi, far_hi, core_swap(far_hi), w1), halves)
+    far_hi, w1 = after((far_hi, w1))
+    t0, t1, t2 = call(product_kernel, (a_hi, near_hi, far_hi, *core_swaps(far_hi, 2), w1), halves)
     up = shifted(t0, hop1)
     far_lo, t1 = after((far_lo, t1))
-    u0, u1, u2 = call(product_kernel, (a_lo, near_lo, far_lo, core_swap(far_lo), w1), halves)
+    u0, u1, u2 = call(product_kernel, (a_lo, near_lo, far_lo, *core_swaps(far_lo, 2), w1), halves)
     down = shifted(u2, -hop1)
     s_lo, a_lo = call(join_kernel, (s_lo, u1, up, t2, vec1), halves[:2])
     far_lo = chip_swap(a_lo)
@@ -192,14 +199,14 @@
     far_hi = chip_swap(a_hi)
     near_hi = core_swap(a_hi)
 
-    def last(own, near, far):
-        q0, q1, q2 = call(product_kernel, (own, near, far, core_swap(far), w2), halves)
+    def last(own, near, far, parts):
+        q0, q1, q2 = call(product_kernel, (own, near, far, *core_swaps(far, parts), w2), halves)
         return q1, shifted(q0, hop2), shifted(q2, -hop2)
 
     far_lo, a_hi = after((far_lo, a_hi))
-    q_lo, up_lo, down_lo = last(a_lo, near_lo, far_lo)
+    q_lo, up_lo, down_lo = last(a_lo, near_lo, far_lo, 2)
     far_hi, q_lo = after((far_hi, q_lo))
-    q_hi, up_hi, down_hi = last(a_hi, near_hi, far_hi)
+    q_hi, up_hi, down_hi = last(a_hi, near_hi, far_hi, 2)
     (out,) = call(out_kernel, (s_lo, q_lo, up_lo, down_lo, s_hi, q_hi, up_hi, down_hi, vec2), [ROWS])
     return out
 

time: 153 us -> 146 us (0.954)
  the two profiles are of different devices: /device:TPU:48 before, /device:TPU:32 now
where the time goes in v5:
time: 146 us; the launch traced here: 145 us
  waiting for transfers between devices  72.1 us (49%)
  starting transfers between devices  42 us (29%)
  Pallas kernels  25.9 us (18%)
  other arithmetic  3.93 us (3%)
    ppermute x8, waiting for transfers between devices, shifted(): return lax.ppermute(array, 'seq', pairs)  46.6 us
    ppermute x8, starting transfers between devices, shifted(): return lax.ppermute(array, 'seq', pairs)  32.7 us
    pallas_call x9, Pallas kernels, call(): pl.pallas_call(kernel, out_shape=[jax.ShapeDtypeStruct((r, W), BF16) for...  19.7 us
    ppermute x7, waiting for transfers between devices, chip_swap(): return lax.ppermute(array, 'ch', [(i, i ^ 2) for i in range(4)])  19.1 us
    ppermute x18, waiting for transfers between devices, core_swap(): return lax.ppermute(array, 'ch', [(i, i ^ 1) for i in range(4)])  6.32 us
    pallas_call x3, Pallas kernels, staged(): pl.pallas_call(functools.partial(stage_kernel, layer), out_shape=jax.Shap...  6.2 us
    ppermute x7, starting transfers between devices, chip_swap(): return lax.ppermute(array, 'ch', [(i, i ^ 2) for i in range(4)])  5.43 us
    convert_element_type x2, other arithmetic, entry(): return gelu(x.astype(F32) * pre_scale[0] + pre_shift[0]).astype(BF16)  3.91 us
  transfers between devices with their start and end apart: 33, of which 22 were waited for; matrix products, arithmetic and copies ran while one was open for 1% of the time, Pallas kernels for 14%

profile of v5, /device:TPU:32, one launch (start us, length us, event | category | flops | bytes accessed | tf_op | source)
XLA Modules:
  0.0 145.3 jit_solution(7121321781507052261)
XLA Ops:
  0.9 2.1 %fusion.1.refs_0_ = bf16[576,384]{1,0:T(8,128)(2,1)S(1)} fusion(f32[384]{0:T(512)S(1)} %get-tuple-element.103, f32[384]{0:T(512)S(1)} %get-tuple-element.97, bf16[1024,384]{1,0:T(8,128)(2,1)} %refs_12_.1), kind=kLoop, calls=%fused_computation.3 | loop fusion | flops 7741440 | bytes 887808 | tf_op jit(solution)/shard_map/convert_element_type | solution.py:152
  4.6 4.8 %collective-permute-start.2 = (bf16[64,384]{1,0:T(8,128)(2,1)S(1)}, bf16[64,384]{1,0:T(8,128)(2,1)S(1)}, u32[]{:S(2)}, u32[]{:S(2)}) collective-permute-start(bf16[64,384]{1,0:T(8,128)(2,1)S(1)} %slice.86), channel_id=1, source_target_pairs={{0,4},{4,8},{8,12},{12,16},{16,20},{20,24},{24,28},{28,32},{32,36}... | collective-permute-start | bytes 147464 | tf_op jit(solution)/shard_map/ppermute | solution.py:39
  11.5 4.3 %collective-permute-start.3 = (bf16[64,384]{1,0:T(8,128)(2,1)S(1)}, bf16[64,384]{1,0:T(8,128)(2,1)S(1)}, u32[]{:S(2)}, u32[]{:S(2)}) collective-permute-start(bf16[64,384]{1,0:T(8,128)(2,1)S(1)} %slice.87), channel_id=1, source_target_pairs={{4,0},{8,4},{12,8},{16,12},{20,16},{24,20},{28,24},{32,28},{36,32}... | collective-permute-start | bytes 147464 | tf_op jit(solution)/shard_map/ppermute | solution.py:39
  16.3 10.6 %collective-permute-done.3 = bf16[64,384]{1,0:T(8,128)(2,1)S(1)} collective-permute-done((bf16[64,384]{1,0:T(8,128)(2,1)S(1)}, bf16[64,384]{1,0:T(8,128)(2,1)S(1)}, u32[]{:S(2)}, u32[]{:S(2)}) %collective-permute-start.3) | collective-permute-done | bytes 49184 | tf_op jit(solution)/shard_map/ppermute | solution.py:39
  27.1 2.1 %shard_map.55.refs_10_.refs_14_ = bf16[1536,1152]{1,0:T(8,128)(2,1)S(1)} custom-call(s32[1]{0:T(128)} %bitcast.ch_ref, bf16[3,3,1536,384]{3,2,1,0:T(8,128)(2,1)} %w_hbm.5), custom_call_target="tpu_custom_call" | custom-call | tf_op jit(solution)/shard_map/pallas_call | solution.py:131
  29.3 2.3 %collective-permute-done.4.refs_6_ = bf16[128,384]{1,0:T(8,128)(2,1)S(1)} collective-permute-done((bf16[128,384]{1,0:T(8,128)(2,1)S(1)}, bf16[128,384]{1,0:T(8,128)(2,1)S(1)}, u32[]{:S(2)}, u32[]{:S(2)}) %collective-permute-start.4) | collective-permute-done | bytes 98336 | tf_op jit(solution)/shard_map/ppermute | solution.py:43
  33.7 3.6 %shard_map.56 = (bf16[512,384]{1,0:T(8,128)(2,1)S(1)}, bf16[512,384]{1,0:T(8,128)(2,1)S(1)}) custom-call(bf16[576,384]{1,0:T(8,128)(2,1)S(1)} %fusion.1.refs_0_, bf16[576,384]{1,0:T(8,128)(2,1)S(1)} %collective-permute-done.refs_1_, bf16[576,384]{1,0:T(8,128)(2,1)S(1)} %collective-permute-done.1.refs_2_, ...), custom_call_target="tpu_custom_call" | custom-call | bytes 1024 | tf_op jit(solution)/shard_map/pallas_call | solution.py:119
  39.7 3.6 %shard_map.57 = (bf16[512,384]{1,0:T(8,128)(2,1)S(1)}, bf16[512,384]{1,0:T(8,128)(2,1)S(1)}) custom-call(bf16[576,384]{1,0:T(8,128)(2,1)S(1)} %fusion.1.refs_0_, bf16[576,384]{1,0:T(8,128)(2,1)S(1)} %collective-permute-done.refs_1_, bf16[576,384]{1,0:T(8,128)(2,1)S(1)} %collective-permute-done.1.refs_2_, ...), custom_call_target="tpu_custom_call" | custom-call | bytes 1024 | tf_op jit(solution)/shard_map/pallas_call | solution.py:119
  47.3 2.0 %collective-permute-done.14.refs_2_ = bf16[512,384]{1,0:T(8,128)(2,1)S(1)} collective-permute-done((bf16[512,384]{1,0:T(8,128)(2,1)S(1)}, bf16[512,384]{1,0:T(8,128)(2,1)S(1)}, u32[]{:S(2)}, u32[]{:S(2)}) %collective-permute-start.14) | collective-permute-done | bytes 393248 | tf_op jit(solution)/shard_map/ppermute | solution.py:43
  51.2 2.2 %shard_map.59 = (bf16[512,384]{1,0:T(8,128)(2,1)S(1)}, bf16[512,384]{1,0:T(8,128)(2,1)S(1)}, bf16[512,384]{1,0:T(8,128)(2,1)S(1)}) custom-call(bf16[512,384]{1,0:T(8,128)(2,1)S(1)} %get-tuple-element.54.refs_0_, bf16[512,384]{1,0:T(8,128)(2,1)S(1)} %collective-permute-done.13.refs_1_, bf16[512,384]{1,0:T(8,128)(2,1)S(1)} %collective-permute-done.14.refs_2_, ...), custom_call_target="tpu_custom_call" | custom-call | bytes 1024 | tf_op jit(solution)/shard_map/pallas_call | solution.py:119
  53.4 3.6 %collective-permute-done.12.refs_2_ = bf16[512,384]{1,0:T(8,128)(2,1)S(1)} collective-permute-done((bf16[512,384]{1,0:T(8,128)(2,1)S(1)}, bf16[512,384]{1,0:T(8,128)(2,1)S(1)}, u32[]{:S(2)}, u32[]{:S(2)}) %collective-permute-start.12) | collective-permute-done | bytes 393248 | tf_op jit(solution)/shard_map/ppermute | solution.py:43
  60.8 2.2 %shard_map.60 = (bf16[512,384]{1,0:T(8,128)(2,1)S(1)}, bf16[512,384]{1,0:T(8,128)(2,1)S(1)}, bf16[512,384]{1,0:T(8,128)(2,1)S(1)}) custom-call(bf16[512,384]{1,0:T(8,128)(2,1)S(1)} %get-tuple-element.53.refs_0_, bf16[512,384]{1,0:T(8,128)(2,1)S(1)} %collective-permute-done.11.refs_1_, bf16[512,384]{1,0:T(8,128)(2,1)S(1)} %collective-permute-done.12.refs_2_, ...), custom_call_target="tpu_custom_call" | custom-call | bytes 1024 | tf_op jit(solution)/shard_map/pallas_call | solution.py:119
  63.0 6.3 %collective-permute-start.20 = (bf16[512,384]{1,0:T(8,128)(2,1)S(1)}, bf16[512,384]{1,0:T(8,128)(2,1)S(1)}, u32[]{:S(2)}, u32[]{:S(2)}) collective-permute-start(bf16[512,384]{1,0:T(8,128)(2,1)S(1)} %get-tuple-element.67), channel_id=1, source_target_pairs={{4,0},{8,4},{12,8},{16,12},{20,16},{24,20},{28,24},{32,28},{36,32}... | collective-permute-start | bytes 1179656 | tf_op jit(solution)/shard_map/ppermute | solution.py:39
  69.3 2.4 %collective-permute-done.19.t1 = bf16[512,384]{1,0:T(8,128)(2,1)S(1)} collective-permute-done((bf16[512,384]{1,0:T(8,128)(2,1)S(1)}, bf16[512,384]{1,0:T(8,128)(2,1)S(1)}, u32[]{:S(2)}, u32[]{:S(2)}) %collective-permute-start.19) | collective-permute-done | bytes 393248 | tf_op jit(solution)/shard_map/ppermute | solution.py:39
  75.5 4.6 %collective-permute-done.20.t2 = bf16[512,384]{1,0:T(8,128)(2,1)S(1)} collective-permute-done((bf16[512,384]{1,0:T(8,128)(2,1)S(1)}, bf16[512,384]{1,0:T(8,128)(2,1)S(1)}, u32[]{:S(2)}, u32[]{:S(2)}) %collective-permute-start.20) | collective-permute-done | bytes 393248 | tf_op jit(solution)/shard_map/ppermute | solution.py:39
  81.8 6.9 %collective-permute-done.23.refs_2_ = bf16[512,384]{1,0:T(8,128)(2,1)S(1)} collective-permute-done((bf16[512,384]{1,0:T(8,128)(2,1)S(1)}, bf16[512,384]{1,0:T(8,128)(2,1)S(1)}, u32[]{:S(2)}, u32[]{:S(2)}) %collective-permute-start.23) | collective-permute-done | bytes 393248 | tf_op jit(solution)/shard_map/ppermute | solution.py:43
  90.5 2.2 %shard_map.64 = (bf16[512,384]{1,0:T(8,128)(2,1)S(1)}, bf16[512,384]{1,0:T(8,128)(2,1)S(1)}, bf16[512,384]{1,0:T(8,128)(2,1)S(1)}) custom-call(bf16[512,384]{1,0:T(8,128)(2,1)S(1)} %get-tuple-element.72.refs_0_, bf16[512,384]{1,0:T(8,128)(2,1)S(1)} %collective-permute-done.22.refs_1_, bf16[512,384]{1,0:T(8,128)(2,1)S(1)} %collective-permute-done.23.refs_2_, ...), custom_call_target="tpu_custom_call" | custom-call | bytes 1024 | tf_op jit(solution)/shard_map/pallas_call | solution.py:119
  92.7 4.3 %collective-permute-done.21.refs_2_ = bf16[512,384]{1,0:T(8,128)(2,1)S(1)} collective-permute-done((bf16[512,384]{1,0:T(8,128)(2,1)S(1)}, bf16[512,384]{1,0:T(8,128)(2,1)S(1)}, u32[]{:S(2)}, u32[]{:S(2)}) %collective-permute-start.21) | collective-permute-done | bytes 393248 | tf_op jit(solution)/shard_map/ppermute | solution.py:43
  97.6 7.3 %collective-permute-start.26 = (bf16[512,384]{1,0:T(8,128)(2,1)S(1)}, bf16[512,384]{1,0:T(8,128)(2,1)S(1)}, u32[]{:S(2)}, u32[]{:S(2)}) collective-permute-start(bf16[512,384]{1,0:T(8,128)(2,1)S(1)} %get-tuple-element.77), channel_id=1, source_target_pairs={{0,16},{4,20},{8,24},{12,28},{16,32},{20,36},{24,40},{28,44},{32,4... | collective-permute-start | bytes 1179656 | tf_op jit(solution)/shard_map/ppermute | solution.py:39
  106.3 2.2 %shard_map.65 = (bf16[512,384]{1,0:T(8,128)(2,1)S(1)}, bf16[512,384]{1,0:T(8,128)(2,1)S(1)}, bf16[512,384]{1,0:T(8,128)(2,1)S(1)}) custom-call(bf16[512,384]{1,0:T(8,128)(2,1)S(1)} %get-tuple-element.80.refs_0_, bf16[512,384]{1,0:T(8,128)(2,1)S(1)} %collective-permute-done.28.refs_1_, bf16[512,384]{1,0:T(8,128)(2,1)S(1)} %collective-permute-done.21.refs_2_, ...), custom_call_target="tpu_custom_call" | custom-call | bytes 1024 | tf_op jit(solution)/shard_map/pallas_call | solution.py:119
  108.5 5.5 %collective-permute-start.31 = (bf16[512,384]{1,0:T(8,128)(2,1)S(1)}, bf16[512,384]{1,0:T(8,128)(2,1)S(1)}, u32[]{:S(2)}, u32[]{:S(2)}) collective-permute-start(bf16[512,384]{1,0:T(8,128)(2,1)S(1)} %get-tuple-element.83), channel_id=1, source_target_pairs={{0,16},{4,20},{8,24},{12,28},{16,32},{20,36},{24,40},{28,44},{32,4... | collective-permute-start | bytes 1179656 | tf_op jit(solution)/shard_map/ppermute | solution.py:39
  115.3 12.2 %collective-permute-done.26.up_lo = bf16[512,384]{1,0:T(8,128)(2,1)S(1)} collective-permute-done((bf16[512,384]{1,0:T(8,128)(2,1)S(1)}, bf16[512,384]{1,0:T(8,128)(2,1)S(1)}, u32[]{:S(2)}, u32[]{:S(2)}) %collective-permute-start.26) | collective-permute-done | bytes 393248 | tf_op jit(solution)/shard_map/ppermute | solution.py:39
  127.5 9.3 %collective-permute-done.31.up_hi = bf16[512,384]{1,0:T(8,128)(2,1)S(1)} collective-permute-done((bf16[512,384]{1,0:T(8,128)(2,1)S(1)}, bf16[512,384]{1,0:T(8,128)(2,1)S(1)}, u32[]{:S(2)}, u32[]{:S(2)}) %collective-permute-start.31) | collective-permute-done | bytes 393248 | tf_op jit(solution)/shard_map/ppermute | solution.py:39
  136.8 7.2 %collective-permute-done.32.down_hi = bf16[512,384]{1,0:T(8,128)(2,1)S(1)} collective-permute-done((bf16[512,384]{1,0:T(8,128)(2,1)S(1)}, bf16[512,384]{1,0:T(8,128)(2,1)S(1)}, u32[]{:S(2)}, u32[]{:S(2)}) %collective-permute-start.32) | collective-permute-done | bytes 393248 | tf_op jit(solution)/shard_map/ppermute | solution.py:39
  (72 shorter events, 31.2 us)
Async XLA Ops:
  3.0 28.7 %collective-permute-start.1 = (bf16[576,384]{1,0:T(8,128)(2,1)S(1)}, bf16[576,384]{1,0:T(8,128)(2,1)S(1)}, u32[]{:S(2)}, u32[]{:S(2)}) collective-permute-start(bf16[576,384]{1,0:T(8,128)(2,1)S(1)} %fusion.1.refs_0_), channel_id=1, source_target_pairs={{0,2},{1,3},{2,0},{3,1},{4,6},{5,7},{6,4},{7,5},{8,10},{9,11},{10,... | collective-permute-start | bytes 1327112 | tf_op jit(solution)/shard_map/ppermute | solution.py:43
  4.6 11.6 %collective-permute-start.2 = (bf16[64,384]{1,0:T(8,128)(2,1)S(1)}, bf16[64,384]{1,0:T(8,128)(2,1)S(1)}, u32[]{:S(2)}, u32[]{:S(2)}) collective-permute-start(bf16[64,384]{1,0:T(8,128)(2,1)S(1)} %slice.86), channel_id=1, source_target_pairs={{0,4},{4,8},{8,12},{12,16},{16,20},{20,24},{24,28},{28,32},{32,36}... | collective-permute-start | bytes 147464 | tf_op jit(solution)/shard_map/ppermute | solution.py:39
  11.3 20.4 %collective-permute-start.5 = (bf16[448,384]{1,0:T(8,128)(2,1)S(1)}, bf16[448,384]{1,0:T(8,128)(2,1)S(1)}, u32[]{:S(2)}, u32[]{:S(2)}) collective-permute-start(bf16[448,384]{1,0:T(8,128)(2,1)S(1)} %fusion.4.refs_8_), channel_id=1, source_target_pairs={{0,2},{1,3},{2,0},{3,1},{4,6},{5,7},{6,4},{7,5},{8,10},{9,11},{10,... | collective-permute-start | bytes 1032200 | tf_op jit(solution)/shard_map/ppermute | solution.py:43
  11.5 15.4 %collective-permute-start.3 = (bf16[64,384]{1,0:T(8,128)(2,1)S(1)}, bf16[64,384]{1,0:T(8,128)(2,1)S(1)}, u32[]{:S(2)}, u32[]{:S(2)}) collective-permute-start(bf16[64,384]{1,0:T(8,128)(2,1)S(1)} %slice.87), channel_id=1, source_target_pairs={{4,0},{8,4},{12,8},{16,12},{20,16},{24,20},{28,24},{32,28},{36,32}... | collective-permute-start | bytes 147464 | tf_op jit(solution)/shard_map/ppermute | solution.py:39
  26.9 4.7 %collective-permute-start.4 = (bf16[128,384]{1,0:T(8,128)(2,1)S(1)}, bf16[128,384]{1,0:T(8,128)(2,1)S(1)}, u32[]{:S(2)}, u32[]{:S(2)}) collective-permute-start(bf16[128,384]{1,0:T(8,128)(2,1)S(1)} %constant_dynamic-update-slice_fusion.refs_4_), channel_id=1, source_target_pairs={{0,2},{1,3},{2,0},{3,1},{4,6},{5,7},{6,4},{7,5},{8,10},{9,11},{10,... | collective-permute-start | bytes 294920 | tf_op jit(solution)/shard_map/ppermute | solution.py:43
  27.1 6.4 %collective-permute-start = (bf16[576,384]{1,0:T(8,128)(2,1)S(1)}, bf16[576,384]{1,0:T(8,128)(2,1)S(1)}, u32[]{:S(2)}, u32[]{:S(2)}) collective-permute-start(bf16[576,384]{1,0:T(8,128)(2,1)S(1)} %fusion.1.refs_0_), channel_id=1, source_target_pairs={{0,1},{1,0},{2,3},{3,2},{4,5},{5,4},{6,7},{7,6},{8,9},{9,8},{10,11... | collective-permute-start | bytes 1327112 | tf_op jit(solution)/shard_map/ppermute | solution.py:47
  31.6 2.1 %collective-permute-start.6 = (bf16[576,384]{1,0:T(8,128)(2,1)S(1)}, bf16[576,384]{1,0:T(8,128)(2,1)S(1)}, u32[]{:S(2)}, u32[]{:S(2)}) collective-permute-start(bf16[576,384]{1,0:T(8,128)(2,1)S(1)} %collective-permute-done.1.refs_2_), channel_id=1, source_target_pairs={{0,1},{1,0},{2,3},{3,2},{4,5},{5,4},{6,7},{7,6},{8,9},{9,8},{10,11... | collective-permute-start | bytes 1327112 | tf_op jit(solution)/shard_map/ppermute | solution.py:47
  37.3 12.0 %collective-permute-start.14 = (bf16[512,384]{1,0:T(8,128)(2,1)S(1)}, bf16[512,384]{1,0:T(8,128)(2,1)S(1)}, u32[]{:S(2)}, u32[]{:S(2)}) collective-permute-start(bf16[512,384]{1,0:T(8,128)(2,1)S(1)} %get-tuple-element.54.refs_0_), channel_id=1, source_target_pairs={{0,2},{1,3},{2,0},{3,1},{4,6},{5,7},{6,4},{7,5},{8,10},{9,11},{10,... | collective-permute-start | bytes 1179656 | tf_op jit(solution)/shard_map/ppermute | solution.py:43
  37.6 2.0 %collective-permute-start.10 = (bf16[448,384]{1,0:T(8,128)(2,1)S(1)}, bf16[448,384]{1,0:T(8,128)(2,1)S(1)}, u32[]{:S(2)}, u32[]{:S(2)}) collective-permute-start(bf16[448,384]{1,0:T(8,128)(2,1)S(1)} %collective-permute-done.5.refs_10_), channel_id=1, source_target_pairs={{0,1},{1,0},{2,3},{3,2},{4,5},{5,4},{6,7},{7,6},{8,9},{9,8},{10,11... | collective-permute-start | bytes 1032200 | tf_op jit(solution)/shard_map/ppermute | solution.py:47
  38.0 12.1 %collective-permute-start.13 = (bf16[512,384]{1,0:T(8,128)(2,1)S(1)}, bf16[512,384]{1,0:T(8,128)(2,1)S(1)}, u32[]{:S(2)}, u32[]{:S(2)}) collective-permute-start(bf16[512,384]{1,0:T(8,128)(2,1)S(1)} %get-tuple-element.54.refs_0_), channel_id=1, source_target_pairs={{0,1},{1,0},{2,3},{3,2},{4,5},{5,4},{6,7},{7,6},{8,9},{9,8},{10,11... | collective-permute-start | bytes 1179656 | tf_op jit(solution)/shard_map/ppermute | solution.py:47
  43.3 13.7 %collective-permute-start.12 = (bf16[512,384]{1,0:T(8,128)(2,1)S(1)}, bf16[512,384]{1,0:T(8,128)(2,1)S(1)}, u32[]{:S(2)}, u32[]{:S(2)}) collective-permute-start(bf16[512,384]{1,0:T(8,128)(2,1)S(1)} %get-tuple-element.53.refs_0_), channel_id=1, source_target_pairs={{0,2},{1,3},{2,0},{3,1},{4,6},{5,7},{6,4},{7,5},{8,10},{9,11},{10,... | collective-permute-start | bytes 1179656 | tf_op jit(solution)/shard_map/ppermute | solution.py:43
  50.0 9.6 %collective-permute-start.11 = (bf16[512,384]{1,0:T(8,128)(2,1)S(1)}, bf16[512,384]{1,0:T(8,128)(2,1)S(1)}, u32[]{:S(2)}, u32[]{:S(2)}) collective-permute-start(bf16[512,384]{1,0:T(8,128)(2,1)S(1)} %get-tuple-element.53.refs_0_), channel_id=1, source_target_pairs={{0,1},{1,0},{2,3},{3,2},{4,5},{5,4},{6,7},{7,6},{8,9},{9,8},{10,11... | collective-permute-start | bytes 1179656 | tf_op jit(solution)/shard_map/ppermute | solution.py:47
  57.0 14.7 %collective-permute-start.19 = (bf16[512,384]{1,0:T(8,128)(2,1)S(1)}, bf16[512,384]{1,0:T(8,128)(2,1)S(1)}, u32[]{:S(2)}, u32[]{:S(2)}) collective-permute-start(bf16[512,384]{1,0:T(8,128)(2,1)S(1)} %get-tuple-element.61), channel_id=1, source_target_pairs={{0,4},{4,8},{8,12},{12,16},{16,20},{20,24},{24,28},{28,32},{32,36}... | collective-permute-start | bytes 1179656 | tf_op jit(solution)/shard_map/ppermute | solution.py:39
  63.0 17.1 %collective-permute-start.20 = (bf16[512,384]{1,0:T(8,128)(2,1)S(1)}, bf16[512,384]{1,0:T(8,128)(2,1)S(1)}, u32[]{:S(2)}, u32[]{:S(2)}) collective-permute-start(bf16[512,384]{1,0:T(8,128)(2,1)S(1)} %get-tuple-element.67), channel_id=1, source_target_pairs={{4,0},{8,4},{12,8},{16,12},{20,16},{24,20},{28,24},{32,28},{36,32}... | collective-permute-start | bytes 1179656 | tf_op jit(solution)/shard_map/ppermute | solution.py:39
  72.9 15.8 %collective-permute-start.23 = (bf16[512,384]{1,0:T(8,128)(2,1)S(1)}, bf16[512,384]{1,0:T(8,128)(2,1)S(1)}, u32[]{:S(2)}, u32[]{:S(2)}) collective-permute-start(bf16[512,384]{1,0:T(8,128)(2,1)S(1)} %get-tuple-element.72.refs_0_), channel_id=1, source_target_pairs={{0,2},{1,3},{2,0},{3,1},{4,6},{5,7},{6,4},{7,5},{8,10},{9,11},{10,... | collective-permute-start | bytes 1179656 | tf_op jit(solution)/shard_map/ppermute | solution.py:43
  73.4 16.0 %collective-permute-start.22 = (bf16[512,384]{1,0:T(8,128)(2,1)S(1)}, bf16[512,384]{1,0:T(8,128)(2,1)S(1)}, u32[]{:S(2)}, u32[]{:S(2)}) collective-permute-start(bf16[512,384]{1,0:T(8,128)(2,1)S(1)} %get-tuple-element.72.refs_0_), channel_id=1, source_target_pairs={{0,1},{1,0},{2,3},{3,2},{4,5},{5,4},{6,7},{7,6},{8,9},{9,8},{10,11... | collective-permute-start | bytes 1179656 | tf_op jit(solution)/shard_map/ppermute | solution.py:47
  81.2 15.8 %collective-permute-start.21 = (bf16[512,384]{1,0:T(8,128)(2,1)S(1)}, bf16[512,384]{1,0:T(8,128)(2,1)S(1)}, u32[]{:S(2)}, u32[]{:S(2)}) collective-permute-start(bf16[512,384]{1,0:T(8,128)(2,1)S(1)} %get-tuple-element.80.refs_0_), channel_id=1, source_target_pairs={{0,2},{1,3},{2,0},{3,1},{4,6},{5,7},{6,4},{7,5},{8,10},{9,11},{10,... | collective-permute-start | bytes 1179656 | tf_op jit(solution)/shard_map/ppermute | solution.py:43
  89.3 17.0 %collective-permute-start.28 = (bf16[512,384]{1,0:T(8,128)(2,1)S(1)}, bf16[512,384]{1,0:T(8,128)(2,1)S(1)}, u32[]{:S(2)}, u32[]{:S(2)}) collective-permute-start(bf16[512,384]{1,0:T(8,128)(2,1)S(1)} %get-tuple-element.80.refs_0_), channel_id=1, source_target_pairs={{0,1},{1,0},{2,3},{3,2},{4,5},{5,4},{6,7},{7,6},{8,9},{9,8},{10,11... | collective-permute-start | bytes 1179656 | tf_op jit(solution)/shard_map/ppermute | solution.py:47
  97.0 9.2 %collective-permute-start.29 = (bf16[256,384]{1,0:T(8,128)(2,1)S(1)}, bf16[256,384]{1,0:T(8,128)(2,1)S(1)}, u32[]{:S(2)}, u32[]{:S(2)}) collective-permute-start(bf16[256,384]{1,0:T(8,128)(2,1)S(1)} %get-tuple-element.86), channel_id=1, source_target_pairs={{0,1},{1,0},{2,3},{3,2},{4,5},{5,4},{6,7},{7,6},{8,9},{9,8},{10,11... | collective-permute-start | bytes 589832 | tf_op jit(solution)/shard_map/ppermute | solution.py:47
  97.2 9.1 %collective-permute-start.30 = (bf16[256,384]{1,0:T(8,128)(2,1)S(1)}, bf16[256,384]{1,0:T(8,128)(2,1)S(1)}, u32[]{:S(2)}, u32[]{:S(2)}) collective-permute-start(bf16[256,384]{1,0:T(8,128)(2,1)S(1)} %get-tuple-element.85), channel_id=1, source_target_pairs={{0,1},{1,0},{2,3},{3,2},{4,5},{5,4},{6,7},{7,6},{8,9},{9,8},{10,11... | collective-permute-start | bytes 589832 | tf_op jit(solution)/shard_map/ppermute | solution.py:47
  97.6 29.9 %collective-permute-start.26 = (bf16[512,384]{1,0:T(8,128)(2,1)S(1)}, bf16[512,384]{1,0:T(8,128)(2,1)S(1)}, u32[]{:S(2)}, u32[]{:S(2)}) collective-permute-start(bf16[512,384]{1,0:T(8,128)(2,1)S(1)} %get-tuple-element.77), channel_id=1, source_target_pairs={{0,16},{4,20},{8,24},{12,28},{16,32},{20,36},{24,40},{28,44},{32,4... | collective-permute-start | bytes 1179656 | tf_op jit(solution)/shard_map/ppermute | solution.py:39
  105.0 22.5 %collective-permute-start.27 = (bf16[512,384]{1,0:T(8,128)(2,1)S(1)}, bf16[512,384]{1,0:T(8,128)(2,1)S(1)}, u32[]{:S(2)}, u32[]{:S(2)}) collective-permute-start(bf16[512,384]{1,0:T(8,128)(2,1)S(1)} %get-tuple-element.78), channel_id=1, source_target_pairs={{16,0},{20,4},{24,8},{28,12},{32,16},{36,20},{40,24},{44,28},{48,3... | collective-permute-start | bytes 1179656 | tf_op jit(solution)/shard_map/ppermute | solution.py:39
  108.5 28.2 %collective-permute-start.31 = (bf16[512,384]{1,0:T(8,128)(2,1)S(1)}, bf16[512,384]{1,0:T(8,128)(2,1)S(1)}, u32[]{:S(2)}, u32[]{:S(2)}) collective-permute-start(bf16[512,384]{1,0:T(8,128)(2,1)S(1)} %get-tuple-element.83), channel_id=1, source_target_pairs={{0,16},{4,20},{8,24},{12,28},{16,32},{20,36},{24,40},{28,44},{32,4... | collective-permute-start | bytes 1179656 | tf_op jit(solution)/shard_map/ppermute | solution.py:39
  114.0 30.0 %collective-permute-start.32 = (bf16[512,384]{1,0:T(8,128)(2,1)S(1)}, bf16[512,384]{1,0:T(8,128)(2,1)S(1)}, u32[]{:S(2)}, u32[]{:S(2)}) collective-permute-start(bf16[512,384]{1,0:T(8,128)(2,1)S(1)} %get-tuple-element.84), channel_id=1, source_target_pairs={{16,0},{20,4},{24,8},{28,12},{32,16},{36,20},{40,24},{44,28},{48,3... | collective-permute-start | bytes 1179656 | tf_op jit(solution)/shard_map/ppermute | solution.py:39
  (11 other events, 25.8 us)

commit v6 on v5

--- a/solution.py
+++ b/solution.py
@@ -18,6 +18,7 @@
 W = 384
 R = 64
 FIRST = MID - R
+COST = 10**10
 VMEM = pl.BlockSpec(memory_space=pltpu.VMEM)
 SMEM = pl.BlockSpec(memory_space=pltpu.SMEM)
 HBM = pl.BlockSpec(memory_space=pltpu.HBM)
@@ -96,8 +97,7 @@
 
 def product_kernel(*refs):
     pieces, (w_ref, o0, o1, o2) = refs[:-4], refs[-4:]
-    near_far = jnp.concatenate([p[...] for p in pieces[3:]], axis=0)
-    full = dot(jnp.concatenate([p[...] for p in pieces[:3]] + [near_far], axis=1), w_ref[...])
+    full = dot(joined(pieces), w_ref[...])
     for k, o in enumerate((o0, o1, o2)):
         o[...] = full[:, k * W : (k + 1) * W].astype(BF16)
 
@@ -107,23 +107,41 @@
     finish(f(s0) + f(t0) + f(t1) + f(t2), vec_ref, s_ref, a_ref)
 
 
-def out_kernel(s_lo, q_lo, up_lo, down_lo, s_hi, q_hi, up_hi, down_hi, vec_ref, o_ref):
-    for to, refs in ((0, (s_lo, q_lo, up_lo, down_lo)), (MID, (s_hi, q_hi, up_hi, down_hi))):
-        total = vec_ref[0:1, :]
-        for ref in refs:
-            total = total + ref[...].astype(F32)
-        o_ref[to : to + MID, :] = total.astype(BF16)
-
-
-def call(kernel, args, rows, scratch=()):
+def joined(refs, fars=1):
+    far = jnp.concatenate([p[...] for p in refs[2 : 2 + fars]], axis=0)
+    near_far = jnp.concatenate([p[...] for p in refs[2 + fars :]], axis=0)
+    return jnp.concatenate([refs[0][...], refs[1][...], far, near_far], axis=1)
+
+
+def part_kernel(*refs):
+    own, low, (s_ref, vec_ref, w_ref, o_ref) = refs[:4], refs[4:8], refs[8:]
+    total = s_ref[...].astype(F32) + vec_ref[0:1, :]
+    total = total + dot(joined(own, 1), w_ref[:, W : 2 * W])
+    o_ref[...] = total + dot(joined(low, 1), w_ref[:, 0:W])
+
+
+def upper_kernel(s_hi, q_hi, up_hi, down_hi, vec_ref, o_ref):
+    total = vec_ref[0:1, :]
+    for ref in (s_hi, q_hi, up_hi, down_hi):
+        total = total + ref[...].astype(F32)
+    o_ref[...] = total.astype(BF16)
+
+
+def out_kernel(*refs):
+    high, (part, upper, w_ref, o_ref) = refs[:4], refs[4:]
+    o_ref[:MID, :] = (part[...] + dot(joined(high), w_ref[:, 2 * W : 3 * W])).astype(BF16)
+    o_ref[MID:, :] = upper[...]
+
+
+def call(kernel, args, rows, scratch=(), dtype=BF16, flops=0):
     return pl.pallas_call(
         kernel,
-        out_shape=[jax.ShapeDtypeStruct((r, W), BF16) for r in rows],
+        out_shape=[jax.ShapeDtypeStruct((r, W), dtype) for r in rows],
         in_specs=[VMEM] * len(args),
         out_specs=[VMEM] * len(rows),
         scratch_shapes=list(scratch),
         compiler_params=pltpu.CompilerParams(vmem_limit_bytes=20 * 1024 * 1024),
-        cost_estimate=pl.CostEstimate(flops=0, bytes_accessed=1024, transcendentals=0),
+        cost_estimate=pl.CostEstimate(flops=flops, bytes_accessed=1024, transcendentals=0),
     )(*args)
 
 
@@ -157,6 +175,7 @@
     act_3 = entry(bins_in[:FIRST])
     low = shifted(act_1[-R:], 1)
     high = shifted(act_3[:R], -1)
+    low, act_3 = after((low, act_3))
     w0 = staged(0, ch, conv_weight)
     act_2 = jnp.concatenate([low, high], axis=0)
     far_2 = chip_swap(act_2)
@@ -190,24 +209,35 @@
     u0, u1, u2 = call(product_kernel, (a_lo, near_lo, far_lo, *core_swaps(far_lo, 2), w1), halves)
     down = shifted(u2, -hop1)
     s_lo, a_lo = call(join_kernel, (s_lo, u1, up, t2, vec1), halves[:2])
-    far_lo = chip_swap(a_lo)
-    near_lo = core_swap(a_lo)
+    from_low = shifted(a_lo, hop2)
+    from_high = shifted(a_lo, -hop2)
     ch, a_lo = after((ch, a_lo))
     w2 = staged(2, ch, conv_weight)
-    down, w2 = after((down, w2))
     s_hi, a_hi = call(join_kernel, (s_hi, t1, u0, down, vec1), halves[:2])
     far_hi = chip_swap(a_hi)
     near_hi = core_swap(a_hi)
-
-    def last(own, near, far, parts):
-        q0, q1, q2 = call(product_kernel, (own, near, far, *core_swaps(far, parts), w2), halves)
-        return q1, shifted(q0, hop2), shifted(q2, -hop2)
-
-    far_lo, a_hi = after((far_lo, a_hi))
-    q_lo, up_lo, down_lo = last(a_lo, near_lo, far_lo, 2)
-    far_hi, q_lo = after((far_hi, q_lo))
-    q_hi, up_hi, down_hi = last(a_hi, near_hi, far_hi, 2)
-    (out,) = call(out_kernel, (s_lo, q_lo, up_lo, down_lo, s_hi, q_hi, up_hi, down_hi, vec2), [ROWS])
+    far_hi, from_low, from_high, w2 = after((far_hi, from_low, from_high, w2))
+    a_lo, a_hi = after((a_lo, a_hi))
+
+    far_own = chip_swap(a_lo)
+    near_own = core_swap(a_lo)
+    near_low = core_swap(from_low)
+    near_high = core_swap(from_high)
+    g_hi = [a_hi, near_hi, far_hi, *core_swaps(far_hi, 2)]
+    *g_hi, far_own, near_own, near_low, near_high = after((*g_hi, far_own, near_own, near_low, near_high))
+    q0, q_hi, q2 = call(product_kernel, (*g_hi, w2), halves)
+    up_hi = shifted(q0, hop2)
+    down_hi = shifted(q2, -hop2)
+    from_low, from_high, far_own, q_hi = after((from_low, from_high, far_own, q_hi))
+    far_low = chip_swap(from_low)
+    far_high = chip_swap(from_high)
+    g_own = (a_lo, near_own, far_own, core_swap(far_own))
+    g_low = (from_low, near_low, far_low, core_swap(far_low))
+    g_high = (from_high, near_high, far_high, core_swap(far_high))
+    (part,) = call(part_kernel, (*g_own, *g_low, s_lo, vec2, w2), halves[:1], dtype=F32)
+    up_hi, down_hi, part = after((up_hi, down_hi, part))
+    (upper,) = call(upper_kernel, (s_hi, q_hi, up_hi, down_hi, vec2), halves[:1], flops=COST)
+    (out,) = call(out_kernel, (*g_high, part, upper, w2), [ROWS])
     return out
 
 

time: 146 us -> 155 us (1.062)
  the two profiles are of different devices: /device:TPU:32 before, /device:TPU:6 now
where the time goes in v6:
time: 155 us; the launch traced here: 152 us
  waiting for transfers between devices  63 us (41%)
  starting transfers between devices  56.9 us (37%)
  Pallas kernels  26.3 us (17%)
  other arithmetic  3.93 us (3%)
    ppermute x8, starting transfers between devices, shifted(): return lax.ppermute(array, 'seq', pairs)  44.2 us
    ppermute x8, waiting for transfers between devices, shifted(): return lax.ppermute(array, 'seq', pairs)  36.8 us
    ppermute x9, waiting for transfers between devices, chip_swap(): return lax.ppermute(array, 'ch', [(i, i ^ 2) for i in range(4)])  20.9 us
    pallas_call x10, Pallas kernels, call(): pl.pallas_call(kernel, out_shape=[jax.ShapeDtypeStruct((r, W), dtype) for...  20.1 us
    ppermute x9, starting transfers between devices, chip_swap(): return lax.ppermute(array, 'ch', [(i, i ^ 2) for i in range(4)])  9.09 us
    pallas_call x3, Pallas kernels, staged(): pl.pallas_call(functools.partial(stage_kernel, layer), out_shape=jax.Shap...  6.2 us
    ppermute x21, waiting for transfers between devices, core_swap(): return lax.ppermute(array, 'ch', [(i, i ^ 1) for i in range(4)])  5.33 us
    convert_element_type x2, other arithmetic, entry(): return gelu(x.astype(F32) * pre_scale[0] + pre_shift[0]).astype(BF16)  3.91 us
  transfers between devices with their start and end apart: 38, of which 20 were waited for; matrix products, arithmetic and copies ran while one was open for 1% of the time, Pallas kernels for 12%

profile of v6, /device:TPU:6, one launch (start us, length us, event | category | flops | bytes accessed | tf_op | source)
XLA Modules:
  0.0 151.5 jit_solution(1761381166547099659)
XLA Ops:
  0.9 2.1 %fusion.1.refs_0_ = bf16[576,384]{1,0:T(8,128)(2,1)S(1)} fusion(f32[384]{0:T(512)S(1)} %get-tuple-element.131, f32[384]{0:T(512)S(1)} %get-tuple-element.125, bf16[1024,384]{1,0:T(8,128)(2,1)} %refs_12_.1), kind=kLoop, calls=%fused_computation.3 | loop fusion | flops 7741440 | bytes 887808 | tf_op jit(solution)/shard_map/convert_element_type | solution.py:170
  4.6 4.8 %collective-permute-start.2 = (bf16[64,384]{1,0:T(8,128)(2,1)S(1)}, bf16[64,384]{1,0:T(8,128)(2,1)S(1)}, u32[]{:S(2)}, u32[]{:S(2)}) collective-permute-start(bf16[64,384]{1,0:T(8,128)(2,1)S(1)} %slice.78), channel_id=1, source_target_pairs={{0,4},{4,8},{8,12},{12,16},{16,20},{20,24},{24,28},{28,32},{32,36}... | collective-permute-start | bytes 147464 | tf_op jit(solution)/shard_map/ppermute | solution.py:40
  11.3 5.9 %collective-permute-done.2 = bf16[64,384]{1,0:T(8,128)(2,1)S(1)} collective-permute-done((bf16[64,384]{1,0:T(8,128)(2,1)S(1)}, bf16[64,384]{1,0:T(8,128)(2,1)S(1)}, u32[]{:S(2)}, u32[]{:S(2)}) %collective-permute-start.2) | collective-permute-done | bytes 49184 | tf_op jit(solution)/shard_map/ppermute | solution.py:40
  17.3 10.3 %collective-permute-start.3 = (bf16[64,384]{1,0:T(8,128)(2,1)S(1)}, bf16[64,384]{1,0:T(8,128)(2,1)S(1)}, u32[]{:S(2)}, u32[]{:S(2)}) collective-permute-start(bf16[64,384]{1,0:T(8,128)(2,1)S(1)} %slice.79), channel_id=1, source_target_pairs={{4,0},{8,4},{12,8},{16,12},{20,16},{24,20},{28,24},{32,28},{36,32}... | collective-permute-start | bytes 147464 | tf_op jit(solution)/shard_map/ppermute | solution.py:40
  30.2 2.1 %shard_map.55.refs_10_.refs_14_ = bf16[1536,1152]{1,0:T(8,128)(2,1)S(1)} custom-call(s32[1]{0:T(128)} %bitcast.ch_ref, bf16[3,3,1536,384]{3,2,1,0:T(8,128)(2,1)} %w_hbm.5), custom_call_target="tpu_custom_call" | custom-call | tf_op jit(solution)/shard_map/pallas_call | solution.py:149
  36.2 3.6 %shard_map.56 = (bf16[512,384]{1,0:T(8,128)(2,1)S(1)}, bf16[512,384]{1,0:T(8,128)(2,1)S(1)}) custom-call(bf16[576,384]{1,0:T(8,128)(2,1)S(1)} %fusion.1.refs_0_, bf16[576,384]{1,0:T(8,128)(2,1)S(1)} %collective-permute-done.refs_1_, bf16[576,384]{1,0:T(8,128)(2,1)S(1)} %collective-permute-done.1.refs_2_, ...), custom_call_target="tpu_custom_call" | custom-call | bytes 1024 | tf_op jit(solution)/shard_map/pallas_call | solution.py:137
  42.8 3.6 %shard_map.57 = (bf16[512,384]{1,0:T(8,128)(2,1)S(1)}, bf16[512,384]{1,0:T(8,128)(2,1)S(1)}) custom-call(bf16[576,384]{1,0:T(8,128)(2,1)S(1)} %fusion.1.refs_0_, bf16[576,384]{1,0:T(8,128)(2,1)S(1)} %collective-permute-done.refs_1_, bf16[576,384]{1,0:T(8,128)(2,1)S(1)} %collective-permute-done.1.refs_2_, ...), custom_call_target="tpu_custom_call" | custom-call | bytes 1024 | tf_op jit(solution)/shard_map/pallas_call | solution.py:137
  47.7 2.0 %shard_map.58.refs_5_ = bf16[1536,1152]{1,0:T(8,128)(2,1)S(1)} custom-call(s32[1]{0:T(128)} %bitcast.ch_ref, bf16[3,3,1536,384]{3,2,1,0:T(8,128)(2,1)} %w_hbm.5), custom_call_target="tpu_custom_call" | custom-call | tf_op jit(solution)/shard_map/pallas_call | solution.py:149
  49.8 2.0 %collective-permute-done.13.refs_2_ = bf16[512,384]{1,0:T(8,128)(2,1)S(1)} collective-permute-done((bf16[512,384]{1,0:T(8,128)(2,1)S(1)}, bf16[512,384]{1,0:T(8,128)(2,1)S(1)}, u32[]{:S(2)}, u32[]{:S(2)}) %collective-permute-start.13) | collective-permute-done | bytes 393248 | tf_op jit(solution)/shard_map/ppermute | solution.py:44
  53.7 2.2 %shard_map.59 = (bf16[512,384]{1,0:T(8,128)(2,1)S(1)}, bf16[512,384]{1,0:T(8,128)(2,1)S(1)}, bf16[512,384]{1,0:T(8,128)(2,1)S(1)}) custom-call(bf16[512,384]{1,0:T(8,128)(2,1)S(1)} %get-tuple-element.70.refs_0_, bf16[512,384]{1,0:T(8,128)(2,1)S(1)} %collective-permute-done.12.refs_1_, bf16[512,384]{1,0:T(8,128)(2,1)S(1)} %collective-permute-done.13.refs_2_, ...), custom_call_target="tpu_custom_call" | custom-call | bytes 1024 | tf_op jit(solution)/shard_map/pallas_call | solution.py:137
  55.9 3.6 %collective-permute-done.11.refs_2_ = bf16[512,384]{1,0:T(8,128)(2,1)S(1)} collective-permute-done((bf16[512,384]{1,0:T(8,128)(2,1)S(1)}, bf16[512,384]{1,0:T(8,128)(2,1)S(1)}, u32[]{:S(2)}, u32[]{:S(2)}) %collective-permute-start.11) | collective-permute-done | bytes 393248 | tf_op jit(solution)/shard_map/ppermute | solution.py:44
  62.0 2.2 %shard_map.60 = (bf16[512,384]{1,0:T(8,128)(2,1)S(1)}, bf16[512,384]{1,0:T(8,128)(2,1)S(1)}, bf16[512,384]{1,0:T(8,128)(2,1)S(1)}) custom-call(bf16[512,384]{1,0:T(8,128)(2,1)S(1)} %get-tuple-element.76.refs_0_, bf16[512,384]{1,0:T(8,128)(2,1)S(1)} %collective-permute-done.16.refs_1_, bf16[512,384]{1,0:T(8,128)(2,1)S(1)} %collective-permute-done.11.refs_2_, ...), custom_call_target="tpu_custom_call" | custom-call | bytes 1024 | tf_op jit(solution)/shard_map/pallas_call | solution.py:137
  64.2 8.9 %collective-permute-start.19 = (bf16[512,384]{1,0:T(8,128)(2,1)S(1)}, bf16[512,384]{1,0:T(8,128)(2,1)S(1)}, u32[]{:S(2)}, u32[]{:S(2)}) collective-permute-start(bf16[512,384]{1,0:T(8,128)(2,1)S(1)} %get-tuple-element.79), channel_id=1, source_target_pairs={{4,0},{8,4},{12,8},{16,12},{20,16},{24,20},{28,24},{32,28},{36,32}... | collective-permute-start | bytes 1179656 | tf_op jit(solution)/shard_map/ppermute | solution.py:40
  73.1 6.2 %collective-permute-done.21.t1 = bf16[512,384]{1,0:T(8,128)(2,1)S(1)} collective-permute-done((bf16[512,384]{1,0:T(8,128)(2,1)S(1)}, bf16[512,384]{1,0:T(8,128)(2,1)S(1)}, u32[]{:S(2)}, u32[]{:S(2)}) %collective-permute-start.21) | collective-permute-done | bytes 393248 | tf_op jit(solution)/shard_map/ppermute | solution.py:40
  82.5 7.6 %collective-permute-start.23 = (bf16[512,384]{1,0:T(8,128)(2,1)S(1)}, bf16[512,384]{1,0:T(8,128)(2,1)S(1)}, u32[]{:S(2)}, u32[]{:S(2)}) collective-permute-start(bf16[512,384]{1,0:T(8,128)(2,1)S(1)} %get-tuple-element.92.refs_0_), channel_id=1, source_target_pairs={{16,0},{20,4},{24,8},{28,12},{32,16},{36,20},{40,24},{44,28},{48,3... | collective-permute-start | bytes 1179656 | tf_op jit(solution)/shard_map/ppermute | solution.py:40
  93.4 2.0 %shard_map.63.refs_5_.refs_10_.refs_6_ = bf16[1536,1152]{1,0:T(8,128)(2,1)S(1)} custom-call(s32[1]{0:T(128)} %bitcast.ch_ref, bf16[3,3,1536,384]{3,2,1,0:T(8,128)(2,1)} %w_hbm.5), custom_call_target="tpu_custom_call" | custom-call | tf_op jit(solution)/shard_map/pallas_call | solution.py:149
  95.4 4.6 %collective-permute-done.22.refs_4_ = bf16[512,384]{1,0:T(8,128)(2,1)S(1)} collective-permute-done((bf16[512,384]{1,0:T(8,128)(2,1)S(1)}, bf16[512,384]{1,0:T(8,128)(2,1)S(1)}, u32[]{:S(2)}, u32[]{:S(2)}) %collective-permute-start.22) | collective-permute-done | bytes 393248 | tf_op jit(solution)/shard_map/ppermute | solution.py:40
  100.1 4.1 %collective-permute-done.23.refs_0_ = bf16[512,384]{1,0:T(8,128)(2,1)S(1)} collective-permute-done((bf16[512,384]{1,0:T(8,128)(2,1)S(1)}, bf16[512,384]{1,0:T(8,128)(2,1)S(1)}, u32[]{:S(2)}, u32[]{:S(2)}) %collective-permute-start.23) | collective-permute-done | bytes 393248 | tf_op jit(solution)/shard_map/ppermute | solution.py:40
  104.7 3.7 %collective-permute-done.27.refs_2_ = bf16[512,384]{1,0:T(8,128)(2,1)S(1)} collective-permute-done((bf16[512,384]{1,0:T(8,128)(2,1)S(1)}, bf16[512,384]{1,0:T(8,128)(2,1)S(1)}, u32[]{:S(2)}, u32[]{:S(2)}) %collective-permute-start.27) | collective-permute-done | bytes 393248 | tf_op jit(solution)/shard_map/ppermute | solution.py:44
  110.1 2.2 %shard_map.64 = (bf16[512,384]{1,0:T(8,128)(2,1)S(1)}, bf16[512,384]{1,0:T(8,128)(2,1)S(1)}, bf16[512,384]{1,0:T(8,128)(2,1)S(1)}) custom-call(bf16[512,384]{1,0:T(8,128)(2,1)S(1)} %get-tuple-element.94.refs_0_, bf16[512,384]{1,0:T(8,128)(2,1)S(1)} %collective-permute-done.24.refs_1_, bf16[512,384]{1,0:T(8,128)(2,1)S(1)} %collective-permute-done.20.refs_2_, ...), custom_call_target="tpu_custom_call" | custom-call | bytes 1024 | tf_op jit(solution)/shard_map/pallas_call | solution.py:137
  114.4 9.9 %collective-permute-done.36.refs_6_ = bf16[512,384]{1,0:T(8,128)(2,1)S(1)} collective-permute-done((bf16[512,384]{1,0:T(8,128)(2,1)S(1)}, bf16[512,384]{1,0:T(8,128)(2,1)S(1)}, u32[]{:S(2)}, u32[]{:S(2)}) %collective-permute-start.36) | collective-permute-done | bytes 393248 | tf_op jit(solution)/shard_map/ppermute | solution.py:44
  124.3 3.3 %collective-permute-start.33 = (bf16[512,384]{1,0:T(8,128)(2,1)S(1)}, bf16[512,384]{1,0:T(8,128)(2,1)S(1)}, u32[]{:S(2)}, u32[]{:S(2)}) collective-permute-start(bf16[512,384]{1,0:T(8,128)(2,1)S(1)} %get-tuple-element.103), channel_id=1, source_target_pairs={{0,16},{4,20},{8,24},{12,28},{16,32},{20,36},{24,40},{28,44},{32,4... | collective-permute-start | bytes 1179656 | tf_op jit(solution)/shard_map/ppermute | solution.py:40
  127.7 5.5 %collective-permute-start.34 = (bf16[512,384]{1,0:T(8,128)(2,1)S(1)}, bf16[512,384]{1,0:T(8,128)(2,1)S(1)}, u32[]{:S(2)}, u32[]{:S(2)}) collective-permute-start(bf16[512,384]{1,0:T(8,128)(2,1)S(1)} %get-tuple-element.104), channel_id=1, source_target_pairs={{16,0},{20,4},{24,8},{28,12},{32,16},{36,20},{40,24},{44,28},{48,3... | collective-permute-start | bytes 1179656 | tf_op jit(solution)/shard_map/ppermute | solution.py:40
  135.1 14.2 %collective-permute-done.33.up_hi = bf16[512,384]{1,0:T(8,128)(2,1)S(1)} collective-permute-done((bf16[512,384]{1,0:T(8,128)(2,1)S(1)}, bf16[512,384]{1,0:T(8,128)(2,1)S(1)}, u32[]{:S(2)}, u32[]{:S(2)}) %collective-permute-start.33) | collective-permute-done | bytes 393248 | tf_op jit(solution)/shard_map/ppermute | solution.py:40
  (82 shorter events, 34.6 us)
Async XLA Ops:
  3.0 31.1 %collective-permute-start.1 = (bf16[576,384]{1,0:T(8,128)(2,1)S(1)}, bf16[576,384]{1,0:T(8,128)(2,1)S(1)}, u32[]{:S(2)}, u32[]{:S(2)}) collective-permute-start(bf16[576,384]{1,0:T(8,128)(2,1)S(1)} %fusion.1.refs_0_), channel_id=1, source_target_pairs={{0,2},{1,3},{2,0},{3,1},{4,6},{5,7},{6,4},{7,5},{8,10},{9,11},{10,... | collective-permute-start | bytes 1327112 | tf_op jit(solution)/shard_map/ppermute | solution.py:44
  4.6 12.5 %collective-permute-start.2 = (bf16[64,384]{1,0:T(8,128)(2,1)S(1)}, bf16[64,384]{1,0:T(8,128)(2,1)S(1)}, u32[]{:S(2)}, u32[]{:S(2)}) collective-permute-start(bf16[64,384]{1,0:T(8,128)(2,1)S(1)} %slice.78), channel_id=1, source_target_pairs={{0,4},{4,8},{8,12},{12,16},{16,20},{20,24},{24,28},{28,32},{32,36}... | collective-permute-start | bytes 147464 | tf_op jit(solution)/shard_map/ppermute | solution.py:40
  17.2 16.9 %collective-permute-start.5 = (bf16[448,384]{1,0:T(8,128)(2,1)S(1)}, bf16[448,384]{1,0:T(8,128)(2,1)S(1)}, u32[]{:S(2)}, u32[]{:S(2)}) collective-permute-start(bf16[448,384]{1,0:T(8,128)(2,1)S(1)} %fusion.4.refs_8_), channel_id=1, source_target_pairs={{0,2},{1,3},{2,0},{3,1},{4,6},{5,7},{6,4},{7,5},{8,10},{9,11},{10,... | collective-permute-start | bytes 1032200 | tf_op jit(solution)/shard_map/ppermute | solution.py:44
  17.3 12.0 %collective-permute-start.3 = (bf16[64,384]{1,0:T(8,128)(2,1)S(1)}, bf16[64,384]{1,0:T(8,128)(2,1)S(1)}, u32[]{:S(2)}, u32[]{:S(2)}) collective-permute-start(bf16[64,384]{1,0:T(8,128)(2,1)S(1)} %slice.79), channel_id=1, source_target_pairs={{4,0},{8,4},{12,8},{16,12},{20,16},{24,20},{28,24},{32,28},{36,32}... | collective-permute-start | bytes 147464 | tf_op jit(solution)/shard_map/ppermute | solution.py:40
  39.8 12.0 %collective-permute-start.13 = (bf16[512,384]{1,0:T(8,128)(2,1)S(1)}, bf16[512,384]{1,0:T(8,128)(2,1)S(1)}, u32[]{:S(2)}, u32[]{:S(2)}) collective-permute-start(bf16[512,384]{1,0:T(8,128)(2,1)S(1)} %get-tuple-element.70.refs_0_), channel_id=1, source_target_pairs={{0,2},{1,3},{2,0},{3,1},{4,6},{5,7},{6,4},{7,5},{8,10},{9,11},{10,... | collective-permute-start | bytes 1179656 | tf_op jit(solution)/shard_map/ppermute | solution.py:44
  41.1 11.4 %collective-permute-start.12 = (bf16[512,384]{1,0:T(8,128)(2,1)S(1)}, bf16[512,384]{1,0:T(8,128)(2,1)S(1)}, u32[]{:S(2)}, u32[]{:S(2)}) collective-permute-start(bf16[512,384]{1,0:T(8,128)(2,1)S(1)} %get-tuple-element.70.refs_0_), channel_id=1, source_target_pairs={{0,1},{1,0},{2,3},{3,2},{4,5},{5,4},{6,7},{7,6},{8,9},{9,8},{10,11... | collective-permute-start | bytes 1179656 | tf_op jit(solution)/shard_map/ppermute | solution.py:48
  46.4 13.1 %collective-permute-start.11 = (bf16[512,384]{1,0:T(8,128)(2,1)S(1)}, bf16[512,384]{1,0:T(8,128)(2,1)S(1)}, u32[]{:S(2)}, u32[]{:S(2)}) collective-permute-start(bf16[512,384]{1,0:T(8,128)(2,1)S(1)} %get-tuple-element.76.refs_0_), channel_id=1, source_target_pairs={{0,2},{1,3},{2,0},{3,1},{4,6},{5,7},{6,4},{7,5},{8,10},{9,11},{10,... | collective-permute-start | bytes 1179656 | tf_op jit(solution)/shard_map/ppermute | solution.py:44
  52.5 9.5 %collective-permute-start.16 = (bf16[512,384]{1,0:T(8,128)(2,1)S(1)}, bf16[512,384]{1,0:T(8,128)(2,1)S(1)}, u32[]{:S(2)}, u32[]{:S(2)}) collective-permute-start(bf16[512,384]{1,0:T(8,128)(2,1)S(1)} %get-tuple-element.76.refs_0_), channel_id=1, source_target_pairs={{0,1},{1,0},{2,3},{3,2},{4,5},{5,4},{6,7},{7,6},{8,9},{9,8},{10,11... | collective-permute-start | bytes 1179656 | tf_op jit(solution)/shard_map/ppermute | solution.py:48
  60.1 19.3 %collective-permute-start.21 = (bf16[512,384]{1,0:T(8,128)(2,1)S(1)}, bf16[512,384]{1,0:T(8,128)(2,1)S(1)}, u32[]{:S(2)}, u32[]{:S(2)}) collective-permute-start(bf16[512,384]{1,0:T(8,128)(2,1)S(1)} %get-tuple-element.83), channel_id=1, source_target_pairs={{0,4},{4,8},{8,12},{12,16},{16,20},{20,24},{24,28},{28,32},{32,36}... | collective-permute-start | bytes 1179656 | tf_op jit(solution)/shard_map/ppermute | solution.py:40
  64.2 25.8 %collective-permute-start.19 = (bf16[512,384]{1,0:T(8,128)(2,1)S(1)}, bf16[512,384]{1,0:T(8,128)(2,1)S(1)}, u32[]{:S(2)}, u32[]{:S(2)}) collective-permute-start(bf16[512,384]{1,0:T(8,128)(2,1)S(1)} %get-tuple-element.79), channel_id=1, source_target_pairs={{4,0},{8,4},{12,8},{16,12},{20,16},{24,20},{28,24},{32,28},{36,32}... | collective-permute-start | bytes 1179656 | tf_op jit(solution)/shard_map/ppermute | solution.py:40
  80.5 19.5 %collective-permute-start.22 = (bf16[512,384]{1,0:T(8,128)(2,1)S(1)}, bf16[512,384]{1,0:T(8,128)(2,1)S(1)}, u32[]{:S(2)}, u32[]{:S(2)}) collective-permute-start(bf16[512,384]{1,0:T(8,128)(2,1)S(1)} %get-tuple-element.92.refs_0_), channel_id=1, source_target_pairs={{0,16},{4,20},{8,24},{12,28},{16,32},{20,36},{24,40},{28,44},{32,4... | collective-permute-start | bytes 1179656 | tf_op jit(solution)/shard_map/ppermute | solution.py:40
  82.5 21.7 %collective-permute-start.23 = (bf16[512,384]{1,0:T(8,128)(2,1)S(1)}, bf16[512,384]{1,0:T(8,128)(2,1)S(1)}, u32[]{:S(2)}, u32[]{:S(2)}) collective-permute-start(bf16[512,384]{1,0:T(8,128)(2,1)S(1)} %get-tuple-element.92.refs_0_), channel_id=1, source_target_pairs={{16,0},{20,4},{24,8},{28,12},{32,16},{36,20},{40,24},{44,28},{48,3... | collective-permute-start | bytes 1179656 | tf_op jit(solution)/shard_map/ppermute | solution.py:40
  91.3 12.9 %collective-permute-start.20 = (bf16[512,384]{1,0:T(8,128)(2,1)S(1)}, bf16[512,384]{1,0:T(8,128)(2,1)S(1)}, u32[]{:S(2)}, u32[]{:S(2)}) collective-permute-start(bf16[512,384]{1,0:T(8,128)(2,1)S(1)} %get-tuple-element.94.refs_0_), channel_id=1, source_target_pairs={{0,2},{1,3},{2,0},{3,1},{4,6},{5,7},{6,4},{7,5},{8,10},{9,11},{10,... | collective-permute-start | bytes 1179656 | tf_op jit(solution)/shard_map/ppermute | solution.py:44
  92.1 16.2 %collective-permute-start.27 = (bf16[512,384]{1,0:T(8,128)(2,1)S(1)}, bf16[512,384]{1,0:T(8,128)(2,1)S(1)}, u32[]{:S(2)}, u32[]{:S(2)}) collective-permute-start(bf16[512,384]{1,0:T(8,128)(2,1)S(1)} %get-tuple-element.92.refs_0_), channel_id=1, source_target_pairs={{0,2},{1,3},{2,0},{3,1},{4,6},{5,7},{6,4},{7,5},{8,10},{9,11},{10,... | collective-permute-start | bytes 1179656 | tf_op jit(solution)/shard_map/ppermute | solution.py:44
  93.4 15.0 %collective-permute-start.28 = (bf16[512,384]{1,0:T(8,128)(2,1)S(1)}, bf16[512,384]{1,0:T(8,128)(2,1)S(1)}, u32[]{:S(2)}, u32[]{:S(2)}) collective-permute-start(bf16[512,384]{1,0:T(8,128)(2,1)S(1)} %get-tuple-element.92.refs_0_), channel_id=1, source_target_pairs={{0,1},{1,0},{2,3},{3,2},{4,5},{5,4},{6,7},{7,6},{8,9},{9,8},{10,11... | collective-permute-start | bytes 1179656 | tf_op jit(solution)/shard_map/ppermute | solution.py:48
  100.1 8.8 %collective-permute-start.24 = (bf16[512,384]{1,0:T(8,128)(2,1)S(1)}, bf16[512,384]{1,0:T(8,128)(2,1)S(1)}, u32[]{:S(2)}, u32[]{:S(2)}) collective-permute-start(bf16[512,384]{1,0:T(8,128)(2,1)S(1)} %get-tuple-element.94.refs_0_), channel_id=1, source_target_pairs={{0,1},{1,0},{2,3},{3,2},{4,5},{5,4},{6,7},{7,6},{8,9},{9,8},{10,11... | collective-permute-start | bytes 1179656 | tf_op jit(solution)/shard_map/ppermute | solution.py:48
  104.1 5.9 %collective-permute-start.29 = (bf16[512,384]{1,0:T(8,128)(2,1)S(1)}, bf16[512,384]{1,0:T(8,128)(2,1)S(1)}, u32[]{:S(2)}, u32[]{:S(2)}) collective-permute-start(bf16[512,384]{1,0:T(8,128)(2,1)S(1)} %collective-permute-done.22.refs_4_), channel_id=1, source_target_pairs={{0,1},{1,0},{2,3},{3,2},{4,5},{5,4},{6,7},{7,6},{8,9},{9,8},{10,11... | collective-permute-start | bytes 1179656 | tf_op jit(solution)/shard_map/ppermute | solution.py:48
  112.3 12.0 %collective-permute-start.36 = (bf16[512,384]{1,0:T(8,128)(2,1)S(1)}, bf16[512,384]{1,0:T(8,128)(2,1)S(1)}, u32[]{:S(2)}, u32[]{:S(2)}) collective-permute-start(bf16[512,384]{1,0:T(8,128)(2,1)S(1)} %collective-permute-done.22.refs_4_), channel_id=1, source_target_pairs={{0,2},{1,3},{2,0},{3,1},{4,6},{5,7},{6,4},{7,5},{8,10},{9,11},{10,... | collective-permute-start | bytes 1179656 | tf_op jit(solution)/shard_map/ppermute | solution.py:44
  113.0 20.1 %collective-permute-start.31 = (bf16[512,384]{1,0:T(8,128)(2,1)S(1)}, bf16[512,384]{1,0:T(8,128)(2,1)S(1)}, u32[]{:S(2)}, u32[]{:S(2)}) collective-permute-start(bf16[512,384]{1,0:T(8,128)(2,1)S(1)} %collective-permute-done.23.refs_0_), channel_id=1, source_target_pairs={{0,2},{1,3},{2,0},{3,1},{4,6},{5,7},{6,4},{7,5},{8,10},{9,11},{10,... | collective-permute-start | bytes 1179656 | tf_op jit(solution)/shard_map/ppermute | solution.py:44
  114.4 18.9 %collective-permute-start.35 = (bf16[512,384]{1,0:T(8,128)(2,1)S(1)}, bf16[512,384]{1,0:T(8,128)(2,1)S(1)}, u32[]{:S(2)}, u32[]{:S(2)}) collective-permute-start(bf16[512,384]{1,0:T(8,128)(2,1)S(1)} %collective-permute-done.27.refs_2_), channel_id=1, source_target_pairs={{0,1},{1,0},{2,3},{3,2},{4,5},{5,4},{6,7},{7,6},{8,9},{9,8},{10,11... | collective-permute-start | bytes 1179656 | tf_op jit(solution)/shard_map/ppermute | solution.py:48
  124.3 9.0 %collective-permute-start.37 = (bf16[512,384]{1,0:T(8,128)(2,1)S(1)}, bf16[512,384]{1,0:T(8,128)(2,1)S(1)}, u32[]{:S(2)}, u32[]{:S(2)}) collective-permute-start(bf16[512,384]{1,0:T(8,128)(2,1)S(1)} %collective-permute-done.36.refs_6_), channel_id=1, source_target_pairs={{0,1},{1,0},{2,3},{3,2},{4,5},{5,4},{6,7},{7,6},{8,9},{9,8},{10,11... | collective-permute-start | bytes 1179656 | tf_op jit(solution)/shard_map/ppermute | solution.py:48
  124.3 24.9 %collective-permute-start.33 = (bf16[512,384]{1,0:T(8,128)(2,1)S(1)}, bf16[512,384]{1,0:T(8,128)(2,1)S(1)}, u32[]{:S(2)}, u32[]{:S(2)}) collective-permute-start(bf16[512,384]{1,0:T(8,128)(2,1)S(1)} %get-tuple-element.103), channel_id=1, source_target_pairs={{0,16},{4,20},{8,24},{12,28},{16,32},{20,36},{24,40},{28,44},{32,4... | collective-permute-start | bytes 1179656 | tf_op jit(solution)/shard_map/ppermute | solution.py:40
  127.7 21.7 %collective-permute-start.34 = (bf16[512,384]{1,0:T(8,128)(2,1)S(1)}, bf16[512,384]{1,0:T(8,128)(2,1)S(1)}, u32[]{:S(2)}, u32[]{:S(2)}) collective-permute-start(bf16[512,384]{1,0:T(8,128)(2,1)S(1)} %get-tuple-element.104), channel_id=1, source_target_pairs={{16,0},{20,4},{24,8},{28,12},{32,16},{36,20},{40,24},{44,28},{48,3... | collective-permute-start | bytes 1179656 | tf_op jit(solution)/shard_map/ppermute | solution.py:40
  133.2 16.4 %collective-permute-start.32 = (bf16[512,384]{1,0:T(8,128)(2,1)S(1)}, bf16[512,384]{1,0:T(8,128)(2,1)S(1)}, u32[]{:S(2)}, u32[]{:S(2)}) collective-permute-start(bf16[512,384]{1,0:T(8,128)(2,1)S(1)} %collective-permute-done.31.refs_2_), channel_id=1, source_target_pairs={{0,1},{1,0},{2,3},{3,2},{4,5},{5,4},{6,7},{7,6},{8,9},{9,8},{10,11... | collective-permute-start | bytes 1179656 | tf_op jit(solution)/shard_map/ppermute | solution.py:48
  (16 other events, 46.8 us)

commit v7 on v6

--- a/solution.py
+++ b/solution.py
@@ -81,13 +81,22 @@
     a_ref[...] = gelu(s.astype(F32) * vec_ref[1:2, :] + vec_ref[2:3, :]).astype(BF16)
 
 
-def near_kernel(plan, first_row, *refs):
-    groups = max(g for g, _, _ in plan) + 1
-    bins_ref, vec_ref, w_ref, s_ref, a_ref, buf = refs[4 * groups :]
+def near_kernel(plan, parts, first_row, *refs):
+    groups, at = [], 0
+    for part in parts:
+        group = refs[at : at + 3 + part]
+        groups.append([[group[0]], [group[1]], [group[2]], group[3:]])
+        at += 3 + part
+    bins_ref, vec_ref, w_ref, s_ref, a_ref, buf = refs[at:]
     to = 0
     for g, at, count in plan:
-        for p, piece in enumerate(refs[4 * g : 4 * g + 4]):
-            buf[to : to + count, p * W : (p + 1) * W] = piece[at : at + count, :]
+        for p, pieces in enumerate(groups[g]):
+            low = 0
+            for piece in pieces:
+                start, stop = max(at, low), min(at + count, low + piece.shape[0])
+                if start < stop:
+                    buf[to + start - at : to + stop - at, p * W : (p + 1) * W] = piece[start - low : stop - low, :]
+                low += piece.shape[0]
         to += count
     total = bins_ref[first_row : first_row + MID, :].astype(F32)
     for k in range(3):
@@ -111,6 +120,11 @@
     far = jnp.concatenate([p[...] for p in refs[2 : 2 + fars]], axis=0)
     near_far = jnp.concatenate([p[...] for p in refs[2 + fars :]], axis=0)
     return jnp.concatenate([refs[0][...], refs[1][...], far, near_far], axis=1)
+
+
+def rims_kernel(low_ref, high_ref, o_ref):
+    o_ref[:R, :] = low_ref[...]
+    o_ref[R:, :] = high_ref[...]
 
 
 def part_kernel(*refs):
@@ -175,19 +189,21 @@
     act_3 = entry(bins_in[:FIRST])
     low = shifted(act_1[-R:], 1)
     high = shifted(act_3[:R], -1)
-    low, act_3 = after((low, act_3))
     w0 = staged(0, ch, conv_weight)
-    act_2 = jnp.concatenate([low, high], axis=0)
+    low, high, w0 = after((low, high, w0))
+    (act_2,) = call(rims_kernel, (low, high), [2 * R])
+    act_2, act_3 = after((act_2, act_3))
     far_2 = chip_swap(act_2)
     near_2 = core_swap(act_2)
     far_3 = chip_swap(act_3)
     near_3 = core_swap(act_3)
-    far_1, far_2, far_3, w0 = after((far_1, far_2, far_3, w0))
-    g_1 = (act_1, near_1, far_1, core_swap(far_1))
+    far_1, far_2, near_1 = after((far_1, far_2, near_1))
+    g_1 = (act_1, near_1, far_1, *core_swaps(far_1, 2))
     g_2 = (act_2, near_2, far_2, core_swap(far_2))
+    g_1, g_2, far_3 = after((g_1, g_2, far_3))
     plan_hi = ((0, 0, ROWS - FIRST), (1, R, R))
     s_hi, a_hi = call(
-        functools.partial(near_kernel, plan_hi, MID), (*g_1, *g_2, bins_in, vec0, w0), halves[:2], scratch
+        functools.partial(near_kernel, plan_hi, (2, 1), MID), (*g_1, *g_2, bins_in, vec0, w0), halves[:2], scratch
     )
     far_hi = chip_swap(a_hi)
     near_hi = core_swap(a_hi)
@@ -195,7 +211,7 @@
     g_3 = (act_3, near_3, far_3, core_swap(far_3))
     plan_lo = ((1, 0, R), (2, 0, FIRST), (0, 0, 2 * R))
     s_lo, a_lo = call(
-        functools.partial(near_kernel, plan_lo, 0), (*g_1, *g_2, *g_3, bins_in, vec0, w0), halves[:2], scratch
+        functools.partial(near_kernel, plan_lo, (2, 1, 1), 0), (*g_1, *g_2, *g_3, bins_in, vec0, w0), halves[:2], scratch
     )
     far_lo = chip_swap(a_lo)
     near_lo = core_swap(a_lo)
@@ -235,7 +251,6 @@
     g_low = (from_low, near_low, far_low, core_swap(far_low))
     g_high = (from_high, near_high, far_high, core_swap(far_high))
     (part,) = call(part_kernel, (*g_own, *g_low, s_lo, vec2, w2), halves[:1], dtype=F32)
-    up_hi, down_hi, part = after((up_hi, down_hi, part))
     (upper,) = call(upper_kernel, (s_hi, q_hi, up_hi, down_hi, vec2), halves[:1], flops=COST)
     (out,) = call(out_kernel, (*g_high, part, upper, w2), [ROWS])
     return out

time: 155 us -> 143 us (0.923)
  waiting for transfers between devices: 63 us -> 54.6 us
  starting transfers between devices: 56.9 us -> 54.8 us
    ppermute x8, waiting for transfers between devices: 36.8 us -> 24.9 us  [shifted(): return lax.ppermute(array, 'seq', pairs)]
    ppermute x9, waiting for transfers between devices: 20.9 us -> 24.9 us  [chip_swap(): return lax.ppermute(array, 'ch', [(i, i ^ 2) for i in range(4)])]
    ppermute x8, starting transfers between devices: 44.2 us -> 40.5 us  [shifted(): return lax.ppermute(array, 'seq', pairs)]
    ppermute x21 -> x22, waiting for transfers between devices: 5.33 us -> 4.79 us  [core_swap(): return lax.ppermute(array, 'ch', [(i, i ^ 1) for i in range(4)])]
    ppermute x21 -> x22, starting transfers between devices: 3.59 us -> 4.1 us  [core_swap(): return lax.ppermute(array, 'ch', [(i, i ^ 1) for i in range(4)])]
    pallas_call x10 -> x11, Pallas kernels: 20.1 us -> 20.1 us  [call(): pl.pallas_call(kernel, out_shape=[jax.ShapeDtypeStruct((r, W), dtype) for...]
  transfers between devices with their start and end apart: 38 -> 39, of which waited for: 20 -> 19; matrix products, arithmetic and copies ran while one was open for 1% -> 1% of each run, Pallas kernels for 12% -> 13%
where the time goes in v7:
time: 143 us; the launch traced here: 141 us
  starting transfers between devices  54.8 us (38%)
  waiting for transfers between devices  54.6 us (38%)
  Pallas kernels  26.3 us (18%)
  other arithmetic  3.93 us (3%)
    ppermute x8, starting transfers between devices, shifted(): return lax.ppermute(array, 'seq', pairs)  40.5 us
    ppermute x9, waiting for transfers between devices, chip_swap(): return lax.ppermute(array, 'ch', [(i, i ^ 2) for i in range(4)])  24.9 us
    ppermute x8, waiting for transfers between devices, shifted(): return lax.ppermute(array, 'seq', pairs)  24.9 us
    pallas_call x11, Pallas kernels, call(): pl.pallas_call(kernel, out_shape=[jax.ShapeDtypeStruct((r, W), dtype) for...  20.1 us
    ppermute x9, starting transfers between devices, chip_swap(): return lax.ppermute(array, 'ch', [(i, i ^ 2) for i in range(4)])  10.2 us
    pallas_call x3, Pallas kernels, staged(): pl.pallas_call(functools.partial(stage_kernel, layer), out_shape=jax.Shap...  6.2 us
    ppermute x22, waiting for transfers between devices, core_swap(): return lax.ppermute(array, 'ch', [(i, i ^ 1) for i in range(4)])  4.79 us
    ppermute x22, starting transfers between devices, core_swap(): return lax.ppermute(array, 'ch', [(i, i ^ 1) for i in range(4)])  4.1 us
  transfers between devices with their start and end apart: 39, of which 19 were waited for; matrix products, arithmetic and copies ran while one was open for 1% of the time, Pallas kernels for 13%

profile of v7, /device:TPU:6, one launch (start us, length us, event | category | flops | bytes accessed | tf_op | source)
XLA Modules:
  0.0 141.0 jit_solution(4605488808337787245)
XLA Ops:
  0.9 2.1 %fusion.1.refs_0_ = bf16[576,384]{1,0:T(8,128)(2,1)S(1)} fusion(f32[384]{0:T(512)S(1)} %get-tuple-element.151, f32[384]{0:T(512)S(1)} %get-tuple-element.145, bf16[1024,384]{1,0:T(8,128)(2,1)} %refs_13_.1), kind=kLoop, calls=%fused_computation.3 | loop fusion | flops 7741440 | bytes 887808 | tf_op jit(solution)/shard_map/convert_element_type | solution.py:184
  4.6 4.8 %collective-permute-start.1 = (bf16[64,384]{1,0:T(8,128)(2,1)S(1)}, bf16[64,384]{1,0:T(8,128)(2,1)S(1)}, u32[]{:S(2)}, u32[]{:S(2)}) collective-permute-start(bf16[64,384]{1,0:T(8,128)(2,1)S(1)} %slice.86), channel_id=1, source_target_pairs={{0,4},{4,8},{8,12},{12,16},{16,20},{20,24},{24,28},{28,32},{32,36}... | collective-permute-start | bytes 147464 | tf_op jit(solution)/shard_map/ppermute | solution.py:40
  11.3 7.5 %collective-permute-start.2 = (bf16[64,384]{1,0:T(8,128)(2,1)S(1)}, bf16[64,384]{1,0:T(8,128)(2,1)S(1)}, u32[]{:S(2)}, u32[]{:S(2)}) collective-permute-start(bf16[64,384]{1,0:T(8,128)(2,1)S(1)} %slice.87), channel_id=1, source_target_pairs={{4,0},{8,4},{12,8},{16,12},{20,16},{24,20},{28,24},{32,28},{36,32}... | collective-permute-start | bytes 147464 | tf_op jit(solution)/shard_map/ppermute | solution.py:40
  18.8 2.1 %shard_map.55.refs_11_.refs_15_ = bf16[1536,1152]{1,0:T(8,128)(2,1)S(1)} custom-call(s32[1]{0:T(128)} %bitcast.ch_ref, bf16[3,3,1536,384]{3,2,1,0:T(8,128)(2,1)} %w_hbm.5), custom_call_target="tpu_custom_call" | custom-call | tf_op jit(solution)/shard_map/pallas_call | solution.py:163
  23.1 3.6 %collective-permute-done.3.refs_7_ = bf16[128,384]{1,0:T(8,128)(2,1)S(1)} collective-permute-done((bf16[128,384]{1,0:T(8,128)(2,1)S(1)}, bf16[128,384]{1,0:T(8,128)(2,1)S(1)}, u32[]{:S(2)}, u32[]{:S(2)}) %collective-permute-start.3) | collective-permute-done | bytes 98336 | tf_op jit(solution)/shard_map/ppermute | solution.py:44
  28.8 4.6 %collective-permute-done.9.refs_11_ = bf16[448,384]{1,0:T(8,128)(2,1)S(1)} collective-permute-done((bf16[448,384]{1,0:T(8,128)(2,1)S(1)}, bf16[448,384]{1,0:T(8,128)(2,1)S(1)}, u32[]{:S(2)}, u32[]{:S(2)}) %collective-permute-start.9) | collective-permute-done | bytes 344096 | tf_op jit(solution)/shard_map/ppermute | solution.py:44
  33.4 3.6 %shard_map.57 = (bf16[512,384]{1,0:T(8,128)(2,1)S(1)}, bf16[512,384]{1,0:T(8,128)(2,1)S(1)}) custom-call(bf16[576,384]{1,0:T(8,128)(2,1)S(1)} %fusion.1.refs_0_, bf16[576,384]{1,0:T(8,128)(2,1)S(1)} %collective-permute-done.4.refs_1_, bf16[576,384]{1,0:T(8,128)(2,1)S(1)} %collective-permute-done.refs_2_, ...), custom_call_target="tpu_custom_call" | custom-call | bytes 1024 | tf_op jit(solution)/shard_map/pallas_call | solution.py:151
  39.5 3.6 %shard_map.58 = (bf16[512,384]{1,0:T(8,128)(2,1)S(1)}, bf16[512,384]{1,0:T(8,128)(2,1)S(1)}) custom-call(bf16[576,384]{1,0:T(8,128)(2,1)S(1)} %fusion.1.refs_0_, bf16[576,384]{1,0:T(8,128)(2,1)S(1)} %collective-permute-done.4.refs_1_, bf16[576,384]{1,0:T(8,128)(2,1)S(1)} %collective-permute-done.refs_2_, ...), custom_call_target="tpu_custom_call" | custom-call | bytes 1024 | tf_op jit(solution)/shard_map/pallas_call | solution.py:151
  44.9 2.0 %shard_map.59.refs_5_ = bf16[1536,1152]{1,0:T(8,128)(2,1)S(1)} custom-call(s32[1]{0:T(128)} %bitcast.ch_ref, bf16[3,3,1536,384]{3,2,1,0:T(8,128)(2,1)} %w_hbm.5), custom_call_target="tpu_custom_call" | custom-call | tf_op jit(solution)/shard_map/pallas_call | solution.py:163
  50.8 2.2 %shard_map.60 = (bf16[512,384]{1,0:T(8,128)(2,1)S(1)}, bf16[512,384]{1,0:T(8,128)(2,1)S(1)}, bf16[512,384]{1,0:T(8,128)(2,1)S(1)}) custom-call(bf16[512,384]{1,0:T(8,128)(2,1)S(1)} %get-tuple-element.91.refs_0_, bf16[512,384]{1,0:T(8,128)(2,1)S(1)} %collective-permute-done.13.refs_1_, bf16[512,384]{1,0:T(8,128)(2,1)S(1)} %collective-permute-done.14.refs_2_, ...), custom_call_target="tpu_custom_call" | custom-call | bytes 1024 | tf_op jit(solution)/shard_map/pallas_call | solution.py:151
  53.0 2.9 %collective-permute-done.12.refs_2_ = bf16[512,384]{1,0:T(8,128)(2,1)S(1)} collective-permute-done((bf16[512,384]{1,0:T(8,128)(2,1)S(1)}, bf16[512,384]{1,0:T(8,128)(2,1)S(1)}, u32[]{:S(2)}, u32[]{:S(2)}) %collective-permute-start.12) | collective-permute-done | bytes 393248 | tf_op jit(solution)/shard_map/ppermute | solution.py:44
  58.5 2.2 %shard_map.61 = (bf16[512,384]{1,0:T(8,128)(2,1)S(1)}, bf16[512,384]{1,0:T(8,128)(2,1)S(1)}, bf16[512,384]{1,0:T(8,128)(2,1)S(1)}) custom-call(bf16[512,384]{1,0:T(8,128)(2,1)S(1)} %get-tuple-element.97.refs_0_, bf16[512,384]{1,0:T(8,128)(2,1)S(1)} %collective-permute-done.17.refs_1_, bf16[512,384]{1,0:T(8,128)(2,1)S(1)} %collective-permute-done.12.refs_2_, ...), custom_call_target="tpu_custom_call" | custom-call | bytes 1024 | tf_op jit(solution)/shard_map/pallas_call | solution.py:151
  60.7 8.4 %collective-permute-start.20 = (bf16[512,384]{1,0:T(8,128)(2,1)S(1)}, bf16[512,384]{1,0:T(8,128)(2,1)S(1)}, u32[]{:S(2)}, u32[]{:S(2)}) collective-permute-start(bf16[512,384]{1,0:T(8,128)(2,1)S(1)} %get-tuple-element.100), channel_id=1, source_target_pairs={{4,0},{8,4},{12,8},{16,12},{20,16},{24,20},{28,24},{32,28},{36,32}... | collective-permute-start | bytes 1179656 | tf_op jit(solution)/shard_map/ppermute | solution.py:40
  69.2 6.6 %collective-permute-done.22.t1 = bf16[512,384]{1,0:T(8,128)(2,1)S(1)} collective-permute-done((bf16[512,384]{1,0:T(8,128)(2,1)S(1)}, bf16[512,384]{1,0:T(8,128)(2,1)S(1)}, u32[]{:S(2)}, u32[]{:S(2)}) %collective-permute-start.22) | collective-permute-done | bytes 393248 | tf_op jit(solution)/shard_map/ppermute | solution.py:40
  77.0 3.7 %collective-permute-start.23 = (bf16[512,384]{1,0:T(8,128)(2,1)S(1)}, bf16[512,384]{1,0:T(8,128)(2,1)S(1)}, u32[]{:S(2)}, u32[]{:S(2)}) collective-permute-start(bf16[512,384]{1,0:T(8,128)(2,1)S(1)} %get-tuple-element.113.refs_0_), channel_id=1, source_target_pairs={{0,16},{4,20},{8,24},{12,28},{16,32},{20,36},{24,40},{28,44},{32,4... | collective-permute-start | bytes 1179656 | tf_op jit(solution)/shard_map/ppermute | solution.py:40
  80.7 5.4 %collective-permute-start.24 = (bf16[512,384]{1,0:T(8,128)(2,1)S(1)}, bf16[512,384]{1,0:T(8,128)(2,1)S(1)}, u32[]{:S(2)}, u32[]{:S(2)}) collective-permute-start(bf16[512,384]{1,0:T(8,128)(2,1)S(1)} %get-tuple-element.113.refs_0_), channel_id=1, source_target_pairs={{16,0},{20,4},{24,8},{28,12},{32,16},{36,20},{40,24},{44,28},{48,3... | collective-permute-start | bytes 1179656 | tf_op jit(solution)/shard_map/ppermute | solution.py:40
  89.4 2.0 %shard_map.64.refs_5_.refs_10_.refs_6_ = bf16[1536,1152]{1,0:T(8,128)(2,1)S(1)} custom-call(s32[1]{0:T(128)} %bitcast.ch_ref, bf16[3,3,1536,384]{3,2,1,0:T(8,128)(2,1)} %w_hbm.5), custom_call_target="tpu_custom_call" | custom-call | tf_op jit(solution)/shard_map/pallas_call | solution.py:163
  91.4 9.0 %collective-permute-done.23.refs_4_ = bf16[512,384]{1,0:T(8,128)(2,1)S(1)} collective-permute-done((bf16[512,384]{1,0:T(8,128)(2,1)S(1)}, bf16[512,384]{1,0:T(8,128)(2,1)S(1)}, u32[]{:S(2)}, u32[]{:S(2)}) %collective-permute-start.23) | collective-permute-done | bytes 393248 | tf_op jit(solution)/shard_map/ppermute | solution.py:40
  102.7 3.1 %collective-permute-done.28.refs_2_ = bf16[512,384]{1,0:T(8,128)(2,1)S(1)} collective-permute-done((bf16[512,384]{1,0:T(8,128)(2,1)S(1)}, bf16[512,384]{1,0:T(8,128)(2,1)S(1)}, u32[]{:S(2)}, u32[]{:S(2)}) %collective-permute-start.28) | collective-permute-done | bytes 393248 | tf_op jit(solution)/shard_map/ppermute | solution.py:44
  107.6 2.2 %shard_map.65 = (bf16[512,384]{1,0:T(8,128)(2,1)S(1)}, bf16[512,384]{1,0:T(8,128)(2,1)S(1)}, bf16[512,384]{1,0:T(8,128)(2,1)S(1)}) custom-call(bf16[512,384]{1,0:T(8,128)(2,1)S(1)} %get-tuple-element.115.refs_0_, bf16[512,384]{1,0:T(8,128)(2,1)S(1)} %collective-permute-done.25.refs_1_, bf16[512,384]{1,0:T(8,128)(2,1)S(1)} %collective-permute-done.21.refs_2_, ...), custom_call_target="tpu_custom_call" | custom-call | bytes 1024 | tf_op jit(solution)/shard_map/pallas_call | solution.py:151
  113.9 6.8 %collective-permute-start.38 = (bf16[512,384]{1,0:T(8,128)(2,1)S(1)}, bf16[512,384]{1,0:T(8,128)(2,1)S(1)}, u32[]{:S(2)}, u32[]{:S(2)}) collective-permute-start(bf16[512,384]{1,0:T(8,128)(2,1)S(1)} %get-tuple-element.132), channel_id=1, source_target_pairs={{16,0},{20,4},{24,8},{28,12},{32,16},{36,20},{40,24},{44,28},{48,3... | collective-permute-start | bytes 1179656 | tf_op jit(solution)/shard_map/ppermute | solution.py:40
  121.8 7.7 %collective-permute-done.32.refs_2_ = bf16[512,384]{1,0:T(8,128)(2,1)S(1)} collective-permute-done((bf16[512,384]{1,0:T(8,128)(2,1)S(1)}, bf16[512,384]{1,0:T(8,128)(2,1)S(1)}, u32[]{:S(2)}, u32[]{:S(2)}) %collective-permute-start.32) | collective-permute-done | bytes 393248 | tf_op jit(solution)/shard_map/ppermute | solution.py:44
  129.5 5.4 %collective-permute-done.37.up_hi = bf16[512,384]{1,0:T(8,128)(2,1)S(1)} collective-permute-done((bf16[512,384]{1,0:T(8,128)(2,1)S(1)}, bf16[512,384]{1,0:T(8,128)(2,1)S(1)}, u32[]{:S(2)}, u32[]{:S(2)}) %collective-permute-start.37) | collective-permute-done | bytes 393248 | tf_op jit(solution)/shard_map/ppermute | solution.py:40
  134.9 2.2 %collective-permute-done.38.down_hi = bf16[512,384]{1,0:T(8,128)(2,1)S(1)} collective-permute-done((bf16[512,384]{1,0:T(8,128)(2,1)S(1)}, bf16[512,384]{1,0:T(8,128)(2,1)S(1)}, u32[]{:S(2)}, u32[]{:S(2)}) %collective-permute-start.38) | collective-permute-done | bytes 393248 | tf_op jit(solution)/shard_map/ppermute | solution.py:40
  (84 shorter events, 36.9 us)
Async XLA Ops:
  3.0 23.7 %collective-permute-start = (bf16[576,384]{1,0:T(8,128)(2,1)S(1)}, bf16[576,384]{1,0:T(8,128)(2,1)S(1)}, u32[]{:S(2)}, u32[]{:S(2)}) collective-permute-start(bf16[576,384]{1,0:T(8,128)(2,1)S(1)} %fusion.1.refs_0_), channel_id=1, source_target_pairs={{0,2},{1,3},{2,0},{3,1},{4,6},{5,7},{6,4},{7,5},{8,10},{9,11},{10,... | collective-permute-start | bytes 1327112 | tf_op jit(solution)/shard_map/ppermute | solution.py:44
  4.6 22.1 %collective-permute-start.4 = (bf16[576,384]{1,0:T(8,128)(2,1)S(1)}, bf16[576,384]{1,0:T(8,128)(2,1)S(1)}, u32[]{:S(2)}, u32[]{:S(2)}) collective-permute-start(bf16[576,384]{1,0:T(8,128)(2,1)S(1)} %fusion.1.refs_0_), channel_id=1, source_target_pairs={{0,1},{1,0},{2,3},{3,2},{4,5},{5,4},{6,7},{7,6},{8,9},{9,8},{10,11... | collective-permute-start | bytes 1327112 | tf_op jit(solution)/shard_map/ppermute | solution.py:48
  4.6 16.3 %collective-permute-start.1 = (bf16[64,384]{1,0:T(8,128)(2,1)S(1)}, bf16[64,384]{1,0:T(8,128)(2,1)S(1)}, u32[]{:S(2)}, u32[]{:S(2)}) collective-permute-start(bf16[64,384]{1,0:T(8,128)(2,1)S(1)} %slice.86), channel_id=1, source_target_pairs={{0,4},{4,8},{8,12},{12,16},{16,20},{20,24},{24,28},{28,32},{32,36}... | collective-permute-start | bytes 147464 | tf_op jit(solution)/shard_map/ppermute | solution.py:40
  11.3 9.7 %collective-permute-start.2 = (bf16[64,384]{1,0:T(8,128)(2,1)S(1)}, bf16[64,384]{1,0:T(8,128)(2,1)S(1)}, u32[]{:S(2)}, u32[]{:S(2)}) collective-permute-start(bf16[64,384]{1,0:T(8,128)(2,1)S(1)} %slice.87), channel_id=1, source_target_pairs={{4,0},{8,4},{12,8},{16,12},{20,16},{24,20},{28,24},{32,28},{36,32}... | collective-permute-start | bytes 147464 | tf_op jit(solution)/shard_map/ppermute | solution.py:40
  21.2 12.1 %collective-permute-start.9 = (bf16[448,384]{1,0:T(8,128)(2,1)S(1)}, bf16[448,384]{1,0:T(8,128)(2,1)S(1)}, u32[]{:S(2)}, u32[]{:S(2)}) collective-permute-start(bf16[448,384]{1,0:T(8,128)(2,1)S(1)} %fusion.4.refs_9_), channel_id=1, source_target_pairs={{0,2},{1,3},{2,0},{3,1},{4,6},{5,7},{6,4},{7,5},{8,10},{9,11},{10,... | collective-permute-start | bytes 1032200 | tf_op jit(solution)/shard_map/ppermute | solution.py:44
  26.8 6.6 %collective-permute-start.5 = (bf16[288,384]{1,0:T(8,128)(2,1)S(1)}, bf16[288,384]{1,0:T(8,128)(2,1)S(1)}, u32[]{:S(2)}, u32[]{:S(2)}) collective-permute-start(bf16[288,384]{1,0:T(8,128)(2,1)S(1)} %get-tuple-element.134), channel_id=1, source_target_pairs={{0,1},{1,0},{2,3},{3,2},{4,5},{5,4},{6,7},{7,6},{8,9},{9,8},{10,11... | collective-permute-start | bytes 663560 | tf_op jit(solution)/shard_map/ppermute | solution.py:48
  37.0 12.0 %collective-permute-start.14 = (bf16[512,384]{1,0:T(8,128)(2,1)S(1)}, bf16[512,384]{1,0:T(8,128)(2,1)S(1)}, u32[]{:S(2)}, u32[]{:S(2)}) collective-permute-start(bf16[512,384]{1,0:T(8,128)(2,1)S(1)} %get-tuple-element.91.refs_0_), channel_id=1, source_target_pairs={{0,2},{1,3},{2,0},{3,1},{4,6},{5,7},{6,4},{7,5},{8,10},{9,11},{10,... | collective-permute-start | bytes 1179656 | tf_op jit(solution)/shard_map/ppermute | solution.py:44
  37.9 11.9 %collective-permute-start.13 = (bf16[512,384]{1,0:T(8,128)(2,1)S(1)}, bf16[512,384]{1,0:T(8,128)(2,1)S(1)}, u32[]{:S(2)}, u32[]{:S(2)}) collective-permute-start(bf16[512,384]{1,0:T(8,128)(2,1)S(1)} %get-tuple-element.91.refs_0_), channel_id=1, source_target_pairs={{0,1},{1,0},{2,3},{3,2},{4,5},{5,4},{6,7},{7,6},{8,9},{9,8},{10,11... | collective-permute-start | bytes 1179656 | tf_op jit(solution)/shard_map/ppermute | solution.py:48
  43.1 12.8 %collective-permute-start.12 = (bf16[512,384]{1,0:T(8,128)(2,1)S(1)}, bf16[512,384]{1,0:T(8,128)(2,1)S(1)}, u32[]{:S(2)}, u32[]{:S(2)}) collective-permute-start(bf16[512,384]{1,0:T(8,128)(2,1)S(1)} %get-tuple-element.97.refs_0_), channel_id=1, source_target_pairs={{0,2},{1,3},{2,0},{3,1},{4,6},{5,7},{6,4},{7,5},{8,10},{9,11},{10,... | collective-permute-start | bytes 1179656 | tf_op jit(solution)/shard_map/ppermute | solution.py:44
  49.6 8.9 %collective-permute-start.17 = (bf16[512,384]{1,0:T(8,128)(2,1)S(1)}, bf16[512,384]{1,0:T(8,128)(2,1)S(1)}, u32[]{:S(2)}, u32[]{:S(2)}) collective-permute-start(bf16[512,384]{1,0:T(8,128)(2,1)S(1)} %get-tuple-element.97.refs_0_), channel_id=1, source_target_pairs={{0,1},{1,0},{2,3},{3,2},{4,5},{5,4},{6,7},{7,6},{8,9},{9,8},{10,11... | collective-permute-start | bytes 1179656 | tf_op jit(solution)/shard_map/ppermute | solution.py:48
  56.5 19.2 %collective-permute-start.22 = (bf16[512,384]{1,0:T(8,128)(2,1)S(1)}, bf16[512,384]{1,0:T(8,128)(2,1)S(1)}, u32[]{:S(2)}, u32[]{:S(2)}) collective-permute-start(bf16[512,384]{1,0:T(8,128)(2,1)S(1)} %get-tuple-element.104), channel_id=1, source_target_pairs={{0,4},{4,8},{8,12},{12,16},{16,20},{20,24},{24,28},{28,32},{32,36}... | collective-permute-start | bytes 1179656 | tf_op jit(solution)/shard_map/ppermute | solution.py:40
  60.7 25.4 %collective-permute-start.20 = (bf16[512,384]{1,0:T(8,128)(2,1)S(1)}, bf16[512,384]{1,0:T(8,128)(2,1)S(1)}, u32[]{:S(2)}, u32[]{:S(2)}) collective-permute-start(bf16[512,384]{1,0:T(8,128)(2,1)S(1)} %get-tuple-element.100), channel_id=1, source_target_pairs={{4,0},{8,4},{12,8},{16,12},{20,16},{24,20},{28,24},{32,28},{36,32}... | collective-permute-start | bytes 1179656 | tf_op jit(solution)/shard_map/ppermute | solution.py:40
  77.0 23.4 %collective-permute-start.23 = (bf16[512,384]{1,0:T(8,128)(2,1)S(1)}, bf16[512,384]{1,0:T(8,128)(2,1)S(1)}, u32[]{:S(2)}, u32[]{:S(2)}) collective-permute-start(bf16[512,384]{1,0:T(8,128)(2,1)S(1)} %get-tuple-element.113.refs_0_), channel_id=1, source_target_pairs={{0,16},{4,20},{8,24},{12,28},{16,32},{20,36},{24,40},{28,44},{32,4... | collective-permute-start | bytes 1179656 | tf_op jit(solution)/shard_map/ppermute | solution.py:40
  80.7 21.5 %collective-permute-start.24 = (bf16[512,384]{1,0:T(8,128)(2,1)S(1)}, bf16[512,384]{1,0:T(8,128)(2,1)S(1)}, u32[]{:S(2)}, u32[]{:S(2)}) collective-permute-start(bf16[512,384]{1,0:T(8,128)(2,1)S(1)} %get-tuple-element.113.refs_0_), channel_id=1, source_target_pairs={{16,0},{20,4},{24,8},{28,12},{32,16},{36,20},{40,24},{44,28},{48,3... | collective-permute-start | bytes 1179656 | tf_op jit(solution)/shard_map/ppermute | solution.py:40
  87.3 14.9 %collective-permute-start.21 = (bf16[512,384]{1,0:T(8,128)(2,1)S(1)}, bf16[512,384]{1,0:T(8,128)(2,1)S(1)}, u32[]{:S(2)}, u32[]{:S(2)}) collective-permute-start(bf16[512,384]{1,0:T(8,128)(2,1)S(1)} %get-tuple-element.115.refs_0_), channel_id=1, source_target_pairs={{0,2},{1,3},{2,0},{3,1},{4,6},{5,7},{6,4},{7,5},{8,10},{9,11},{10,... | collective-permute-start | bytes 1179656 | tf_op jit(solution)/shard_map/ppermute | solution.py:44
  87.8 18.0 %collective-permute-start.28 = (bf16[512,384]{1,0:T(8,128)(2,1)S(1)}, bf16[512,384]{1,0:T(8,128)(2,1)S(1)}, u32[]{:S(2)}, u32[]{:S(2)}) collective-permute-start(bf16[512,384]{1,0:T(8,128)(2,1)S(1)} %get-tuple-element.113.refs_0_), channel_id=1, source_target_pairs={{0,2},{1,3},{2,0},{3,1},{4,6},{5,7},{6,4},{7,5},{8,10},{9,11},{10,... | collective-permute-start | bytes 1179656 | tf_op jit(solution)/shard_map/ppermute | solution.py:44
  89.4 16.4 %collective-permute-start.29 = (bf16[512,384]{1,0:T(8,128)(2,1)S(1)}, bf16[512,384]{1,0:T(8,128)(2,1)S(1)}, u32[]{:S(2)}, u32[]{:S(2)}) collective-permute-start(bf16[512,384]{1,0:T(8,128)(2,1)S(1)} %get-tuple-element.113.refs_0_), channel_id=1, source_target_pairs={{0,1},{1,0},{2,3},{3,2},{4,5},{5,4},{6,7},{7,6},{8,9},{9,8},{10,11... | collective-permute-start | bytes 1179656 | tf_op jit(solution)/shard_map/ppermute | solution.py:48
  109.8 12.0 %collective-permute-start.35 = (bf16[512,384]{1,0:T(8,128)(2,1)S(1)}, bf16[512,384]{1,0:T(8,128)(2,1)S(1)}, u32[]{:S(2)}, u32[]{:S(2)}) collective-permute-start(bf16[512,384]{1,0:T(8,128)(2,1)S(1)} %collective-permute-done.23.refs_4_), channel_id=1, source_target_pairs={{0,2},{1,3},{2,0},{3,1},{4,6},{5,7},{6,4},{7,5},{8,10},{9,11},{10,... | collective-permute-start | bytes 1179656 | tf_op jit(solution)/shard_map/ppermute | solution.py:44
  110.3 19.2 %collective-permute-start.32 = (bf16[512,384]{1,0:T(8,128)(2,1)S(1)}, bf16[512,384]{1,0:T(8,128)(2,1)S(1)}, u32[]{:S(2)}, u32[]{:S(2)}) collective-permute-start(bf16[512,384]{1,0:T(8,128)(2,1)S(1)} %collective-permute-done.24.refs_0_), channel_id=1, source_target_pairs={{0,2},{1,3},{2,0},{3,1},{4,6},{5,7},{6,4},{7,5},{8,10},{9,11},{10,... | collective-permute-start | bytes 1179656 | tf_op jit(solution)/shard_map/ppermute | solution.py:44
  111.9 23.0 %collective-permute-start.37 = (bf16[512,384]{1,0:T(8,128)(2,1)S(1)}, bf16[512,384]{1,0:T(8,128)(2,1)S(1)}, u32[]{:S(2)}, u32[]{:S(2)}) collective-permute-start(bf16[512,384]{1,0:T(8,128)(2,1)S(1)} %get-tuple-element.131), channel_id=1, source_target_pairs={{0,16},{4,20},{8,24},{12,28},{16,32},{20,36},{24,40},{28,44},{32,4... | collective-permute-start | bytes 1179656 | tf_op jit(solution)/shard_map/ppermute | solution.py:40
  113.9 23.2 %collective-permute-start.38 = (bf16[512,384]{1,0:T(8,128)(2,1)S(1)}, bf16[512,384]{1,0:T(8,128)(2,1)S(1)}, u32[]{:S(2)}, u32[]{:S(2)}) collective-permute-start(bf16[512,384]{1,0:T(8,128)(2,1)S(1)} %get-tuple-element.132), channel_id=1, source_target_pairs={{16,0},{20,4},{24,8},{28,12},{32,16},{36,20},{40,24},{44,28},{48,3... | collective-permute-start | bytes 1179656 | tf_op jit(solution)/shard_map/ppermute | solution.py:40
  120.7 16.6 %collective-permute-start.34 = (bf16[512,384]{1,0:T(8,128)(2,1)S(1)}, bf16[512,384]{1,0:T(8,128)(2,1)S(1)}, u32[]{:S(2)}, u32[]{:S(2)}) collective-permute-start(bf16[512,384]{1,0:T(8,128)(2,1)S(1)} %collective-permute-done.28.refs_2_), channel_id=1, source_target_pairs={{0,1},{1,0},{2,3},{3,2},{4,5},{5,4},{6,7},{7,6},{8,9},{9,8},{10,11... | collective-permute-start | bytes 1179656 | tf_op jit(solution)/shard_map/ppermute | solution.py:48
  121.8 15.6 %collective-permute-start.36 = (bf16[512,384]{1,0:T(8,128)(2,1)S(1)}, bf16[512,384]{1,0:T(8,128)(2,1)S(1)}, u32[]{:S(2)}, u32[]{:S(2)}) collective-permute-start(bf16[512,384]{1,0:T(8,128)(2,1)S(1)} %collective-permute-done.35.refs_6_), channel_id=1, source_target_pairs={{0,1},{1,0},{2,3},{3,2},{4,5},{5,4},{6,7},{7,6},{8,9},{9,8},{10,11... | collective-permute-start | bytes 1179656 | tf_op jit(solution)/shard_map/ppermute | solution.py:48
  129.5 9.6 %collective-permute-start.33 = (bf16[512,384]{1,0:T(8,128)(2,1)S(1)}, bf16[512,384]{1,0:T(8,128)(2,1)S(1)}, u32[]{:S(2)}, u32[]{:S(2)}) collective-permute-start(bf16[512,384]{1,0:T(8,128)(2,1)S(1)} %collective-permute-done.32.refs_2_), channel_id=1, source_target_pairs={{0,1},{1,0},{2,3},{3,2},{4,5},{5,4},{6,7},{7,6},{8,9},{9,8},{10,11... | collective-permute-start | bytes 1179656 | tf_op jit(solution)/shard_map/ppermute | solution.py:48
  (17 other events, 74.5 us)

commit v8 on v7

--- a/solution.py
+++ b/solution.py
@@ -19,6 +19,7 @@
 R = 64
 FIRST = MID - R
 COST = 10**10
+JOIN_COST = 3 * 10**9
 VMEM = pl.BlockSpec(memory_space=pltpu.VMEM)
 SMEM = pl.BlockSpec(memory_space=pltpu.SMEM)
 HBM = pl.BlockSpec(memory_space=pltpu.HBM)
@@ -114,6 +115,14 @@
 def join_kernel(s0, t0, t1, t2, vec_ref, s_ref, a_ref):
     f = lambda ref: ref[...].astype(F32)
     finish(f(s0) + f(t0) + f(t1) + f(t2), vec_ref, s_ref, a_ref)
+
+
+def early_join_kernel(s0, up, t2, o_ref):
+    o_ref[...] = s0[...].astype(F32) + up[...].astype(F32) + t2[...].astype(F32)
+
+
+def late_join_kernel(part, t1, vec_ref, s_ref, a_ref):
+    finish(part[...] + t1[...].astype(F32), vec_ref, s_ref, a_ref)
 
 
 def joined(refs, fars=1):
@@ -224,7 +233,8 @@
     far_lo, t1 = after((far_lo, t1))
     u0, u1, u2 = call(product_kernel, (a_lo, near_lo, far_lo, *core_swaps(far_lo, 2), w1), halves)
     down = shifted(u2, -hop1)
-    s_lo, a_lo = call(join_kernel, (s_lo, u1, up, t2, vec1), halves[:2])
+    (early,) = call(early_join_kernel, (s_lo, up, t2), halves[:1], dtype=F32, flops=JOIN_COST)
+    s_lo, a_lo = call(late_join_kernel, (early, u1, vec1), halves[:2])
     from_low = shifted(a_lo, hop2)
     from_high = shifted(a_lo, -hop2)
     ch, a_lo = after((ch, a_lo))
@@ -232,19 +242,18 @@
     s_hi, a_hi = call(join_kernel, (s_hi, t1, u0, down, vec1), halves[:2])
     far_hi = chip_swap(a_hi)
     near_hi = core_swap(a_hi)
-    far_hi, from_low, from_high, w2 = after((far_hi, from_low, from_high, w2))
-    a_lo, a_hi = after((a_lo, a_hi))
+    near_own = core_swap(a_lo)
+    far_hi, from_low, from_high, near_own, a_lo, w2 = after((far_hi, from_low, from_high, near_own, a_lo, w2))
 
     far_own = chip_swap(a_lo)
-    near_own = core_swap(a_lo)
     near_low = core_swap(from_low)
     near_high = core_swap(from_high)
     g_hi = [a_hi, near_hi, far_hi, *core_swaps(far_hi, 2)]
-    *g_hi, far_own, near_own, near_low, near_high = after((*g_hi, far_own, near_own, near_low, near_high))
+    *g_hi, near_low, near_high = after((*g_hi, near_low, near_high))
     q0, q_hi, q2 = call(product_kernel, (*g_hi, w2), halves)
     up_hi = shifted(q0, hop2)
     down_hi = shifted(q2, -hop2)
-    from_low, from_high, far_own, q_hi = after((from_low, from_high, far_own, q_hi))
+    from_low, from_high, q_hi = after((from_low, from_high, q_hi))
     far_low = chip_swap(from_low)
     far_high = chip_swap(from_high)
     g_own = (a_lo, near_own, far_own, core_swap(far_own))

time: 143 us -> 139 us (0.972)
  waiting for transfers between devices: 54.6 us -> 50.7 us
    ppermute x8, waiting for transfers between devices: 24.9 us -> 21.4 us  [shifted(): return lax.ppermute(array, 'seq', pairs)]
    ppermute x9, waiting for transfers between devices: 24.9 us -> 23.1 us  [chip_swap(): return lax.ppermute(array, 'ch', [(i, i ^ 2) for i in range(4)])]
    ppermute x9, starting transfers between devices: 10.2 us -> 8.47 us  [chip_swap(): return lax.ppermute(array, 'ch', [(i, i ^ 2) for i in range(4)])]
    ppermute x8, starting transfers between devices: 40.5 us -> 42 us  [shifted(): return lax.ppermute(array, 'seq', pairs)]
    pallas_call x11 -> x12, Pallas kernels: 20.1 us -> 20.1 us  [call(): pl.pallas_call(kernel, out_shape=[jax.ShapeDtypeStruct((r, W), dtype) for...]
  transfers between devices with their start and end apart: 39 -> 39, of which waited for: 19 -> 21; matrix products, arithmetic and copies ran while one was open for 1% -> 1% of each run, Pallas kernels for 13% -> 15%
where the time goes in v8:
time: 139 us; the launch traced here: 138 us
  starting transfers between devices  55.1 us (40%)
  waiting for transfers between devices  50.7 us (36%)
  Pallas kernels  26.3 us (19%)
  other arithmetic  3.93 us (3%)
    ppermute x8, starting transfers between devices, shifted(): return lax.ppermute(array, 'seq', pairs)  42 us
    ppermute x9, waiting for transfers between devices, chip_swap(): return lax.ppermute(array, 'ch', [(i, i ^ 2) for i in range(4)])  23.1 us
    ppermute x8, waiting for transfers between devices, shifted(): return lax.ppermute(array, 'seq', pairs)  21.4 us
    pallas_call x12, Pallas kernels, call(): pl.pallas_call(kernel, out_shape=[jax.ShapeDtypeStruct((r, W), dtype) for...  20.1 us
    ppermute x9, starting transfers between devices, chip_swap(): return lax.ppermute(array, 'ch', [(i, i ^ 2) for i in range(4)])  8.47 us
    pallas_call x3, Pallas kernels, staged(): pl.pallas_call(functools.partial(stage_kernel, layer), out_shape=jax.Shap...  6.21 us
    ppermute x22, waiting for transfers between devices, core_swap(): return lax.ppermute(array, 'ch', [(i, i ^ 1) for i in range(4)])  6.19 us
    ppermute x22, starting transfers between devices, core_swap(): return lax.ppermute(array, 'ch', [(i, i ^ 1) for i in range(4)])  4.58 us
  transfers between devices with their start and end apart: 39, of which 21 were waited for; matrix products, arithmetic and copies ran while one was open for 1% of the time, Pallas kernels for 15%

profile of v8, /device:TPU:6, one launch (start us, length us, event | category | flops | bytes accessed | tf_op | source)
XLA Modules:
  0.0 137.5 jit_solution(14456659813193932774)
XLA Ops:
  0.9 2.1 %fusion.1.refs_0_ = bf16[576,384]{1,0:T(8,128)(2,1)S(1)} fusion(f32[384]{0:T(512)S(1)} %get-tuple-element.145, f32[384]{0:T(512)S(1)} %get-tuple-element.139, bf16[1024,384]{1,0:T(8,128)(2,1)} %refs_13_.1), kind=kLoop, calls=%fused_computation.3 | loop fusion | flops 7741440 | bytes 887808 | tf_op jit(solution)/shard_map/convert_element_type | solution.py:193
  4.6 4.8 %collective-permute-start.1 = (bf16[64,384]{1,0:T(8,128)(2,1)S(1)}, bf16[64,384]{1,0:T(8,128)(2,1)S(1)}, u32[]{:S(2)}, u32[]{:S(2)}) collective-permute-start(bf16[64,384]{1,0:T(8,128)(2,1)S(1)} %slice.86), channel_id=1, source_target_pairs={{0,4},{4,8},{8,12},{12,16},{16,20},{20,24},{24,28},{28,32},{32,36}... | collective-permute-start | bytes 147464 | tf_op jit(solution)/shard_map/ppermute | solution.py:41
  11.3 7.5 %collective-permute-start.2 = (bf16[64,384]{1,0:T(8,128)(2,1)S(1)}, bf16[64,384]{1,0:T(8,128)(2,1)S(1)}, u32[]{:S(2)}, u32[]{:S(2)}) collective-permute-start(bf16[64,384]{1,0:T(8,128)(2,1)S(1)} %slice.87), channel_id=1, source_target_pairs={{4,0},{8,4},{12,8},{16,12},{20,16},{24,20},{28,24},{32,28},{36,32}... | collective-permute-start | bytes 147464 | tf_op jit(solution)/shard_map/ppermute | solution.py:41
  18.8 2.1 %shard_map.55.refs_11_.refs_15_ = bf16[1536,1152]{1,0:T(8,128)(2,1)S(1)} custom-call(s32[1]{0:T(128)} %bitcast.ch_ref, bf16[3,3,1536,384]{3,2,1,0:T(8,128)(2,1)} %w_hbm.5), custom_call_target="tpu_custom_call" | custom-call | tf_op jit(solution)/shard_map/pallas_call | solution.py:172
  23.1 3.6 %collective-permute-done.3.refs_7_ = bf16[128,384]{1,0:T(8,128)(2,1)S(1)} collective-permute-done((bf16[128,384]{1,0:T(8,128)(2,1)S(1)}, bf16[128,384]{1,0:T(8,128)(2,1)S(1)}, u32[]{:S(2)}, u32[]{:S(2)}) %collective-permute-start.3) | collective-permute-done | bytes 98336 | tf_op jit(solution)/shard_map/ppermute | solution.py:45
  28.8 4.6 %collective-permute-done.9.refs_11_ = bf16[448,384]{1,0:T(8,128)(2,1)S(1)} collective-permute-done((bf16[448,384]{1,0:T(8,128)(2,1)S(1)}, bf16[448,384]{1,0:T(8,128)(2,1)S(1)}, u32[]{:S(2)}, u32[]{:S(2)}) %collective-permute-start.9) | collective-permute-done | bytes 344096 | tf_op jit(solution)/shard_map/ppermute | solution.py:45
  33.4 3.6 %shard_map.57 = (bf16[512,384]{1,0:T(8,128)(2,1)S(1)}, bf16[512,384]{1,0:T(8,128)(2,1)S(1)}) custom-call(bf16[576,384]{1,0:T(8,128)(2,1)S(1)} %fusion.1.refs_0_, bf16[576,384]{1,0:T(8,128)(2,1)S(1)} %collective-permute-done.4.refs_1_, bf16[576,384]{1,0:T(8,128)(2,1)S(1)} %collective-permute-done.refs_2_, ...), custom_call_target="tpu_custom_call" | custom-call | bytes 1024 | tf_op jit(solution)/shard_map/pallas_call | solution.py:160
  39.5 3.6 %shard_map.58 = (bf16[512,384]{1,0:T(8,128)(2,1)S(1)}, bf16[512,384]{1,0:T(8,128)(2,1)S(1)}) custom-call(bf16[576,384]{1,0:T(8,128)(2,1)S(1)} %fusion.1.refs_0_, bf16[576,384]{1,0:T(8,128)(2,1)S(1)} %collective-permute-done.4.refs_1_, bf16[576,384]{1,0:T(8,128)(2,1)S(1)} %collective-permute-done.refs_2_, ...), custom_call_target="tpu_custom_call" | custom-call | bytes 1024 | tf_op jit(solution)/shard_map/pallas_call | solution.py:160
  44.9 2.0 %shard_map.59.refs_5_ = bf16[1536,1152]{1,0:T(8,128)(2,1)S(1)} custom-call(s32[1]{0:T(128)} %bitcast.ch_ref, bf16[3,3,1536,384]{3,2,1,0:T(8,128)(2,1)} %w_hbm.5), custom_call_target="tpu_custom_call" | custom-call | tf_op jit(solution)/shard_map/pallas_call | solution.py:172
  47.0 2.0 %collective-permute-done.14.refs_2_ = bf16[512,384]{1,0:T(8,128)(2,1)S(1)} collective-permute-done((bf16[512,384]{1,0:T(8,128)(2,1)S(1)}, bf16[512,384]{1,0:T(8,128)(2,1)S(1)}, u32[]{:S(2)}, u32[]{:S(2)}) %collective-permute-start.14) | collective-permute-done | bytes 393248 | tf_op jit(solution)/shard_map/ppermute | solution.py:45
  50.8 2.2 %shard_map.60 = (bf16[512,384]{1,0:T(8,128)(2,1)S(1)}, bf16[512,384]{1,0:T(8,128)(2,1)S(1)}, bf16[512,384]{1,0:T(8,128)(2,1)S(1)}) custom-call(bf16[512,384]{1,0:T(8,128)(2,1)S(1)} %get-tuple-element.88.refs_0_, bf16[512,384]{1,0:T(8,128)(2,1)S(1)} %collective-permute-done.13.refs_1_, bf16[512,384]{1,0:T(8,128)(2,1)S(1)} %collective-permute-done.14.refs_2_, ...), custom_call_target="tpu_custom_call" | custom-call | bytes 1024 | tf_op jit(solution)/shard_map/pallas_call | solution.py:160
  53.0 1.9 %collective-permute-start.22 = (bf16[512,384]{1,0:T(8,128)(2,1)S(1)}, bf16[512,384]{1,0:T(8,128)(2,1)S(1)}, u32[]{:S(2)}, u32[]{:S(2)}) collective-permute-start(bf16[512,384]{1,0:T(8,128)(2,1)S(1)} %get-tuple-element.100), channel_id=1, source_target_pairs={{0,4},{4,8},{8,12},{12,16},{16,20},{20,24},{24,28},{28,32},{32,36}... | collective-permute-start | bytes 1179656 | tf_op jit(solution)/shard_map/ppermute | solution.py:41
  58.0 2.2 %shard_map.61 = (bf16[512,384]{1,0:T(8,128)(2,1)S(1)}, bf16[512,384]{1,0:T(8,128)(2,1)S(1)}, bf16[512,384]{1,0:T(8,128)(2,1)S(1)}) custom-call(bf16[512,384]{1,0:T(8,128)(2,1)S(1)} %get-tuple-element.94.refs_0_, bf16[512,384]{1,0:T(8,128)(2,1)S(1)} %collective-permute-done.17.refs_1_, bf16[512,384]{1,0:T(8,128)(2,1)S(1)} %collective-permute-done.12.refs_2_, ...), custom_call_target="tpu_custom_call" | custom-call | bytes 1024 | tf_op jit(solution)/shard_map/pallas_call | solution.py:160
  60.2 7.2 %collective-permute-start.20 = (bf16[512,384]{1,0:T(8,128)(2,1)S(1)}, bf16[512,384]{1,0:T(8,128)(2,1)S(1)}, u32[]{:S(2)}, u32[]{:S(2)}) collective-permute-start(bf16[512,384]{1,0:T(8,128)(2,1)S(1)} %get-tuple-element.97), channel_id=1, source_target_pairs={{4,0},{8,4},{12,8},{16,12},{20,16},{24,20},{28,24},{32,28},{36,32}... | collective-permute-start | bytes 1179656 | tf_op jit(solution)/shard_map/ppermute | solution.py:41
  67.5 4.9 %collective-permute-done.22.up = bf16[512,384]{1,0:T(8,128)(2,1)S(1)} collective-permute-done((bf16[512,384]{1,0:T(8,128)(2,1)S(1)}, bf16[512,384]{1,0:T(8,128)(2,1)S(1)}, u32[]{:S(2)}, u32[]{:S(2)}) %collective-permute-start.22) | collective-permute-done | bytes 393248 | tf_op jit(solution)/shard_map/ppermute | solution.py:41
  75.6 6.9 %collective-permute-start.24 = (bf16[512,384]{1,0:T(8,128)(2,1)S(1)}, bf16[512,384]{1,0:T(8,128)(2,1)S(1)}, u32[]{:S(2)}, u32[]{:S(2)}) collective-permute-start(bf16[512,384]{1,0:T(8,128)(2,1)S(1)} %get-tuple-element.118.refs_0_), channel_id=1, source_target_pairs={{16,0},{20,4},{24,8},{28,12},{32,16},{36,20},{40,24},{44,28},{48,3... | collective-permute-start | bytes 1179656 | tf_op jit(solution)/shard_map/ppermute | solution.py:41
  82.8 2.3 %collective-permute-done.20.t2 = bf16[512,384]{1,0:T(8,128)(2,1)S(1)} collective-permute-done((bf16[512,384]{1,0:T(8,128)(2,1)S(1)}, bf16[512,384]{1,0:T(8,128)(2,1)S(1)}, u32[]{:S(2)}, u32[]{:S(2)}) %collective-permute-start.20) | collective-permute-done | bytes 393248 | tf_op jit(solution)/shard_map/ppermute | solution.py:41
  86.4 2.1 %shard_map.65.refs_5_.refs_10_.refs_6_ = bf16[1536,1152]{1,0:T(8,128)(2,1)S(1)} custom-call(s32[1]{0:T(128)} %bitcast.ch_ref, bf16[3,3,1536,384]{3,2,1,0:T(8,128)(2,1)} %w_hbm.5), custom_call_target="tpu_custom_call" | custom-call | tf_op jit(solution)/shard_map/pallas_call | solution.py:172
  88.6 3.7 %collective-permute-done.23.refs_4_ = bf16[512,384]{1,0:T(8,128)(2,1)S(1)} collective-permute-done((bf16[512,384]{1,0:T(8,128)(2,1)S(1)}, bf16[512,384]{1,0:T(8,128)(2,1)S(1)}, u32[]{:S(2)}, u32[]{:S(2)}) %collective-permute-start.23) | collective-permute-done | bytes 393248 | tf_op jit(solution)/shard_map/ppermute | solution.py:41
  98.5 2.2 %shard_map.66 = (bf16[512,384]{1,0:T(8,128)(2,1)S(1)}, bf16[512,384]{1,0:T(8,128)(2,1)S(1)}, bf16[512,384]{1,0:T(8,128)(2,1)S(1)}) custom-call(bf16[512,384]{1,0:T(8,128)(2,1)S(1)} %get-tuple-element.109.refs_0_, bf16[512,384]{1,0:T(8,128)(2,1)S(1)} %collective-permute-done.26.refs_1_, bf16[512,384]{1,0:T(8,128)(2,1)S(1)} %collective-permute-done.21.refs_2_, ...), custom_call_target="tpu_custom_call" | custom-call | bytes 1024 | tf_op jit(solution)/shard_map/pallas_call | solution.py:160
  102.8 9.8 %collective-permute-start.37 = (bf16[512,384]{1,0:T(8,128)(2,1)S(1)}, bf16[512,384]{1,0:T(8,128)(2,1)S(1)}, u32[]{:S(2)}, u32[]{:S(2)}) collective-permute-start(bf16[512,384]{1,0:T(8,128)(2,1)S(1)} %get-tuple-element.125), channel_id=1, source_target_pairs={{0,16},{4,20},{8,24},{12,28},{16,32},{20,36},{24,40},{28,44},{32,4... | collective-permute-start | bytes 1179656 | tf_op jit(solution)/shard_map/ppermute | solution.py:41
  114.7 2.5 %collective-permute-done.35.refs_6_ = bf16[512,384]{1,0:T(8,128)(2,1)S(1)} collective-permute-done((bf16[512,384]{1,0:T(8,128)(2,1)S(1)}, bf16[512,384]{1,0:T(8,128)(2,1)S(1)}, u32[]{:S(2)}, u32[]{:S(2)}) %collective-permute-start.35) | collective-permute-done | bytes 393248 | tf_op jit(solution)/shard_map/ppermute | solution.py:45
  117.2 7.6 %collective-permute-done.31.refs_2_ = bf16[512,384]{1,0:T(8,128)(2,1)S(1)} collective-permute-done((bf16[512,384]{1,0:T(8,128)(2,1)S(1)}, bf16[512,384]{1,0:T(8,128)(2,1)S(1)}, u32[]{:S(2)}, u32[]{:S(2)}) %collective-permute-start.31) | collective-permute-done | bytes 393248 | tf_op jit(solution)/shard_map/ppermute | solution.py:45
  124.8 8.8 %collective-permute-done.38.down_hi = bf16[512,384]{1,0:T(8,128)(2,1)S(1)} collective-permute-done((bf16[512,384]{1,0:T(8,128)(2,1)S(1)}, bf16[512,384]{1,0:T(8,128)(2,1)S(1)}, u32[]{:S(2)}, u32[]{:S(2)}) %collective-permute-start.38) | collective-permute-done | bytes 393248 | tf_op jit(solution)/shard_map/ppermute | solution.py:41
  (85 shorter events, 36.9 us)
Async XLA Ops:
  3.0 23.7 %collective-permute-start = (bf16[576,384]{1,0:T(8,128)(2,1)S(1)}, bf16[576,384]{1,0:T(8,128)(2,1)S(1)}, u32[]{:S(2)}, u32[]{:S(2)}) collective-permute-start(bf16[576,384]{1,0:T(8,128)(2,1)S(1)} %fusion.1.refs_0_), channel_id=1, source_target_pairs={{0,2},{1,3},{2,0},{3,1},{4,6},{5,7},{6,4},{7,5},{8,10},{9,11},{10,... | collective-permute-start | bytes 1327112 | tf_op jit(solution)/shard_map/ppermute | solution.py:45
  4.6 22.1 %collective-permute-start.4 = (bf16[576,384]{1,0:T(8,128)(2,1)S(1)}, bf16[576,384]{1,0:T(8,128)(2,1)S(1)}, u32[]{:S(2)}, u32[]{:S(2)}) collective-permute-start(bf16[576,384]{1,0:T(8,128)(2,1)S(1)} %fusion.1.refs_0_), channel_id=1, source_target_pairs={{0,1},{1,0},{2,3},{3,2},{4,5},{5,4},{6,7},{7,6},{8,9},{9,8},{10,11... | collective-permute-start | bytes 1327112 | tf_op jit(solution)/shard_map/ppermute | solution.py:49
  4.6 16.3 %collective-permute-start.1 = (bf16[64,384]{1,0:T(8,128)(2,1)S(1)}, bf16[64,384]{1,0:T(8,128)(2,1)S(1)}, u32[]{:S(2)}, u32[]{:S(2)}) collective-permute-start(bf16[64,384]{1,0:T(8,128)(2,1)S(1)} %slice.86), channel_id=1, source_target_pairs={{0,4},{4,8},{8,12},{12,16},{16,20},{20,24},{24,28},{28,32},{32,36}... | collective-permute-start | bytes 147464 | tf_op jit(solution)/shard_map/ppermute | solution.py:41
  11.3 9.7 %collective-permute-start.2 = (bf16[64,384]{1,0:T(8,128)(2,1)S(1)}, bf16[64,384]{1,0:T(8,128)(2,1)S(1)}, u32[]{:S(2)}, u32[]{:S(2)}) collective-permute-start(bf16[64,384]{1,0:T(8,128)(2,1)S(1)} %slice.87), channel_id=1, source_target_pairs={{4,0},{8,4},{12,8},{16,12},{20,16},{24,20},{28,24},{32,28},{36,32}... | collective-permute-start | bytes 147464 | tf_op jit(solution)/shard_map/ppermute | solution.py:41
  21.2 12.1 %collective-permute-start.9 = (bf16[448,384]{1,0:T(8,128)(2,1)S(1)}, bf16[448,384]{1,0:T(8,128)(2,1)S(1)}, u32[]{:S(2)}, u32[]{:S(2)}) collective-permute-start(bf16[448,384]{1,0:T(8,128)(2,1)S(1)} %fusion.4.refs_9_), channel_id=1, source_target_pairs={{0,2},{1,3},{2,0},{3,1},{4,6},{5,7},{6,4},{7,5},{8,10},{9,11},{10,... | collective-permute-start | bytes 1032200 | tf_op jit(solution)/shard_map/ppermute | solution.py:45
  26.8 6.6 %collective-permute-start.5 = (bf16[288,384]{1,0:T(8,128)(2,1)S(1)}, bf16[288,384]{1,0:T(8,128)(2,1)S(1)}, u32[]{:S(2)}, u32[]{:S(2)}) collective-permute-start(bf16[288,384]{1,0:T(8,128)(2,1)S(1)} %get-tuple-element.128), channel_id=1, source_target_pairs={{0,1},{1,0},{2,3},{3,2},{4,5},{5,4},{6,7},{7,6},{8,9},{9,8},{10,11... | collective-permute-start | bytes 663560 | tf_op jit(solution)/shard_map/ppermute | solution.py:49
  37.0 12.0 %collective-permute-start.14 = (bf16[512,384]{1,0:T(8,128)(2,1)S(1)}, bf16[512,384]{1,0:T(8,128)(2,1)S(1)}, u32[]{:S(2)}, u32[]{:S(2)}) collective-permute-start(bf16[512,384]{1,0:T(8,128)(2,1)S(1)} %get-tuple-element.88.refs_0_), channel_id=1, source_target_pairs={{0,2},{1,3},{2,0},{3,1},{4,6},{5,7},{6,4},{7,5},{8,10},{9,11},{10,... | collective-permute-start | bytes 1179656 | tf_op jit(solution)/shard_map/ppermute | solution.py:45
  37.9 11.9 %collective-permute-start.13 = (bf16[512,384]{1,0:T(8,128)(2,1)S(1)}, bf16[512,384]{1,0:T(8,128)(2,1)S(1)}, u32[]{:S(2)}, u32[]{:S(2)}) collective-permute-start(bf16[512,384]{1,0:T(8,128)(2,1)S(1)} %get-tuple-element.88.refs_0_), channel_id=1, source_target_pairs={{0,1},{1,0},{2,3},{3,2},{4,5},{5,4},{6,7},{7,6},{8,9},{9,8},{10,11... | collective-permute-start | bytes 1179656 | tf_op jit(solution)/shard_map/ppermute | solution.py:49
  43.1 13.1 %collective-permute-start.12 = (bf16[512,384]{1,0:T(8,128)(2,1)S(1)}, bf16[512,384]{1,0:T(8,128)(2,1)S(1)}, u32[]{:S(2)}, u32[]{:S(2)}) collective-permute-start(bf16[512,384]{1,0:T(8,128)(2,1)S(1)} %get-tuple-element.94.refs_0_), channel_id=1, source_target_pairs={{0,2},{1,3},{2,0},{3,1},{4,6},{5,7},{6,4},{7,5},{8,10},{9,11},{10,... | collective-permute-start | bytes 1179656 | tf_op jit(solution)/shard_map/ppermute | solution.py:45
  49.6 7.2 %collective-permute-start.17 = (bf16[512,384]{1,0:T(8,128)(2,1)S(1)}, bf16[512,384]{1,0:T(8,128)(2,1)S(1)}, u32[]{:S(2)}, u32[]{:S(2)}) collective-permute-start(bf16[512,384]{1,0:T(8,128)(2,1)S(1)} %get-tuple-element.94.refs_0_), channel_id=1, source_target_pairs={{0,1},{1,0},{2,3},{3,2},{4,5},{5,4},{6,7},{7,6},{8,9},{9,8},{10,11... | collective-permute-start | bytes 1179656 | tf_op jit(solution)/shard_map/ppermute | solution.py:49
  53.0 19.4 %collective-permute-start.22 = (bf16[512,384]{1,0:T(8,128)(2,1)S(1)}, bf16[512,384]{1,0:T(8,128)(2,1)S(1)}, u32[]{:S(2)}, u32[]{:S(2)}) collective-permute-start(bf16[512,384]{1,0:T(8,128)(2,1)S(1)} %get-tuple-element.100), channel_id=1, source_target_pairs={{0,4},{4,8},{8,12},{12,16},{16,20},{20,24},{24,28},{28,32},{32,36}... | collective-permute-start | bytes 1179656 | tf_op jit(solution)/shard_map/ppermute | solution.py:41
  60.2 24.9 %collective-permute-start.20 = (bf16[512,384]{1,0:T(8,128)(2,1)S(1)}, bf16[512,384]{1,0:T(8,128)(2,1)S(1)}, u32[]{:S(2)}, u32[]{:S(2)}) collective-permute-start(bf16[512,384]{1,0:T(8,128)(2,1)S(1)} %get-tuple-element.97), channel_id=1, source_target_pairs={{4,0},{8,4},{12,8},{16,12},{20,16},{24,20},{28,24},{32,28},{36,32}... | collective-permute-start | bytes 1179656 | tf_op jit(solution)/shard_map/ppermute | solution.py:41
  73.6 18.7 %collective-permute-start.23 = (bf16[512,384]{1,0:T(8,128)(2,1)S(1)}, bf16[512,384]{1,0:T(8,128)(2,1)S(1)}, u32[]{:S(2)}, u32[]{:S(2)}) collective-permute-start(bf16[512,384]{1,0:T(8,128)(2,1)S(1)} %get-tuple-element.118.refs_0_), channel_id=1, source_target_pairs={{0,16},{4,20},{8,24},{12,28},{16,32},{20,36},{24,40},{28,44},{32,4... | collective-permute-start | bytes 1179656 | tf_op jit(solution)/shard_map/ppermute | solution.py:41
  75.6 18.4 %collective-permute-start.24 = (bf16[512,384]{1,0:T(8,128)(2,1)S(1)}, bf16[512,384]{1,0:T(8,128)(2,1)S(1)}, u32[]{:S(2)}, u32[]{:S(2)}) collective-permute-start(bf16[512,384]{1,0:T(8,128)(2,1)S(1)} %get-tuple-element.118.refs_0_), channel_id=1, source_target_pairs={{16,0},{20,4},{24,8},{28,12},{32,16},{36,20},{40,24},{44,28},{48,3... | collective-permute-start | bytes 1179656 | tf_op jit(solution)/shard_map/ppermute | solution.py:41
  86.3 9.3 %collective-permute-start.21 = (bf16[512,384]{1,0:T(8,128)(2,1)S(1)}, bf16[512,384]{1,0:T(8,128)(2,1)S(1)}, u32[]{:S(2)}, u32[]{:S(2)}) collective-permute-start(bf16[512,384]{1,0:T(8,128)(2,1)S(1)} %get-tuple-element.109.refs_0_), channel_id=1, source_target_pairs={{0,2},{1,3},{2,0},{3,1},{4,6},{5,7},{6,4},{7,5},{8,10},{9,11},{10,... | collective-permute-start | bytes 1179656 | tf_op jit(solution)/shard_map/ppermute | solution.py:45
  88.5 8.3 %collective-permute-start.26 = (bf16[512,384]{1,0:T(8,128)(2,1)S(1)}, bf16[512,384]{1,0:T(8,128)(2,1)S(1)}, u32[]{:S(2)}, u32[]{:S(2)}) collective-permute-start(bf16[512,384]{1,0:T(8,128)(2,1)S(1)} %get-tuple-element.109.refs_0_), channel_id=1, source_target_pairs={{0,1},{1,0},{2,3},{3,2},{4,5},{5,4},{6,7},{7,6},{8,9},{9,8},{10,11... | collective-permute-start | bytes 1179656 | tf_op jit(solution)/shard_map/ppermute | solution.py:49
  96.8 17.8 %collective-permute-start.33 = (bf16[512,384]{1,0:T(8,128)(2,1)S(1)}, bf16[512,384]{1,0:T(8,128)(2,1)S(1)}, u32[]{:S(2)}, u32[]{:S(2)}) collective-permute-start(bf16[512,384]{1,0:T(8,128)(2,1)S(1)} %get-tuple-element.118.refs_0_), channel_id=1, source_target_pairs={{0,2},{1,3},{2,0},{3,1},{4,6},{5,7},{6,4},{7,5},{8,10},{9,11},{10,... | collective-permute-start | bytes 1179656 | tf_op jit(solution)/shard_map/ppermute | solution.py:45
  100.7 16.5 %collective-permute-start.35 = (bf16[512,384]{1,0:T(8,128)(2,1)S(1)}, bf16[512,384]{1,0:T(8,128)(2,1)S(1)}, u32[]{:S(2)}, u32[]{:S(2)}) collective-permute-start(bf16[512,384]{1,0:T(8,128)(2,1)S(1)} %collective-permute-done.23.refs_4_), channel_id=1, source_target_pairs={{0,2},{1,3},{2,0},{3,1},{4,6},{5,7},{6,4},{7,5},{8,10},{9,11},{10,... | collective-permute-start | bytes 1179656 | tf_op jit(solution)/shard_map/ppermute | solution.py:45
  101.1 23.6 %collective-permute-start.31 = (bf16[512,384]{1,0:T(8,128)(2,1)S(1)}, bf16[512,384]{1,0:T(8,128)(2,1)S(1)}, u32[]{:S(2)}, u32[]{:S(2)}) collective-permute-start(bf16[512,384]{1,0:T(8,128)(2,1)S(1)} %collective-permute-done.24.refs_0_), channel_id=1, source_target_pairs={{0,2},{1,3},{2,0},{3,1},{4,6},{5,7},{6,4},{7,5},{8,10},{9,11},{10,... | collective-permute-start | bytes 1179656 | tf_op jit(solution)/shard_map/ppermute | solution.py:45
  102.8 22.0 %collective-permute-start.37 = (bf16[512,384]{1,0:T(8,128)(2,1)S(1)}, bf16[512,384]{1,0:T(8,128)(2,1)S(1)}, u32[]{:S(2)}, u32[]{:S(2)}) collective-permute-start(bf16[512,384]{1,0:T(8,128)(2,1)S(1)} %get-tuple-element.125), channel_id=1, source_target_pairs={{0,16},{4,20},{8,24},{12,28},{16,32},{20,36},{24,40},{28,44},{32,4... | collective-permute-start | bytes 1179656 | tf_op jit(solution)/shard_map/ppermute | solution.py:41
  112.6 20.9 %collective-permute-start.38 = (bf16[512,384]{1,0:T(8,128)(2,1)S(1)}, bf16[512,384]{1,0:T(8,128)(2,1)S(1)}, u32[]{:S(2)}, u32[]{:S(2)}) collective-permute-start(bf16[512,384]{1,0:T(8,128)(2,1)S(1)} %get-tuple-element.126), channel_id=1, source_target_pairs={{16,0},{20,4},{24,8},{28,12},{32,16},{36,20},{40,24},{44,28},{48,3... | collective-permute-start | bytes 1179656 | tf_op jit(solution)/shard_map/ppermute | solution.py:41
  114.6 19.2 %collective-permute-start.34 = (bf16[512,384]{1,0:T(8,128)(2,1)S(1)}, bf16[512,384]{1,0:T(8,128)(2,1)S(1)}, u32[]{:S(2)}, u32[]{:S(2)}) collective-permute-start(bf16[512,384]{1,0:T(8,128)(2,1)S(1)} %collective-permute-done.33.refs_2_), channel_id=1, source_target_pairs={{0,1},{1,0},{2,3},{3,2},{4,5},{5,4},{6,7},{7,6},{8,9},{9,8},{10,11... | collective-permute-start | bytes 1179656 | tf_op jit(solution)/shard_map/ppermute | solution.py:49
  117.2 16.7 %collective-permute-start.36 = (bf16[512,384]{1,0:T(8,128)(2,1)S(1)}, bf16[512,384]{1,0:T(8,128)(2,1)S(1)}, u32[]{:S(2)}, u32[]{:S(2)}) collective-permute-start(bf16[512,384]{1,0:T(8,128)(2,1)S(1)} %collective-permute-done.35.refs_6_), channel_id=1, source_target_pairs={{0,1},{1,0},{2,3},{3,2},{4,5},{5,4},{6,7},{7,6},{8,9},{9,8},{10,11... | collective-permute-start | bytes 1179656 | tf_op jit(solution)/shard_map/ppermute | solution.py:49
  124.8 10.9 %collective-permute-start.32 = (bf16[512,384]{1,0:T(8,128)(2,1)S(1)}, bf16[512,384]{1,0:T(8,128)(2,1)S(1)}, u32[]{:S(2)}, u32[]{:S(2)}) collective-permute-start(bf16[512,384]{1,0:T(8,128)(2,1)S(1)} %collective-permute-done.31.refs_2_), channel_id=1, source_target_pairs={{0,1},{1,0},{2,3},{3,2},{4,5},{5,4},{6,7},{7,6},{8,9},{9,8},{10,11... | collective-permute-start | bytes 1179656 | tf_op jit(solution)/shard_map/ppermute | solution.py:49
  (17 other events, 68.8 us)

commit v9 on v8

--- a/solution.py
+++ b/solution.py
@@ -19,6 +19,7 @@
 R = 64
 FIRST = MID - R
 COST = 10**10
+RIM_COST = 10**10
 JOIN_COST = 3 * 10**9
 VMEM = pl.BlockSpec(memory_space=pltpu.VMEM)
 SMEM = pl.BlockSpec(memory_space=pltpu.SMEM)
@@ -192,15 +193,15 @@
     def entry(x):
         return gelu(x.astype(F32) * pre_scale[0] + pre_shift[0]).astype(BF16)
 
+    rim = entry(jnp.concatenate([bins_in[ROWS - R :], bins_in[:R]], axis=0))
+    low = shifted(rim[:R], 1)
+    high = shifted(rim[R:], -1)
+    (act_2,) = call(rims_kernel, (low, high), [2 * R], flops=RIM_COST)
     act_1 = entry(bins_in[FIRST:])
     far_1 = chip_swap(act_1)
     near_1 = core_swap(act_1)
     act_3 = entry(bins_in[:FIRST])
-    low = shifted(act_1[-R:], 1)
-    high = shifted(act_3[:R], -1)
     w0 = staged(0, ch, conv_weight)
-    low, high, w0 = after((low, high, w0))
-    (act_2,) = call(rims_kernel, (low, high), [2 * R])
     act_2, act_3 = after((act_2, act_3))
     far_2 = chip_swap(act_2)
     near_2 = core_swap(act_2)

time: 139 us -> 133 us (0.957)
  waiting for transfers between devices: 50.7 us -> 46.1 us
  starting transfers between devices: 55.1 us -> 52.6 us
    ppermute x8, waiting for transfers between devices: 21.4 us -> 17.4 us  [shifted(): return lax.ppermute(array, 'seq', pairs)]
    ppermute x8, starting transfers between devices: 42 us -> 39.3 us  [shifted(): return lax.ppermute(array, 'seq', pairs)]
    convert_element_type x2 -> x3, other arithmetic: 3.91 us -> 4.17 us  [entry(): return gelu(x.astype(F32) * pre_scale[0] + pre_shift[0]).astype(BF16)]
  transfers between devices with their start and end apart: 39 -> 39, of which waited for: 21 -> 19; matrix products, arithmetic and copies ran while one was open for 1% -> 2% of each run, Pallas kernels for 15% -> 16%
where the time goes in v9:
time: 133 us; the launch traced here: 131 us
  starting transfers between devices  52.6 us (40%)
  waiting for transfers between devices  46.1 us (35%)
  Pallas kernels  26.3 us (20%)
  other arithmetic  4.19 us (3%)
  local copies, waits for them, and re-layouts  1.9 us (1%)
    ppermute x8, starting transfers between devices, shifted(): return lax.ppermute(array, 'seq', pairs)  39.3 us
    ppermute x9, waiting for transfers between devices, chip_swap(): return lax.ppermute(array, 'ch', [(i, i ^ 2) for i in range(4)])  22.3 us
    pallas_call x12, Pallas kernels, call(): pl.pallas_call(kernel, out_shape=[jax.ShapeDtypeStruct((r, W), dtype) for...  20.1 us
    ppermute x8, waiting for transfers between devices, shifted(): return lax.ppermute(array, 'seq', pairs)  17.4 us
    ppermute x9, starting transfers between devices, chip_swap(): return lax.ppermute(array, 'ch', [(i, i ^ 2) for i in range(4)])  8.18 us
    ppermute x22, waiting for transfers between devices, core_swap(): return lax.ppermute(array, 'ch', [(i, i ^ 1) for i in range(4)])  6.35 us
    pallas_call x3, Pallas kernels, staged(): pl.pallas_call(functools.partial(stage_kernel, layer), out_shape=jax.Shap...  6.21 us
    ppermute x22, starting transfers between devices, core_swap(): return lax.ppermute(array, 'ch', [(i, i ^ 1) for i in range(4)])  5.17 us
  transfers between devices with their start and end apart: 39, of which 19 were waited for; matrix products, arithmetic and copies ran while one was open for 2% of the time, Pallas kernels for 16%

profile of v9, /device:TPU:6, one launch (start us, length us, event | category | flops | bytes accessed | tf_op | source)
XLA Modules:
  0.0 131.4 jit_solution(6442873193660491163)
XLA Ops:
  0.9 2.1 %fusion.1.refs_0_ = bf16[576,384]{1,0:T(8,128)(2,1)S(1)} fusion(f32[384]{0:T(512)S(1)} %get-tuple-element.143, f32[384]{0:T(512)S(1)} %get-tuple-element.137, bf16[1024,384]{1,0:T(8,128)(2,1)} %refs_13_.1), kind=kLoop, calls=%fused_computation.3 | loop fusion | flops 7741440 | bytes 887808 | tf_op jit(solution)/shard_map/convert_element_type | solution.py:194
  5.7 4.8 %collective-permute-start.1 = (bf16[64,384]{1,0:T(8,128)(2,1)S(1)}, bf16[64,384]{1,0:T(8,128)(2,1)S(1)}, u32[]{:S(2)}, u32[]{:S(2)}) collective-permute-start(bf16[64,384]{1,0:T(8,128)(2,1)S(1)} %get-tuple-element.132), channel_id=1, source_target_pairs={{0,4},{4,8},{8,12},{12,16},{16,20},{20,24},{24,28},{28,32},{32,36}... | collective-permute-start | bytes 147464 | tf_op jit(solution)/shard_map/ppermute | solution.py:42
  10.6 7.5 %collective-permute-start.2 = (bf16[64,384]{1,0:T(8,128)(2,1)S(1)}, bf16[64,384]{1,0:T(8,128)(2,1)S(1)}, u32[]{:S(2)}, u32[]{:S(2)}) collective-permute-start(bf16[64,384]{1,0:T(8,128)(2,1)S(1)} %get-tuple-element.131), channel_id=1, source_target_pairs={{4,0},{8,4},{12,8},{16,12},{20,16},{24,20},{28,24},{32,28},{36,32}... | collective-permute-start | bytes 147464 | tf_op jit(solution)/shard_map/ppermute | solution.py:42
  22.0 3.6 %collective-permute-done.3.refs_7_ = bf16[128,384]{1,0:T(8,128)(2,1)S(1)} collective-permute-done((bf16[128,384]{1,0:T(8,128)(2,1)S(1)}, bf16[128,384]{1,0:T(8,128)(2,1)S(1)}, u32[]{:S(2)}, u32[]{:S(2)}) %collective-permute-start.3) | collective-permute-done | bytes 98336 | tf_op jit(solution)/shard_map/ppermute | solution.py:46
  26.3 2.1 %shard_map.56.refs_11_.refs_15_ = bf16[1536,1152]{1,0:T(8,128)(2,1)S(1)} custom-call(s32[1]{0:T(128)} %bitcast.ch_ref, bf16[3,3,1536,384]{3,2,1,0:T(8,128)(2,1)} %w_hbm.5), custom_call_target="tpu_custom_call" | custom-call | tf_op jit(solution)/shard_map/pallas_call | solution.py:173
  29.8 2.5 %collective-permute-done.9.refs_11_ = bf16[448,384]{1,0:T(8,128)(2,1)S(1)} collective-permute-done((bf16[448,384]{1,0:T(8,128)(2,1)S(1)}, bf16[448,384]{1,0:T(8,128)(2,1)S(1)}, u32[]{:S(2)}, u32[]{:S(2)}) %collective-permute-start.9) | collective-permute-done | bytes 344096 | tf_op jit(solution)/shard_map/ppermute | solution.py:46
  32.3 3.6 %shard_map.57 = (bf16[512,384]{1,0:T(8,128)(2,1)S(1)}, bf16[512,384]{1,0:T(8,128)(2,1)S(1)}) custom-call(bf16[576,384]{1,0:T(8,128)(2,1)S(1)} %fusion.1.refs_0_, bf16[576,384]{1,0:T(8,128)(2,1)S(1)} %collective-permute-done.4.refs_1_, bf16[576,384]{1,0:T(8,128)(2,1)S(1)} %collective-permute-done.refs_2_, ...), custom_call_target="tpu_custom_call" | custom-call | bytes 1024 | tf_op jit(solution)/shard_map/pallas_call | solution.py:161
  38.5 3.6 %shard_map.58 = (bf16[512,384]{1,0:T(8,128)(2,1)S(1)}, bf16[512,384]{1,0:T(8,128)(2,1)S(1)}) custom-call(bf16[576,384]{1,0:T(8,128)(2,1)S(1)} %fusion.1.refs_0_, bf16[576,384]{1,0:T(8,128)(2,1)S(1)} %collective-permute-done.4.refs_1_, bf16[576,384]{1,0:T(8,128)(2,1)S(1)} %collective-permute-done.refs_2_, ...), custom_call_target="tpu_custom_call" | custom-call | bytes 1024 | tf_op jit(solution)/shard_map/pallas_call | solution.py:161
  43.9 2.0 %shard_map.59.refs_5_ = bf16[1536,1152]{1,0:T(8,128)(2,1)S(1)} custom-call(s32[1]{0:T(128)} %bitcast.ch_ref, bf16[3,3,1536,384]{3,2,1,0:T(8,128)(2,1)} %w_hbm.5), custom_call_target="tpu_custom_call" | custom-call | tf_op jit(solution)/shard_map/pallas_call | solution.py:173
  45.9 2.0 %collective-permute-done.14.refs_2_ = bf16[512,384]{1,0:T(8,128)(2,1)S(1)} collective-permute-done((bf16[512,384]{1,0:T(8,128)(2,1)S(1)}, bf16[512,384]{1,0:T(8,128)(2,1)S(1)}, u32[]{:S(2)}, u32[]{:S(2)}) %collective-permute-start.14) | collective-permute-done | bytes 393248 | tf_op jit(solution)/shard_map/ppermute | solution.py:46
  49.8 2.2 %shard_map.60 = (bf16[512,384]{1,0:T(8,128)(2,1)S(1)}, bf16[512,384]{1,0:T(8,128)(2,1)S(1)}, bf16[512,384]{1,0:T(8,128)(2,1)S(1)}) custom-call(bf16[512,384]{1,0:T(8,128)(2,1)S(1)} %get-tuple-element.82.refs_0_, bf16[512,384]{1,0:T(8,128)(2,1)S(1)} %collective-permute-done.13.refs_1_, bf16[512,384]{1,0:T(8,128)(2,1)S(1)} %collective-permute-done.14.refs_2_, ...), custom_call_target="tpu_custom_call" | custom-call | bytes 1024 | tf_op jit(solution)/shard_map/pallas_call | solution.py:161
  52.0 1.9 %collective-permute-start.22 = (bf16[512,384]{1,0:T(8,128)(2,1)S(1)}, bf16[512,384]{1,0:T(8,128)(2,1)S(1)}, u32[]{:S(2)}, u32[]{:S(2)}) collective-permute-start(bf16[512,384]{1,0:T(8,128)(2,1)S(1)} %get-tuple-element.94), channel_id=1, source_target_pairs={{0,4},{4,8},{8,12},{12,16},{16,20},{20,24},{24,28},{28,32},{32,36}... | collective-permute-start | bytes 1179656 | tf_op jit(solution)/shard_map/ppermute | solution.py:42
  57.0 2.2 %shard_map.61 = (bf16[512,384]{1,0:T(8,128)(2,1)S(1)}, bf16[512,384]{1,0:T(8,128)(2,1)S(1)}, bf16[512,384]{1,0:T(8,128)(2,1)S(1)}) custom-call(bf16[512,384]{1,0:T(8,128)(2,1)S(1)} %get-tuple-element.88.refs_0_, bf16[512,384]{1,0:T(8,128)(2,1)S(1)} %collective-permute-done.17.refs_1_, bf16[512,384]{1,0:T(8,128)(2,1)S(1)} %collective-permute-done.12.refs_2_, ...), custom_call_target="tpu_custom_call" | custom-call | bytes 1024 | tf_op jit(solution)/shard_map/pallas_call | solution.py:161
  59.2 7.4 %collective-permute-start.20 = (bf16[512,384]{1,0:T(8,128)(2,1)S(1)}, bf16[512,384]{1,0:T(8,128)(2,1)S(1)}, u32[]{:S(2)}, u32[]{:S(2)}) collective-permute-start(bf16[512,384]{1,0:T(8,128)(2,1)S(1)} %get-tuple-element.91), channel_id=1, source_target_pairs={{4,0},{8,4},{12,8},{16,12},{20,16},{24,20},{28,24},{32,28},{36,32}... | collective-permute-start | bytes 1179656 | tf_op jit(solution)/shard_map/ppermute | solution.py:42
  66.6 3.2 %collective-permute-done.22.up = bf16[512,384]{1,0:T(8,128)(2,1)S(1)} collective-permute-done((bf16[512,384]{1,0:T(8,128)(2,1)S(1)}, bf16[512,384]{1,0:T(8,128)(2,1)S(1)}, u32[]{:S(2)}, u32[]{:S(2)}) %collective-permute-start.22) | collective-permute-done | bytes 393248 | tf_op jit(solution)/shard_map/ppermute | solution.py:42
  72.9 6.9 %collective-permute-start.24 = (bf16[512,384]{1,0:T(8,128)(2,1)S(1)}, bf16[512,384]{1,0:T(8,128)(2,1)S(1)}, u32[]{:S(2)}, u32[]{:S(2)}) collective-permute-start(bf16[512,384]{1,0:T(8,128)(2,1)S(1)} %get-tuple-element.112.refs_0_), channel_id=1, source_target_pairs={{16,0},{20,4},{24,8},{28,12},{32,16},{36,20},{40,24},{44,28},{48,3... | collective-permute-start | bytes 1179656 | tf_op jit(solution)/shard_map/ppermute | solution.py:42
  81.5 2.1 %shard_map.65.refs_5_.refs_10_.refs_6_ = bf16[1536,1152]{1,0:T(8,128)(2,1)S(1)} custom-call(s32[1]{0:T(128)} %bitcast.ch_ref, bf16[3,3,1536,384]{3,2,1,0:T(8,128)(2,1)} %w_hbm.5), custom_call_target="tpu_custom_call" | custom-call | tf_op jit(solution)/shard_map/pallas_call | solution.py:173
  84.1 10.1 %collective-permute-done.23.refs_4_ = bf16[512,384]{1,0:T(8,128)(2,1)S(1)} collective-permute-done((bf16[512,384]{1,0:T(8,128)(2,1)S(1)}, bf16[512,384]{1,0:T(8,128)(2,1)S(1)}, u32[]{:S(2)}, u32[]{:S(2)}) %collective-permute-start.23) | collective-permute-done | bytes 393248 | tf_op jit(solution)/shard_map/ppermute | solution.py:42
  98.6 2.2 %shard_map.66 = (bf16[512,384]{1,0:T(8,128)(2,1)S(1)}, bf16[512,384]{1,0:T(8,128)(2,1)S(1)}, bf16[512,384]{1,0:T(8,128)(2,1)S(1)}) custom-call(bf16[512,384]{1,0:T(8,128)(2,1)S(1)} %get-tuple-element.103.refs_0_, bf16[512,384]{1,0:T(8,128)(2,1)S(1)} %collective-permute-done.26.refs_1_, bf16[512,384]{1,0:T(8,128)(2,1)S(1)} %collective-permute-done.21.refs_2_, ...), custom_call_target="tpu_custom_call" | custom-call | bytes 1024 | tf_op jit(solution)/shard_map/pallas_call | solution.py:161
  103.0 5.7 %collective-permute-start.37 = (bf16[512,384]{1,0:T(8,128)(2,1)S(1)}, bf16[512,384]{1,0:T(8,128)(2,1)S(1)}, u32[]{:S(2)}, u32[]{:S(2)}) collective-permute-start(bf16[512,384]{1,0:T(8,128)(2,1)S(1)} %get-tuple-element.119), channel_id=1, source_target_pairs={{0,16},{4,20},{8,24},{12,28},{16,32},{20,36},{24,40},{28,44},{32,4... | collective-permute-start | bytes 1179656 | tf_op jit(solution)/shard_map/ppermute | solution.py:42
  108.7 3.1 %collective-permute-start.38 = (bf16[512,384]{1,0:T(8,128)(2,1)S(1)}, bf16[512,384]{1,0:T(8,128)(2,1)S(1)}, u32[]{:S(2)}, u32[]{:S(2)}) collective-permute-start(bf16[512,384]{1,0:T(8,128)(2,1)S(1)} %get-tuple-element.120), channel_id=1, source_target_pairs={{16,0},{20,4},{24,8},{28,12},{32,16},{36,20},{40,24},{44,28},{48,3... | collective-permute-start | bytes 1179656 | tf_op jit(solution)/shard_map/ppermute | solution.py:42
  111.9 5.4 %collective-permute-done.35.refs_6_ = bf16[512,384]{1,0:T(8,128)(2,1)S(1)} collective-permute-done((bf16[512,384]{1,0:T(8,128)(2,1)S(1)}, bf16[512,384]{1,0:T(8,128)(2,1)S(1)}, u32[]{:S(2)}, u32[]{:S(2)}) %collective-permute-start.35) | collective-permute-done | bytes 393248 | tf_op jit(solution)/shard_map/ppermute | solution.py:46
  117.3 7.6 %collective-permute-done.31.refs_2_ = bf16[512,384]{1,0:T(8,128)(2,1)S(1)} collective-permute-done((bf16[512,384]{1,0:T(8,128)(2,1)S(1)}, bf16[512,384]{1,0:T(8,128)(2,1)S(1)}, u32[]{:S(2)}, u32[]{:S(2)}) %collective-permute-start.31) | collective-permute-done | bytes 393248 | tf_op jit(solution)/shard_map/ppermute | solution.py:46
  124.9 2.5 %collective-permute-done.38.down_hi = bf16[512,384]{1,0:T(8,128)(2,1)S(1)} collective-permute-done((bf16[512,384]{1,0:T(8,128)(2,1)S(1)}, bf16[512,384]{1,0:T(8,128)(2,1)S(1)}, u32[]{:S(2)}, u32[]{:S(2)}) %collective-permute-start.38) | collective-permute-done | bytes 393248 | tf_op jit(solution)/shard_map/ppermute | solution.py:42
  (86 shorter events, 34.7 us)
Async XLA Ops:
  3.0 22.7 %collective-permute-start = (bf16[576,384]{1,0:T(8,128)(2,1)S(1)}, bf16[576,384]{1,0:T(8,128)(2,1)S(1)}, u32[]{:S(2)}, u32[]{:S(2)}) collective-permute-start(bf16[576,384]{1,0:T(8,128)(2,1)S(1)} %fusion.1.refs_0_), channel_id=1, source_target_pairs={{0,2},{1,3},{2,0},{3,1},{4,6},{5,7},{6,4},{7,5},{8,10},{9,11},{10,... | collective-permute-start | bytes 1327112 | tf_op jit(solution)/shard_map/ppermute | solution.py:46
  4.6 21.0 %collective-permute-start.4 = (bf16[576,384]{1,0:T(8,128)(2,1)S(1)}, bf16[576,384]{1,0:T(8,128)(2,1)S(1)}, u32[]{:S(2)}, u32[]{:S(2)}) collective-permute-start(bf16[576,384]{1,0:T(8,128)(2,1)S(1)} %fusion.1.refs_0_), channel_id=1, source_target_pairs={{0,1},{1,0},{2,3},{3,2},{4,5},{5,4},{6,7},{7,6},{8,9},{9,8},{10,11... | collective-permute-start | bytes 1327112 | tf_op jit(solution)/shard_map/ppermute | solution.py:50
  5.7 14.1 %collective-permute-start.1 = (bf16[64,384]{1,0:T(8,128)(2,1)S(1)}, bf16[64,384]{1,0:T(8,128)(2,1)S(1)}, u32[]{:S(2)}, u32[]{:S(2)}) collective-permute-start(bf16[64,384]{1,0:T(8,128)(2,1)S(1)} %get-tuple-element.132), channel_id=1, source_target_pairs={{0,4},{4,8},{8,12},{12,16},{16,20},{20,24},{24,28},{28,32},{32,36}... | collective-permute-start | bytes 147464 | tf_op jit(solution)/shard_map/ppermute | solution.py:42
  10.6 9.3 %collective-permute-start.2 = (bf16[64,384]{1,0:T(8,128)(2,1)S(1)}, bf16[64,384]{1,0:T(8,128)(2,1)S(1)}, u32[]{:S(2)}, u32[]{:S(2)}) collective-permute-start(bf16[64,384]{1,0:T(8,128)(2,1)S(1)} %get-tuple-element.131), channel_id=1, source_target_pairs={{4,0},{8,4},{12,8},{16,12},{20,16},{24,20},{28,24},{32,28},{36,32}... | collective-permute-start | bytes 147464 | tf_op jit(solution)/shard_map/ppermute | solution.py:42
  20.2 12.2 %collective-permute-start.9 = (bf16[448,384]{1,0:T(8,128)(2,1)S(1)}, bf16[448,384]{1,0:T(8,128)(2,1)S(1)}, u32[]{:S(2)}, u32[]{:S(2)}) collective-permute-start(bf16[448,384]{1,0:T(8,128)(2,1)S(1)} %fusion.4.refs_9_), channel_id=1, source_target_pairs={{0,2},{1,3},{2,0},{3,1},{4,6},{5,7},{6,4},{7,5},{8,10},{9,11},{10,... | collective-permute-start | bytes 1032200 | tf_op jit(solution)/shard_map/ppermute | solution.py:46
  25.7 6.6 %collective-permute-start.5 = (bf16[288,384]{1,0:T(8,128)(2,1)S(1)}, bf16[288,384]{1,0:T(8,128)(2,1)S(1)}, u32[]{:S(2)}, u32[]{:S(2)}) collective-permute-start(bf16[288,384]{1,0:T(8,128)(2,1)S(1)} %get-tuple-element.124), channel_id=1, source_target_pairs={{0,1},{1,0},{2,3},{3,2},{4,5},{5,4},{6,7},{7,6},{8,9},{9,8},{10,11... | collective-permute-start | bytes 663560 | tf_op jit(solution)/shard_map/ppermute | solution.py:50
  25.8 6.5 %collective-permute-start.6 = (bf16[288,384]{1,0:T(8,128)(2,1)S(1)}, bf16[288,384]{1,0:T(8,128)(2,1)S(1)}, u32[]{:S(2)}, u32[]{:S(2)}) collective-permute-start(bf16[288,384]{1,0:T(8,128)(2,1)S(1)} %get-tuple-element.123), channel_id=1, source_target_pairs={{0,1},{1,0},{2,3},{3,2},{4,5},{5,4},{6,7},{7,6},{8,9},{9,8},{10,11... | collective-permute-start | bytes 663560 | tf_op jit(solution)/shard_map/ppermute | solution.py:50
  35.9 12.0 %collective-permute-start.14 = (bf16[512,384]{1,0:T(8,128)(2,1)S(1)}, bf16[512,384]{1,0:T(8,128)(2,1)S(1)}, u32[]{:S(2)}, u32[]{:S(2)}) collective-permute-start(bf16[512,384]{1,0:T(8,128)(2,1)S(1)} %get-tuple-element.82.refs_0_), channel_id=1, source_target_pairs={{0,2},{1,3},{2,0},{3,1},{4,6},{5,7},{6,4},{7,5},{8,10},{9,11},{10,... | collective-permute-start | bytes 1179656 | tf_op jit(solution)/shard_map/ppermute | solution.py:46
  36.8 11.9 %collective-permute-start.13 = (bf16[512,384]{1,0:T(8,128)(2,1)S(1)}, bf16[512,384]{1,0:T(8,128)(2,1)S(1)}, u32[]{:S(2)}, u32[]{:S(2)}) collective-permute-start(bf16[512,384]{1,0:T(8,128)(2,1)S(1)} %get-tuple-element.82.refs_0_), channel_id=1, source_target_pairs={{0,1},{1,0},{2,3},{3,2},{4,5},{5,4},{6,7},{7,6},{8,9},{9,8},{10,11... | collective-permute-start | bytes 1179656 | tf_op jit(solution)/shard_map/ppermute | solution.py:50
  42.1 13.1 %collective-permute-start.12 = (bf16[512,384]{1,0:T(8,128)(2,1)S(1)}, bf16[512,384]{1,0:T(8,128)(2,1)S(1)}, u32[]{:S(2)}, u32[]{:S(2)}) collective-permute-start(bf16[512,384]{1,0:T(8,128)(2,1)S(1)} %get-tuple-element.88.refs_0_), channel_id=1, source_target_pairs={{0,2},{1,3},{2,0},{3,1},{4,6},{5,7},{6,4},{7,5},{8,10},{9,11},{10,... | collective-permute-start | bytes 1179656 | tf_op jit(solution)/shard_map/ppermute | solution.py:46
  48.6 7.2 %collective-permute-start.17 = (bf16[512,384]{1,0:T(8,128)(2,1)S(1)}, bf16[512,384]{1,0:T(8,128)(2,1)S(1)}, u32[]{:S(2)}, u32[]{:S(2)}) collective-permute-start(bf16[512,384]{1,0:T(8,128)(2,1)S(1)} %get-tuple-element.88.refs_0_), channel_id=1, source_target_pairs={{0,1},{1,0},{2,3},{3,2},{4,5},{5,4},{6,7},{7,6},{8,9},{9,8},{10,11... | collective-permute-start | bytes 1179656 | tf_op jit(solution)/shard_map/ppermute | solution.py:50
  52.0 17.8 %collective-permute-start.22 = (bf16[512,384]{1,0:T(8,128)(2,1)S(1)}, bf16[512,384]{1,0:T(8,128)(2,1)S(1)}, u32[]{:S(2)}, u32[]{:S(2)}) collective-permute-start(bf16[512,384]{1,0:T(8,128)(2,1)S(1)} %get-tuple-element.94), channel_id=1, source_target_pairs={{0,4},{4,8},{8,12},{12,16},{16,20},{20,24},{24,28},{28,32},{32,36}... | collective-permute-start | bytes 1179656 | tf_op jit(solution)/shard_map/ppermute | solution.py:42
  59.2 21.0 %collective-permute-start.20 = (bf16[512,384]{1,0:T(8,128)(2,1)S(1)}, bf16[512,384]{1,0:T(8,128)(2,1)S(1)}, u32[]{:S(2)}, u32[]{:S(2)}) collective-permute-start(bf16[512,384]{1,0:T(8,128)(2,1)S(1)} %get-tuple-element.91), channel_id=1, source_target_pairs={{4,0},{8,4},{12,8},{16,12},{20,16},{24,20},{28,24},{32,28},{36,32}... | collective-permute-start | bytes 1179656 | tf_op jit(solution)/shard_map/ppermute | solution.py:42
  71.0 23.2 %collective-permute-start.23 = (bf16[512,384]{1,0:T(8,128)(2,1)S(1)}, bf16[512,384]{1,0:T(8,128)(2,1)S(1)}, u32[]{:S(2)}, u32[]{:S(2)}) collective-permute-start(bf16[512,384]{1,0:T(8,128)(2,1)S(1)} %get-tuple-element.112.refs_0_), channel_id=1, source_target_pairs={{0,16},{4,20},{8,24},{12,28},{16,32},{20,36},{24,40},{28,44},{32,4... | collective-permute-start | bytes 1179656 | tf_op jit(solution)/shard_map/ppermute | solution.py:42
  72.9 22.9 %collective-permute-start.24 = (bf16[512,384]{1,0:T(8,128)(2,1)S(1)}, bf16[512,384]{1,0:T(8,128)(2,1)S(1)}, u32[]{:S(2)}, u32[]{:S(2)}) collective-permute-start(bf16[512,384]{1,0:T(8,128)(2,1)S(1)} %get-tuple-element.112.refs_0_), channel_id=1, source_target_pairs={{16,0},{20,4},{24,8},{28,12},{32,16},{36,20},{40,24},{44,28},{48,3... | collective-permute-start | bytes 1179656 | tf_op jit(solution)/shard_map/ppermute | solution.py:42
  81.4 14.4 %collective-permute-start.21 = (bf16[512,384]{1,0:T(8,128)(2,1)S(1)}, bf16[512,384]{1,0:T(8,128)(2,1)S(1)}, u32[]{:S(2)}, u32[]{:S(2)}) collective-permute-start(bf16[512,384]{1,0:T(8,128)(2,1)S(1)} %get-tuple-element.103.refs_0_), channel_id=1, source_target_pairs={{0,2},{1,3},{2,0},{3,1},{4,6},{5,7},{6,4},{7,5},{8,10},{9,11},{10,... | collective-permute-start | bytes 1179656 | tf_op jit(solution)/shard_map/ppermute | solution.py:46
  83.5 13.4 %collective-permute-start.26 = (bf16[512,384]{1,0:T(8,128)(2,1)S(1)}, bf16[512,384]{1,0:T(8,128)(2,1)S(1)}, u32[]{:S(2)}, u32[]{:S(2)}) collective-permute-start(bf16[512,384]{1,0:T(8,128)(2,1)S(1)} %get-tuple-element.103.refs_0_), channel_id=1, source_target_pairs={{0,1},{1,0},{2,3},{3,2},{4,5},{5,4},{6,7},{7,6},{8,9},{9,8},{10,11... | collective-permute-start | bytes 1179656 | tf_op jit(solution)/shard_map/ppermute | solution.py:50
  97.0 14.9 %collective-permute-start.33 = (bf16[512,384]{1,0:T(8,128)(2,1)S(1)}, bf16[512,384]{1,0:T(8,128)(2,1)S(1)}, u32[]{:S(2)}, u32[]{:S(2)}) collective-permute-start(bf16[512,384]{1,0:T(8,128)(2,1)S(1)} %get-tuple-element.112.refs_0_), channel_id=1, source_target_pairs={{0,2},{1,3},{2,0},{3,1},{4,6},{5,7},{6,4},{7,5},{8,10},{9,11},{10,... | collective-permute-start | bytes 1179656 | tf_op jit(solution)/shard_map/ppermute | solution.py:46
  100.9 16.5 %collective-permute-start.35 = (bf16[512,384]{1,0:T(8,128)(2,1)S(1)}, bf16[512,384]{1,0:T(8,128)(2,1)S(1)}, u32[]{:S(2)}, u32[]{:S(2)}) collective-permute-start(bf16[512,384]{1,0:T(8,128)(2,1)S(1)} %collective-permute-done.23.refs_4_), channel_id=1, source_target_pairs={{0,2},{1,3},{2,0},{3,1},{4,6},{5,7},{6,4},{7,5},{8,10},{9,11},{10,... | collective-permute-start | bytes 1179656 | tf_op jit(solution)/shard_map/ppermute | solution.py:46
  101.3 23.6 %collective-permute-start.31 = (bf16[512,384]{1,0:T(8,128)(2,1)S(1)}, bf16[512,384]{1,0:T(8,128)(2,1)S(1)}, u32[]{:S(2)}, u32[]{:S(2)}) collective-permute-start(bf16[512,384]{1,0:T(8,128)(2,1)S(1)} %collective-permute-done.24.refs_0_), channel_id=1, source_target_pairs={{0,2},{1,3},{2,0},{3,1},{4,6},{5,7},{6,4},{7,5},{8,10},{9,11},{10,... | collective-permute-start | bytes 1179656 | tf_op jit(solution)/shard_map/ppermute | solution.py:46
  103.0 22.0 %collective-permute-start.37 = (bf16[512,384]{1,0:T(8,128)(2,1)S(1)}, bf16[512,384]{1,0:T(8,128)(2,1)S(1)}, u32[]{:S(2)}, u32[]{:S(2)}) collective-permute-start(bf16[512,384]{1,0:T(8,128)(2,1)S(1)} %get-tuple-element.119), channel_id=1, source_target_pairs={{0,16},{4,20},{8,24},{12,28},{16,32},{20,36},{24,40},{28,44},{32,4... | collective-permute-start | bytes 1179656 | tf_op jit(solution)/shard_map/ppermute | solution.py:42
  108.7 18.8 %collective-permute-start.38 = (bf16[512,384]{1,0:T(8,128)(2,1)S(1)}, bf16[512,384]{1,0:T(8,128)(2,1)S(1)}, u32[]{:S(2)}, u32[]{:S(2)}) collective-permute-start(bf16[512,384]{1,0:T(8,128)(2,1)S(1)} %get-tuple-element.120), channel_id=1, source_target_pairs={{16,0},{20,4},{24,8},{28,12},{32,16},{36,20},{40,24},{44,28},{48,3... | collective-permute-start | bytes 1179656 | tf_op jit(solution)/shard_map/ppermute | solution.py:42
  111.8 15.9 %collective-permute-start.34 = (bf16[512,384]{1,0:T(8,128)(2,1)S(1)}, bf16[512,384]{1,0:T(8,128)(2,1)S(1)}, u32[]{:S(2)}, u32[]{:S(2)}) collective-permute-start(bf16[512,384]{1,0:T(8,128)(2,1)S(1)} %collective-permute-done.33.refs_2_), channel_id=1, source_target_pairs={{0,1},{1,0},{2,3},{3,2},{4,5},{5,4},{6,7},{7,6},{8,9},{9,8},{10,11... | collective-permute-start | bytes 1179656 | tf_op jit(solution)/shard_map/ppermute | solution.py:50
  117.3 10.4 %collective-permute-start.36 = (bf16[512,384]{1,0:T(8,128)(2,1)S(1)}, bf16[512,384]{1,0:T(8,128)(2,1)S(1)}, u32[]{:S(2)}, u32[]{:S(2)}) collective-permute-start(bf16[512,384]{1,0:T(8,128)(2,1)S(1)} %collective-permute-done.35.refs_6_), channel_id=1, source_target_pairs={{0,1},{1,0},{2,3},{3,2},{4,5},{5,4},{6,7},{7,6},{8,9},{9,8},{10,11... | collective-permute-start | bytes 1179656 | tf_op jit(solution)/shard_map/ppermute | solution.py:50
  (17 other events, 52.3 us)

commit v10 on v9

--- a/solution.py
+++ b/solution.py
@@ -196,12 +196,13 @@
     rim = entry(jnp.concatenate([bins_in[ROWS - R :], bins_in[:R]], axis=0))
     low = shifted(rim[:R], 1)
     high = shifted(rim[R:], -1)
-    (act_2,) = call(rims_kernel, (low, high), [2 * R], flops=RIM_COST)
     act_1 = entry(bins_in[FIRST:])
     far_1 = chip_swap(act_1)
     near_1 = core_swap(act_1)
     act_3 = entry(bins_in[:FIRST])
     w0 = staged(0, ch, conv_weight)
+    low, high, w0 = after((low, high, w0))
+    (act_2,) = call(rims_kernel, (low, high), [2 * R], flops=RIM_COST)
     act_2, act_3 = after((act_2, act_3))
     far_2 = chip_swap(act_2)
     near_2 = core_swap(act_2)
@@ -210,7 +211,6 @@
     far_1, far_2, near_1 = after((far_1, far_2, near_1))
     g_1 = (act_1, near_1, far_1, *core_swaps(far_1, 2))
     g_2 = (act_2, near_2, far_2, core_swap(far_2))
-    g_1, g_2, far_3 = after((g_1, g_2, far_3))
     plan_hi = ((0, 0, ROWS - FIRST), (1, R, R))
     s_hi, a_hi = call(
         functools.partial(near_kernel, plan_hi, (2, 1), MID), (*g_1, *g_2, bins_in, vec0, w0), halves[:2], scratch

time: 133 us -> 130 us (0.977)
  transfers between devices with their start and end apart: 39 -> 39, of which waited for: 19 -> 20; matrix products, arithmetic and copies ran while one was open for 2% -> 2% of each run, Pallas kernels for 16% -> 19%
where the time goes in v10:
time: 130 us; the launch traced here: 129 us
  starting transfers between devices  51.5 us (40%)
  waiting for transfers between devices  44.9 us (35%)
  Pallas kernels  26.3 us (20%)
  other arithmetic  4.19 us (3%)
  local copies, waits for them, and re-layouts  1.9 us (1%)
    ppermute x8, starting transfers between devices, shifted(): return lax.ppermute(array, 'seq', pairs)  38 us
    ppermute x9, waiting for transfers between devices, chip_swap(): return lax.ppermute(array, 'ch', [(i, i ^ 2) for i in range(4)])  21.4 us
    pallas_call x12, Pallas kernels, call(): pl.pallas_call(kernel, out_shape=[jax.ShapeDtypeStruct((r, W), dtype) for...  20.1 us
    ppermute x8, waiting for transfers between devices, shifted(): return lax.ppermute(array, 'seq', pairs)  17.4 us
    ppermute x9, starting transfers between devices, chip_swap(): return lax.ppermute(array, 'ch', [(i, i ^ 2) for i in range(4)])  8.13 us
    pallas_call x3, Pallas kernels, staged(): pl.pallas_call(functools.partial(stage_kernel, layer), out_shape=jax.Shap...  6.13 us
    ppermute x22, waiting for transfers between devices, core_swap(): return lax.ppermute(array, 'ch', [(i, i ^ 1) for i in range(4)])  6.13 us
    ppermute x22, starting transfers between devices, core_swap(): return lax.ppermute(array, 'ch', [(i, i ^ 1) for i in range(4)])  5.33 us
  transfers between devices with their start and end apart: 39, of which 20 were waited for; matrix products, arithmetic and copies ran while one was open for 2% of the time, Pallas kernels for 19%

profile of v10, /device:TPU:6, one launch (start us, length us, event | category | flops | bytes accessed | tf_op | source)
XLA Modules:
  0.0 129.0 jit_solution(11490889553712230233)
XLA Ops:
  0.9 2.1 %fusion.1.refs_0_ = bf16[576,384]{1,0:T(8,128)(2,1)S(1)} fusion(f32[384]{0:T(512)S(1)} %get-tuple-element.129, f32[384]{0:T(512)S(1)} %get-tuple-element.123, bf16[1024,384]{1,0:T(8,128)(2,1)} %refs_13_.1), kind=kLoop, calls=%fused_computation.3 | loop fusion | flops 7741440 | bytes 887808 | tf_op jit(solution)/shard_map/convert_element_type | solution.py:194
  5.7 4.8 %collective-permute-start.1 = (bf16[64,384]{1,0:T(8,128)(2,1)S(1)}, bf16[64,384]{1,0:T(8,128)(2,1)S(1)}, u32[]{:S(2)}, u32[]{:S(2)}) collective-permute-start(bf16[64,384]{1,0:T(8,128)(2,1)S(1)} %get-tuple-element.118), channel_id=1, source_target_pairs={{0,4},{4,8},{8,12},{12,16},{16,20},{20,24},{24,28},{28,32},{32,36}... | collective-permute-start | bytes 147464 | tf_op jit(solution)/shard_map/ppermute | solution.py:42
  10.6 7.5 %collective-permute-start.2 = (bf16[64,384]{1,0:T(8,128)(2,1)S(1)}, bf16[64,384]{1,0:T(8,128)(2,1)S(1)}, u32[]{:S(2)}, u32[]{:S(2)}) collective-permute-start(bf16[64,384]{1,0:T(8,128)(2,1)S(1)} %get-tuple-element.117), channel_id=1, source_target_pairs={{4,0},{8,4},{12,8},{16,12},{20,16},{24,20},{28,24},{32,28},{36,32}... | collective-permute-start | bytes 147464 | tf_op jit(solution)/shard_map/ppermute | solution.py:42
  19.9 2.0 %shard_map.55.refs_11_.refs_15_ = bf16[1536,1152]{1,0:T(8,128)(2,1)S(1)} custom-call(s32[1]{0:T(128)} %bitcast.ch_ref, bf16[3,3,1536,384]{3,2,1,0:T(8,128)(2,1)} %w_hbm.5), custom_call_target="tpu_custom_call" | custom-call | tf_op jit(solution)/shard_map/pallas_call | solution.py:173
  24.1 3.6 %collective-permute-done.3.refs_7_ = bf16[128,384]{1,0:T(8,128)(2,1)S(1)} collective-permute-done((bf16[128,384]{1,0:T(8,128)(2,1)S(1)}, bf16[128,384]{1,0:T(8,128)(2,1)S(1)}, u32[]{:S(2)}, u32[]{:S(2)}) %collective-permute-start.3) | collective-permute-done | bytes 98336 | tf_op jit(solution)/shard_map/ppermute | solution.py:46
  29.9 3.6 %shard_map.57 = (bf16[512,384]{1,0:T(8,128)(2,1)S(1)}, bf16[512,384]{1,0:T(8,128)(2,1)S(1)}) custom-call(bf16[576,384]{1,0:T(8,128)(2,1)S(1)} %fusion.1.refs_0_, bf16[576,384]{1,0:T(8,128)(2,1)S(1)} %collective-permute-done.4.refs_1_, bf16[576,384]{1,0:T(8,128)(2,1)S(1)} %collective-permute-done.refs_2_, ...), custom_call_target="tpu_custom_call" | custom-call | bytes 1024 | tf_op jit(solution)/shard_map/pallas_call | solution.py:161
  36.0 3.6 %shard_map.58 = (bf16[512,384]{1,0:T(8,128)(2,1)S(1)}, bf16[512,384]{1,0:T(8,128)(2,1)S(1)}) custom-call(bf16[576,384]{1,0:T(8,128)(2,1)S(1)} %fusion.1.refs_0_, bf16[576,384]{1,0:T(8,128)(2,1)S(1)} %collective-permute-done.4.refs_1_, bf16[576,384]{1,0:T(8,128)(2,1)S(1)} %collective-permute-done.refs_2_, ...), custom_call_target="tpu_custom_call" | custom-call | bytes 1024 | tf_op jit(solution)/shard_map/pallas_call | solution.py:161
  41.5 2.0 %shard_map.59.refs_5_ = bf16[1536,1152]{1,0:T(8,128)(2,1)S(1)} custom-call(s32[1]{0:T(128)} %bitcast.ch_ref, bf16[3,3,1536,384]{3,2,1,0:T(8,128)(2,1)} %w_hbm.5), custom_call_target="tpu_custom_call" | custom-call | tf_op jit(solution)/shard_map/pallas_call | solution.py:173
  43.5 2.0 %collective-permute-done.14.refs_2_ = bf16[512,384]{1,0:T(8,128)(2,1)S(1)} collective-permute-done((bf16[512,384]{1,0:T(8,128)(2,1)S(1)}, bf16[512,384]{1,0:T(8,128)(2,1)S(1)}, u32[]{:S(2)}, u32[]{:S(2)}) %collective-permute-start.14) | collective-permute-done | bytes 393248 | tf_op jit(solution)/shard_map/ppermute | solution.py:46
  47.4 2.2 %shard_map.60 = (bf16[512,384]{1,0:T(8,128)(2,1)S(1)}, bf16[512,384]{1,0:T(8,128)(2,1)S(1)}, bf16[512,384]{1,0:T(8,128)(2,1)S(1)}) custom-call(bf16[512,384]{1,0:T(8,128)(2,1)S(1)} %get-tuple-element.68.refs_0_, bf16[512,384]{1,0:T(8,128)(2,1)S(1)} %collective-permute-done.13.refs_1_, bf16[512,384]{1,0:T(8,128)(2,1)S(1)} %collective-permute-done.14.refs_2_, ...), custom_call_target="tpu_custom_call" | custom-call | bytes 1024 | tf_op jit(solution)/shard_map/pallas_call | solution.py:161
  49.6 1.9 %collective-permute-start.22 = (bf16[512,384]{1,0:T(8,128)(2,1)S(1)}, bf16[512,384]{1,0:T(8,128)(2,1)S(1)}, u32[]{:S(2)}, u32[]{:S(2)}) collective-permute-start(bf16[512,384]{1,0:T(8,128)(2,1)S(1)} %get-tuple-element.80), channel_id=1, source_target_pairs={{0,4},{4,8},{8,12},{12,16},{16,20},{20,24},{24,28},{28,32},{32,36}... | collective-permute-start | bytes 1179656 | tf_op jit(solution)/shard_map/ppermute | solution.py:42
  51.6 2.4 %collective-permute-done.12.refs_2_ = bf16[512,384]{1,0:T(8,128)(2,1)S(1)} collective-permute-done((bf16[512,384]{1,0:T(8,128)(2,1)S(1)}, bf16[512,384]{1,0:T(8,128)(2,1)S(1)}, u32[]{:S(2)}, u32[]{:S(2)}) %collective-permute-start.12) | collective-permute-done | bytes 393248 | tf_op jit(solution)/shard_map/ppermute | solution.py:46
  55.9 2.2 %shard_map.61 = (bf16[512,384]{1,0:T(8,128)(2,1)S(1)}, bf16[512,384]{1,0:T(8,128)(2,1)S(1)}, bf16[512,384]{1,0:T(8,128)(2,1)S(1)}) custom-call(bf16[512,384]{1,0:T(8,128)(2,1)S(1)} %get-tuple-element.74.refs_0_, bf16[512,384]{1,0:T(8,128)(2,1)S(1)} %collective-permute-done.17.refs_1_, bf16[512,384]{1,0:T(8,128)(2,1)S(1)} %collective-permute-done.12.refs_2_, ...), custom_call_target="tpu_custom_call" | custom-call | bytes 1024 | tf_op jit(solution)/shard_map/pallas_call | solution.py:161
  58.1 6.1 %collective-permute-start.20 = (bf16[512,384]{1,0:T(8,128)(2,1)S(1)}, bf16[512,384]{1,0:T(8,128)(2,1)S(1)}, u32[]{:S(2)}, u32[]{:S(2)}) collective-permute-start(bf16[512,384]{1,0:T(8,128)(2,1)S(1)} %get-tuple-element.77), channel_id=1, source_target_pairs={{4,0},{8,4},{12,8},{16,12},{20,16},{24,20},{28,24},{32,28},{36,32}... | collective-permute-start | bytes 1179656 | tf_op jit(solution)/shard_map/ppermute | solution.py:42
  64.2 3.2 %collective-permute-done.22.up = bf16[512,384]{1,0:T(8,128)(2,1)S(1)} collective-permute-done((bf16[512,384]{1,0:T(8,128)(2,1)S(1)}, bf16[512,384]{1,0:T(8,128)(2,1)S(1)}, u32[]{:S(2)}, u32[]{:S(2)}) %collective-permute-start.22) | collective-permute-done | bytes 393248 | tf_op jit(solution)/shard_map/ppermute | solution.py:42
  70.5 6.9 %collective-permute-start.24 = (bf16[512,384]{1,0:T(8,128)(2,1)S(1)}, bf16[512,384]{1,0:T(8,128)(2,1)S(1)}, u32[]{:S(2)}, u32[]{:S(2)}) collective-permute-start(bf16[512,384]{1,0:T(8,128)(2,1)S(1)} %get-tuple-element.98.refs_0_), channel_id=1, source_target_pairs={{16,0},{20,4},{24,8},{28,12},{32,16},{36,20},{40,24},{44,28},{48,3... | collective-permute-start | bytes 1179656 | tf_op jit(solution)/shard_map/ppermute | solution.py:42
  79.2 2.0 %shard_map.65.refs_5_.refs_10_.refs_6_ = bf16[1536,1152]{1,0:T(8,128)(2,1)S(1)} custom-call(s32[1]{0:T(128)} %bitcast.ch_ref, bf16[3,3,1536,384]{3,2,1,0:T(8,128)(2,1)} %w_hbm.5), custom_call_target="tpu_custom_call" | custom-call | tf_op jit(solution)/shard_map/pallas_call | solution.py:173
  81.7 10.0 %collective-permute-done.23.refs_4_ = bf16[512,384]{1,0:T(8,128)(2,1)S(1)} collective-permute-done((bf16[512,384]{1,0:T(8,128)(2,1)S(1)}, bf16[512,384]{1,0:T(8,128)(2,1)S(1)}, u32[]{:S(2)}, u32[]{:S(2)}) %collective-permute-start.23) | collective-permute-done | bytes 393248 | tf_op jit(solution)/shard_map/ppermute | solution.py:42
  95.8 2.2 %shard_map.66 = (bf16[512,384]{1,0:T(8,128)(2,1)S(1)}, bf16[512,384]{1,0:T(8,128)(2,1)S(1)}, bf16[512,384]{1,0:T(8,128)(2,1)S(1)}) custom-call(bf16[512,384]{1,0:T(8,128)(2,1)S(1)} %get-tuple-element.89.refs_0_, bf16[512,384]{1,0:T(8,128)(2,1)S(1)} %collective-permute-done.26.refs_1_, bf16[512,384]{1,0:T(8,128)(2,1)S(1)} %collective-permute-done.21.refs_2_, ...), custom_call_target="tpu_custom_call" | custom-call | bytes 1024 | tf_op jit(solution)/shard_map/pallas_call | solution.py:161
  100.1 5.7 %collective-permute-start.37 = (bf16[512,384]{1,0:T(8,128)(2,1)S(1)}, bf16[512,384]{1,0:T(8,128)(2,1)S(1)}, u32[]{:S(2)}, u32[]{:S(2)}) collective-permute-start(bf16[512,384]{1,0:T(8,128)(2,1)S(1)} %get-tuple-element.105), channel_id=1, source_target_pairs={{0,16},{4,20},{8,24},{12,28},{16,32},{20,36},{24,40},{28,44},{32,4... | collective-permute-start | bytes 1179656 | tf_op jit(solution)/shard_map/ppermute | solution.py:42
  105.8 3.1 %collective-permute-start.38 = (bf16[512,384]{1,0:T(8,128)(2,1)S(1)}, bf16[512,384]{1,0:T(8,128)(2,1)S(1)}, u32[]{:S(2)}, u32[]{:S(2)}) collective-permute-start(bf16[512,384]{1,0:T(8,128)(2,1)S(1)} %get-tuple-element.106), channel_id=1, source_target_pairs={{16,0},{20,4},{24,8},{28,12},{32,16},{36,20},{40,24},{44,28},{48,3... | collective-permute-start | bytes 1179656 | tf_op jit(solution)/shard_map/ppermute | solution.py:42
  109.0 5.4 %collective-permute-done.35.refs_6_ = bf16[512,384]{1,0:T(8,128)(2,1)S(1)} collective-permute-done((bf16[512,384]{1,0:T(8,128)(2,1)S(1)}, bf16[512,384]{1,0:T(8,128)(2,1)S(1)}, u32[]{:S(2)}, u32[]{:S(2)}) %collective-permute-start.35) | collective-permute-done | bytes 393248 | tf_op jit(solution)/shard_map/ppermute | solution.py:46
  114.5 7.6 %collective-permute-done.31.refs_2_ = bf16[512,384]{1,0:T(8,128)(2,1)S(1)} collective-permute-done((bf16[512,384]{1,0:T(8,128)(2,1)S(1)}, bf16[512,384]{1,0:T(8,128)(2,1)S(1)}, u32[]{:S(2)}, u32[]{:S(2)}) %collective-permute-start.31) | collective-permute-done | bytes 393248 | tf_op jit(solution)/shard_map/ppermute | solution.py:46
  122.0 3.0 %collective-permute-done.38.down_hi = bf16[512,384]{1,0:T(8,128)(2,1)S(1)} collective-permute-done((bf16[512,384]{1,0:T(8,128)(2,1)S(1)}, bf16[512,384]{1,0:T(8,128)(2,1)S(1)}, u32[]{:S(2)}, u32[]{:S(2)}) %collective-permute-start.38) | collective-permute-done | bytes 393248 | tf_op jit(solution)/shard_map/ppermute | solution.py:42
  (86 shorter events, 33.3 us)
Async XLA Ops:
  3.0 24.7 %collective-permute-start = (bf16[576,384]{1,0:T(8,128)(2,1)S(1)}, bf16[576,384]{1,0:T(8,128)(2,1)S(1)}, u32[]{:S(2)}, u32[]{:S(2)}) collective-permute-start(bf16[576,384]{1,0:T(8,128)(2,1)S(1)} %fusion.1.refs_0_), channel_id=1, source_target_pairs={{0,2},{1,3},{2,0},{3,1},{4,6},{5,7},{6,4},{7,5},{8,10},{9,11},{10,... | collective-permute-start | bytes 1327112 | tf_op jit(solution)/shard_map/ppermute | solution.py:46
  4.6 23.1 %collective-permute-start.4 = (bf16[576,384]{1,0:T(8,128)(2,1)S(1)}, bf16[576,384]{1,0:T(8,128)(2,1)S(1)}, u32[]{:S(2)}, u32[]{:S(2)}) collective-permute-start(bf16[576,384]{1,0:T(8,128)(2,1)S(1)} %fusion.1.refs_0_), channel_id=1, source_target_pairs={{0,1},{1,0},{2,3},{3,2},{4,5},{5,4},{6,7},{7,6},{8,9},{9,8},{10,11... | collective-permute-start | bytes 1327112 | tf_op jit(solution)/shard_map/ppermute | solution.py:50
  5.7 16.2 %collective-permute-start.1 = (bf16[64,384]{1,0:T(8,128)(2,1)S(1)}, bf16[64,384]{1,0:T(8,128)(2,1)S(1)}, u32[]{:S(2)}, u32[]{:S(2)}) collective-permute-start(bf16[64,384]{1,0:T(8,128)(2,1)S(1)} %get-tuple-element.118), channel_id=1, source_target_pairs={{0,4},{4,8},{8,12},{12,16},{16,20},{20,24},{24,28},{28,32},{32,36}... | collective-permute-start | bytes 147464 | tf_op jit(solution)/shard_map/ppermute | solution.py:42
  10.6 11.4 %collective-permute-start.2 = (bf16[64,384]{1,0:T(8,128)(2,1)S(1)}, bf16[64,384]{1,0:T(8,128)(2,1)S(1)}, u32[]{:S(2)}, u32[]{:S(2)}) collective-permute-start(bf16[64,384]{1,0:T(8,128)(2,1)S(1)} %get-tuple-element.117), channel_id=1, source_target_pairs={{4,0},{8,4},{12,8},{16,12},{20,16},{24,20},{28,24},{32,28},{36,32}... | collective-permute-start | bytes 147464 | tf_op jit(solution)/shard_map/ppermute | solution.py:42
  22.0 5.7 %collective-permute-start.3 = (bf16[128,384]{1,0:T(8,128)(2,1)S(1)}, bf16[128,384]{1,0:T(8,128)(2,1)S(1)}, u32[]{:S(2)}, u32[]{:S(2)}) collective-permute-start(bf16[128,384]{1,0:T(8,128)(2,1)S(1)} %shard_map.56.refs_5_), channel_id=1, source_target_pairs={{0,2},{1,3},{2,0},{3,1},{4,6},{5,7},{6,4},{7,5},{8,10},{9,11},{10,... | collective-permute-start | bytes 294920 | tf_op jit(solution)/shard_map/ppermute | solution.py:46
  22.2 12.2 %collective-permute-start.10 = (bf16[448,384]{1,0:T(8,128)(2,1)S(1)}, bf16[448,384]{1,0:T(8,128)(2,1)S(1)}, u32[]{:S(2)}, u32[]{:S(2)}) collective-permute-start(bf16[448,384]{1,0:T(8,128)(2,1)S(1)} %fusion.4.refs_9_), channel_id=1, source_target_pairs={{0,2},{1,3},{2,0},{3,1},{4,6},{5,7},{6,4},{7,5},{8,10},{9,11},{10,... | collective-permute-start | bytes 1032200 | tf_op jit(solution)/shard_map/ppermute | solution.py:46
  33.5 12.0 %collective-permute-start.14 = (bf16[512,384]{1,0:T(8,128)(2,1)S(1)}, bf16[512,384]{1,0:T(8,128)(2,1)S(1)}, u32[]{:S(2)}, u32[]{:S(2)}) collective-permute-start(bf16[512,384]{1,0:T(8,128)(2,1)S(1)} %get-tuple-element.68.refs_0_), channel_id=1, source_target_pairs={{0,2},{1,3},{2,0},{3,1},{4,6},{5,7},{6,4},{7,5},{8,10},{9,11},{10,... | collective-permute-start | bytes 1179656 | tf_op jit(solution)/shard_map/ppermute | solution.py:46
  34.4 11.9 %collective-permute-start.13 = (bf16[512,384]{1,0:T(8,128)(2,1)S(1)}, bf16[512,384]{1,0:T(8,128)(2,1)S(1)}, u32[]{:S(2)}, u32[]{:S(2)}) collective-permute-start(bf16[512,384]{1,0:T(8,128)(2,1)S(1)} %get-tuple-element.68.refs_0_), channel_id=1, source_target_pairs={{0,1},{1,0},{2,3},{3,2},{4,5},{5,4},{6,7},{7,6},{8,9},{9,8},{10,11... | collective-permute-start | bytes 1179656 | tf_op jit(solution)/shard_map/ppermute | solution.py:50
  39.6 14.4 %collective-permute-start.12 = (bf16[512,384]{1,0:T(8,128)(2,1)S(1)}, bf16[512,384]{1,0:T(8,128)(2,1)S(1)}, u32[]{:S(2)}, u32[]{:S(2)}) collective-permute-start(bf16[512,384]{1,0:T(8,128)(2,1)S(1)} %get-tuple-element.74.refs_0_), channel_id=1, source_target_pairs={{0,2},{1,3},{2,0},{3,1},{4,6},{5,7},{6,4},{7,5},{8,10},{9,11},{10,... | collective-permute-start | bytes 1179656 | tf_op jit(solution)/shard_map/ppermute | solution.py:46
  46.2 8.4 %collective-permute-start.17 = (bf16[512,384]{1,0:T(8,128)(2,1)S(1)}, bf16[512,384]{1,0:T(8,128)(2,1)S(1)}, u32[]{:S(2)}, u32[]{:S(2)}) collective-permute-start(bf16[512,384]{1,0:T(8,128)(2,1)S(1)} %get-tuple-element.74.refs_0_), channel_id=1, source_target_pairs={{0,1},{1,0},{2,3},{3,2},{4,5},{5,4},{6,7},{7,6},{8,9},{9,8},{10,11... | collective-permute-start | bytes 1179656 | tf_op jit(solution)/shard_map/ppermute | solution.py:50
  49.6 17.8 %collective-permute-start.22 = (bf16[512,384]{1,0:T(8,128)(2,1)S(1)}, bf16[512,384]{1,0:T(8,128)(2,1)S(1)}, u32[]{:S(2)}, u32[]{:S(2)}) collective-permute-start(bf16[512,384]{1,0:T(8,128)(2,1)S(1)} %get-tuple-element.80), channel_id=1, source_target_pairs={{0,4},{4,8},{8,12},{12,16},{16,20},{20,24},{24,28},{28,32},{32,36}... | collective-permute-start | bytes 1179656 | tf_op jit(solution)/shard_map/ppermute | solution.py:42
  58.1 19.7 %collective-permute-start.20 = (bf16[512,384]{1,0:T(8,128)(2,1)S(1)}, bf16[512,384]{1,0:T(8,128)(2,1)S(1)}, u32[]{:S(2)}, u32[]{:S(2)}) collective-permute-start(bf16[512,384]{1,0:T(8,128)(2,1)S(1)} %get-tuple-element.77), channel_id=1, source_target_pairs={{4,0},{8,4},{12,8},{16,12},{20,16},{24,20},{28,24},{32,28},{36,32}... | collective-permute-start | bytes 1179656 | tf_op jit(solution)/shard_map/ppermute | solution.py:42
  68.6 23.2 %collective-permute-start.23 = (bf16[512,384]{1,0:T(8,128)(2,1)S(1)}, bf16[512,384]{1,0:T(8,128)(2,1)S(1)}, u32[]{:S(2)}, u32[]{:S(2)}) collective-permute-start(bf16[512,384]{1,0:T(8,128)(2,1)S(1)} %get-tuple-element.98.refs_0_), channel_id=1, source_target_pairs={{0,16},{4,20},{8,24},{12,28},{16,32},{20,36},{24,40},{28,44},{32,4... | collective-permute-start | bytes 1179656 | tf_op jit(solution)/shard_map/ppermute | solution.py:42
  70.5 22.4 %collective-permute-start.24 = (bf16[512,384]{1,0:T(8,128)(2,1)S(1)}, bf16[512,384]{1,0:T(8,128)(2,1)S(1)}, u32[]{:S(2)}, u32[]{:S(2)}) collective-permute-start(bf16[512,384]{1,0:T(8,128)(2,1)S(1)} %get-tuple-element.98.refs_0_), channel_id=1, source_target_pairs={{16,0},{20,4},{24,8},{28,12},{32,16},{36,20},{40,24},{44,28},{48,3... | collective-permute-start | bytes 1179656 | tf_op jit(solution)/shard_map/ppermute | solution.py:42
  79.0 13.9 %collective-permute-start.21 = (bf16[512,384]{1,0:T(8,128)(2,1)S(1)}, bf16[512,384]{1,0:T(8,128)(2,1)S(1)}, u32[]{:S(2)}, u32[]{:S(2)}) collective-permute-start(bf16[512,384]{1,0:T(8,128)(2,1)S(1)} %get-tuple-element.89.refs_0_), channel_id=1, source_target_pairs={{0,2},{1,3},{2,0},{3,1},{4,6},{5,7},{6,4},{7,5},{8,10},{9,11},{10,... | collective-permute-start | bytes 1179656 | tf_op jit(solution)/shard_map/ppermute | solution.py:46
  81.2 12.8 %collective-permute-start.26 = (bf16[512,384]{1,0:T(8,128)(2,1)S(1)}, bf16[512,384]{1,0:T(8,128)(2,1)S(1)}, u32[]{:S(2)}, u32[]{:S(2)}) collective-permute-start(bf16[512,384]{1,0:T(8,128)(2,1)S(1)} %get-tuple-element.89.refs_0_), channel_id=1, source_target_pairs={{0,1},{1,0},{2,3},{3,2},{4,5},{5,4},{6,7},{7,6},{8,9},{9,8},{10,11... | collective-permute-start | bytes 1179656 | tf_op jit(solution)/shard_map/ppermute | solution.py:50
  94.1 14.9 %collective-permute-start.33 = (bf16[512,384]{1,0:T(8,128)(2,1)S(1)}, bf16[512,384]{1,0:T(8,128)(2,1)S(1)}, u32[]{:S(2)}, u32[]{:S(2)}) collective-permute-start(bf16[512,384]{1,0:T(8,128)(2,1)S(1)} %get-tuple-element.98.refs_0_), channel_id=1, source_target_pairs={{0,2},{1,3},{2,0},{3,1},{4,6},{5,7},{6,4},{7,5},{8,10},{9,11},{10,... | collective-permute-start | bytes 1179656 | tf_op jit(solution)/shard_map/ppermute | solution.py:46
  98.0 16.5 %collective-permute-start.35 = (bf16[512,384]{1,0:T(8,128)(2,1)S(1)}, bf16[512,384]{1,0:T(8,128)(2,1)S(1)}, u32[]{:S(2)}, u32[]{:S(2)}) collective-permute-start(bf16[512,384]{1,0:T(8,128)(2,1)S(1)} %collective-permute-done.23.refs_4_), channel_id=1, source_target_pairs={{0,2},{1,3},{2,0},{3,1},{4,6},{5,7},{6,4},{7,5},{8,10},{9,11},{10,... | collective-permute-start | bytes 1179656 | tf_op jit(solution)/shard_map/ppermute | solution.py:46
  98.4 23.6 %collective-permute-start.31 = (bf16[512,384]{1,0:T(8,128)(2,1)S(1)}, bf16[512,384]{1,0:T(8,128)(2,1)S(1)}, u32[]{:S(2)}, u32[]{:S(2)}) collective-permute-start(bf16[512,384]{1,0:T(8,128)(2,1)S(1)} %collective-permute-done.24.refs_0_), channel_id=1, source_target_pairs={{0,2},{1,3},{2,0},{3,1},{4,6},{5,7},{6,4},{7,5},{8,10},{9,11},{10,... | collective-permute-start | bytes 1179656 | tf_op jit(solution)/shard_map/ppermute | solution.py:46
  100.1 22.0 %collective-permute-start.37 = (bf16[512,384]{1,0:T(8,128)(2,1)S(1)}, bf16[512,384]{1,0:T(8,128)(2,1)S(1)}, u32[]{:S(2)}, u32[]{:S(2)}) collective-permute-start(bf16[512,384]{1,0:T(8,128)(2,1)S(1)} %get-tuple-element.105), channel_id=1, source_target_pairs={{0,16},{4,20},{8,24},{12,28},{16,32},{20,36},{24,40},{28,44},{32,4... | collective-permute-start | bytes 1179656 | tf_op jit(solution)/shard_map/ppermute | solution.py:42
  105.8 19.3 %collective-permute-start.38 = (bf16[512,384]{1,0:T(8,128)(2,1)S(1)}, bf16[512,384]{1,0:T(8,128)(2,1)S(1)}, u32[]{:S(2)}, u32[]{:S(2)}) collective-permute-start(bf16[512,384]{1,0:T(8,128)(2,1)S(1)} %get-tuple-element.106), channel_id=1, source_target_pairs={{16,0},{20,4},{24,8},{28,12},{32,16},{36,20},{40,24},{44,28},{48,3... | collective-permute-start | bytes 1179656 | tf_op jit(solution)/shard_map/ppermute | solution.py:42
  108.9 16.4 %collective-permute-start.34 = (bf16[512,384]{1,0:T(8,128)(2,1)S(1)}, bf16[512,384]{1,0:T(8,128)(2,1)S(1)}, u32[]{:S(2)}, u32[]{:S(2)}) collective-permute-start(bf16[512,384]{1,0:T(8,128)(2,1)S(1)} %collective-permute-done.33.refs_2_), channel_id=1, source_target_pairs={{0,1},{1,0},{2,3},{3,2},{4,5},{5,4},{6,7},{7,6},{8,9},{9,8},{10,11... | collective-permute-start | bytes 1179656 | tf_op jit(solution)/shard_map/ppermute | solution.py:50
  114.5 10.9 %collective-permute-start.36 = (bf16[512,384]{1,0:T(8,128)(2,1)S(1)}, bf16[512,384]{1,0:T(8,128)(2,1)S(1)}, u32[]{:S(2)}, u32[]{:S(2)}) collective-permute-start(bf16[512,384]{1,0:T(8,128)(2,1)S(1)} %collective-permute-done.35.refs_6_), channel_id=1, source_target_pairs={{0,1},{1,0},{2,3},{3,2},{4,5},{5,4},{6,7},{7,6},{8,9},{9,8},{10,11... | collective-permute-start | bytes 1179656 | tf_op jit(solution)/shard_map/ppermute | solution.py:50
  122.0 5.1 %collective-permute-start.32 = (bf16[512,384]{1,0:T(8,128)(2,1)S(1)}, bf16[512,384]{1,0:T(8,128)(2,1)S(1)}, u32[]{:S(2)}, u32[]{:S(2)}) collective-permute-start(bf16[512,384]{1,0:T(8,128)(2,1)S(1)} %collective-permute-done.31.refs_2_), channel_id=1, source_target_pairs={{0,1},{1,0},{2,3},{3,2},{4,5},{5,4},{6,7},{7,6},{8,9},{9,8},{10,11... | collective-permute-start | bytes 1179656 | tf_op jit(solution)/shard_map/ppermute | solution.py:50
  (17 other events, 45.4 us)

commit v11 on v10

--- a/solution.py
+++ b/solution.py
@@ -137,13 +137,6 @@
     o_ref[R:, :] = high_ref[...]
 
 
-def part_kernel(*refs):
-    own, low, (s_ref, vec_ref, w_ref, o_ref) = refs[:4], refs[4:8], refs[8:]
-    total = s_ref[...].astype(F32) + vec_ref[0:1, :]
-    total = total + dot(joined(own, 1), w_ref[:, W : 2 * W])
-    o_ref[...] = total + dot(joined(low, 1), w_ref[:, 0:W])
-
-
 def upper_kernel(s_hi, q_hi, up_hi, down_hi, vec_ref, o_ref):
     total = vec_ref[0:1, :]
     for ref in (s_hi, q_hi, up_hi, down_hi):
@@ -152,8 +145,12 @@
 
 
 def out_kernel(*refs):
-    high, (part, upper, w_ref, o_ref) = refs[:4], refs[4:]
-    o_ref[:MID, :] = (part[...] + dot(joined(high), w_ref[:, 2 * W : 3 * W])).astype(BF16)
+    own, low, high, (s_lo, upper, vec_ref, w_ref, o_ref) = refs[:4], refs[4:8], refs[8:12], refs[12:]
+    total = s_lo[...].astype(F32) + vec_ref[0:1, :]
+    total = total + dot(joined(own), w_ref[:, W : 2 * W])
+    total = total + dot(joined(low), w_ref[:, 0:W])
+    total = total + dot(joined(high), w_ref[:, 2 * W : 3 * W])
+    o_ref[:MID, :] = total.astype(BF16)
     o_ref[MID:, :] = upper[...]
 
 
@@ -260,9 +257,8 @@
     g_own = (a_lo, near_own, far_own, core_swap(far_own))
     g_low = (from_low, near_low, far_low, core_swap(far_low))
     g_high = (from_high, near_high, far_high, core_swap(far_high))
-    (part,) = call(part_kernel, (*g_own, *g_low, s_lo, vec2, w2), halves[:1], dtype=F32)
     (upper,) = call(upper_kernel, (s_hi, q_hi, up_hi, down_hi, vec2), halves[:1], flops=COST)
-    (out,) = call(out_kernel, (*g_high, part, upper, w2), [ROWS])
+    (out,) = call(out_kernel, (*g_own, *g_low, *g_high, s_lo, upper, vec2, w2), [ROWS])
     return out
 
 

time: 130 us -> 130 us (level)
    pallas_call x12 -> x11, Pallas kernels: 20.1 us -> 20 us  [call(): pl.pallas_call(kernel, out_shape=[jax.ShapeDtypeStruct((r, W), dtype) for...]
  transfers between devices with their start and end apart: 39 -> 39, of which waited for: 20 -> 20; matrix products, arithmetic and copies ran while one was open for 2% -> 2% of each run, Pallas kernels for 19% -> 18%
where the time goes in v11:
time: 130 us; the launch traced here: 129 us
  starting transfers between devices  51.5 us (40%)
  waiting for transfers between devices  44.9 us (35%)
  Pallas kernels  26.1 us (20%)
  other arithmetic  4.19 us (3%)
  local copies, waits for them, and re-layouts  1.9 us (1%)
    ppermute x8, starting transfers between devices, shifted(): return lax.ppermute(array, 'seq', pairs)  38 us
    ppermute x9, waiting for transfers between devices, chip_swap(): return lax.ppermute(array, 'ch', [(i, i ^ 2) for i in range(4)])  21.4 us
    pallas_call x11, Pallas kernels, call(): pl.pallas_call(kernel, out_shape=[jax.ShapeDtypeStruct((r, W), dtype) for...  20 us
    ppermute x8, waiting for transfers between devices, shifted(): return lax.ppermute(array, 'seq', pairs)  17.4 us
    ppermute x9, starting transfers between devices, chip_swap(): return lax.ppermute(array, 'ch', [(i, i ^ 2) for i in range(4)])  8.13 us
    pallas_call x3, Pallas kernels, staged(): pl.pallas_call(functools.partial(stage_kernel, layer), out_shape=jax.Shap...  6.13 us
    ppermute x22, waiting for transfers between devices, core_swap(): return lax.ppermute(array, 'ch', [(i, i ^ 1) for i in range(4)])  6.13 us
    ppermute x22, starting transfers between devices, core_swap(): return lax.ppermute(array, 'ch', [(i, i ^ 1) for i in range(4)])  5.33 us
  transfers between devices with their start and end apart: 39, of which 20 were waited for; matrix products, arithmetic and copies ran while one was open for 2% of the time, Pallas kernels for 18%

profile of v11, /device:TPU:6, one launch (start us, length us, event | category | flops | bytes accessed | tf_op | source)
XLA Modules:
  0.0 128.9 jit_solution(2472691582496065888)
XLA Ops:
  0.9 2.1 %fusion.1.refs_0_ = bf16[576,384]{1,0:T(8,128)(2,1)S(1)} fusion(f32[384]{0:T(512)S(1)} %get-tuple-element.129, f32[384]{0:T(512)S(1)} %get-tuple-element.123, bf16[1024,384]{1,0:T(8,128)(2,1)} %refs_13_.1), kind=kLoop, calls=%fused_computation.3 | loop fusion | flops 7741440 | bytes 887808 | tf_op jit(solution)/shard_map/convert_element_type | solution.py:191
  5.7 4.8 %collective-permute-start.1 = (bf16[64,384]{1,0:T(8,128)(2,1)S(1)}, bf16[64,384]{1,0:T(8,128)(2,1)S(1)}, u32[]{:S(2)}, u32[]{:S(2)}) collective-permute-start(bf16[64,384]{1,0:T(8,128)(2,1)S(1)} %get-tuple-element.118), channel_id=1, source_target_pairs={{0,4},{4,8},{8,12},{12,16},{16,20},{20,24},{24,28},{28,32},{32,36}... | collective-permute-start | bytes 147464 | tf_op jit(solution)/shard_map/ppermute | solution.py:42
  10.6 7.5 %collective-permute-start.2 = (bf16[64,384]{1,0:T(8,128)(2,1)S(1)}, bf16[64,384]{1,0:T(8,128)(2,1)S(1)}, u32[]{:S(2)}, u32[]{:S(2)}) collective-permute-start(bf16[64,384]{1,0:T(8,128)(2,1)S(1)} %get-tuple-element.117), channel_id=1, source_target_pairs={{4,0},{8,4},{12,8},{16,12},{20,16},{24,20},{28,24},{32,28},{36,32}... | collective-permute-start | bytes 147464 | tf_op jit(solution)/shard_map/ppermute | solution.py:42
  19.9 2.0 %shard_map.55.refs_11_.refs_15_ = bf16[1536,1152]{1,0:T(8,128)(2,1)S(1)} custom-call(s32[1]{0:T(128)} %bitcast.ch_ref, bf16[3,3,1536,384]{3,2,1,0:T(8,128)(2,1)} %w_hbm.5), custom_call_target="tpu_custom_call" | custom-call | tf_op jit(solution)/shard_map/pallas_call | solution.py:170
  24.1 3.6 %collective-permute-done.3.refs_7_ = bf16[128,384]{1,0:T(8,128)(2,1)S(1)} collective-permute-done((bf16[128,384]{1,0:T(8,128)(2,1)S(1)}, bf16[128,384]{1,0:T(8,128)(2,1)S(1)}, u32[]{:S(2)}, u32[]{:S(2)}) %collective-permute-start.3) | collective-permute-done | bytes 98336 | tf_op jit(solution)/shard_map/ppermute | solution.py:46
  29.9 3.6 %shard_map.57 = (bf16[512,384]{1,0:T(8,128)(2,1)S(1)}, bf16[512,384]{1,0:T(8,128)(2,1)S(1)}) custom-call(bf16[576,384]{1,0:T(8,128)(2,1)S(1)} %fusion.1.refs_0_, bf16[576,384]{1,0:T(8,128)(2,1)S(1)} %collective-permute-done.4.refs_1_, bf16[576,384]{1,0:T(8,128)(2,1)S(1)} %collective-permute-done.refs_2_, ...), custom_call_target="tpu_custom_call" | custom-call | bytes 1024 | tf_op jit(solution)/shard_map/pallas_call | solution.py:158
  36.0 3.6 %shard_map.58 = (bf16[512,384]{1,0:T(8,128)(2,1)S(1)}, bf16[512,384]{1,0:T(8,128)(2,1)S(1)}) custom-call(bf16[576,384]{1,0:T(8,128)(2,1)S(1)} %fusion.1.refs_0_, bf16[576,384]{1,0:T(8,128)(2,1)S(1)} %collective-permute-done.4.refs_1_, bf16[576,384]{1,0:T(8,128)(2,1)S(1)} %collective-permute-done.refs_2_, ...), custom_call_target="tpu_custom_call" | custom-call | bytes 1024 | tf_op jit(solution)/shard_map/pallas_call | solution.py:158
  41.5 2.0 %shard_map.59.refs_5_ = bf16[1536,1152]{1,0:T(8,128)(2,1)S(1)} custom-call(s32[1]{0:T(128)} %bitcast.ch_ref, bf16[3,3,1536,384]{3,2,1,0:T(8,128)(2,1)} %w_hbm.5), custom_call_target="tpu_custom_call" | custom-call | tf_op jit(solution)/shard_map/pallas_call | solution.py:170
  43.5 2.0 %collective-permute-done.14.refs_2_ = bf16[512,384]{1,0:T(8,128)(2,1)S(1)} collective-permute-done((bf16[512,384]{1,0:T(8,128)(2,1)S(1)}, bf16[512,384]{1,0:T(8,128)(2,1)S(1)}, u32[]{:S(2)}, u32[]{:S(2)}) %collective-permute-start.14) | collective-permute-done | bytes 393248 | tf_op jit(solution)/shard_map/ppermute | solution.py:46
  47.4 2.2 %shard_map.60 = (bf16[512,384]{1,0:T(8,128)(2,1)S(1)}, bf16[512,384]{1,0:T(8,128)(2,1)S(1)}, bf16[512,384]{1,0:T(8,128)(2,1)S(1)}) custom-call(bf16[512,384]{1,0:T(8,128)(2,1)S(1)} %get-tuple-element.68.refs_0_, bf16[512,384]{1,0:T(8,128)(2,1)S(1)} %collective-permute-done.13.refs_1_, bf16[512,384]{1,0:T(8,128)(2,1)S(1)} %collective-permute-done.14.refs_2_, ...), custom_call_target="tpu_custom_call" | custom-call | bytes 1024 | tf_op jit(solution)/shard_map/pallas_call | solution.py:158
  51.6 2.4 %collective-permute-done.12.refs_2_ = bf16[512,384]{1,0:T(8,128)(2,1)S(1)} collective-permute-done((bf16[512,384]{1,0:T(8,128)(2,1)S(1)}, bf16[512,384]{1,0:T(8,128)(2,1)S(1)}, u32[]{:S(2)}, u32[]{:S(2)}) %collective-permute-start.12) | collective-permute-done | bytes 393248 | tf_op jit(solution)/shard_map/ppermute | solution.py:46
  55.9 2.2 %shard_map.61 = (bf16[512,384]{1,0:T(8,128)(2,1)S(1)}, bf16[512,384]{1,0:T(8,128)(2,1)S(1)}, bf16[512,384]{1,0:T(8,128)(2,1)S(1)}) custom-call(bf16[512,384]{1,0:T(8,128)(2,1)S(1)} %get-tuple-element.74.refs_0_, bf16[512,384]{1,0:T(8,128)(2,1)S(1)} %collective-permute-done.17.refs_1_, bf16[512,384]{1,0:T(8,128)(2,1)S(1)} %collective-permute-done.12.refs_2_, ...), custom_call_target="tpu_custom_call" | custom-call | bytes 1024 | tf_op jit(solution)/shard_map/pallas_call | solution.py:158
  58.1 6.1 %collective-permute-start.20 = (bf16[512,384]{1,0:T(8,128)(2,1)S(1)}, bf16[512,384]{1,0:T(8,128)(2,1)S(1)}, u32[]{:S(2)}, u32[]{:S(2)}) collective-permute-start(bf16[512,384]{1,0:T(8,128)(2,1)S(1)} %get-tuple-element.77), channel_id=1, source_target_pairs={{4,0},{8,4},{12,8},{16,12},{20,16},{24,20},{28,24},{32,28},{36,32}... | collective-permute-start | bytes 1179656 | tf_op jit(solution)/shard_map/ppermute | solution.py:42
  64.2 3.2 %collective-permute-done.22.up = bf16[512,384]{1,0:T(8,128)(2,1)S(1)} collective-permute-done((bf16[512,384]{1,0:T(8,128)(2,1)S(1)}, bf16[512,384]{1,0:T(8,128)(2,1)S(1)}, u32[]{:S(2)}, u32[]{:S(2)}) %collective-permute-start.22) | collective-permute-done | bytes 393248 | tf_op jit(solution)/shard_map/ppermute | solution.py:42
  70.5 6.9 %collective-permute-start.24 = (bf16[512,384]{1,0:T(8,128)(2,1)S(1)}, bf16[512,384]{1,0:T(8,128)(2,1)S(1)}, u32[]{:S(2)}, u32[]{:S(2)}) collective-permute-start(bf16[512,384]{1,0:T(8,128)(2,1)S(1)} %get-tuple-element.86.refs_0_), channel_id=1, source_target_pairs={{16,0},{20,4},{24,8},{28,12},{32,16},{36,20},{40,24},{44,28},{48,3... | collective-permute-start | bytes 1179656 | tf_op jit(solution)/shard_map/ppermute | solution.py:42
  79.2 2.0 %shard_map.65.refs_5_.refs_15_ = bf16[1536,1152]{1,0:T(8,128)(2,1)S(1)} custom-call(s32[1]{0:T(128)} %bitcast.ch_ref, bf16[3,3,1536,384]{3,2,1,0:T(8,128)(2,1)} %w_hbm.5), custom_call_target="tpu_custom_call" | custom-call | tf_op jit(solution)/shard_map/pallas_call | solution.py:170
  81.7 10.0 %collective-permute-done.23.refs_4_ = bf16[512,384]{1,0:T(8,128)(2,1)S(1)} collective-permute-done((bf16[512,384]{1,0:T(8,128)(2,1)S(1)}, bf16[512,384]{1,0:T(8,128)(2,1)S(1)}, u32[]{:S(2)}, u32[]{:S(2)}) %collective-permute-start.23) | collective-permute-done | bytes 393248 | tf_op jit(solution)/shard_map/ppermute | solution.py:42
  95.8 2.2 %shard_map.66 = (bf16[512,384]{1,0:T(8,128)(2,1)S(1)}, bf16[512,384]{1,0:T(8,128)(2,1)S(1)}, bf16[512,384]{1,0:T(8,128)(2,1)S(1)}) custom-call(bf16[512,384]{1,0:T(8,128)(2,1)S(1)} %get-tuple-element.91.refs_0_, bf16[512,384]{1,0:T(8,128)(2,1)S(1)} %collective-permute-done.28.refs_1_, bf16[512,384]{1,0:T(8,128)(2,1)S(1)} %collective-permute-done.21.refs_2_, ...), custom_call_target="tpu_custom_call" | custom-call | bytes 1024 | tf_op jit(solution)/shard_map/pallas_call | solution.py:158
  100.1 5.7 %collective-permute-start.37 = (bf16[512,384]{1,0:T(8,128)(2,1)S(1)}, bf16[512,384]{1,0:T(8,128)(2,1)S(1)}, u32[]{:S(2)}, u32[]{:S(2)}) collective-permute-start(bf16[512,384]{1,0:T(8,128)(2,1)S(1)} %get-tuple-element.105), channel_id=1, source_target_pairs={{0,16},{4,20},{8,24},{12,28},{16,32},{20,36},{24,40},{28,44},{32,4... | collective-permute-start | bytes 1179656 | tf_op jit(solution)/shard_map/ppermute | solution.py:42
  105.8 3.1 %collective-permute-start.38 = (bf16[512,384]{1,0:T(8,128)(2,1)S(1)}, bf16[512,384]{1,0:T(8,128)(2,1)S(1)}, u32[]{:S(2)}, u32[]{:S(2)}) collective-permute-start(bf16[512,384]{1,0:T(8,128)(2,1)S(1)} %get-tuple-element.106), channel_id=1, source_target_pairs={{16,0},{20,4},{24,8},{28,12},{32,16},{36,20},{40,24},{44,28},{48,3... | collective-permute-start | bytes 1179656 | tf_op jit(solution)/shard_map/ppermute | solution.py:42
  109.1 5.4 %collective-permute-done.33.refs_6_ = bf16[512,384]{1,0:T(8,128)(2,1)S(1)} collective-permute-done((bf16[512,384]{1,0:T(8,128)(2,1)S(1)}, bf16[512,384]{1,0:T(8,128)(2,1)S(1)}, u32[]{:S(2)}, u32[]{:S(2)}) %collective-permute-start.33) | collective-permute-done | bytes 393248 | tf_op jit(solution)/shard_map/ppermute | solution.py:46
  114.5 7.6 %collective-permute-done.35.refs_10_ = bf16[512,384]{1,0:T(8,128)(2,1)S(1)} collective-permute-done((bf16[512,384]{1,0:T(8,128)(2,1)S(1)}, bf16[512,384]{1,0:T(8,128)(2,1)S(1)}, u32[]{:S(2)}, u32[]{:S(2)}) %collective-permute-start.35) | collective-permute-done | bytes 393248 | tf_op jit(solution)/shard_map/ppermute | solution.py:46
  122.0 3.1 %collective-permute-done.38.down_hi = bf16[512,384]{1,0:T(8,128)(2,1)S(1)} collective-permute-done((bf16[512,384]{1,0:T(8,128)(2,1)S(1)}, bf16[512,384]{1,0:T(8,128)(2,1)S(1)}, u32[]{:S(2)}, u32[]{:S(2)}) %collective-permute-start.38) | collective-permute-done | bytes 393248 | tf_op jit(solution)/shard_map/ppermute | solution.py:42
  125.4 3.5 %shard_map.68 = bf16[1024,384]{1,0:T(8,128)(2,1)} custom-call(bf16[512,384]{1,0:T(8,128)(2,1)S(1)} %get-tuple-element.86.refs_0_, bf16[512,384]{1,0:T(8,128)(2,1)S(1)} %collective-permute-done.25.refs_1_, bf16[512,384]{1,0:T(8,128)(2,1)S(1)} %collective-permute-done.26.refs_2_, bf16[512,384]{1,0:T(8,128)(2,1)S(1)} %collective-permute-done.27.refs_3_, ...), custom_call_target="tpu_custom_call" | custom-call | bytes 1024 | tf_op jit(solution)/shard_map/pallas_call | solution.py:158
  (85 shorter events, 31.5 us)
Async XLA Ops:
  3.0 24.7 %collective-permute-start = (bf16[576,384]{1,0:T(8,128)(2,1)S(1)}, bf16[576,384]{1,0:T(8,128)(2,1)S(1)}, u32[]{:S(2)}, u32[]{:S(2)}) collective-permute-start(bf16[576,384]{1,0:T(8,128)(2,1)S(1)} %fusion.1.refs_0_), channel_id=1, source_target_pairs={{0,2},{1,3},{2,0},{3,1},{4,6},{5,7},{6,4},{7,5},{8,10},{9,11},{10,... | collective-permute-start | bytes 1327112 | tf_op jit(solution)/shard_map/ppermute | solution.py:46
  4.6 23.1 %collective-permute-start.4 = (bf16[576,384]{1,0:T(8,128)(2,1)S(1)}, bf16[576,384]{1,0:T(8,128)(2,1)S(1)}, u32[]{:S(2)}, u32[]{:S(2)}) collective-permute-start(bf16[576,384]{1,0:T(8,128)(2,1)S(1)} %fusion.1.refs_0_), channel_id=1, source_target_pairs={{0,1},{1,0},{2,3},{3,2},{4,5},{5,4},{6,7},{7,6},{8,9},{9,8},{10,11... | collective-permute-start | bytes 1327112 | tf_op jit(solution)/shard_map/ppermute | solution.py:50
  5.7 16.2 %collective-permute-start.1 = (bf16[64,384]{1,0:T(8,128)(2,1)S(1)}, bf16[64,384]{1,0:T(8,128)(2,1)S(1)}, u32[]{:S(2)}, u32[]{:S(2)}) collective-permute-start(bf16[64,384]{1,0:T(8,128)(2,1)S(1)} %get-tuple-element.118), channel_id=1, source_target_pairs={{0,4},{4,8},{8,12},{12,16},{16,20},{20,24},{24,28},{28,32},{32,36}... | collective-permute-start | bytes 147464 | tf_op jit(solution)/shard_map/ppermute | solution.py:42
  10.6 11.4 %collective-permute-start.2 = (bf16[64,384]{1,0:T(8,128)(2,1)S(1)}, bf16[64,384]{1,0:T(8,128)(2,1)S(1)}, u32[]{:S(2)}, u32[]{:S(2)}) collective-permute-start(bf16[64,384]{1,0:T(8,128)(2,1)S(1)} %get-tuple-element.117), channel_id=1, source_target_pairs={{4,0},{8,4},{12,8},{16,12},{20,16},{24,20},{28,24},{32,28},{36,32}... | collective-permute-start | bytes 147464 | tf_op jit(solution)/shard_map/ppermute | solution.py:42
  22.0 5.7 %collective-permute-start.3 = (bf16[128,384]{1,0:T(8,128)(2,1)S(1)}, bf16[128,384]{1,0:T(8,128)(2,1)S(1)}, u32[]{:S(2)}, u32[]{:S(2)}) collective-permute-start(bf16[128,384]{1,0:T(8,128)(2,1)S(1)} %shard_map.56.refs_5_), channel_id=1, source_target_pairs={{0,2},{1,3},{2,0},{3,1},{4,6},{5,7},{6,4},{7,5},{8,10},{9,11},{10,... | collective-permute-start | bytes 294920 | tf_op jit(solution)/shard_map/ppermute | solution.py:46
  22.2 12.2 %collective-permute-start.10 = (bf16[448,384]{1,0:T(8,128)(2,1)S(1)}, bf16[448,384]{1,0:T(8,128)(2,1)S(1)}, u32[]{:S(2)}, u32[]{:S(2)}) collective-permute-start(bf16[448,384]{1,0:T(8,128)(2,1)S(1)} %fusion.4.refs_9_), channel_id=1, source_target_pairs={{0,2},{1,3},{2,0},{3,1},{4,6},{5,7},{6,4},{7,5},{8,10},{9,11},{10,... | collective-permute-start | bytes 1032200 | tf_op jit(solution)/shard_map/ppermute | solution.py:46
  33.5 12.0 %collective-permute-start.14 = (bf16[512,384]{1,0:T(8,128)(2,1)S(1)}, bf16[512,384]{1,0:T(8,128)(2,1)S(1)}, u32[]{:S(2)}, u32[]{:S(2)}) collective-permute-start(bf16[512,384]{1,0:T(8,128)(2,1)S(1)} %get-tuple-element.68.refs_0_), channel_id=1, source_target_pairs={{0,2},{1,3},{2,0},{3,1},{4,6},{5,7},{6,4},{7,5},{8,10},{9,11},{10,... | collective-permute-start | bytes 1179656 | tf_op jit(solution)/shard_map/ppermute | solution.py:46
  34.4 11.9 %collective-permute-start.13 = (bf16[512,384]{1,0:T(8,128)(2,1)S(1)}, bf16[512,384]{1,0:T(8,128)(2,1)S(1)}, u32[]{:S(2)}, u32[]{:S(2)}) collective-permute-start(bf16[512,384]{1,0:T(8,128)(2,1)S(1)} %get-tuple-element.68.refs_0_), channel_id=1, source_target_pairs={{0,1},{1,0},{2,3},{3,2},{4,5},{5,4},{6,7},{7,6},{8,9},{9,8},{10,11... | collective-permute-start | bytes 1179656 | tf_op jit(solution)/shard_map/ppermute | solution.py:50
  39.6 14.4 %collective-permute-start.12 = (bf16[512,384]{1,0:T(8,128)(2,1)S(1)}, bf16[512,384]{1,0:T(8,128)(2,1)S(1)}, u32[]{:S(2)}, u32[]{:S(2)}) collective-permute-start(bf16[512,384]{1,0:T(8,128)(2,1)S(1)} %get-tuple-element.74.refs_0_), channel_id=1, source_target_pairs={{0,2},{1,3},{2,0},{3,1},{4,6},{5,7},{6,4},{7,5},{8,10},{9,11},{10,... | collective-permute-start | bytes 1179656 | tf_op jit(solution)/shard_map/ppermute | solution.py:46
  46.2 8.4 %collective-permute-start.17 = (bf16[512,384]{1,0:T(8,128)(2,1)S(1)}, bf16[512,384]{1,0:T(8,128)(2,1)S(1)}, u32[]{:S(2)}, u32[]{:S(2)}) collective-permute-start(bf16[512,384]{1,0:T(8,128)(2,1)S(1)} %get-tuple-element.74.refs_0_), channel_id=1, source_target_pairs={{0,1},{1,0},{2,3},{3,2},{4,5},{5,4},{6,7},{7,6},{8,9},{9,8},{10,11... | collective-permute-start | bytes 1179656 | tf_op jit(solution)/shard_map/ppermute | solution.py:50
  49.6 17.8 %collective-permute-start.22 = (bf16[512,384]{1,0:T(8,128)(2,1)S(1)}, bf16[512,384]{1,0:T(8,128)(2,1)S(1)}, u32[]{:S(2)}, u32[]{:S(2)}) collective-permute-start(bf16[512,384]{1,0:T(8,128)(2,1)S(1)} %get-tuple-element.80), channel_id=1, source_target_pairs={{0,4},{4,8},{8,12},{12,16},{16,20},{20,24},{24,28},{28,32},{32,36}... | collective-permute-start | bytes 1179656 | tf_op jit(solution)/shard_map/ppermute | solution.py:42
  58.1 19.7 %collective-permute-start.20 = (bf16[512,384]{1,0:T(8,128)(2,1)S(1)}, bf16[512,384]{1,0:T(8,128)(2,1)S(1)}, u32[]{:S(2)}, u32[]{:S(2)}) collective-permute-start(bf16[512,384]{1,0:T(8,128)(2,1)S(1)} %get-tuple-element.77), channel_id=1, source_target_pairs={{4,0},{8,4},{12,8},{16,12},{20,16},{24,20},{28,24},{32,28},{36,32}... | collective-permute-start | bytes 1179656 | tf_op jit(solution)/shard_map/ppermute | solution.py:42
  68.6 23.2 %collective-permute-start.23 = (bf16[512,384]{1,0:T(8,128)(2,1)S(1)}, bf16[512,384]{1,0:T(8,128)(2,1)S(1)}, u32[]{:S(2)}, u32[]{:S(2)}) collective-permute-start(bf16[512,384]{1,0:T(8,128)(2,1)S(1)} %get-tuple-element.86.refs_0_), channel_id=1, source_target_pairs={{0,16},{4,20},{8,24},{12,28},{16,32},{20,36},{24,40},{28,44},{32,4... | collective-permute-start | bytes 1179656 | tf_op jit(solution)/shard_map/ppermute | solution.py:42
  70.5 22.4 %collective-permute-start.24 = (bf16[512,384]{1,0:T(8,128)(2,1)S(1)}, bf16[512,384]{1,0:T(8,128)(2,1)S(1)}, u32[]{:S(2)}, u32[]{:S(2)}) collective-permute-start(bf16[512,384]{1,0:T(8,128)(2,1)S(1)} %get-tuple-element.86.refs_0_), channel_id=1, source_target_pairs={{16,0},{20,4},{24,8},{28,12},{32,16},{36,20},{40,24},{44,28},{48,3... | collective-permute-start | bytes 1179656 | tf_op jit(solution)/shard_map/ppermute | solution.py:42
  77.5 4.3 %collective-permute-start.25 = (bf16[512,384]{1,0:T(8,128)(2,1)S(1)}, bf16[512,384]{1,0:T(8,128)(2,1)S(1)}, u32[]{:S(2)}, u32[]{:S(2)}) collective-permute-start(bf16[512,384]{1,0:T(8,128)(2,1)S(1)} %get-tuple-element.86.refs_0_), channel_id=1, source_target_pairs={{0,1},{1,0},{2,3},{3,2},{4,5},{5,4},{6,7},{7,6},{8,9},{9,8},{10,11... | collective-permute-start | bytes 1179656 | tf_op jit(solution)/shard_map/ppermute | solution.py:50
  79.0 13.9 %collective-permute-start.21 = (bf16[512,384]{1,0:T(8,128)(2,1)S(1)}, bf16[512,384]{1,0:T(8,128)(2,1)S(1)}, u32[]{:S(2)}, u32[]{:S(2)}) collective-permute-start(bf16[512,384]{1,0:T(8,128)(2,1)S(1)} %get-tuple-element.91.refs_0_), channel_id=1, source_target_pairs={{0,2},{1,3},{2,0},{3,1},{4,6},{5,7},{6,4},{7,5},{8,10},{9,11},{10,... | collective-permute-start | bytes 1179656 | tf_op jit(solution)/shard_map/ppermute | solution.py:46
  81.2 12.8 %collective-permute-start.28 = (bf16[512,384]{1,0:T(8,128)(2,1)S(1)}, bf16[512,384]{1,0:T(8,128)(2,1)S(1)}, u32[]{:S(2)}, u32[]{:S(2)}) collective-permute-start(bf16[512,384]{1,0:T(8,128)(2,1)S(1)} %get-tuple-element.91.refs_0_), channel_id=1, source_target_pairs={{0,1},{1,0},{2,3},{3,2},{4,5},{5,4},{6,7},{7,6},{8,9},{9,8},{10,11... | collective-permute-start | bytes 1179656 | tf_op jit(solution)/shard_map/ppermute | solution.py:50
  94.1 14.9 %collective-permute-start.26 = (bf16[512,384]{1,0:T(8,128)(2,1)S(1)}, bf16[512,384]{1,0:T(8,128)(2,1)S(1)}, u32[]{:S(2)}, u32[]{:S(2)}) collective-permute-start(bf16[512,384]{1,0:T(8,128)(2,1)S(1)} %get-tuple-element.86.refs_0_), channel_id=1, source_target_pairs={{0,2},{1,3},{2,0},{3,1},{4,6},{5,7},{6,4},{7,5},{8,10},{9,11},{10,... | collective-permute-start | bytes 1179656 | tf_op jit(solution)/shard_map/ppermute | solution.py:46
  98.0 16.5 %collective-permute-start.33 = (bf16[512,384]{1,0:T(8,128)(2,1)S(1)}, bf16[512,384]{1,0:T(8,128)(2,1)S(1)}, u32[]{:S(2)}, u32[]{:S(2)}) collective-permute-start(bf16[512,384]{1,0:T(8,128)(2,1)S(1)} %collective-permute-done.23.refs_4_), channel_id=1, source_target_pairs={{0,2},{1,3},{2,0},{3,1},{4,6},{5,7},{6,4},{7,5},{8,10},{9,11},{10,... | collective-permute-start | bytes 1179656 | tf_op jit(solution)/shard_map/ppermute | solution.py:46
  98.4 23.6 %collective-permute-start.35 = (bf16[512,384]{1,0:T(8,128)(2,1)S(1)}, bf16[512,384]{1,0:T(8,128)(2,1)S(1)}, u32[]{:S(2)}, u32[]{:S(2)}) collective-permute-start(bf16[512,384]{1,0:T(8,128)(2,1)S(1)} %collective-permute-done.24.refs_8_), channel_id=1, source_target_pairs={{0,2},{1,3},{2,0},{3,1},{4,6},{5,7},{6,4},{7,5},{8,10},{9,11},{10,... | collective-permute-start | bytes 1179656 | tf_op jit(solution)/shard_map/ppermute | solution.py:46
  100.1 21.9 %collective-permute-start.37 = (bf16[512,384]{1,0:T(8,128)(2,1)S(1)}, bf16[512,384]{1,0:T(8,128)(2,1)S(1)}, u32[]{:S(2)}, u32[]{:S(2)}) collective-permute-start(bf16[512,384]{1,0:T(8,128)(2,1)S(1)} %get-tuple-element.105), channel_id=1, source_target_pairs={{0,16},{4,20},{8,24},{12,28},{16,32},{20,36},{24,40},{28,44},{32,4... | collective-permute-start | bytes 1179656 | tf_op jit(solution)/shard_map/ppermute | solution.py:42
  105.8 19.3 %collective-permute-start.38 = (bf16[512,384]{1,0:T(8,128)(2,1)S(1)}, bf16[512,384]{1,0:T(8,128)(2,1)S(1)}, u32[]{:S(2)}, u32[]{:S(2)}) collective-permute-start(bf16[512,384]{1,0:T(8,128)(2,1)S(1)} %get-tuple-element.106), channel_id=1, source_target_pairs={{16,0},{20,4},{24,8},{28,12},{32,16},{36,20},{40,24},{44,28},{48,3... | collective-permute-start | bytes 1179656 | tf_op jit(solution)/shard_map/ppermute | solution.py:42
  109.0 16.4 %collective-permute-start.27 = (bf16[512,384]{1,0:T(8,128)(2,1)S(1)}, bf16[512,384]{1,0:T(8,128)(2,1)S(1)}, u32[]{:S(2)}, u32[]{:S(2)}) collective-permute-start(bf16[512,384]{1,0:T(8,128)(2,1)S(1)} %collective-permute-done.26.refs_2_), channel_id=1, source_target_pairs={{0,1},{1,0},{2,3},{3,2},{4,5},{5,4},{6,7},{7,6},{8,9},{9,8},{10,11... | collective-permute-start | bytes 1179656 | tf_op jit(solution)/shard_map/ppermute | solution.py:50
  114.5 10.9 %collective-permute-start.34 = (bf16[512,384]{1,0:T(8,128)(2,1)S(1)}, bf16[512,384]{1,0:T(8,128)(2,1)S(1)}, u32[]{:S(2)}, u32[]{:S(2)}) collective-permute-start(bf16[512,384]{1,0:T(8,128)(2,1)S(1)} %collective-permute-done.33.refs_6_), channel_id=1, source_target_pairs={{0,1},{1,0},{2,3},{3,2},{4,5},{5,4},{6,7},{7,6},{8,9},{9,8},{10,11... | collective-permute-start | bytes 1179656 | tf_op jit(solution)/shard_map/ppermute | solution.py:50
  (17 other events, 44.5 us)

commit v12 on v11

--- a/solution.py
+++ b/solution.py
@@ -106,7 +106,14 @@
     finish(total, vec_ref, s_ref, a_ref)
 
 
-def product_kernel(*refs):
+def product_kernel(taps, *refs):
+    pieces, (w_ref, *outs) = refs[: -1 - len(taps)], refs[-1 - len(taps) :]
+    rows = joined(pieces)
+    for k, o in zip(taps, outs):
+        o[...] = dot(rows, w_ref[:, k * W : (k + 1) * W]).astype(BF16)
+
+
+def product3_kernel(*refs):
     pieces, (w_ref, o0, o1, o2) = refs[:-4], refs[-4:]
     full = dot(joined(pieces), w_ref[...])
     for k, o in enumerate((o0, o1, o2)):
@@ -226,10 +233,13 @@
     ch, a_lo = after((ch, a_lo))
     w1 = staged(1, ch, conv_weight)
     far_hi, w1 = after((far_hi, w1))
-    t0, t1, t2 = call(product_kernel, (a_hi, near_hi, far_hi, *core_swaps(far_hi, 2), w1), halves)
+    t0, t1, t2 = call(product3_kernel, (a_hi, near_hi, far_hi, *core_swaps(far_hi, 2), w1), halves)
     up = shifted(t0, hop1)
     far_lo, t1 = after((far_lo, t1))
-    u0, u1, u2 = call(product_kernel, (a_lo, near_lo, far_lo, *core_swaps(far_lo, 2), w1), halves)
+    g_lo = (a_lo, near_lo, far_lo, *core_swaps(far_lo, 2), w1)
+    (u2,) = call(functools.partial(product_kernel, (2,)), g_lo, halves[:1])
+    u2, g_lo = after((u2, g_lo))
+    u0, u1 = call(functools.partial(product_kernel, (0, 1)), g_lo, halves[:2])
     down = shifted(u2, -hop1)
     (early,) = call(early_join_kernel, (s_lo, up, t2), halves[:1], dtype=F32, flops=JOIN_COST)
     s_lo, a_lo = call(late_join_kernel, (early, u1, vec1), halves[:2])
@@ -248,15 +258,17 @@
     near_high = core_swap(from_high)
     g_hi = [a_hi, near_hi, far_hi, *core_swaps(far_hi, 2)]
     *g_hi, near_low, near_high = after((*g_hi, near_low, near_high))
-    q0, q_hi, q2 = call(product_kernel, (*g_hi, w2), halves)
+    q0, q2 = call(functools.partial(product_kernel, (0, 2)), (*g_hi, w2), halves[:2])
+    q2, g_hi = after((q2, g_hi))
     up_hi = shifted(q0, hop2)
     down_hi = shifted(q2, -hop2)
-    from_low, from_high, q_hi = after((from_low, from_high, q_hi))
+    from_low, from_high, q2 = after((from_low, from_high, q2))
     far_low = chip_swap(from_low)
     far_high = chip_swap(from_high)
     g_own = (a_lo, near_own, far_own, core_swap(far_own))
     g_low = (from_low, near_low, far_low, core_swap(far_low))
     g_high = (from_high, near_high, far_high, core_swap(far_high))
+    (q_hi,) = call(functools.partial(product_kernel, (1,)), (*g_hi, w2), halves[:1])
     (upper,) = call(upper_kernel, (s_hi, q_hi, up_hi, down_hi, vec2), halves[:1], flops=COST)
     (out,) = call(out_kernel, (*g_own, *g_low, *g_high, s_lo, upper, vec2, w2), [ROWS])
     return out

time: 130 us -> 132 us (1.015)
  waiting for transfers between devices: 44.9 us -> 47.3 us
    ppermute x8, waiting for transfers between devices: 17.4 us -> 19.4 us  [shifted(): return lax.ppermute(array, 'seq', pairs)]
    pallas_call x11 -> x13, Pallas kernels: 20 us -> 21.1 us  [call(): pl.pallas_call(kernel, out_shape=[jax.ShapeDtypeStruct((r, W), dtype) for...]
  transfers between devices with their start and end apart: 39 -> 39, of which waited for: 20 -> 21; matrix products, arithmetic and copies ran while one was open for 2% -> 2% of each run, Pallas kernels for 18% -> 18%
where the time goes in v12:
time: 132 us
  starting transfers between devices  50.9 us (39%)
  waiting for transfers between devices  47.3 us (36%)
  Pallas kernels  27.2 us (21%)
  other arithmetic  4.19 us (3%)
  local copies, waits for them, and re-layouts  1.9 us (1%)
    ppermute x8, starting transfers between devices, shifted(): return lax.ppermute(array, 'seq', pairs)  36.9 us
    ppermute x9, waiting for transfers between devices, chip_swap(): return lax.ppermute(array, 'ch', [(i, i ^ 2) for i in range(4)])  21.9 us
    pallas_call x13, Pallas kernels, call(): pl.pallas_call(kernel, out_shape=[jax.ShapeDtypeStruct((r, W), dtype) for...  21.1 us
    ppermute x8, waiting for transfers between devices, shifted(): return lax.ppermute(array, 'seq', pairs)  19.4 us
    ppermute x9, starting transfers between devices, chip_swap(): return lax.ppermute(array, 'ch', [(i, i ^ 2) for i in range(4)])  8.88 us
    pallas_call x3, Pallas kernels, staged(): pl.pallas_call(functools.partial(stage_kernel, layer), out_shape=jax.Shap...  6.13 us
    ppermute x22, waiting for transfers between devices, core_swap(): return lax.ppermute(array, 'ch', [(i, i ^ 1) for i in range(4)])  6.06 us
    ppermute x22, starting transfers between devices, core_swap(): return lax.ppermute(array, 'ch', [(i, i ^ 1) for i in range(4)])  5.11 us
  transfers between devices with their start and end apart: 39, of which 21 were waited for; matrix products, arithmetic and copies ran while one was open for 2% of the time, Pallas kernels for 18%

profile of v12, /device:TPU:6, one launch (start us, length us, event | category | flops | bytes accessed | tf_op | source)
XLA Modules:
  0.0 131.8 jit_solution(10691543583828723737)
XLA Ops:
  0.9 2.1 %fusion.1.refs_0_ = bf16[576,384]{1,0:T(8,128)(2,1)S(1)} fusion(f32[384]{0:T(512)S(1)} %get-tuple-element.149, f32[384]{0:T(512)S(1)} %get-tuple-element.143, bf16[1024,384]{1,0:T(8,128)(2,1)} %refs_13_.1), kind=kLoop, calls=%fused_computation.3 | loop fusion | flops 7741440 | bytes 887808 | tf_op jit(solution)/shard_map/convert_element_type | solution.py:198
  5.7 4.8 %collective-permute-start.1 = (bf16[64,384]{1,0:T(8,128)(2,1)S(1)}, bf16[64,384]{1,0:T(8,128)(2,1)S(1)}, u32[]{:S(2)}, u32[]{:S(2)}) collective-permute-start(bf16[64,384]{1,0:T(8,128)(2,1)S(1)} %get-tuple-element.138), channel_id=1, source_target_pairs={{0,4},{4,8},{8,12},{12,16},{16,20},{20,24},{24,28},{28,32},{32,36}... | collective-permute-start | bytes 147464 | tf_op jit(solution)/shard_map/ppermute | solution.py:42
  10.6 7.5 %collective-permute-start.2 = (bf16[64,384]{1,0:T(8,128)(2,1)S(1)}, bf16[64,384]{1,0:T(8,128)(2,1)S(1)}, u32[]{:S(2)}, u32[]{:S(2)}) collective-permute-start(bf16[64,384]{1,0:T(8,128)(2,1)S(1)} %get-tuple-element.137), channel_id=1, source_target_pairs={{4,0},{8,4},{12,8},{16,12},{20,16},{24,20},{28,24},{32,28},{36,32}... | collective-permute-start | bytes 147464 | tf_op jit(solution)/shard_map/ppermute | solution.py:42
  19.9 2.0 %shard_map.55.refs_11_.refs_15_ = bf16[1536,1152]{1,0:T(8,128)(2,1)S(1)} custom-call(s32[1]{0:T(128)} %bitcast.ch_ref, bf16[3,3,1536,384]{3,2,1,0:T(8,128)(2,1)} %w_hbm.5), custom_call_target="tpu_custom_call" | custom-call | tf_op jit(solution)/shard_map/pallas_call | solution.py:177
  24.1 3.6 %collective-permute-done.3.refs_7_ = bf16[128,384]{1,0:T(8,128)(2,1)S(1)} collective-permute-done((bf16[128,384]{1,0:T(8,128)(2,1)S(1)}, bf16[128,384]{1,0:T(8,128)(2,1)S(1)}, u32[]{:S(2)}, u32[]{:S(2)}) %collective-permute-start.3) | collective-permute-done | bytes 98336 | tf_op jit(solution)/shard_map/ppermute | solution.py:46
  29.9 3.6 %shard_map.57 = (bf16[512,384]{1,0:T(8,128)(2,1)S(1)}, bf16[512,384]{1,0:T(8,128)(2,1)S(1)}) custom-call(bf16[576,384]{1,0:T(8,128)(2,1)S(1)} %fusion.1.refs_0_, bf16[576,384]{1,0:T(8,128)(2,1)S(1)} %collective-permute-done.4.refs_1_, bf16[576,384]{1,0:T(8,128)(2,1)S(1)} %collective-permute-done.refs_2_, ...), custom_call_target="tpu_custom_call" | custom-call | bytes 1024 | tf_op jit(solution)/shard_map/pallas_call | solution.py:165
  36.0 3.6 %shard_map.58 = (bf16[512,384]{1,0:T(8,128)(2,1)S(1)}, bf16[512,384]{1,0:T(8,128)(2,1)S(1)}) custom-call(bf16[576,384]{1,0:T(8,128)(2,1)S(1)} %fusion.1.refs_0_, bf16[576,384]{1,0:T(8,128)(2,1)S(1)} %collective-permute-done.4.refs_1_, bf16[576,384]{1,0:T(8,128)(2,1)S(1)} %collective-permute-done.refs_2_, ...), custom_call_target="tpu_custom_call" | custom-call | bytes 1024 | tf_op jit(solution)/shard_map/pallas_call | solution.py:165
  41.5 2.0 %shard_map.59.refs_5_ = bf16[1536,1152]{1,0:T(8,128)(2,1)S(1)} custom-call(s32[1]{0:T(128)} %bitcast.ch_ref, bf16[3,3,1536,384]{3,2,1,0:T(8,128)(2,1)} %w_hbm.5), custom_call_target="tpu_custom_call" | custom-call | tf_op jit(solution)/shard_map/pallas_call | solution.py:177
  43.5 2.0 %collective-permute-done.14.refs_2_ = bf16[512,384]{1,0:T(8,128)(2,1)S(1)} collective-permute-done((bf16[512,384]{1,0:T(8,128)(2,1)S(1)}, bf16[512,384]{1,0:T(8,128)(2,1)S(1)}, u32[]{:S(2)}, u32[]{:S(2)}) %collective-permute-start.14) | collective-permute-done | bytes 393248 | tf_op jit(solution)/shard_map/ppermute | solution.py:46
  47.4 2.2 %shard_map.60 = (bf16[512,384]{1,0:T(8,128)(2,1)S(1)}, bf16[512,384]{1,0:T(8,128)(2,1)S(1)}, bf16[512,384]{1,0:T(8,128)(2,1)S(1)}) custom-call(bf16[512,384]{1,0:T(8,128)(2,1)S(1)} %get-tuple-element.78.refs_0_, bf16[512,384]{1,0:T(8,128)(2,1)S(1)} %collective-permute-done.13.refs_1_, bf16[512,384]{1,0:T(8,128)(2,1)S(1)} %collective-permute-done.14.refs_2_, ...), custom_call_target="tpu_custom_call" | custom-call | bytes 1024 | tf_op jit(solution)/shard_map/pallas_call | solution.py:165
  49.6 1.9 %collective-permute-start.22 = (bf16[512,384]{1,0:T(8,128)(2,1)S(1)}, bf16[512,384]{1,0:T(8,128)(2,1)S(1)}, u32[]{:S(2)}, u32[]{:S(2)}) collective-permute-start(bf16[512,384]{1,0:T(8,128)(2,1)S(1)} %get-tuple-element.96), channel_id=1, source_target_pairs={{0,4},{4,8},{8,12},{12,16},{16,20},{20,24},{24,28},{28,32},{32,36}... | collective-permute-start | bytes 1179656 | tf_op jit(solution)/shard_map/ppermute | solution.py:42
  51.6 2.4 %collective-permute-done.12.refs_2_ = bf16[512,384]{1,0:T(8,128)(2,1)S(1)} collective-permute-done((bf16[512,384]{1,0:T(8,128)(2,1)S(1)}, bf16[512,384]{1,0:T(8,128)(2,1)S(1)}, u32[]{:S(2)}, u32[]{:S(2)}) %collective-permute-start.12) | collective-permute-done | bytes 393248 | tf_op jit(solution)/shard_map/ppermute | solution.py:46
  56.8 6.1 %collective-permute-start.20 = (bf16[512,384]{1,0:T(8,128)(2,1)S(1)}, bf16[512,384]{1,0:T(8,128)(2,1)S(1)}, u32[]{:S(2)}, u32[]{:S(2)}) collective-permute-start(bf16[512,384]{1,0:T(8,128)(2,1)S(1)} %shard_map.61), channel_id=1, source_target_pairs={{4,0},{8,4},{12,8},{16,12},{20,16},{24,20},{28,24},{32,28},{36,32}... | collective-permute-start | bytes 1179656 | tf_op jit(solution)/shard_map/ppermute | solution.py:42
  64.8 4.3 %collective-permute-done.22.up = bf16[512,384]{1,0:T(8,128)(2,1)S(1)} collective-permute-done((bf16[512,384]{1,0:T(8,128)(2,1)S(1)}, bf16[512,384]{1,0:T(8,128)(2,1)S(1)}, u32[]{:S(2)}, u32[]{:S(2)}) %collective-permute-start.22) | collective-permute-done | bytes 393248 | tf_op jit(solution)/shard_map/ppermute | solution.py:42
  70.3 1.9 %collective-permute-start.23 = (bf16[512,384]{1,0:T(8,128)(2,1)S(1)}, bf16[512,384]{1,0:T(8,128)(2,1)S(1)}, u32[]{:S(2)}, u32[]{:S(2)}) collective-permute-start(bf16[512,384]{1,0:T(8,128)(2,1)S(1)} %get-tuple-element.102.refs_0_), channel_id=1, source_target_pairs={{0,16},{4,20},{8,24},{12,28},{16,32},{20,36},{24,40},{28,44},{32,4... | collective-permute-start | bytes 1179656 | tf_op jit(solution)/shard_map/ppermute | solution.py:42
  72.2 6.9 %collective-permute-start.24 = (bf16[512,384]{1,0:T(8,128)(2,1)S(1)}, bf16[512,384]{1,0:T(8,128)(2,1)S(1)}, u32[]{:S(2)}, u32[]{:S(2)}) collective-permute-start(bf16[512,384]{1,0:T(8,128)(2,1)S(1)} %get-tuple-element.102.refs_0_), channel_id=1, source_target_pairs={{16,0},{20,4},{24,8},{28,12},{32,16},{36,20},{40,24},{44,28},{48,3... | collective-permute-start | bytes 1179656 | tf_op jit(solution)/shard_map/ppermute | solution.py:42
  81.5 2.0 %shard_map.66.refs_5_.refs_15_ = bf16[1536,1152]{1,0:T(8,128)(2,1)S(1)} custom-call(s32[1]{0:T(128)} %bitcast.ch_ref, bf16[3,3,1536,384]{3,2,1,0:T(8,128)(2,1)} %w_hbm.5), custom_call_target="tpu_custom_call" | custom-call | tf_op jit(solution)/shard_map/pallas_call | solution.py:177
  83.9 7.9 %collective-permute-done.23.refs_4_ = bf16[512,384]{1,0:T(8,128)(2,1)S(1)} collective-permute-done((bf16[512,384]{1,0:T(8,128)(2,1)S(1)}, bf16[512,384]{1,0:T(8,128)(2,1)S(1)}, u32[]{:S(2)}, u32[]{:S(2)}) %collective-permute-start.23) | collective-permute-done | bytes 393248 | tf_op jit(solution)/shard_map/ppermute | solution.py:42
  99.7 5.8 %collective-permute-start.38 = (bf16[512,384]{1,0:T(8,128)(2,1)S(1)}, bf16[512,384]{1,0:T(8,128)(2,1)S(1)}, u32[]{:S(2)}, u32[]{:S(2)}) collective-permute-start(bf16[512,384]{1,0:T(8,128)(2,1)S(1)} %get-tuple-element.114), channel_id=1, source_target_pairs={{16,0},{20,4},{24,8},{28,12},{32,16},{36,20},{40,24},{44,28},{48,3... | collective-permute-start | bytes 1179656 | tf_op jit(solution)/shard_map/ppermute | solution.py:42
  105.5 1.9 %collective-permute-start.37 = (bf16[512,384]{1,0:T(8,128)(2,1)S(1)}, bf16[512,384]{1,0:T(8,128)(2,1)S(1)}, u32[]{:S(2)}, u32[]{:S(2)}) collective-permute-start(bf16[512,384]{1,0:T(8,128)(2,1)S(1)} %get-tuple-element.126), channel_id=1, source_target_pairs={{0,16},{4,20},{8,24},{12,28},{16,32},{20,36},{24,40},{28,44},{32,4... | collective-permute-start | bytes 1179656 | tf_op jit(solution)/shard_map/ppermute | solution.py:42
  108.6 5.9 %collective-permute-done.33.refs_6_ = bf16[512,384]{1,0:T(8,128)(2,1)S(1)} collective-permute-done((bf16[512,384]{1,0:T(8,128)(2,1)S(1)}, bf16[512,384]{1,0:T(8,128)(2,1)S(1)}, u32[]{:S(2)}, u32[]{:S(2)}) %collective-permute-start.33) | collective-permute-done | bytes 393248 | tf_op jit(solution)/shard_map/ppermute | solution.py:46
  114.5 7.6 %collective-permute-done.35.refs_10_ = bf16[512,384]{1,0:T(8,128)(2,1)S(1)} collective-permute-done((bf16[512,384]{1,0:T(8,128)(2,1)S(1)}, bf16[512,384]{1,0:T(8,128)(2,1)S(1)}, u32[]{:S(2)}, u32[]{:S(2)}) %collective-permute-start.35) | collective-permute-done | bytes 393248 | tf_op jit(solution)/shard_map/ppermute | solution.py:46
  122.4 5.7 %collective-permute-done.37.up_hi = bf16[512,384]{1,0:T(8,128)(2,1)S(1)} collective-permute-done((bf16[512,384]{1,0:T(8,128)(2,1)S(1)}, bf16[512,384]{1,0:T(8,128)(2,1)S(1)}, u32[]{:S(2)}, u32[]{:S(2)}) %collective-permute-start.37) | collective-permute-done | bytes 393248 | tf_op jit(solution)/shard_map/ppermute | solution.py:42
  128.3 3.5 %shard_map.70 = bf16[1024,384]{1,0:T(8,128)(2,1)} custom-call(bf16[512,384]{1,0:T(8,128)(2,1)S(1)} %get-tuple-element.102.refs_0_, bf16[512,384]{1,0:T(8,128)(2,1)S(1)} %collective-permute-done.25.refs_1_, bf16[512,384]{1,0:T(8,128)(2,1)S(1)} %collective-permute-done.26.refs_2_, bf16[512,384]{1,0:T(8,128)(2,1)S(1)} %collective-permute-done.27.refs_3_, ...), custom_call_target="tpu_custom_call" | custom-call | bytes 1024 | tf_op jit(solution)/shard_map/pallas_call | solution.py:165
  (87 shorter events, 34.0 us)
Async XLA Ops:
  3.0 24.7 %collective-permute-start = (bf16[576,384]{1,0:T(8,128)(2,1)S(1)}, bf16[576,384]{1,0:T(8,128)(2,1)S(1)}, u32[]{:S(2)}, u32[]{:S(2)}) collective-permute-start(bf16[576,384]{1,0:T(8,128)(2,1)S(1)} %fusion.1.refs_0_), channel_id=1, source_target_pairs={{0,2},{1,3},{2,0},{3,1},{4,6},{5,7},{6,4},{7,5},{8,10},{9,11},{10,... | collective-permute-start | bytes 1327112 | tf_op jit(solution)/shard_map/ppermute | solution.py:46
  4.6 23.1 %collective-permute-start.4 = (bf16[576,384]{1,0:T(8,128)(2,1)S(1)}, bf16[576,384]{1,0:T(8,128)(2,1)S(1)}, u32[]{:S(2)}, u32[]{:S(2)}) collective-permute-start(bf16[576,384]{1,0:T(8,128)(2,1)S(1)} %fusion.1.refs_0_), channel_id=1, source_target_pairs={{0,1},{1,0},{2,3},{3,2},{4,5},{5,4},{6,7},{7,6},{8,9},{9,8},{10,11... | collective-permute-start | bytes 1327112 | tf_op jit(solution)/shard_map/ppermute | solution.py:50
  5.7 16.2 %collective-permute-start.1 = (bf16[64,384]{1,0:T(8,128)(2,1)S(1)}, bf16[64,384]{1,0:T(8,128)(2,1)S(1)}, u32[]{:S(2)}, u32[]{:S(2)}) collective-permute-start(bf16[64,384]{1,0:T(8,128)(2,1)S(1)} %get-tuple-element.138), channel_id=1, source_target_pairs={{0,4},{4,8},{8,12},{12,16},{16,20},{20,24},{24,28},{28,32},{32,36}... | collective-permute-start | bytes 147464 | tf_op jit(solution)/shard_map/ppermute | solution.py:42
  10.6 11.4 %collective-permute-start.2 = (bf16[64,384]{1,0:T(8,128)(2,1)S(1)}, bf16[64,384]{1,0:T(8,128)(2,1)S(1)}, u32[]{:S(2)}, u32[]{:S(2)}) collective-permute-start(bf16[64,384]{1,0:T(8,128)(2,1)S(1)} %get-tuple-element.137), channel_id=1, source_target_pairs={{4,0},{8,4},{12,8},{16,12},{20,16},{24,20},{28,24},{32,28},{36,32}... | collective-permute-start | bytes 147464 | tf_op jit(solution)/shard_map/ppermute | solution.py:42
  22.0 5.7 %collective-permute-start.3 = (bf16[128,384]{1,0:T(8,128)(2,1)S(1)}, bf16[128,384]{1,0:T(8,128)(2,1)S(1)}, u32[]{:S(2)}, u32[]{:S(2)}) collective-permute-start(bf16[128,384]{1,0:T(8,128)(2,1)S(1)} %shard_map.56.refs_5_), channel_id=1, source_target_pairs={{0,2},{1,3},{2,0},{3,1},{4,6},{5,7},{6,4},{7,5},{8,10},{9,11},{10,... | collective-permute-start | bytes 294920 | tf_op jit(solution)/shard_map/ppermute | solution.py:46
  22.2 12.2 %collective-permute-start.10 = (bf16[448,384]{1,0:T(8,128)(2,1)S(1)}, bf16[448,384]{1,0:T(8,128)(2,1)S(1)}, u32[]{:S(2)}, u32[]{:S(2)}) collective-permute-start(bf16[448,384]{1,0:T(8,128)(2,1)S(1)} %fusion.4.refs_9_), channel_id=1, source_target_pairs={{0,2},{1,3},{2,0},{3,1},{4,6},{5,7},{6,4},{7,5},{8,10},{9,11},{10,... | collective-permute-start | bytes 1032200 | tf_op jit(solution)/shard_map/ppermute | solution.py:46
  33.6 12.0 %collective-permute-start.14 = (bf16[512,384]{1,0:T(8,128)(2,1)S(1)}, bf16[512,384]{1,0:T(8,128)(2,1)S(1)}, u32[]{:S(2)}, u32[]{:S(2)}) collective-permute-start(bf16[512,384]{1,0:T(8,128)(2,1)S(1)} %get-tuple-element.78.refs_0_), channel_id=1, source_target_pairs={{0,2},{1,3},{2,0},{3,1},{4,6},{5,7},{6,4},{7,5},{8,10},{9,11},{10,... | collective-permute-start | bytes 1179656 | tf_op jit(solution)/shard_map/ppermute | solution.py:46
  34.4 11.9 %collective-permute-start.13 = (bf16[512,384]{1,0:T(8,128)(2,1)S(1)}, bf16[512,384]{1,0:T(8,128)(2,1)S(1)}, u32[]{:S(2)}, u32[]{:S(2)}) collective-permute-start(bf16[512,384]{1,0:T(8,128)(2,1)S(1)} %get-tuple-element.78.refs_0_), channel_id=1, source_target_pairs={{0,1},{1,0},{2,3},{3,2},{4,5},{5,4},{6,7},{7,6},{8,9},{9,8},{10,11... | collective-permute-start | bytes 1179656 | tf_op jit(solution)/shard_map/ppermute | solution.py:50
  39.6 14.4 %collective-permute-start.12 = (bf16[512,384]{1,0:T(8,128)(2,1)S(1)}, bf16[512,384]{1,0:T(8,128)(2,1)S(1)}, u32[]{:S(2)}, u32[]{:S(2)}) collective-permute-start(bf16[512,384]{1,0:T(8,128)(2,1)S(1)} %get-tuple-element.86.refs_0_), channel_id=1, source_target_pairs={{0,2},{1,3},{2,0},{3,1},{4,6},{5,7},{6,4},{7,5},{8,10},{9,11},{10,... | collective-permute-start | bytes 1179656 | tf_op jit(solution)/shard_map/ppermute | solution.py:46
  46.2 8.4 %collective-permute-start.17 = (bf16[512,384]{1,0:T(8,128)(2,1)S(1)}, bf16[512,384]{1,0:T(8,128)(2,1)S(1)}, u32[]{:S(2)}, u32[]{:S(2)}) collective-permute-start(bf16[512,384]{1,0:T(8,128)(2,1)S(1)} %get-tuple-element.86.refs_0_), channel_id=1, source_target_pairs={{0,1},{1,0},{2,3},{3,2},{4,5},{5,4},{6,7},{7,6},{8,9},{9,8},{10,11... | collective-permute-start | bytes 1179656 | tf_op jit(solution)/shard_map/ppermute | solution.py:50
  49.6 19.4 %collective-permute-start.22 = (bf16[512,384]{1,0:T(8,128)(2,1)S(1)}, bf16[512,384]{1,0:T(8,128)(2,1)S(1)}, u32[]{:S(2)}, u32[]{:S(2)}) collective-permute-start(bf16[512,384]{1,0:T(8,128)(2,1)S(1)} %get-tuple-element.96), channel_id=1, source_target_pairs={{0,4},{4,8},{8,12},{12,16},{16,20},{20,24},{24,28},{28,32},{32,36}... | collective-permute-start | bytes 1179656 | tf_op jit(solution)/shard_map/ppermute | solution.py:42
  56.8 22.6 %collective-permute-start.20 = (bf16[512,384]{1,0:T(8,128)(2,1)S(1)}, bf16[512,384]{1,0:T(8,128)(2,1)S(1)}, u32[]{:S(2)}, u32[]{:S(2)}) collective-permute-start(bf16[512,384]{1,0:T(8,128)(2,1)S(1)} %shard_map.61), channel_id=1, source_target_pairs={{4,0},{8,4},{12,8},{16,12},{20,16},{24,20},{28,24},{32,28},{36,32}... | collective-permute-start | bytes 1179656 | tf_op jit(solution)/shard_map/ppermute | solution.py:42
  70.3 21.5 %collective-permute-start.23 = (bf16[512,384]{1,0:T(8,128)(2,1)S(1)}, bf16[512,384]{1,0:T(8,128)(2,1)S(1)}, u32[]{:S(2)}, u32[]{:S(2)}) collective-permute-start(bf16[512,384]{1,0:T(8,128)(2,1)S(1)} %get-tuple-element.102.refs_0_), channel_id=1, source_target_pairs={{0,16},{4,20},{8,24},{12,28},{16,32},{20,36},{24,40},{28,44},{32,4... | collective-permute-start | bytes 1179656 | tf_op jit(solution)/shard_map/ppermute | solution.py:42
  72.2 20.8 %collective-permute-start.24 = (bf16[512,384]{1,0:T(8,128)(2,1)S(1)}, bf16[512,384]{1,0:T(8,128)(2,1)S(1)}, u32[]{:S(2)}, u32[]{:S(2)}) collective-permute-start(bf16[512,384]{1,0:T(8,128)(2,1)S(1)} %get-tuple-element.102.refs_0_), channel_id=1, source_target_pairs={{16,0},{20,4},{24,8},{28,12},{32,16},{36,20},{40,24},{44,28},{48,3... | collective-permute-start | bytes 1179656 | tf_op jit(solution)/shard_map/ppermute | solution.py:42
  80.6 12.3 %collective-permute-start.21 = (bf16[512,384]{1,0:T(8,128)(2,1)S(1)}, bf16[512,384]{1,0:T(8,128)(2,1)S(1)}, u32[]{:S(2)}, u32[]{:S(2)}) collective-permute-start(bf16[512,384]{1,0:T(8,128)(2,1)S(1)} %get-tuple-element.121.refs_0_), channel_id=1, source_target_pairs={{0,2},{1,3},{2,0},{3,1},{4,6},{5,7},{6,4},{7,5},{8,10},{9,11},{10,... | collective-permute-start | bytes 1179656 | tf_op jit(solution)/shard_map/ppermute | solution.py:46
  83.6 10.5 %collective-permute-start.28 = (bf16[512,384]{1,0:T(8,128)(2,1)S(1)}, bf16[512,384]{1,0:T(8,128)(2,1)S(1)}, u32[]{:S(2)}, u32[]{:S(2)}) collective-permute-start(bf16[512,384]{1,0:T(8,128)(2,1)S(1)} %get-tuple-element.121.refs_0_), channel_id=1, source_target_pairs={{0,1},{1,0},{2,3},{3,2},{4,5},{5,4},{6,7},{7,6},{8,9},{9,8},{10,11... | collective-permute-start | bytes 1179656 | tf_op jit(solution)/shard_map/ppermute | solution.py:50
  94.1 14.3 %collective-permute-start.26 = (bf16[512,384]{1,0:T(8,128)(2,1)S(1)}, bf16[512,384]{1,0:T(8,128)(2,1)S(1)}, u32[]{:S(2)}, u32[]{:S(2)}) collective-permute-start(bf16[512,384]{1,0:T(8,128)(2,1)S(1)} %get-tuple-element.102.refs_0_), channel_id=1, source_target_pairs={{0,2},{1,3},{2,0},{3,1},{4,6},{5,7},{6,4},{7,5},{8,10},{9,11},{10,... | collective-permute-start | bytes 1179656 | tf_op jit(solution)/shard_map/ppermute | solution.py:46
  97.6 16.9 %collective-permute-start.33 = (bf16[512,384]{1,0:T(8,128)(2,1)S(1)}, bf16[512,384]{1,0:T(8,128)(2,1)S(1)}, u32[]{:S(2)}, u32[]{:S(2)}) collective-permute-start(bf16[512,384]{1,0:T(8,128)(2,1)S(1)} %collective-permute-done.23.refs_4_), channel_id=1, source_target_pairs={{0,2},{1,3},{2,0},{3,1},{4,6},{5,7},{6,4},{7,5},{8,10},{9,11},{10,... | collective-permute-start | bytes 1179656 | tf_op jit(solution)/shard_map/ppermute | solution.py:46
  98.0 24.0 %collective-permute-start.35 = (bf16[512,384]{1,0:T(8,128)(2,1)S(1)}, bf16[512,384]{1,0:T(8,128)(2,1)S(1)}, u32[]{:S(2)}, u32[]{:S(2)}) collective-permute-start(bf16[512,384]{1,0:T(8,128)(2,1)S(1)} %collective-permute-done.24.refs_8_), channel_id=1, source_target_pairs={{0,2},{1,3},{2,0},{3,1},{4,6},{5,7},{6,4},{7,5},{8,10},{9,11},{10,... | collective-permute-start | bytes 1179656 | tf_op jit(solution)/shard_map/ppermute | solution.py:46
  99.7 22.7 %collective-permute-start.38 = (bf16[512,384]{1,0:T(8,128)(2,1)S(1)}, bf16[512,384]{1,0:T(8,128)(2,1)S(1)}, u32[]{:S(2)}, u32[]{:S(2)}) collective-permute-start(bf16[512,384]{1,0:T(8,128)(2,1)S(1)} %get-tuple-element.114), channel_id=1, source_target_pairs={{16,0},{20,4},{24,8},{28,12},{32,16},{36,20},{40,24},{44,28},{48,3... | collective-permute-start | bytes 1179656 | tf_op jit(solution)/shard_map/ppermute | solution.py:42
  105.5 22.5 %collective-permute-start.37 = (bf16[512,384]{1,0:T(8,128)(2,1)S(1)}, bf16[512,384]{1,0:T(8,128)(2,1)S(1)}, u32[]{:S(2)}, u32[]{:S(2)}) collective-permute-start(bf16[512,384]{1,0:T(8,128)(2,1)S(1)} %get-tuple-element.126), channel_id=1, source_target_pairs={{0,16},{4,20},{8,24},{12,28},{16,32},{20,36},{24,40},{28,44},{32,4... | collective-permute-start | bytes 1179656 | tf_op jit(solution)/shard_map/ppermute | solution.py:42
  108.5 19.9 %collective-permute-start.27 = (bf16[512,384]{1,0:T(8,128)(2,1)S(1)}, bf16[512,384]{1,0:T(8,128)(2,1)S(1)}, u32[]{:S(2)}, u32[]{:S(2)}) collective-permute-start(bf16[512,384]{1,0:T(8,128)(2,1)S(1)} %collective-permute-done.26.refs_2_), channel_id=1, source_target_pairs={{0,1},{1,0},{2,3},{3,2},{4,5},{5,4},{6,7},{7,6},{8,9},{9,8},{10,11... | collective-permute-start | bytes 1179656 | tf_op jit(solution)/shard_map/ppermute | solution.py:50
  114.5 13.8 %collective-permute-start.34 = (bf16[512,384]{1,0:T(8,128)(2,1)S(1)}, bf16[512,384]{1,0:T(8,128)(2,1)S(1)}, u32[]{:S(2)}, u32[]{:S(2)}) collective-permute-start(bf16[512,384]{1,0:T(8,128)(2,1)S(1)} %collective-permute-done.33.refs_6_), channel_id=1, source_target_pairs={{0,1},{1,0},{2,3},{3,2},{4,5},{5,4},{6,7},{7,6},{8,9},{9,8},{10,11... | collective-permute-start | bytes 1179656 | tf_op jit(solution)/shard_map/ppermute | solution.py:50
  122.1 6.3 %collective-permute-start.36 = (bf16[512,384]{1,0:T(8,128)(2,1)S(1)}, bf16[512,384]{1,0:T(8,128)(2,1)S(1)}, u32[]{:S(2)}, u32[]{:S(2)}) collective-permute-start(bf16[512,384]{1,0:T(8,128)(2,1)S(1)} %collective-permute-done.35.refs_10_), channel_id=1, source_target_pairs={{0,1},{1,0},{2,3},{3,2},{4,5},{5,4},{6,7},{7,6},{8,9},{9,8},{10,11... | collective-permute-start | bytes 1179656 | tf_op jit(solution)/shard_map/ppermute | solution.py:50
  (17 other events, 45.9 us)

commit v13 on v12

--- a/solution.py
+++ b/solution.py
@@ -236,10 +236,7 @@
     t0, t1, t2 = call(product3_kernel, (a_hi, near_hi, far_hi, *core_swaps(far_hi, 2), w1), halves)
     up = shifted(t0, hop1)
     far_lo, t1 = after((far_lo, t1))
-    g_lo = (a_lo, near_lo, far_lo, *core_swaps(far_lo, 2), w1)
-    (u2,) = call(functools.partial(product_kernel, (2,)), g_lo, halves[:1])
-    u2, g_lo = after((u2, g_lo))
-    u0, u1 = call(functools.partial(product_kernel, (0, 1)), g_lo, halves[:2])
+    u0, u1, u2 = call(product3_kernel, (a_lo, near_lo, far_lo, *core_swaps(far_lo, 2), w1), halves)
     down = shifted(u2, -hop1)
     (early,) = call(early_join_kernel, (s_lo, up, t2), halves[:1], dtype=F32, flops=JOIN_COST)
     s_lo, a_lo = call(late_join_kernel, (early, u1, vec1), halves[:2])

time: 132 us -> 132 us (level)
    pallas_call x13 -> x12, Pallas kernels: 21.1 us -> 20.5 us  [call(): pl.pallas_call(kernel, out_shape=[jax.ShapeDtypeStruct((r, W), dtype) for...]
  transfers between devices with their start and end apart: 39 -> 39, of which waited for: 21 -> 20; matrix products, arithmetic and copies ran while one was open for 2% -> 2% of each run, Pallas kernels for 18% -> 18%
where the time goes in v13:
time: 132 us
  starting transfers between devices  50.4 us (38%)
  waiting for transfers between devices  48.4 us (37%)
  Pallas kernels  26.6 us (20%)
  other arithmetic  4.19 us (3%)
  local copies, waits for them, and re-layouts  1.9 us (1%)
    ppermute x8, starting transfers between devices, shifted(): return lax.ppermute(array, 'seq', pairs)  36.9 us
    ppermute x9, waiting for transfers between devices, chip_swap(): return lax.ppermute(array, 'ch', [(i, i ^ 2) for i in range(4)])  21.9 us
    pallas_call x12, Pallas kernels, call(): pl.pallas_call(kernel, out_shape=[jax.ShapeDtypeStruct((r, W), dtype) for...  20.5 us
    ppermute x8, waiting for transfers between devices, shifted(): return lax.ppermute(array, 'seq', pairs)  20.4 us
    ppermute x9, starting transfers between devices, chip_swap(): return lax.ppermute(array, 'ch', [(i, i ^ 2) for i in range(4)])  8.13 us
    pallas_call x3, Pallas kernels, staged(): pl.pallas_call(functools.partial(stage_kernel, layer), out_shape=jax.Shap...  6.13 us
    ppermute x22, waiting for transfers between devices, core_swap(): return lax.ppermute(array, 'ch', [(i, i ^ 1) for i in range(4)])  6.13 us
    ppermute x22, starting transfers between devices, core_swap(): return lax.ppermute(array, 'ch', [(i, i ^ 1) for i in range(4)])  5.33 us
  transfers between devices with their start and end apart: 39, of which 20 were waited for; matrix products, arithmetic and copies ran while one was open for 2% of the time, Pallas kernels for 18%

profile of v13, /device:TPU:6, one launch (start us, length us, event | category | flops | bytes accessed | tf_op | source)
XLA Modules:
  0.0 131.8 jit_solution(15616505113399067119)
XLA Ops:
  0.9 2.1 %fusion.1.refs_0_ = bf16[576,384]{1,0:T(8,128)(2,1)S(1)} fusion(f32[384]{0:T(512)S(1)} %get-tuple-element.137, f32[384]{0:T(512)S(1)} %get-tuple-element.131, bf16[1024,384]{1,0:T(8,128)(2,1)} %refs_13_.1), kind=kLoop, calls=%fused_computation.3 | loop fusion | flops 7741440 | bytes 887808 | tf_op jit(solution)/shard_map/convert_element_type | solution.py:198
  5.7 4.8 %collective-permute-start.1 = (bf16[64,384]{1,0:T(8,128)(2,1)S(1)}, bf16[64,384]{1,0:T(8,128)(2,1)S(1)}, u32[]{:S(2)}, u32[]{:S(2)}) collective-permute-start(bf16[64,384]{1,0:T(8,128)(2,1)S(1)} %get-tuple-element.126), channel_id=1, source_target_pairs={{0,4},{4,8},{8,12},{12,16},{16,20},{20,24},{24,28},{28,32},{32,36}... | collective-permute-start | bytes 147464 | tf_op jit(solution)/shard_map/ppermute | solution.py:42
  10.6 7.5 %collective-permute-start.2 = (bf16[64,384]{1,0:T(8,128)(2,1)S(1)}, bf16[64,384]{1,0:T(8,128)(2,1)S(1)}, u32[]{:S(2)}, u32[]{:S(2)}) collective-permute-start(bf16[64,384]{1,0:T(8,128)(2,1)S(1)} %get-tuple-element.125), channel_id=1, source_target_pairs={{4,0},{8,4},{12,8},{16,12},{20,16},{24,20},{28,24},{32,28},{36,32}... | collective-permute-start | bytes 147464 | tf_op jit(solution)/shard_map/ppermute | solution.py:42
  19.9 2.0 %shard_map.55.refs_11_.refs_15_ = bf16[1536,1152]{1,0:T(8,128)(2,1)S(1)} custom-call(s32[1]{0:T(128)} %bitcast.ch_ref, bf16[3,3,1536,384]{3,2,1,0:T(8,128)(2,1)} %w_hbm.5), custom_call_target="tpu_custom_call" | custom-call | tf_op jit(solution)/shard_map/pallas_call | solution.py:177
  24.1 3.6 %collective-permute-done.3.refs_7_ = bf16[128,384]{1,0:T(8,128)(2,1)S(1)} collective-permute-done((bf16[128,384]{1,0:T(8,128)(2,1)S(1)}, bf16[128,384]{1,0:T(8,128)(2,1)S(1)}, u32[]{:S(2)}, u32[]{:S(2)}) %collective-permute-start.3) | collective-permute-done | bytes 98336 | tf_op jit(solution)/shard_map/ppermute | solution.py:46
  29.9 3.6 %shard_map.57 = (bf16[512,384]{1,0:T(8,128)(2,1)S(1)}, bf16[512,384]{1,0:T(8,128)(2,1)S(1)}) custom-call(bf16[576,384]{1,0:T(8,128)(2,1)S(1)} %fusion.1.refs_0_, bf16[576,384]{1,0:T(8,128)(2,1)S(1)} %collective-permute-done.4.refs_1_, bf16[576,384]{1,0:T(8,128)(2,1)S(1)} %collective-permute-done.refs_2_, ...), custom_call_target="tpu_custom_call" | custom-call | bytes 1024 | tf_op jit(solution)/shard_map/pallas_call | solution.py:165
  36.0 3.6 %shard_map.58 = (bf16[512,384]{1,0:T(8,128)(2,1)S(1)}, bf16[512,384]{1,0:T(8,128)(2,1)S(1)}) custom-call(bf16[576,384]{1,0:T(8,128)(2,1)S(1)} %fusion.1.refs_0_, bf16[576,384]{1,0:T(8,128)(2,1)S(1)} %collective-permute-done.4.refs_1_, bf16[576,384]{1,0:T(8,128)(2,1)S(1)} %collective-permute-done.refs_2_, ...), custom_call_target="tpu_custom_call" | custom-call | bytes 1024 | tf_op jit(solution)/shard_map/pallas_call | solution.py:165
  41.5 2.0 %shard_map.59.refs_5_ = bf16[1536,1152]{1,0:T(8,128)(2,1)S(1)} custom-call(s32[1]{0:T(128)} %bitcast.ch_ref, bf16[3,3,1536,384]{3,2,1,0:T(8,128)(2,1)} %w_hbm.5), custom_call_target="tpu_custom_call" | custom-call | tf_op jit(solution)/shard_map/pallas_call | solution.py:177
  43.5 2.0 %collective-permute-done.14.refs_2_ = bf16[512,384]{1,0:T(8,128)(2,1)S(1)} collective-permute-done((bf16[512,384]{1,0:T(8,128)(2,1)S(1)}, bf16[512,384]{1,0:T(8,128)(2,1)S(1)}, u32[]{:S(2)}, u32[]{:S(2)}) %collective-permute-start.14) | collective-permute-done | bytes 393248 | tf_op jit(solution)/shard_map/ppermute | solution.py:46
  47.4 2.2 %shard_map.60 = (bf16[512,384]{1,0:T(8,128)(2,1)S(1)}, bf16[512,384]{1,0:T(8,128)(2,1)S(1)}, bf16[512,384]{1,0:T(8,128)(2,1)S(1)}) custom-call(bf16[512,384]{1,0:T(8,128)(2,1)S(1)} %get-tuple-element.72.refs_0_, bf16[512,384]{1,0:T(8,128)(2,1)S(1)} %collective-permute-done.13.refs_1_, bf16[512,384]{1,0:T(8,128)(2,1)S(1)} %collective-permute-done.14.refs_2_, ...), custom_call_target="tpu_custom_call" | custom-call | bytes 1024 | tf_op jit(solution)/shard_map/pallas_call | solution.py:165
  49.6 1.9 %collective-permute-start.22 = (bf16[512,384]{1,0:T(8,128)(2,1)S(1)}, bf16[512,384]{1,0:T(8,128)(2,1)S(1)}, u32[]{:S(2)}, u32[]{:S(2)}) collective-permute-start(bf16[512,384]{1,0:T(8,128)(2,1)S(1)} %get-tuple-element.84), channel_id=1, source_target_pairs={{0,4},{4,8},{8,12},{12,16},{16,20},{20,24},{24,28},{28,32},{32,36}... | collective-permute-start | bytes 1179656 | tf_op jit(solution)/shard_map/ppermute | solution.py:42
  51.6 2.4 %collective-permute-done.12.refs_2_ = bf16[512,384]{1,0:T(8,128)(2,1)S(1)} collective-permute-done((bf16[512,384]{1,0:T(8,128)(2,1)S(1)}, bf16[512,384]{1,0:T(8,128)(2,1)S(1)}, u32[]{:S(2)}, u32[]{:S(2)}) %collective-permute-start.12) | collective-permute-done | bytes 393248 | tf_op jit(solution)/shard_map/ppermute | solution.py:46
  55.9 2.2 %shard_map.61 = (bf16[512,384]{1,0:T(8,128)(2,1)S(1)}, bf16[512,384]{1,0:T(8,128)(2,1)S(1)}, bf16[512,384]{1,0:T(8,128)(2,1)S(1)}) custom-call(bf16[512,384]{1,0:T(8,128)(2,1)S(1)} %get-tuple-element.78.refs_0_, bf16[512,384]{1,0:T(8,128)(2,1)S(1)} %collective-permute-done.17.refs_1_, bf16[512,384]{1,0:T(8,128)(2,1)S(1)} %collective-permute-done.12.refs_2_, ...), custom_call_target="tpu_custom_call" | custom-call | bytes 1024 | tf_op jit(solution)/shard_map/pallas_call | solution.py:165
  58.1 6.1 %collective-permute-start.20 = (bf16[512,384]{1,0:T(8,128)(2,1)S(1)}, bf16[512,384]{1,0:T(8,128)(2,1)S(1)}, u32[]{:S(2)}, u32[]{:S(2)}) collective-permute-start(bf16[512,384]{1,0:T(8,128)(2,1)S(1)} %get-tuple-element.81), channel_id=1, source_target_pairs={{4,0},{8,4},{12,8},{16,12},{20,16},{24,20},{28,24},{32,28},{36,32}... | collective-permute-start | bytes 1179656 | tf_op jit(solution)/shard_map/ppermute | solution.py:42
  64.2 3.2 %collective-permute-done.22.up = bf16[512,384]{1,0:T(8,128)(2,1)S(1)} collective-permute-done((bf16[512,384]{1,0:T(8,128)(2,1)S(1)}, bf16[512,384]{1,0:T(8,128)(2,1)S(1)}, u32[]{:S(2)}, u32[]{:S(2)}) %collective-permute-start.22) | collective-permute-done | bytes 393248 | tf_op jit(solution)/shard_map/ppermute | solution.py:42
  68.6 1.9 %collective-permute-start.23 = (bf16[512,384]{1,0:T(8,128)(2,1)S(1)}, bf16[512,384]{1,0:T(8,128)(2,1)S(1)}, u32[]{:S(2)}, u32[]{:S(2)}) collective-permute-start(bf16[512,384]{1,0:T(8,128)(2,1)S(1)} %get-tuple-element.90.refs_0_), channel_id=1, source_target_pairs={{0,16},{4,20},{8,24},{12,28},{16,32},{20,36},{24,40},{28,44},{32,4... | collective-permute-start | bytes 1179656 | tf_op jit(solution)/shard_map/ppermute | solution.py:42
  70.5 6.9 %collective-permute-start.24 = (bf16[512,384]{1,0:T(8,128)(2,1)S(1)}, bf16[512,384]{1,0:T(8,128)(2,1)S(1)}, u32[]{:S(2)}, u32[]{:S(2)}) collective-permute-start(bf16[512,384]{1,0:T(8,128)(2,1)S(1)} %get-tuple-element.90.refs_0_), channel_id=1, source_target_pairs={{16,0},{20,4},{24,8},{28,12},{32,16},{36,20},{40,24},{44,28},{48,3... | collective-permute-start | bytes 1179656 | tf_op jit(solution)/shard_map/ppermute | solution.py:42
  79.2 2.0 %shard_map.65.refs_5_.refs_15_ = bf16[1536,1152]{1,0:T(8,128)(2,1)S(1)} custom-call(s32[1]{0:T(128)} %bitcast.ch_ref, bf16[3,3,1536,384]{3,2,1,0:T(8,128)(2,1)} %w_hbm.5), custom_call_target="tpu_custom_call" | custom-call | tf_op jit(solution)/shard_map/pallas_call | solution.py:177
  81.7 10.0 %collective-permute-done.23.refs_4_ = bf16[512,384]{1,0:T(8,128)(2,1)S(1)} collective-permute-done((bf16[512,384]{1,0:T(8,128)(2,1)S(1)}, bf16[512,384]{1,0:T(8,128)(2,1)S(1)}, u32[]{:S(2)}, u32[]{:S(2)}) %collective-permute-start.23) | collective-permute-done | bytes 393248 | tf_op jit(solution)/shard_map/ppermute | solution.py:42
  99.7 5.8 %collective-permute-start.38 = (bf16[512,384]{1,0:T(8,128)(2,1)S(1)}, bf16[512,384]{1,0:T(8,128)(2,1)S(1)}, u32[]{:S(2)}, u32[]{:S(2)}) collective-permute-start(bf16[512,384]{1,0:T(8,128)(2,1)S(1)} %get-tuple-element.102), channel_id=1, source_target_pairs={{16,0},{20,4},{24,8},{28,12},{32,16},{36,20},{40,24},{44,28},{48,3... | collective-permute-start | bytes 1179656 | tf_op jit(solution)/shard_map/ppermute | solution.py:42
  108.5 5.9 %collective-permute-done.33.refs_6_ = bf16[512,384]{1,0:T(8,128)(2,1)S(1)} collective-permute-done((bf16[512,384]{1,0:T(8,128)(2,1)S(1)}, bf16[512,384]{1,0:T(8,128)(2,1)S(1)}, u32[]{:S(2)}, u32[]{:S(2)}) %collective-permute-start.33) | collective-permute-done | bytes 393248 | tf_op jit(solution)/shard_map/ppermute | solution.py:46
  114.5 7.6 %collective-permute-done.35.refs_10_ = bf16[512,384]{1,0:T(8,128)(2,1)S(1)} collective-permute-done((bf16[512,384]{1,0:T(8,128)(2,1)S(1)}, bf16[512,384]{1,0:T(8,128)(2,1)S(1)}, u32[]{:S(2)}, u32[]{:S(2)}) %collective-permute-start.35) | collective-permute-done | bytes 393248 | tf_op jit(solution)/shard_map/ppermute | solution.py:46
  122.0 6.0 %collective-permute-done.37.up_hi = bf16[512,384]{1,0:T(8,128)(2,1)S(1)} collective-permute-done((bf16[512,384]{1,0:T(8,128)(2,1)S(1)}, bf16[512,384]{1,0:T(8,128)(2,1)S(1)}, u32[]{:S(2)}, u32[]{:S(2)}) %collective-permute-start.37) | collective-permute-done | bytes 393248 | tf_op jit(solution)/shard_map/ppermute | solution.py:42
  128.4 3.5 %shard_map.69 = bf16[1024,384]{1,0:T(8,128)(2,1)} custom-call(bf16[512,384]{1,0:T(8,128)(2,1)S(1)} %get-tuple-element.90.refs_0_, bf16[512,384]{1,0:T(8,128)(2,1)S(1)} %collective-permute-done.25.refs_1_, bf16[512,384]{1,0:T(8,128)(2,1)S(1)} %collective-permute-done.26.refs_2_, bf16[512,384]{1,0:T(8,128)(2,1)S(1)} %collective-permute-done.27.refs_3_, ...), custom_call_target="tpu_custom_call" | custom-call | bytes 1024 | tf_op jit(solution)/shard_map/pallas_call | solution.py:165
  (86 shorter events, 32.4 us)
Async XLA Ops:
  3.0 24.7 %collective-permute-start = (bf16[576,384]{1,0:T(8,128)(2,1)S(1)}, bf16[576,384]{1,0:T(8,128)(2,1)S(1)}, u32[]{:S(2)}, u32[]{:S(2)}) collective-permute-start(bf16[576,384]{1,0:T(8,128)(2,1)S(1)} %fusion.1.refs_0_), channel_id=1, source_target_pairs={{0,2},{1,3},{2,0},{3,1},{4,6},{5,7},{6,4},{7,5},{8,10},{9,11},{10,... | collective-permute-start | bytes 1327112 | tf_op jit(solution)/shard_map/ppermute | solution.py:46
  4.6 23.1 %collective-permute-start.4 = (bf16[576,384]{1,0:T(8,128)(2,1)S(1)}, bf16[576,384]{1,0:T(8,128)(2,1)S(1)}, u32[]{:S(2)}, u32[]{:S(2)}) collective-permute-start(bf16[576,384]{1,0:T(8,128)(2,1)S(1)} %fusion.1.refs_0_), channel_id=1, source_target_pairs={{0,1},{1,0},{2,3},{3,2},{4,5},{5,4},{6,7},{7,6},{8,9},{9,8},{10,11... | collective-permute-start | bytes 1327112 | tf_op jit(solution)/shard_map/ppermute | solution.py:50
  5.7 16.2 %collective-permute-start.1 = (bf16[64,384]{1,0:T(8,128)(2,1)S(1)}, bf16[64,384]{1,0:T(8,128)(2,1)S(1)}, u32[]{:S(2)}, u32[]{:S(2)}) collective-permute-start(bf16[64,384]{1,0:T(8,128)(2,1)S(1)} %get-tuple-element.126), channel_id=1, source_target_pairs={{0,4},{4,8},{8,12},{12,16},{16,20},{20,24},{24,28},{28,32},{32,36}... | collective-permute-start | bytes 147464 | tf_op jit(solution)/shard_map/ppermute | solution.py:42
  10.6 11.4 %collective-permute-start.2 = (bf16[64,384]{1,0:T(8,128)(2,1)S(1)}, bf16[64,384]{1,0:T(8,128)(2,1)S(1)}, u32[]{:S(2)}, u32[]{:S(2)}) collective-permute-start(bf16[64,384]{1,0:T(8,128)(2,1)S(1)} %get-tuple-element.125), channel_id=1, source_target_pairs={{4,0},{8,4},{12,8},{16,12},{20,16},{24,20},{28,24},{32,28},{36,32}... | collective-permute-start | bytes 147464 | tf_op jit(solution)/shard_map/ppermute | solution.py:42
  22.0 5.7 %collective-permute-start.3 = (bf16[128,384]{1,0:T(8,128)(2,1)S(1)}, bf16[128,384]{1,0:T(8,128)(2,1)S(1)}, u32[]{:S(2)}, u32[]{:S(2)}) collective-permute-start(bf16[128,384]{1,0:T(8,128)(2,1)S(1)} %shard_map.56.refs_5_), channel_id=1, source_target_pairs={{0,2},{1,3},{2,0},{3,1},{4,6},{5,7},{6,4},{7,5},{8,10},{9,11},{10,... | collective-permute-start | bytes 294920 | tf_op jit(solution)/shard_map/ppermute | solution.py:46
  22.2 12.2 %collective-permute-start.10 = (bf16[448,384]{1,0:T(8,128)(2,1)S(1)}, bf16[448,384]{1,0:T(8,128)(2,1)S(1)}, u32[]{:S(2)}, u32[]{:S(2)}) collective-permute-start(bf16[448,384]{1,0:T(8,128)(2,1)S(1)} %fusion.4.refs_9_), channel_id=1, source_target_pairs={{0,2},{1,3},{2,0},{3,1},{4,6},{5,7},{6,4},{7,5},{8,10},{9,11},{10,... | collective-permute-start | bytes 1032200 | tf_op jit(solution)/shard_map/ppermute | solution.py:46
  33.5 12.0 %collective-permute-start.14 = (bf16[512,384]{1,0:T(8,128)(2,1)S(1)}, bf16[512,384]{1,0:T(8,128)(2,1)S(1)}, u32[]{:S(2)}, u32[]{:S(2)}) collective-permute-start(bf16[512,384]{1,0:T(8,128)(2,1)S(1)} %get-tuple-element.72.refs_0_), channel_id=1, source_target_pairs={{0,2},{1,3},{2,0},{3,1},{4,6},{5,7},{6,4},{7,5},{8,10},{9,11},{10,... | collective-permute-start | bytes 1179656 | tf_op jit(solution)/shard_map/ppermute | solution.py:46
  34.4 11.9 %collective-permute-start.13 = (bf16[512,384]{1,0:T(8,128)(2,1)S(1)}, bf16[512,384]{1,0:T(8,128)(2,1)S(1)}, u32[]{:S(2)}, u32[]{:S(2)}) collective-permute-start(bf16[512,384]{1,0:T(8,128)(2,1)S(1)} %get-tuple-element.72.refs_0_), channel_id=1, source_target_pairs={{0,1},{1,0},{2,3},{3,2},{4,5},{5,4},{6,7},{7,6},{8,9},{9,8},{10,11... | collective-permute-start | bytes 1179656 | tf_op jit(solution)/shard_map/ppermute | solution.py:50
  39.6 14.4 %collective-permute-start.12 = (bf16[512,384]{1,0:T(8,128)(2,1)S(1)}, bf16[512,384]{1,0:T(8,128)(2,1)S(1)}, u32[]{:S(2)}, u32[]{:S(2)}) collective-permute-start(bf16[512,384]{1,0:T(8,128)(2,1)S(1)} %get-tuple-element.78.refs_0_), channel_id=1, source_target_pairs={{0,2},{1,3},{2,0},{3,1},{4,6},{5,7},{6,4},{7,5},{8,10},{9,11},{10,... | collective-permute-start | bytes 1179656 | tf_op jit(solution)/shard_map/ppermute | solution.py:46
  46.2 8.4 %collective-permute-start.17 = (bf16[512,384]{1,0:T(8,128)(2,1)S(1)}, bf16[512,384]{1,0:T(8,128)(2,1)S(1)}, u32[]{:S(2)}, u32[]{:S(2)}) collective-permute-start(bf16[512,384]{1,0:T(8,128)(2,1)S(1)} %get-tuple-element.78.refs_0_), channel_id=1, source_target_pairs={{0,1},{1,0},{2,3},{3,2},{4,5},{5,4},{6,7},{7,6},{8,9},{9,8},{10,11... | collective-permute-start | bytes 1179656 | tf_op jit(solution)/shard_map/ppermute | solution.py:50
  49.6 17.8 %collective-permute-start.22 = (bf16[512,384]{1,0:T(8,128)(2,1)S(1)}, bf16[512,384]{1,0:T(8,128)(2,1)S(1)}, u32[]{:S(2)}, u32[]{:S(2)}) collective-permute-start(bf16[512,384]{1,0:T(8,128)(2,1)S(1)} %get-tuple-element.84), channel_id=1, source_target_pairs={{0,4},{4,8},{8,12},{12,16},{16,20},{20,24},{24,28},{28,32},{32,36}... | collective-permute-start | bytes 1179656 | tf_op jit(solution)/shard_map/ppermute | solution.py:42
  58.1 19.7 %collective-permute-start.20 = (bf16[512,384]{1,0:T(8,128)(2,1)S(1)}, bf16[512,384]{1,0:T(8,128)(2,1)S(1)}, u32[]{:S(2)}, u32[]{:S(2)}) collective-permute-start(bf16[512,384]{1,0:T(8,128)(2,1)S(1)} %get-tuple-element.81), channel_id=1, source_target_pairs={{4,0},{8,4},{12,8},{16,12},{20,16},{24,20},{28,24},{32,28},{36,32}... | collective-permute-start | bytes 1179656 | tf_op jit(solution)/shard_map/ppermute | solution.py:42
  68.6 23.2 %collective-permute-start.23 = (bf16[512,384]{1,0:T(8,128)(2,1)S(1)}, bf16[512,384]{1,0:T(8,128)(2,1)S(1)}, u32[]{:S(2)}, u32[]{:S(2)}) collective-permute-start(bf16[512,384]{1,0:T(8,128)(2,1)S(1)} %get-tuple-element.90.refs_0_), channel_id=1, source_target_pairs={{0,16},{4,20},{8,24},{12,28},{16,32},{20,36},{24,40},{28,44},{32,4... | collective-permute-start | bytes 1179656 | tf_op jit(solution)/shard_map/ppermute | solution.py:42
  70.5 22.4 %collective-permute-start.24 = (bf16[512,384]{1,0:T(8,128)(2,1)S(1)}, bf16[512,384]{1,0:T(8,128)(2,1)S(1)}, u32[]{:S(2)}, u32[]{:S(2)}) collective-permute-start(bf16[512,384]{1,0:T(8,128)(2,1)S(1)} %get-tuple-element.90.refs_0_), channel_id=1, source_target_pairs={{16,0},{20,4},{24,8},{28,12},{32,16},{36,20},{40,24},{44,28},{48,3... | collective-permute-start | bytes 1179656 | tf_op jit(solution)/shard_map/ppermute | solution.py:42
  79.0 13.9 %collective-permute-start.21 = (bf16[512,384]{1,0:T(8,128)(2,1)S(1)}, bf16[512,384]{1,0:T(8,128)(2,1)S(1)}, u32[]{:S(2)}, u32[]{:S(2)}) collective-permute-start(bf16[512,384]{1,0:T(8,128)(2,1)S(1)} %get-tuple-element.109.refs_0_), channel_id=1, source_target_pairs={{0,2},{1,3},{2,0},{3,1},{4,6},{5,7},{6,4},{7,5},{8,10},{9,11},{10,... | collective-permute-start | bytes 1179656 | tf_op jit(solution)/shard_map/ppermute | solution.py:46
  81.2 12.8 %collective-permute-start.28 = (bf16[512,384]{1,0:T(8,128)(2,1)S(1)}, bf16[512,384]{1,0:T(8,128)(2,1)S(1)}, u32[]{:S(2)}, u32[]{:S(2)}) collective-permute-start(bf16[512,384]{1,0:T(8,128)(2,1)S(1)} %get-tuple-element.109.refs_0_), channel_id=1, source_target_pairs={{0,1},{1,0},{2,3},{3,2},{4,5},{5,4},{6,7},{7,6},{8,9},{9,8},{10,11... | collective-permute-start | bytes 1179656 | tf_op jit(solution)/shard_map/ppermute | solution.py:50
  94.1 14.4 %collective-permute-start.26 = (bf16[512,384]{1,0:T(8,128)(2,1)S(1)}, bf16[512,384]{1,0:T(8,128)(2,1)S(1)}, u32[]{:S(2)}, u32[]{:S(2)}) collective-permute-start(bf16[512,384]{1,0:T(8,128)(2,1)S(1)} %get-tuple-element.90.refs_0_), channel_id=1, source_target_pairs={{0,2},{1,3},{2,0},{3,1},{4,6},{5,7},{6,4},{7,5},{8,10},{9,11},{10,... | collective-permute-start | bytes 1179656 | tf_op jit(solution)/shard_map/ppermute | solution.py:46
  97.6 16.9 %collective-permute-start.33 = (bf16[512,384]{1,0:T(8,128)(2,1)S(1)}, bf16[512,384]{1,0:T(8,128)(2,1)S(1)}, u32[]{:S(2)}, u32[]{:S(2)}) collective-permute-start(bf16[512,384]{1,0:T(8,128)(2,1)S(1)} %collective-permute-done.23.refs_4_), channel_id=1, source_target_pairs={{0,2},{1,3},{2,0},{3,1},{4,6},{5,7},{6,4},{7,5},{8,10},{9,11},{10,... | collective-permute-start | bytes 1179656 | tf_op jit(solution)/shard_map/ppermute | solution.py:46
  98.0 24.0 %collective-permute-start.35 = (bf16[512,384]{1,0:T(8,128)(2,1)S(1)}, bf16[512,384]{1,0:T(8,128)(2,1)S(1)}, u32[]{:S(2)}, u32[]{:S(2)}) collective-permute-start(bf16[512,384]{1,0:T(8,128)(2,1)S(1)} %collective-permute-done.24.refs_8_), channel_id=1, source_target_pairs={{0,2},{1,3},{2,0},{3,1},{4,6},{5,7},{6,4},{7,5},{8,10},{9,11},{10,... | collective-permute-start | bytes 1179656 | tf_op jit(solution)/shard_map/ppermute | solution.py:46
  99.7 22.4 %collective-permute-start.38 = (bf16[512,384]{1,0:T(8,128)(2,1)S(1)}, bf16[512,384]{1,0:T(8,128)(2,1)S(1)}, u32[]{:S(2)}, u32[]{:S(2)}) collective-permute-start(bf16[512,384]{1,0:T(8,128)(2,1)S(1)} %get-tuple-element.102), channel_id=1, source_target_pairs={{16,0},{20,4},{24,8},{28,12},{32,16},{36,20},{40,24},{44,28},{48,3... | collective-permute-start | bytes 1179656 | tf_op jit(solution)/shard_map/ppermute | solution.py:42
  105.5 22.6 %collective-permute-start.37 = (bf16[512,384]{1,0:T(8,128)(2,1)S(1)}, bf16[512,384]{1,0:T(8,128)(2,1)S(1)}, u32[]{:S(2)}, u32[]{:S(2)}) collective-permute-start(bf16[512,384]{1,0:T(8,128)(2,1)S(1)} %get-tuple-element.114), channel_id=1, source_target_pairs={{0,16},{4,20},{8,24},{12,28},{16,32},{20,36},{24,40},{28,44},{32,4... | collective-permute-start | bytes 1179656 | tf_op jit(solution)/shard_map/ppermute | solution.py:42
  108.4 19.9 %collective-permute-start.27 = (bf16[512,384]{1,0:T(8,128)(2,1)S(1)}, bf16[512,384]{1,0:T(8,128)(2,1)S(1)}, u32[]{:S(2)}, u32[]{:S(2)}) collective-permute-start(bf16[512,384]{1,0:T(8,128)(2,1)S(1)} %collective-permute-done.26.refs_2_), channel_id=1, source_target_pairs={{0,1},{1,0},{2,3},{3,2},{4,5},{5,4},{6,7},{7,6},{8,9},{9,8},{10,11... | collective-permute-start | bytes 1179656 | tf_op jit(solution)/shard_map/ppermute | solution.py:50
  114.5 13.9 %collective-permute-start.34 = (bf16[512,384]{1,0:T(8,128)(2,1)S(1)}, bf16[512,384]{1,0:T(8,128)(2,1)S(1)}, u32[]{:S(2)}, u32[]{:S(2)}) collective-permute-start(bf16[512,384]{1,0:T(8,128)(2,1)S(1)} %collective-permute-done.33.refs_6_), channel_id=1, source_target_pairs={{0,1},{1,0},{2,3},{3,2},{4,5},{5,4},{6,7},{7,6},{8,9},{9,8},{10,11... | collective-permute-start | bytes 1179656 | tf_op jit(solution)/shard_map/ppermute | solution.py:50
  122.0 6.3 %collective-permute-start.36 = (bf16[512,384]{1,0:T(8,128)(2,1)S(1)}, bf16[512,384]{1,0:T(8,128)(2,1)S(1)}, u32[]{:S(2)}, u32[]{:S(2)}) collective-permute-start(bf16[512,384]{1,0:T(8,128)(2,1)S(1)} %collective-permute-done.35.refs_10_), channel_id=1, source_target_pairs={{0,1},{1,0},{2,3},{3,2},{4,5},{5,4},{6,7},{7,6},{8,9},{9,8},{10,11... | collective-permute-start | bytes 1179656 | tf_op jit(solution)/shard_map/ppermute | solution.py:50
  (17 other events, 45.4 us)
